TPU v7x, 32 devices: a whole 2x2x4 slice. The times are simulated.
32 devices in a mesh: slab: 4 (over y, core), ray: 8 (over z, x).
Axes of the slice: x: 2, y: 2, z: 4, core: 2. Of those that a mesh axis runs over, the one named last changes fastest.
Arguments:
- intensity: float32 [4, 8, 256, 2048], P('slab', 'ray'), may hold values from 0.2 to 1
- angles: float32 [4, 8], replicated, may hold values from 0 to 3.14159
- volume: float32 [256, 64, 256], P('slab', 'ray'), may hold values from -3 to 3
- vol_list: int32 [64], replicated, may hold values from 0 to 63, as said below
Outputs:
- reconstruction: float32 [256, 64, 256], P('slab', 'ray')
- residual: float32 [4, 8, 256, 2048], P(None, 'ray', 'slab')
Inputs may be any that keep to these rules, and one draw needn't show every extreme that they name: vol_list is a permutation of the patch ids that follows a Hilbert curve over the 8 x 8 grid of patches.
All inputs are finite; a program needn't handle non-finite values.
Results may differ from a plain program's by a relative error of at most 0.0003.
Values sent between devices are 32-bit elements; how exact they have to be, the bound alone decides.
No kernel may reach another device: no remote copies, remote signals or barrier semaphores. Data moves between devices by JAX's collectives and lax.ppermute only.
A program may use at most 192 MiB of HBM per device.

v0:
```python
import math

import jax
import jax.numpy as jnp
from jax import lax
from jax.sharding import PartitionSpec as P

BAND = 2048
TR = 32
PGRID = 8
ROI = 128


paganin_strength = 10.0
relax = 1.8
row_floor = 0.25
highest = lax.Precision.HIGHEST


def split_length(length):
    return max((divisor for divisor in range(1, math.isqrt(length) + 1) if length % divisor == 0))


def phase_table(count_a, count_b, total):
    index_a = jnp.arange(count_a, dtype=jnp.int32)[:, None]
    index_b = jnp.arange(count_b, dtype=jnp.int32)[None, :]
    phases = (index_a * index_b % total).astype(jnp.float32) * (2.0 * jnp.pi / total)
    return (jnp.cos(phases), jnp.sin(phases))


def permuted_freq(length, outer):
    inner = length // outer
    position = jnp.arange(length, dtype=jnp.int32)
    return position // inner + outer * (position % inner)


def gain_values(row_freq, col_freq, height, width_px):
    row_part = 2.0 - 2.0 * jnp.cos(2.0 * jnp.pi * row_freq.astype(jnp.float32) / height)
    col_part = 2.0 - 2.0 * jnp.cos(2.0 * jnp.pi * col_freq.astype(jnp.float32) / width_px)
    return 1.0 / (1.0 + paganin_strength * (row_part[:, None] + col_part[None, :]))


def cols_outer(table, values):
    return jnp.einsum("kn,asnm->askm", table, values, precision=highest)


def cols_inner(values, table):
    return jnp.einsum("askm,ml->askl", values, table, precision=highest)


def rows_outer(table, values):
    return jnp.einsum("kn,anmc->akmc", table, values, precision=highest)


def rows_inner(table, values):
    return jnp.einsum("lm,akmc->aklc", table, values, precision=highest)


def paganin(images):
    num_images, height, width_px = images.shape
    inner_cols = min(width_px, 128)
    outer_cols = width_px // inner_cols
    outer_rows = split_length(height)
    inner_rows = height // outer_rows
    col_outer_cos, col_outer_sin = phase_table(outer_cols, outer_cols, outer_cols)
    col_turn_cos, col_turn_sin = phase_table(outer_cols, inner_cols, width_px)
    col_inner_cos, col_inner_sin = phase_table(inner_cols, inner_cols, inner_cols)
    row_outer_cos, row_outer_sin = phase_table(outer_rows, outer_rows, outer_rows)
    row_turn_cos, row_turn_sin = phase_table(outer_rows, inner_rows, height)
    row_turn_cos = row_turn_cos[None, :, :, None]
    row_turn_sin = row_turn_sin[None, :, :, None]
    row_inner_cos, row_inner_sin = phase_table(inner_rows, inner_rows, inner_rows)
    col_shape = (num_images, height, outer_cols, inner_cols)
    row_shape = (num_images, outer_rows, inner_rows, width_px)
    pieces = images.reshape(col_shape)
    first_real = cols_outer(col_outer_cos, pieces)
    first_imag = -cols_outer(col_outer_sin, pieces)
    turned_real = first_real * col_turn_cos + first_imag * col_turn_sin
    turned_imag = first_imag * col_turn_cos - first_real * col_turn_sin
    col_real = (
        cols_inner(turned_real, col_inner_cos) + cols_inner(turned_imag, col_inner_sin)
    ).reshape(row_shape)
    col_imag = (
        cols_inner(turned_imag, col_inner_cos) - cols_inner(turned_real, col_inner_sin)
    ).reshape(row_shape)
    row_real = rows_outer(row_outer_cos, col_real) + rows_outer(row_outer_sin, col_imag)
    row_imag = rows_outer(row_outer_cos, col_imag) - rows_outer(row_outer_sin, col_real)
    mixed_real = row_real * row_turn_cos + row_imag * row_turn_sin
    mixed_imag = row_imag * row_turn_cos - row_real * row_turn_sin
    gain_table = gain_values(
        permuted_freq(height, outer_rows), permuted_freq(width_px, outer_cols), height, width_px
    ).reshape(1, outer_rows, inner_rows, width_px)
    spec_real = (
        rows_inner(row_inner_cos, mixed_real) + rows_inner(row_inner_sin, mixed_imag)
    ) * gain_table
    spec_imag = (
        rows_inner(row_inner_cos, mixed_imag) - rows_inner(row_inner_sin, mixed_real)
    ) * gain_table
    back_real = rows_inner(row_inner_cos, spec_real) - rows_inner(row_inner_sin, spec_imag)
    back_imag = rows_inner(row_inner_cos, spec_imag) + rows_inner(row_inner_sin, spec_real)
    reverted_real = back_real * row_turn_cos - back_imag * row_turn_sin
    reverted_imag = back_imag * row_turn_cos + back_real * row_turn_sin
    rows_real = (
        rows_outer(row_outer_cos, reverted_real) - rows_outer(row_outer_sin, reverted_imag)
    ).reshape(col_shape)
    rows_imag = (
        rows_outer(row_outer_cos, reverted_imag) + rows_outer(row_outer_sin, reverted_real)
    ).reshape(col_shape)
    last_real = cols_inner(rows_real, col_inner_cos) - cols_inner(rows_imag, col_inner_sin)
    last_imag = cols_inner(rows_imag, col_inner_cos) + cols_inner(rows_real, col_inner_sin)
    final_real = last_real * col_turn_cos - last_imag * col_turn_sin
    final_imag = last_imag * col_turn_cos + last_real * col_turn_sin
    result = (
        cols_outer(col_outer_cos, final_real) - cols_outer(col_outer_sin, final_imag)
    ).reshape(num_images, height, width_px)
    offset = (width_px - BAND) // 2
    return result / (height * width_px)


def mat_dot(left_op, right_op):
    return jnp.dot(left_op, right_op, precision=highest, preferred_element_type=jnp.float32)


def ray_windows(patch_ids, theta):
    half_roi = (ROI - 1) / 2.0
    half_band = (BAND - 1) / 2.0
    centre_x = (patch_ids // PGRID).astype(jnp.float32) * 16.0 + 7.5 - half_roi
    centre_y = (patch_ids % PGRID).astype(jnp.float32) * 16.0 + 7.5 - half_roi
    centre = (
        half_band
        + centre_x[:, None] * jnp.cos(theta)[None, :]
        + centre_y[:, None] * jnp.sin(theta)[None, :]
    )
    starts = jnp.floor(centre).astype(jnp.int32) - 15
    return starts[:, :, None] + jnp.arange(TR, dtype=jnp.int32)[None, None, :]


def tile_weights(patch_id, theta):
    half_roi = (ROI - 1) / 2.0
    half_band = (BAND - 1) / 2.0
    ray_index = ray_windows(jnp.reshape(patch_id, (1,)), theta)[0]
    voxels = jnp.arange(256, dtype=jnp.int32)
    voxel_x = (
        (patch_id // PGRID).astype(jnp.float32) * 16.0
        + (voxels // 16).astype(jnp.float32)
        - half_roi
    )
    voxel_y = (
        (patch_id % PGRID).astype(jnp.float32) * 16.0 + (voxels % 16).astype(jnp.float32) - half_roi
    )
    cosine = jnp.cos(theta)
    sine = jnp.sin(theta)
    along = (
        voxel_x[:, None, None] * cosine[None, :, None]
        + voxel_y[:, None, None] * sine[None, :, None]
    )
    distance = (ray_index.astype(jnp.float32) - half_band)[None, :, :] - along
    weights = jnp.maximum(0.0, 1.0 - jnp.abs(distance)) / ROI
    return (weights.reshape(256, -1), ray_index)


def window_index(starts):
    num_angles = starts.shape[1]
    window_lane = jnp.arange(TR, dtype=jnp.int32)
    angle_base = jnp.arange(num_angles, dtype=jnp.int32) * BAND
    return (angle_base[None, :, None] + starts[:, :, None] + window_lane[None, None, :]).reshape(-1)


def place_windows(tiles, starts):
    num_rows = tiles.shape[0]
    num_angles = starts.shape[1]
    flat_index = window_index(starts)
    empty = jnp.zeros((num_rows, num_angles * BAND), jnp.float32)
    return empty.at[:, flat_index].add(tiles.reshape(num_rows, -1))


def take_windows(values, starts):
    flat_index = window_index(starts)
    return values[:, flat_index].reshape(values.shape[0], starts.shape[0], starts.shape[1], TR)


def local(intensity, angles, volume, vol_list):
    per_device = intensity.shape[0]
    n_slab = lax.axis_size("slab")
    n_ray = lax.axis_size("ray")
    slab_rows = intensity.shape[2] // n_slab
    images = intensity.reshape(per_device, intensity.shape[2], intensity.shape[3])
    projected = -jnp.log(paganin(images))
    pieces = projected.reshape(per_device, n_slab, slab_rows, BAND)
    moved = lax.all_to_all(pieces, "slab", split_axis=1, concat_axis=0, tiled=True)
    own_count = moved.shape[0]
    sinogram = jnp.transpose(moved[:, 0], (1, 0, 2)).reshape(slab_rows, own_count * BAND)
    rank = lax.axis_index("ray")
    theta_own = lax.dynamic_index_in_dim(angles, rank, 1, keepdims=False)
    slots = volume.shape[1]
    num_patches = vol_list.shape[0]
    step_size = relax * ROI / (angles.shape[0] * angles.shape[1])
    starts = ray_windows(vol_list, theta_own)[:, :, 0]
    my_ids = lax.dynamic_slice_in_dim(vol_list, rank * slots, slots)
    theta_all = jnp.transpose(angles).reshape(-1)

    def forward(current, with_sums):
        values = []
        sums = []
        for slot_idx in range(slots):
            weights, _ = tile_weights(my_ids[slot_idx], theta_all)
            values.append(mat_dot(current[:, slot_idx, :], weights))
            if with_sums:
                sums.append(jnp.sum(weights, axis=0))
        stacked = jnp.stack(values, axis=1).reshape(slab_rows, slots, n_ray, own_count * TR)
        if with_sums:
            sum_rows = jnp.stack(sums, axis=0).reshape(1, slots, n_ray, own_count * TR)
            got_vals, got_sums = (
                lax.all_to_all(stacked, "ray", split_axis=2, concat_axis=1, tiled=True),
                lax.all_to_all(sum_rows, "ray", split_axis=2, concat_axis=1, tiled=True),
            )
            tiles = jnp.concatenate(
                [
                    got_vals.reshape(slab_rows, num_patches, own_count, TR),
                    got_sums.reshape(1, num_patches, own_count, TR),
                ],
                axis=0,
            )
            placed = place_windows(tiles, starts)
            return (placed[:slab_rows], placed[slab_rows])
        got_vals = lax.all_to_all(stacked, "ray", split_axis=2, concat_axis=1, tiled=True)
        return (
            place_windows(got_vals.reshape(slab_rows, num_patches, own_count, TR), starts),
            None,
        )

    def backward(scaled):
        windows = take_windows(scaled, starts).reshape(slab_rows, num_patches, 1, own_count * TR)
        got_back = lax.all_to_all(windows, "ray", split_axis=1, concat_axis=2, tiled=True).reshape(
            slab_rows, slots, -1
        )
        updates = []
        for slot_idx in range(slots):
            weights, _ = tile_weights(my_ids[slot_idx], theta_all)
            updates.append(
                lax.dot_general(
                    got_back[:, slot_idx, :],
                    weights,
                    (((1,), (1,)), ((), ())),
                    precision=highest,
                    preferred_element_type=jnp.float32,
                )
            )
        return jnp.stack(updates, axis=1)

    predicted, row_sums = forward(volume, True)
    row_weight = 1.0 / jnp.maximum(row_sums, row_floor)
    difference = sinogram - predicted
    first_iterate = volume + step_size * backward(difference * row_weight[None, :])
    predicted_next, _ = forward(first_iterate, False)
    residual = sinogram - predicted_next
    reconstruction = first_iterate + step_size * backward(residual * row_weight[None, :])
    residual_out = jnp.transpose(residual.reshape(slab_rows, own_count, BAND), (1, 0, 2))[:, None]
    return (reconstruction, residual_out)


def solution(mesh):
    placed = (P("slab", "ray", None, None), P(), P("slab", "ray", None), P())
    return jax.shard_map(
        local,
        mesh=mesh,
        in_specs=placed,
        out_specs=(P("slab", "ray", None), P(None, "ray", "slab", None)),
        check_vma=False,
    )
```

profile of v0, /device:TPU:0, one launch (start us, length us, event | category | flops | bytes accessed | tf_op | source)
XLA Modules:
  0.0 630.8 jit_solution(9062803580758378952)
XLA Ops:
  9.5 3.8 fusion.55
  13.6 2.8 fusion.66
  18.9 2.7 reshape.2422
  21.7 6.1 fusion.47
  36.4 4.5 fusion.51
  40.9 6.3 fusion.9
  47.3 6.1 subtract_bitcast_fusion.1
  53.4 3.4 fusion.45
  56.7 3.2 fusion.41
  59.9 3.5 fusion.12
  63.5 3.6 fusion.14
  73.5 3.0 subtract_bitcast_fusion
  76.5 3.2 fusion.39
  79.7 3.6 fusion.35
  83.2 3.3 fusion.3
  90.7 2.8 fusion.27
  93.5 3.2 fusion.4
  100.9 3.0 multiply_subtract_fusion
  103.9 3.5 fusion.19
  107.4 3.4 negate_bitcast_fusion
  112.3 4.6 all-to-all-start
  179.0 7.4 %all-to-all-start.1 = ((f32[64,8,8,128]{3,0,1,2:T(8,128)}), f32[64,8,8,128]{3,0,1,2:T(8,128)}, u32[]{:S(2)}, u32[]{:S(2)}) async-start(f32[64,8,8,128]{3,0,1,2:T(8,128)} %copy_dynamic-update-slice_fusion), calls=%async_computation.1 | async-start | bytes 4194304 | tf_op jit(solution)/shard_map/all_to_all | solution.py:214
  198.0 37.3 %all-to-all-done.1 = f32[64,8,8,128]{3,0,1,2:T(8,128)} async-done(((f32[64,8,8,128]{3,0,1,2:T(8,128)}), f32[64,8,8,128]{3,0,1,2:T(8,128)}, u32[]{:S(2)}, u32[]{:S(2)}) %all-to-all-start.1) | async-done | bytes 2097184 | tf_op jit(solution)/shard_map/all_to_all | solution.py:214
  235.3 3.6 all-to-all-start.2
  239.0 3.8 copy.214
  242.8 4.1 copy.234
  246.9 2.8 concatenate.11
  249.7 3.2 maximum_bitcast_fusion
  252.9 4.9 copy.235
  257.8 46.5 %scatter_custom_fusion = f32[65,8192]{0,1:T(8,128)} fusion(s32[8192]{0:T(1024)S(1)} %bitcast.715, f32[8192,65]{1,0:T(8,128)} %copy.235, f32[]{:T(128)} %constant.879.clone.1), kind=kCustom, calls=%fused_computation.49 | custom fusion | flops 532480 | bytes 2130432 | tf_op jit(solution)/shard_map/scatter-add | solution.py:174
  304.3 4.6 fusion.2
  308.9 4.2 fusion.1
  313.2 30.1 %gather_fusion = f32[8192,64]{1,0:T(8,128)} fusion(f32[64,8192]{0,1:T(8,128)} %fusion.1, s32[8192]{0:T(1024)S(1)} %broadcast_clamp_fusion), kind=kCustom, calls=%fused_computation | custom fusion | bytes 4227072 | tf_op jit(solution)/shard_map/gather | solution.py:179
  343.3 3.8 copy.236
  347.1 6.3 %all-to-all-start.3 = ((f32[64,64,1,128]{3,0,2,1:T(8,128)}), f32[64,64,1,128]{3,0,2,1:T(8,128)}, u32[]{:S(2)}, u32[]{:S(2)}) async-start(f32[64,64,1,128]{3,0,2,1:T(8,128)} %copy.236), calls=%async_computation.3 | async-start | bytes 4194304 | tf_op jit(solution)/shard_map/all_to_all | solution.py:234
  365.0 36.2 %all-to-all-done.3 = f32[64,64,1,128]{3,0,2,1:T(8,128)} async-done(((f32[64,64,1,128]{3,0,2,1:T(8,128)}), f32[64,64,1,128]{3,0,2,1:T(8,128)}, u32[]{:S(2)}, u32[]{:S(2)}) %all-to-all-start.3) | async-done | bytes 2097184 | tf_op jit(solution)/shard_map/all_to_all | solution.py:234
  401.2 2.8 copy.407
  420.7 51.8 %all_to_all.84 = f32[64,8,8,128]{3,0,1,2:T(8,128)S(1)} all-to-all(f32[64,8,8,128]{3,0,1,2:T(8,128)S(1)} %copy.239), channel_id=1, replica_groups=mesh['slab'=4,'ray'=8] {'ray'}, dimensions={2} | all-to-all | bytes 4194304 | tf_op jit(solution)/shard_map/all_to_all | solution.py:226
  475.1 2.8 reshape.2469
  477.8 3.9 copy.241
  481.7 46.5 %scatter_custom_fusion.1 = f32[64,8192]{0,1:T(8,128)} fusion(s32[8192]{0:T(1024)} %bitcast.716, f32[8192,64]{1,0:T(8,128)} %copy.241, f32[]{:T(128)} %constant.879.clone.1), kind=kCustom, calls=%fused_computation.46 | custom fusion | flops 524288 | bytes 2097664 | tf_op jit(solution)/shard_map/scatter-add | solution.py:174
  528.2 6.0 broadcast_multiply_fusion
  534.2 30.1 %gather_fusion.1 = f32[8192,64]{1,0:T(8,128)} fusion(f32[64,8192]{0,1:T(8,128)} %get-tuple-element.14, s32[8192]{0:T(1024)S(1)} %broadcast_clamp_fusion), kind=kCustom, calls=%fused_computation.1 | custom fusion | bytes 4227072 | tf_op jit(solution)/shard_map/gather | solution.py:179
  564.3 3.8 copy.242
  568.1 4.5 all-to-all-start.5
  572.6 3.8 copy.244
  576.4 43.5 %all-to-all-done.5 = f32[64,64,1,128]{3,0,2,1:T(8,128)} async-done(((f32[64,64,1,128]{3,0,2,1:T(8,128)}), f32[64,64,1,128]{3,0,2,1:T(8,128)}, u32[]{:S(2)}, u32[]{:S(2)}) %all-to-all-start.5) | async-done | bytes 2097184 | tf_op jit(solution)/shard_map/all_to_all | solution.py:234
  619.9 2.8 copy.406
  (250 shorter events, 108.9 us)
Async XLA Ops:
  21.7 6.1 copy-start.18
  36.4 4.5 copy-start.19
  40.9 6.4 %copy-start.1 = (f32[16,16,2048]{2,1,0:T(8,128)S(1)}, f32[16,16,2048]{2,1,0:T(8,128)}, u32[]{:S(2)}) copy-start(f32[16,16,2048]{2,1,0:T(8,128)} %reshape.2422) | copy-start | bytes 6291460
  112.3 4.6 copy-start.49
  112.3 44.7 %copy-start.46 = (f32[4,8]{1,0:T(4,128)S(1)}, f32[4,8]{1,0:T(4,128)}, u32[]{:S(2)}) copy-start(f32[4,8]{1,0:T(4,128)} %param.5) | copy-start | bytes 388
  112.3 46.2 %copy-start.30 = (f32[64,8,256]{2,1,0:T(8,128)S(1)}, f32[64,8,256]{2,1,0:T(8,128)}, u32[]{:S(2)}) copy-start(f32[64,8,256]{2,1,0:T(8,128)} %param.6) | copy-start | bytes 1572868
  112.3 66.7 %all-to-all-start = ((f32[1,4,64,2048]{3,2,0,1:T(8,128)}), f32[1,4,64,2048]{3,2,0,1:T(8,128)}, u32[]{:S(2)}, u32[]{:S(2)}) async-start(f32[1,4,64,2048]{3,2,0,1:T(8,128)} %bitcast.689), calls=%async_computation | async-start | bytes 4194304 | tf_op jit(solution)/shard_map/all_to_all | solution.py:190
  158.0 2.7 copy-start.32
  162.8 3.2 copy-start.34
  162.9 3.2 copy-start.36
  163.7 3.4 copy-start.3
  166.2 3.3 copy-start.38
  166.3 3.2 copy-start.40
  167.1 4.0 copy-start.6
  167.1 4.0 copy-start.9
  167.1 2.4 copy-start.48
  167.1 2.5 copy-start.47
  169.6 3.8 copy-start.41
  169.7 3.8 copy-start.42
  171.1 3.2 copy-start.12
  171.1 3.2 copy-start.15
  179.0 10.1 %copy-start.45 = (f32[32,32]{1,0:T(8,128)S(1)}, f32[32,32]{1,0:T(8,128)}, u32[]{:S(2)}) copy-start(f32[32,32]{1,0:T(8,128)} %get-tuple-element.92) | copy-start | bytes 12292
  179.0 10.7 %copy-start.44 = (f32[32,32]{1,0:T(8,128)S(1)}, f32[32,32]{1,0:T(8,128)}, u32[]{:S(2)}) copy-start(f32[32,32]{1,0:T(8,128)} %get-tuple-element.41) | copy-start | bytes 12292
  179.0 56.3 %all-to-all-start.1 = ((f32[64,8,8,128]{3,0,1,2:T(8,128)}), f32[64,8,8,128]{3,0,1,2:T(8,128)}, u32[]{:S(2)}, u32[]{:S(2)}) async-start(f32[64,8,8,128]{3,0,1,2:T(8,128)} %copy_dynamic-update-slice_fusion), calls=%async_computation.1 | async-start | bytes 4194304 | tf_op jit(solution)/shard_map/all_to_all | solution.py:214
  198.0 59.8 %copy-start.43 = (s32[8192,1]{0,1:T(1,128)}, s32[8192,1]{0,1:T(1,128)S(1)}, u32[]{:S(2)}) copy-start(s32[8192,1]{0,1:T(1,128)S(1)} %compare_select_fusion) | copy-start | bytes 98308
  235.3 14.4 %all-to-all-start.2 = ((f32[1,8,8,128]{3,1,0,2:T(8,128)}), f32[1,8,8,128]{3,1,0,2:T(8,128)S(1)}, u32[]{:S(2)}, u32[]{:S(2)}) async-start(f32[1,8,8,128]{3,1,0,2:T(8,128)} %stack.136), calls=%async_computation.2 | async-start | bytes 65536 | tf_op jit(solution)/shard_map/all_to_all | solution.py:215
  304.3 4.6 copy-start
  347.1 6.4 %copy-start.33 = (f32[32,32]{1,0:T(8,128)S(1)}, f32[32,32]{1,0:T(8,128)}, u32[]{:S(2)}) copy-start(f32[32,32]{1,0:T(8,128)} %copy-done.32) | copy-start | bytes 12292
  347.1 7.7 %copy-start.37 = (f32[32,32]{1,0:T(8,128)S(1)}, f32[32,32]{1,0:T(8,128)}, u32[]{:S(2)}) copy-start(f32[32,32]{1,0:T(8,128)} %copy-done.36) | copy-start | bytes 12292
  347.1 7.8 %copy-start.35 = (f32[32,32]{1,0:T(8,128)S(1)}, f32[32,32]{1,0:T(8,128)}, u32[]{:S(2)}) copy-start(f32[32,32]{1,0:T(8,128)} %copy-done.34) | copy-start | bytes 12292
  347.1 8.6 %copy-start.39 = (f32[32,32]{1,0:T(8,128)S(1)}, f32[32,32]{1,0:T(8,128)}, u32[]{:S(2)}) copy-start(f32[32,32]{1,0:T(8,128)} %copy-done.38) | copy-start | bytes 12292
  347.1 54.1 %all-to-all-start.3 = ((f32[64,64,1,128]{3,0,2,1:T(8,128)}), f32[64,64,1,128]{3,0,2,1:T(8,128)}, u32[]{:S(2)}, u32[]{:S(2)}) async-start(f32[64,64,1,128]{3,0,2,1:T(8,128)} %copy.236), calls=%async_computation.3 | async-start | bytes 4194304 | tf_op jit(solution)/shard_map/all_to_all | solution.py:234
  406.7 2.0 copy-start.7
  407.4 2.0 copy-start.16
  408.1 2.0 copy-start.13
  408.8 2.0 copy-start.31
  410.1 2.0 copy-start.22
  410.8 2.5 copy-start.27
  411.0 8.4 %copy-start.20 = (f32[64,8,256]{2,0,1:T(8,128)}, f32[64,8,256]{2,0,1:T(8,128)S(1)}, u32[]{:S(2)}) copy-start(f32[64,8,256]{2,0,1:T(8,128)S(1)} %multiply_add_fusion.2) | copy-start | bytes 1572868
  411.0 3.4 copy-start.23
  412.1 3.8 copy-start.28
  413.3 3.8 copy-start.24
  414.4 3.8 copy-start.29
  415.9 3.4 copy-start.25
  568.1 51.8 %all-to-all-start.5 = ((f32[64,64,1,128]{3,0,2,1:T(8,128)}), f32[64,64,1,128]{3,0,2,1:T(8,128)}, u32[]{:S(2)}, u32[]{:S(2)}) async-start(f32[64,64,1,128]{3,0,2,1:T(8,128)} %copy.242), calls=%async_computation.5 | async-start | bytes 4194304 | tf_op jit(solution)/shard_map/all_to_all | solution.py:234
  625.4 2.0 copy-start.8
  626.1 2.0 copy-start.17
  626.8 2.0 copy-start.14
  (7 other events, 11.6 us)
where the time goes:
time: 642 us; the launch traced here: 631 us
  local copies, waits for them, and re-layouts  145 us (23%)
  other arithmetic  127 us (20%)
  matrix products  122 us (19%)
  waiting for transfers between devices  117 us (18%)
  blocking collectives  51.8 us (8%)
  between operations  41.5 us (6%)
  starting transfers between devices  26.5 us (4%)
    scatter-add x2, other arithmetic, place_windows(): return empty.at[:, flat_index].add(tiles.reshape(num_rows, -1))  93.1 us
    all_to_all x2, waiting for transfers between devices, backward(): lax.all_to_all(windows, 'ray', split_axis=1, concat_axis=2, tiled=True)  79.7 us
    gather x2, local copies, waits for them, and re-layouts, take_windows(): values[:, flat_index]  60.2 us
    all_to_all x1, blocking collectives, forward(): lax.all_to_all(stacked, 'ray', split_axis=2, concat_axis=1, tiled=True)  51.8 us
    all_to_all x1, waiting for transfers between devices, forward(): lax.all_to_all(stacked, 'ray', split_axis=2, concat_axis=1, tiled=True)  37.3 us
    dot_general x8, matrix products, rows_outer(): return jnp.einsum('kn,anmc->akmc', table, values, precision=highest)  36.1 us
    dot_general x8, matrix products, rows_inner(): return jnp.einsum('lm,akmc->aklc', table, values, precision=highest)  23.1 us
    dot_general x8, matrix products, cols_inner(): return jnp.einsum('askm,ml->askl', values, table, precision=highest)  22.6 us
  transfers between devices with their start and end apart: 5, of which 3 were waited for; matrix products, arithmetic and copies ran while one was open for 9% of the time, Pallas kernels for 0%

commit v1 on v0

v1 whole, which is shorter than its diff:
```python
import functools
import math

import jax
import jax.numpy as jnp
import ml_dtypes
import numpy as np
from jax import lax
from jax.experimental import pallas as pl
from jax.experimental.pallas import tpu as pltpu
from jax.sharding import PartitionSpec as P

BAND = 2048
PGRID = 8
ROI = 128
SIDE = 16
VOX = SIDE * SIDE
WIN = 24
ACTIVE = 256
LANES = 128
ROWS = 8
SPLIT = 64

paganin_strength = 10.0
relax = 1.8
row_floor = 0.25

bf16 = jnp.bfloat16
f32 = jnp.float32


def halves(values):
    high = values.astype(bf16)
    low = (values - high.astype(f32)).astype(bf16)
    return high, low


def thirds(values):
    high = values.astype(bf16)
    rest = values - high.astype(f32)
    middle = rest.astype(bf16)
    low = (rest - middle.astype(f32)).astype(bf16)
    return high, middle, low


def dot(left, right):
    return jnp.dot(left, right, preferred_element_type=f32)


def numpy_halves(table):
    high = table.astype(ml_dtypes.bfloat16)
    low = (table - high.astype(np.float64)).astype(ml_dtypes.bfloat16)
    return high, low


def filter_tables(height):
    index = np.arange(height)
    phase = 2.0 * np.pi * (np.outer(index, index) % height) / height
    cas = (np.cos(phase) + np.sin(phase)) / math.sqrt(height)
    cas_high, cas_low = numpy_halves(cas)
    row_freq = 2.0 - 2.0 * np.cos(2.0 * np.pi * index / height)
    middle = (1.0 + paganin_strength * row_freq) / paganin_strength + 2.0
    rho = (middle - np.sqrt(middle * middle - 4.0)) / 2.0
    rho_wide = np.repeat(rho[:, None], LANES, axis=1).astype(np.float32)
    return cas_high, cas_low, rho_wide


def circular_decay(parts, rho, forward, lane):
    count = len(parts)
    step = 1
    power = rho
    while step < LANES:
        shift = step if forward else LANES - step
        turned = [pltpu.roll(part, shift, 1) for part in parts]
        if forward:
            keep = lane >= step
            moved = [jnp.where(keep, turned[i], turned[i - 1]) for i in range(count)]
        else:
            keep = lane < LANES - step
            moved = [jnp.where(keep, turned[i], turned[(i + 1) % count]) for i in range(count)]
        parts = [part + power * other for part, other in zip(parts, moved)]
        power = power * power
        step *= 2
    order = list(range(count)) if forward else list(range(count - 1, -1, -1))
    wrapped = parts[order[0]]
    for position in order[1:]:
        wrapped = parts[position] + power * wrapped
    whole = power
    for _ in range(int(math.log2(count))):
        whole = whole * whole
    carry = wrapped / (1.0 - whole)
    results = [None] * count
    for position in order:
        carry = parts[position] + power * carry
        results[position] = carry
    return results


def filter_kernel(image_ref, high_ref, low_ref, rho_ref, out_ref, active_ref, spec_ref):
    height, width = image_ref.shape
    tile = 256
    cas_high = high_ref[...]
    cas_low = low_ref[...]

    def transform(values):
        high, low = halves(values)
        return dot(cas_high, high) + dot(cas_high, low) + dot(cas_low, high)

    for start in range(0, width, tile):
        spec_ref[:, start : start + tile] = transform(1.0 - image_ref[:, start : start + tile])

    lane = lax.broadcasted_iota(jnp.int32, (ROWS, LANES), 1)

    def solve(index, carry):
        row = pl.ds(pl.multiple_of(index * ROWS, ROWS), ROWS)
        rho = rho_ref[row, :]
        scale = rho / paganin_strength
        parts = [
            spec_ref[row, start : start + LANES] * scale for start in range(0, width, LANES)
        ]
        parts = circular_decay(parts, rho, True, lane)
        parts = circular_decay(parts, rho, False, lane)
        for position, part in enumerate(parts):
            spec_ref[row, position * LANES : (position + 1) * LANES] = part
        return carry

    lax.fori_loop(0, height // ROWS, solve, 0)
    offset = (width - ACTIVE) // 2
    for start in range(0, width, tile):
        values = -jnp.log(1.0 - transform(spec_ref[:, start : start + tile]))
        out_ref[:, start : start + tile] = values
    active_ref[...] = out_ref[:, offset : offset + ACTIVE]


def paganin(image):
    height, width = image.shape
    tables = filter_tables(height)
    return pl.pallas_call(
        filter_kernel,
        out_shape=(
            jax.ShapeDtypeStruct((height, width), f32),
            jax.ShapeDtypeStruct((height, ACTIVE), f32),
        ),
        in_specs=[pl.BlockSpec(memory_space=pltpu.VMEM)] * 4,
        out_specs=[pl.BlockSpec(memory_space=pltpu.VMEM)] * 2,
        scratch_shapes=[pltpu.VMEM((height, width), f32)],
        compiler_params=pltpu.CompilerParams(vmem_limit_bytes=32 * 2**20),
        cost_estimate=pl.CostEstimate(
            flops=12 * height * height * width,
            bytes_accessed=8 * height * width,
            transcendentals=height * width,
        ),
        name="paganin",
    )(image, *[jnp.asarray(table) for table in tables])


def sirt_kernel(
    step_size,
    chunk,
    offset_ref,
    tile_ref,
    turn_ref,
    place_ref,
    slot_ref,
    cos_ref,
    sin_ref,
    vol_ref,
    sino_ref,
    flip_ref,
    shift_x_ref,
    shift_y_ref,
    out_ref,
    res_ref,
    weight_ref,
    acc_ref,
    along_ref,
    start_ref,
    update_ref,
    diff_ref,
    gain_ref,
    window_ref,
):
    patches, slices, _ = vol_ref.shape
    angles = sino_ref.shape[0]
    pairs = patches // 2
    both = 2 * slices
    chunks = angles // chunk
    cached = chunks == 1
    width = chunk * WIN
    flip = flip_ref[...]
    lane_rows = lax.broadcasted_iota(jnp.int32, (both, LANES), 1)

    def reversed_exact(values):
        return sum(dot(part, flip) for part in thirds(values))

    def along_angle(t, carry):
        along_ref[t] = shift_x_ref[...] * cos_ref[t] + shift_y_ref[...] * sin_ref[t]
        return carry

    lax.fori_loop(0, angles, along_angle, 0)

    def first_order(q, carry):
        diff_ref[q] = vol_ref[slot_ref[patches - 1 - q]]
        return carry

    lax.fori_loop(0, pairs, first_order, 0)
    turned = reversed_exact(diff_ref[0:pairs].reshape(pairs * slices, VOX))
    start_ref[:, slices:both, :] = turned.reshape(pairs, slices, VOX)

    def second_order(q, carry):
        start_ref[q, 0:slices, :] = vol_ref[slot_ref[q]]
        return carry

    lax.fori_loop(0, pairs, second_order, 0)

    ray = lax.broadcasted_iota(jnp.int32, (ROWS, VOX), 0).astype(f32)

    def make_weights(q, c):
        held = q if cached else 0
        for two in range(chunk // 2):
            pieces = []
            for t in (2 * two, 2 * two + 1):
                angle = c * chunk + t
                base = ray - (along_ref[angle] + place_ref[q * angles + angle])
                for group in range(WIN // ROWS):
                    distance = base + float(group * ROWS)
                    pieces.append(jnp.maximum(0.0, 1.0 - jnp.abs(distance)))
            high, low = halves(jnp.concatenate(pieces, axis=0))
            weight_ref[held, 2 * two * WIN : (2 * two + 2) * WIN, 0:VOX] = high
            weight_ref[held, 2 * two * WIN : (2 * two + 2) * WIN, VOX : 2 * VOX] = low

    def forward(first):
        acc_ref[...] = jnp.zeros(acc_ref.shape, f32)

        def pair(q, carry):
            values = start_ref[q]
            if not first:
                values = values + step_size * update_ref[q]
            high, low = halves(values)
            operand = jnp.concatenate(
                [
                    jnp.concatenate([high, high], axis=1),
                    jnp.concatenate([low, jnp.zeros_like(low)], axis=1),
                    jnp.ones((both, 2 * VOX), bf16),
                ],
                axis=0,
            )
            for c in range(chunks):
                if first or not cached:
                    make_weights(q, c)
                held = q if cached else 0
                sums = lax.dot_general(
                    weight_ref[held],
                    operand,
                    (((1,), (1,)), ((), ())),
                    preferred_element_type=f32,
                )
                for t in range(chunk):
                    angle = c * chunk + t
                    rows = pl.ds(offset_ref[q * angles + angle], WIN)
                    acc_ref[angle, rows, :] = (
                        acc_ref[angle, rows, :] + sums[t * WIN : (t + 1) * WIN, :]
                    )
            return carry

        lax.fori_loop(0, pairs, pair, 0)

        def spread(t, carry):
            rows = jnp.transpose(acc_ref[t]) * (1.0 / ROI)
            diff_ref[t] = rows[0:slices] + rows[both : both + slices]
            res_ref[t] = rows[slices:both] + rows[both + slices : 2 * both]
            if first:
                gain_ref[t] = rows[2 * both : 2 * both + slices]
            return carry

        lax.fori_loop(0, angles, spread, 0)
        flat = (angles * slices, ACTIVE)
        full = (angles, slices, ACTIVE)
        mirrored = reversed_exact(res_ref[...].reshape(flat)).reshape(full)
        res_ref[...] = sino_ref[...] - diff_ref[0:angles] - mirrored
        if first:
            direct = gain_ref[...]
            total = direct + reversed_exact(direct.reshape(flat)).reshape(full)
            gain_ref[...] = 1.0 / jnp.maximum(total, row_floor)

    def backward(first):
        weighted = res_ref[...] * gain_ref[...] * (1.0 / ROI)
        flat = (angles * slices, ACTIVE)
        full = (angles, slices, ACTIVE)
        high, low = halves(weighted.reshape(flat))
        mirrored = (dot(high, flip) + dot(low, flip)).reshape(full)
        lane = lax.broadcasted_iota(jnp.int32, (angles, slices, LANES), 2)
        for part, source in enumerate((weighted, mirrored)):
            rows = slice(part * slices, (part + 1) * slices)
            left = source[:, :, 0:LANES]
            right = source[:, :, LANES : 2 * LANES]
            window_ref[:, 0, rows, :] = left
            window_ref[:, 2, rows, :] = right
            mixed = jnp.where(lane >= SPLIT, left, right)
            window_ref[:, 1, rows, :] = pltpu.roll(mixed, SPLIT, 2)

        def pair(q, carry):
            total = None
            for c in range(chunks):
                if not cached:
                    make_weights(q, c)
                held = q if cached else 0
                tiles = [None] * (-(-width // LANES))
                for t in range(chunk):
                    index = q * angles + c * chunk + t
                    piece = pltpu.roll(
                        window_ref[c * chunk + t, tile_ref[index]], turn_ref[index], 1
                    )
                    begin = t * WIN
                    for place in range(begin // LANES, (begin + WIN - 1) // LANES + 1):
                        if tiles[place] is None:
                            tiles[place] = piece
                        else:
                            tiles[place] = jnp.where(
                                lane_rows >= begin - place * LANES, piece, tiles[place]
                            )
                high, low = halves(jnp.concatenate(tiles, axis=1))
                operand = jnp.concatenate([high, low], axis=0)
                sums = dot(operand, weight_ref[held])
                piece = sums[0:both, 0:VOX] + sums[both:, 0:VOX] + sums[0:both, VOX:]
                total = piece if total is None else total + piece
            update_ref[q] = total if first else update_ref[q] + total
            return carry

        lax.fori_loop(0, pairs, pair, 0)

    forward(True)
    backward(True)
    forward(False)
    backward(False)
    turned = reversed_exact(update_ref[:, slices:both, :].reshape(pairs * slices, VOX))
    diff_ref[0:pairs] = turned.reshape(pairs, slices, VOX)

    def finish(q, carry):
        direct = slot_ref[q]
        mirror = slot_ref[patches - 1 - q]
        out_ref[direct] = vol_ref[direct] + step_size * update_ref[q, 0:slices, :]
        out_ref[mirror] = vol_ref[mirror] + step_size * diff_ref[q]
        return carry

    lax.fori_loop(0, pairs, finish, 0)


def sirt(volume, sino, theta, vol_list, step_size):
    patches, slices, _ = volume.shape
    angles = sino.shape[0]
    pairs = patches // 2
    chunk = math.gcd(angles, 32)
    held = pairs if angles == chunk else 1
    centre = (ROI - 1) / 2.0
    ids = np.arange(pairs)
    centre_x = (ids // PGRID * float(SIDE) + (SIDE - 1) / 2.0 - centre).astype(np.float32)
    centre_y = (ids % PGRID * float(SIDE) + (SIDE - 1) / 2.0 - centre).astype(np.float32)
    cosine = jnp.cos(theta)
    sine = jnp.sin(theta)
    along = centre_x[:, None] * cosine[None, :] + centre_y[:, None] * sine[None, :] + 0.5
    whole = jnp.floor(along)
    lead = WIN // 2 - 1
    place = along - whole + float(lead)
    offset = whole.astype(jnp.int32) + (ACTIVE // 2 - 1 - lead)
    tile = jnp.minimum(offset // SPLIT, 2)
    local = jnp.arange(angles, dtype=jnp.int32) % chunk * WIN
    turn = (local[None, :] - offset + tile * SPLIT) % LANES
    slot = jnp.sum(
        jnp.where(
            vol_list[None, :] == jnp.arange(patches, dtype=jnp.int32)[:, None],
            jnp.arange(patches, dtype=jnp.int32)[None, :],
            0,
        ),
        axis=1,
    )
    voxel = np.arange(VOX)
    shift_x = np.repeat((voxel // SIDE - (SIDE - 1) / 2.0)[None, :], ROWS, axis=0)
    shift_y = np.repeat((voxel % SIDE - (SIDE - 1) / 2.0)[None, :], ROWS, axis=0)
    flip = np.eye(ACTIVE)[::-1].astype(ml_dtypes.bfloat16)
    smem = pl.BlockSpec(memory_space=pltpu.SMEM)
    vmem = pl.BlockSpec(memory_space=pltpu.VMEM)
    both = 2 * slices
    macs = 3 * patches * VOX * angles * WIN * slices
    return pl.pallas_call(
        functools.partial(sirt_kernel, step_size, chunk),
        out_shape=(
            jax.ShapeDtypeStruct(volume.shape, f32),
            jax.ShapeDtypeStruct(sino.shape, f32),
        ),
        in_specs=[smem] * 7 + [vmem] * 5,
        out_specs=[vmem] * 2,
        scratch_shapes=[
            pltpu.VMEM((held, chunk * WIN, 2 * VOX), bf16),
            pltpu.VMEM((angles, ACTIVE, 3 * both), f32),
            pltpu.VMEM((angles, ROWS, VOX), f32),
            pltpu.VMEM((pairs, both, VOX), f32),
            pltpu.VMEM((pairs, both, VOX), f32),
            pltpu.VMEM((max(pairs, angles), slices, ACTIVE), f32),
            pltpu.VMEM((angles, slices, ACTIVE), f32),
            pltpu.VMEM((angles, 3, both, LANES), f32),
        ],
        compiler_params=pltpu.CompilerParams(vmem_limit_bytes=56 * 2**20),
        cost_estimate=pl.CostEstimate(
            flops=8 * macs, bytes_accessed=4 * volume.size * 4, transcendentals=0
        ),
        name="sirt",
    )(
        offset.reshape(-1),
        tile.reshape(-1),
        turn.reshape(-1),
        place.reshape(-1),
        slot,
        cosine,
        sine,
        volume,
        sino,
        jnp.asarray(flip),
        jnp.asarray(shift_x, f32),
        jnp.asarray(shift_y, f32),
    )


def local(intensity, angles, volume, vol_list):
    n_slab = lax.axis_size("slab")
    n_ray = lax.axis_size("ray")
    devices = n_slab * n_ray
    height, band = intensity.shape[2:]
    slab_rows = height // n_slab
    slices = height // devices
    slots = volume.shape[1]
    count = angles.shape[0] * angles.shape[1]
    step_size = relax * ROI / count
    theta = angles.reshape(-1)

    spread = jnp.transpose(volume.reshape(n_ray, slices, slots, VOX), (0, 2, 1, 3))
    spread = lax.all_to_all(spread, "ray", split_axis=0, concat_axis=0, tiled=True)
    own_volume = spread.reshape(n_ray * slots, slices, VOX)

    projected, active = paganin(intensity.reshape(height, band))
    own_rays = lax.all_to_all(
        active.reshape(devices, slices, ACTIVE),
        ("slab", "ray"),
        split_axis=0,
        concat_axis=0,
        tiled=True,
    )
    pieces = projected.reshape(n_slab, slab_rows, band)
    sinogram = lax.all_to_all(pieces, "slab", split_axis=0, concat_axis=0, tiled=True)

    padded = -(-slices // ROWS) * ROWS
    if padded != slices:
        widen = ((0, 0), (0, padded - slices), (0, 0))
        own_volume = jnp.pad(own_volume, widen)
        own_rays = jnp.pad(own_rays, widen)
    result, residual = sirt(own_volume, own_rays, theta, vol_list, step_size)
    result = result[:, :slices].reshape(n_ray, slots, slices, VOX)
    residual = residual[:, :slices].reshape(n_slab, n_ray, slices, ACTIVE)

    result = lax.all_to_all(result, "ray", split_axis=0, concat_axis=0, tiled=True)
    reconstruction = jnp.transpose(result, (0, 2, 1, 3)).reshape(volume.shape)
    residual = lax.all_to_all(residual, "ray", split_axis=1, concat_axis=1, tiled=True)
    residual = residual.reshape(n_slab, slab_rows, ACTIVE)
    offset = (band - ACTIVE) // 2
    residual_out = lax.dynamic_update_slice(sinogram, residual, (0, 0, offset))
    return (reconstruction, residual_out[:, None])


def solution(mesh):
    placed = (P("slab", "ray", None, None), P(), P("slab", "ray", None), P())
    return jax.shard_map(
        local,
        mesh=mesh,
        in_specs=placed,
        out_specs=(P("slab", "ray", None), P(None, "ray", "slab", None)),
        check_vma=False,
    )
```

time: 642 us -> 199 us (0.31); the launches traced: 631 us -> 198 us
  local copies, waits for them, and re-layouts: 145 us -> 12.2 us
  other arithmetic: 127 us -> 1.99 us
  matrix products: 122 us -> 0 us
  Pallas kernels: 0 us -> 92.1 us
  waiting for transfers between devices: 117 us -> 35.4 us
  between operations: 41.5 us -> 0.71 us
  starting transfers between devices: 26.5 us -> 14.4 us
  blocking collectives: 51.8 us -> 41.5 us
    dot_general x60 -> x0, matrix products: 122 us -> none  [the longest x8 36.1 us: rows_outer(): return jnp.einsum('kn,anmc->akmc', table, values, precision=highest)]
    scatter-add x2 -> x0, other arithmetic: 93.1 us -> none  [place_windows(): return empty.at[:, flat_index].add(tiles.reshape(num_rows, -1))]
    pallas_call x0 -> x2, Pallas kernels: none -> 92.1 us  [the longest x1 53.2 us: sirt(): pl.pallas_call(functools.partial(sirt_kernel, step_size, chunk), out_shap...]
    all_to_all x5 -> x3, waiting for transfers between devices: 117 us -> 35.4 us  [the longest x1 13.5 us: local(): lax.all_to_all(result, 'ray', split_axis=0, concat_axis=0, tiled=True)]
    gather x2 -> x0, local copies, waits for them, and re-layouts: 60.2 us -> none  [take_windows(): values[:, flat_index]]
    another operation x17 -> x0, local copies, waits for them, and re-layouts: 26.7 us -> none  [the longest x2 7.57 us: backward(): take_windows(scaled, starts)]
    div x9 -> x0, other arithmetic: 16.1 us -> none  [the longest x8 11.5 us: tile_weights(): weights = jnp.maximum(0.0, 1.0 - jnp.abs(distance)) / ROI]
    all_to_all x4 -> x0, local copies, waits for them, and re-layouts: 12.3 us -> none  [the longest x2 6.66 us: forward(): lax.all_to_all(stacked, 'ray', split_axis=2, concat_axis=1, tiled=True)]
  transfers between devices with their start and end apart: 5 -> 3, of which waited for: 3 -> 3; matrix products, arithmetic and copies ran while one was open for 9% -> 2% of each run, Pallas kernels for 0% -> 0%
where the time goes in v1:
time: 199 us; the launch traced here: 198 us
  Pallas kernels  92.1 us (46%)
  blocking collectives  41.5 us (21%)
  waiting for transfers between devices  35.4 us (18%)
  starting transfers between devices  14.4 us (7%)
  local copies, waits for them, and re-layouts  12.2 us (6%)
  other arithmetic  1.99 us (1%)
    pallas_call x1, Pallas kernels, sirt(): pl.pallas_call(functools.partial(sirt_kernel, step_size, chunk), out_shap...  53.2 us
    pallas_call x1, Pallas kernels, paganin(): pl.pallas_call(filter_kernel, out_shape=(jax.ShapeDtypeStruct((height, wi...  39 us
    all_to_all x1, blocking collectives, local(): lax.all_to_all(pieces, 'slab', split_axis=0, concat_axis=0, tiled=True)  28.9 us
    all_to_all x1, waiting for transfers between devices, local(): lax.all_to_all(result, 'ray', split_axis=0, concat_axis=0, tiled=True)  13.5 us
    all_to_all x1, blocking collectives, local(): lax.all_to_all(residual, 'ray', split_axis=1, concat_axis=1, tiled=True)  12.6 us
    all_to_all x1, waiting for transfers between devices, local(): lax.all_to_all(spread, 'ray', split_axis=0, concat_axis=0, tiled=True)  12.2 us
    all_to_all x1, waiting for transfers between devices, local(): lax.all_to_all(active.reshape(devices, slices, ACTIVE), ('slab', 'ray'),...  9.68 us
    unnamed x27, local copies, waits for them, and re-layouts  8.24 us
  transfers between devices with their start and end apart: 3, of which 3 were waited for; matrix products, arithmetic and copies ran while one was open for 2% of the time, Pallas kernels for 0%

profile of v1, /device:TPU:0, one launch (start us, length us, event | category | flops | bytes accessed | tf_op | source)
XLA Modules:
  0.0 198.4 jit_solution(16996754108661339741)
XLA Ops:
  0.6 0.0 copy-start
  0.6 1.6 copy-done
  2.2 0.0 copy-start.1
  2.2 0.9 copy-done.1
  3.1 0.0 copy-start.2
  3.1 0.9 copy-done.2
  4.0 0.0 copy-start.3
  4.0 0.9 copy-done.3
  4.9 0.0 copy-start.4
  4.9 39.0 %paganin.1 = (f32[256,2048]{1,0:T(8,128)S(1)}, f32[256,256]{1,0:T(8,128)}) custom-call(f32[256,2048]{1,0:T(8,128)S(1)} %bitcast.18, bf16[256,256]{1,0:T(8,128)(2,1)S(1)} %copy-done.1, bf16[256,256]{1,0:T(8,128)(2,1)S(1)} %copy-done.2, f32[256,128]{1,0:T(8,128)S(1)} %copy-done.3), custom_call_target="tpu_custom_call" | custom-call | flops 1610612736 | bytes 4194304 | tf_op jit(solution)/shard_map/paganin/pallas_call | solution.py:138
  43.9 0.0 copy-start.7
  43.9 0.0 copy-start.10
  43.9 0.0 copy-start.11
  43.9 0.0 copy-start.12
  43.9 7.3 %all-to-all-start.1 = ((f32[32,8,256]{2,1,0:T(8,128)}), f32[32,8,256]{2,1,0:T(8,128)S(1)}, u32[]{:S(2)}, u32[]{:S(2)}) async-start(f32[32,8,256]{2,1,0:T(8,128)} %bitcast.4), calls=%async_computation.1 | async-start | bytes 524288 | tf_op jit(solution)/shard_map/all_to_all | solution.py:441
  51.3 0.0 copy-done.4
  51.3 1.0 copy.31
  52.2 9.7 %all-to-all-done.1.sino_ref = f32[32,8,256]{2,1,0:T(8,128)S(1)} async-done(((f32[32,8,256]{2,1,0:T(8,128)}), f32[32,8,256]{2,1,0:T(8,128)S(1)}, u32[]{:S(2)}, u32[]{:S(2)}) %all-to-all-start.1) | async-done | bytes 262176 | tf_op jit(solution)/shard_map/all_to_all | solution.py:441
  61.9 0.0 copy-start.6
  61.9 3.5 %all-to-all-start = ((f32[8,8,8,256]{3,2,1,0:T(8,128)}), f32[8,8,8,256]{3,2,1,0:T(8,128)S(1)}, u32[]{:S(2)}, u32[]{:S(2)}) async-start(f32[8,8,8,256]{3,2,1,0:T(8,128)} %bitcast.16), calls=%async_computation | async-start | bytes 1048576 | tf_op jit(solution)/shard_map/all_to_all | solution.py:437
  65.4 0.0 copy-done.7
  65.5 0.1 cos.6.cos_ref
  65.5 0.0 copy-start.8
  65.5 0.1 sin.6.sin_ref
  65.6 0.0 copy-done.10
  65.6 0.0 copy-done.11
  65.6 0.1 add_add_fusion
  65.7 0.1 add.64
  65.8 0.1 sub.23
  65.9 0.0 copy-done.12
  65.9 0.7 select_reduce_fusion.slot_ref
  66.6 0.6 fusion.1.place_ref
  67.2 0.6 add_select_fusion
  67.8 12.2 %all-to-all-done = f32[8,8,8,256]{3,2,1,0:T(8,128)S(1)} async-done(((f32[8,8,8,256]{3,2,1,0:T(8,128)}), f32[8,8,8,256]{3,2,1,0:T(8,128)S(1)}, u32[]{:S(2)}, u32[]{:S(2)}) %all-to-all-start) | async-done | bytes 524320 | tf_op jit(solution)/shard_map/all_to_all | solution.py:437
  80.0 0.0 copy-start.5
  80.0 0.0 copy-done.6
  80.0 0.0 copy-done.8
  80.0 0.0 copy-done.9
  80.0 0.8 copy-done.5
  80.8 53.2 %sirt.1 = (f32[64,8,256]{2,1,0:T(8,128)}, f32[32,8,256]{2,1,0:T(8,128)}) custom-call(s32[1024]{0:T(1024)} %get-tuple-element.12.offset_ref, s32[1024]{0:T(1024)} %get-tuple-element.11.tile_ref, s32[1024]{0:T(1024)} %get-tuple-element.10.turn_ref, f32[1024]{0:T(1024)} %fusion.1.place_ref, s32[64]{0:T(128)} %select_reduce_fusion.slot_ref, f32[32]{0:T(128)} %copy-done.8, ...), custom_call_target="tpu_custom_call" | custom-call | flops 2415919104 | bytes 2097152 | tf_op jit(solution)/shard_map/sirt/pallas_call | solution.py:385
  134.0 1.0 copy.26
  134.9 12.6 %all_to_all.25 = f32[4,8,8,256]{3,2,0,1:T(8,128)S(1)} all-to-all(f32[4,8,8,256]{3,2,0,1:T(8,128)S(1)} %copy.26), channel_id=1, replica_groups=mesh['slab'=4,'ray'=8] {'ray'}, dimensions={1} | all-to-all | bytes 524288 | tf_op jit(solution)/shard_map/all_to_all | solution.py:462
  147.5 28.9 %all_to_all.26 = f32[4,64,2048]{2,1,0:T(8,128)} all-to-all(f32[4,64,2048]{2,1,0:T(8,128)S(1)} %bitcast.17), channel_id=1, replica_groups=mesh['slab'=4,'ray'=8] {'slab'}, dimensions={0} | all-to-all | bytes 4194304 | tf_op jit(solution)/shard_map/all_to_all | solution.py:449
  176.4 3.6 %all-to-all-start.2 = ((f32[8,8,8,256]{3,2,1,0:T(8,128)}), f32[8,8,8,256]{3,2,1,0:T(8,128)S(1)}, u32[]{:S(2)}, u32[]{:S(2)}) async-start(f32[8,8,8,256]{3,2,1,0:T(8,128)} %bitcast.5), calls=%async_computation.2 | async-start | bytes 1048576 | tf_op jit(solution)/shard_map/all_to_all | solution.py:460
  180.0 0.7 bitcast_dynamic-update-slice_fusion
  180.8 13.5 %all-to-all-done.2 = f32[8,8,8,256]{3,2,1,0:T(8,128)S(1)} async-done(((f32[8,8,8,256]{3,2,1,0:T(8,128)}), f32[8,8,8,256]{3,2,1,0:T(8,128)S(1)}, u32[]{:S(2)}, u32[]{:S(2)}) %all-to-all-start.2) | async-done | bytes 524320 | tf_op jit(solution)/shard_map/all_to_all | solution.py:460
  194.3 1.0 copy.25
  195.2 3.1 %copy.34 = f32[4,1,64,2048]{3,2,1,0:T(8,128)} copy(f32[4,1,64,2048]{3,2,1,0:T(8,128)} %bitcast_dynamic-update-slice_fusion) | data formatting | bytes 4194304
  (4 shorter events, 0.1 us)
Async XLA Ops:
  0.6 1.6 copy-start
  2.2 0.9 copy-start.1
  3.1 0.9 copy-start.2
  4.0 0.9 copy-start.3
  4.9 46.3 %copy-start.4 = (f32[64,8,256]{2,1,0:T(8,128)S(1)}, f32[64,8,256]{2,1,0:T(8,128)}, u32[]{:S(2)}) copy-start(f32[64,8,256]{2,1,0:T(8,128)} %param.14) | copy-start | bytes 1572868
  43.9 21.5 %copy-start.7 = (f32[4,8]{1,0:T(4,128)S(1)}, f32[4,8]{1,0:T(4,128)}, u32[]{:S(2)}) copy-start(f32[4,8]{1,0:T(4,128)} %param.13) | copy-start | bytes 388
  43.9 21.7 %copy-start.10 = (f32[32]{0:T(128)S(1)}, f32[32]{0:T(128)}, u32[]{:S(2)}) copy-start(f32[32]{0:T(128)} %constant.86) | copy-start | bytes 388
  43.9 21.7 %copy-start.11 = (f32[32]{0:T(128)S(1)}, f32[32]{0:T(128)}, u32[]{:S(2)}) copy-start(f32[32]{0:T(128)} %constant.87) | copy-start | bytes 388
  43.9 21.9 %copy-start.12 = (s32[64]{0:T(128)S(1)}, s32[64]{0:T(128)}, u32[]{:S(2)}) copy-start(s32[64]{0:T(128)} %param.15) | copy-start | bytes 772
  43.9 18.0 %all-to-all-start.1 = ((f32[32,8,256]{2,1,0:T(8,128)}), f32[32,8,256]{2,1,0:T(8,128)S(1)}, u32[]{:S(2)}, u32[]{:S(2)}) async-start(f32[32,8,256]{2,1,0:T(8,128)} %bitcast.4), calls=%async_computation.1 | async-start | bytes 524288 | tf_op jit(solution)/shard_map/all_to_all | solution.py:441
  61.9 18.1 %copy-start.6 = (f32[32,8,256]{2,1,0:T(8,128)}, f32[32,8,256]{2,1,0:T(8,128)S(1)}, u32[]{:S(2)}) copy-start(f32[32,8,256]{2,1,0:T(8,128)S(1)} %all-to-all-done.1.sino_ref) | copy-start | bytes 786436
  61.9 18.1 %all-to-all-start = ((f32[8,8,8,256]{3,2,1,0:T(8,128)}), f32[8,8,8,256]{3,2,1,0:T(8,128)S(1)}, u32[]{:S(2)}, u32[]{:S(2)}) async-start(f32[8,8,8,256]{3,2,1,0:T(8,128)} %bitcast.16), calls=%async_computation | async-start | bytes 1048576 | tf_op jit(solution)/shard_map/all_to_all | solution.py:437
  65.5 14.5 %copy-start.8 = (f32[32]{0:T(128)}, f32[32]{0:T(128)S(1)}, u32[]{:S(2)}) copy-start(f32[32]{0:T(128)S(1)} %cos.6.cos_ref) | copy-start | bytes 388
  65.6 14.4 %copy-start.9 = (f32[32]{0:T(128)}, f32[32]{0:T(128)S(1)}, u32[]{:S(2)}) copy-start(f32[32]{0:T(128)S(1)} %sin.6.sin_ref) | copy-start | bytes 388
  80.0 0.8 copy-start.5
  176.4 17.9 %all-to-all-start.2 = ((f32[8,8,8,256]{3,2,1,0:T(8,128)}), f32[8,8,8,256]{3,2,1,0:T(8,128)S(1)}, u32[]{:S(2)}, u32[]{:S(2)}) async-start(f32[8,8,8,256]{3,2,1,0:T(8,128)} %bitcast.5), calls=%async_computation.2 | async-start | bytes 1048576 | tf_op jit(solution)/shard_map/all_to_all | solution.py:460

commit v2 on v1

--- a/solution.py
+++ b/solution.py
@@ -47,111 +47,136 @@
     return jnp.dot(left, right, preferred_element_type=f32)
 
 
-def numpy_halves(table):
-    high = table.astype(ml_dtypes.bfloat16)
-    low = (table - high.astype(np.float64)).astype(ml_dtypes.bfloat16)
-    return high, low
-
-
 def filter_tables(height):
     index = np.arange(height)
     phase = 2.0 * np.pi * (np.outer(index, index) % height) / height
     cas = (np.cos(phase) + np.sin(phase)) / math.sqrt(height)
-    cas_high, cas_low = numpy_halves(cas)
     row_freq = 2.0 - 2.0 * np.cos(2.0 * np.pi * index / height)
     middle = (1.0 + paganin_strength * row_freq) / paganin_strength + 2.0
     rho = (middle - np.sqrt(middle * middle - 4.0)) / 2.0
-    rho_wide = np.repeat(rho[:, None], LANES, axis=1).astype(np.float32)
-    return cas_high, cas_low, rho_wide
-
-
-def circular_decay(parts, rho, forward, lane):
-    count = len(parts)
-    step = 1
-    power = rho
-    while step < LANES:
-        shift = step if forward else LANES - step
-        turned = [pltpu.roll(part, shift, 1) for part in parts]
-        if forward:
-            keep = lane >= step
-            moved = [jnp.where(keep, turned[i], turned[i - 1]) for i in range(count)]
-        else:
-            keep = lane < LANES - step
-            moved = [jnp.where(keep, turned[i], turned[(i + 1) % count]) for i in range(count)]
-        parts = [part + power * other for part, other in zip(parts, moved)]
+    return np.concatenate([cas, np.repeat(rho[None, :], ROWS, axis=0)], axis=0).astype(np.float32)
+
+
+def chunk_carry(ends, power, forward):
+    shift = 1
+    for _ in range(3):
+        ends = ends + power * pltpu.roll(ends, shift if forward else ROWS - shift, 0)
         power = power * power
-        step *= 2
-    order = list(range(count)) if forward else list(range(count - 1, -1, -1))
-    wrapped = parts[order[0]]
-    for position in order[1:]:
-        wrapped = parts[position] + power * wrapped
-    whole = power
-    for _ in range(int(math.log2(count))):
-        whole = whole * whole
-    carry = wrapped / (1.0 - whole)
-    results = [None] * count
-    for position in order:
-        carry = parts[position] + power * carry
-        results[position] = carry
-    return results
-
-
-def filter_kernel(image_ref, high_ref, low_ref, rho_ref, out_ref, active_ref, spec_ref):
+        shift *= 2
+    return pltpu.roll(ends, 1 if forward else ROWS - 1, 0) / (1.0 - power)
+
+
+def filter_kernel(rank_ref, image_ref, table_ref, *refs):
+    *part_refs, active_ref, out_ref, spec_ref, up_ref, down_ref = refs
     height, width = image_ref.shape
-    tile = 256
-    cas_high = high_ref[...]
-    cas_low = low_ref[...]
+    rank = rank_ref[0]
+    share = height // len(part_refs)
+    length = width // ROWS
+    blocks = height // LANES
+    unroll = 8
+    cas_high, cas_low = halves(table_ref[0:height, :])
+    rho_all = table_ref[height : height + ROWS, :]
+    rhos = [rho_all[:, b * LANES : (b + 1) * LANES] for b in range(blocks)]
+    zeros = [jnp.zeros((ROWS, LANES), f32)] * blocks
 
     def transform(values):
         high, low = halves(values)
-        return dot(cas_high, high) + dot(cas_high, low) + dot(cas_low, high)
-
-    for start in range(0, width, tile):
-        spec_ref[:, start : start + tile] = transform(1.0 - image_ref[:, start : start + tile])
-
-    lane = lax.broadcasted_iota(jnp.int32, (ROWS, LANES), 1)
-
-    def solve(index, carry):
-        row = pl.ds(pl.multiple_of(index * ROWS, ROWS), ROWS)
-        rho = rho_ref[row, :]
-        scale = rho / paganin_strength
-        parts = [
-            spec_ref[row, start : start + LANES] * scale for start in range(0, width, LANES)
-        ]
-        parts = circular_decay(parts, rho, True, lane)
-        parts = circular_decay(parts, rho, False, lane)
-        for position, part in enumerate(parts):
-            spec_ref[row, position * LANES : (position + 1) * LANES] = part
-        return carry
-
-    lax.fori_loop(0, height // ROWS, solve, 0)
+        return dot(high, cas_high) + dot(low, cas_high) + dot(high, cas_low)
+
+    for c in range(ROWS):
+        image = 1.0 - image_ref[:, c * length : (c + 1) * length]
+        spectrum = transform(jnp.transpose(image))
+        for b in range(blocks):
+            spec_ref[b, pl.ds(c, length, stride=ROWS), :] = spectrum[
+                :, b * LANES : (b + 1) * LANES
+            ]
+
+    def rows(position):
+        return pl.ds(pl.multiple_of(position * ROWS, ROWS), ROWS)
+
+    def advance(position, ups, downs):
+        ups = [spec_ref[b, rows(position), :] + rhos[b] * ups[b] for b in range(blocks)]
+        back = length - 1 - position
+        downs = [spec_ref[b, rows(back), :] + rhos[b] * downs[b] for b in range(blocks)]
+        return ups, downs
+
+    def sweep(index, carry):
+        ups, downs = carry
+        for step in range(unroll):
+            ups, downs = advance(index * unroll + step, ups, downs)
+        return ups, downs
+
+    ups, downs = lax.fori_loop(0, length // unroll, sweep, (zeros, zeros))
+    powers = list(rhos)
+    for _ in range(int(math.log2(length))):
+        powers = [power * power for power in powers]
+    ups = [chunk_carry(ups[b], powers[b], True) for b in range(blocks)]
+    downs = [chunk_carry(downs[b], powers[b], False) for b in range(blocks)]
+    scales = [rho / (paganin_strength * (1.0 - rho * rho)) for rho in rhos]
+
+    def outer(index, carry):
+        ups, downs = carry
+        for step in range(unroll):
+            position = index * unroll + step
+            ups, downs = advance(position, ups, downs)
+            for b in range(blocks):
+                up_ref[b, rows(position), :] = ups[b]
+                down_ref[b, rows(position), :] = downs[b]
+        return ups, downs
+
+    def inner(index, carry):
+        ups, downs = carry
+        for step in range(unroll):
+            position = index * unroll + step
+            back = length - 1 - position
+            ups, downs = advance(position, ups, downs)
+            for b in range(blocks):
+                here = ups[b] + down_ref[b, rows(back), :] - spec_ref[b, rows(position), :]
+                there = downs[b] + up_ref[b, rows(back), :] - spec_ref[b, rows(back), :]
+                up_ref[b, rows(position), :] = here * scales[b]
+                up_ref[b, rows(back), :] = there * scales[b]
+        return ups, downs
+
+    half = length // 2 // unroll
+    carry = lax.fori_loop(0, half, outer, (ups, downs))
+    lax.fori_loop(half, 2 * half, inner, carry)
+
     offset = (width - ACTIVE) // 2
-    for start in range(0, width, tile):
-        values = -jnp.log(1.0 - transform(spec_ref[:, start : start + tile]))
-        out_ref[:, start : start + tile] = values
+    for c in range(ROWS):
+        spectrum = jnp.concatenate(
+            [up_ref[b, pl.ds(c, length, stride=ROWS), :] for b in range(blocks)], axis=1
+        )
+        filtered = 1.0 - jnp.transpose(transform(spectrum))
+        out_ref[:, c * length : (c + 1) * length] = -jnp.log(filtered)
     active_ref[...] = out_ref[:, offset : offset + ACTIVE]
-
-
-def paganin(image):
+    for d, part_ref in enumerate(part_refs):
+        part_ref[...] = out_ref[pl.ds(pl.multiple_of((rank ^ d) * share, share), share), :]
+
+
+def paganin(image, rank, parts):
     height, width = image.shape
-    tables = filter_tables(height)
+    blocks = height // LANES
     return pl.pallas_call(
         filter_kernel,
-        out_shape=(
-            jax.ShapeDtypeStruct((height, width), f32),
-            jax.ShapeDtypeStruct((height, ACTIVE), f32),
-        ),
-        in_specs=[pl.BlockSpec(memory_space=pltpu.VMEM)] * 4,
-        out_specs=[pl.BlockSpec(memory_space=pltpu.VMEM)] * 2,
-        scratch_shapes=[pltpu.VMEM((height, width), f32)],
+        out_shape=[jax.ShapeDtypeStruct((height // parts, width), f32)] * parts
+        + [jax.ShapeDtypeStruct((height, ACTIVE), f32)],
+        in_specs=[pl.BlockSpec(memory_space=pltpu.SMEM)]
+        + [pl.BlockSpec(memory_space=pltpu.VMEM)] * 2,
+        out_specs=[pl.BlockSpec(memory_space=pltpu.VMEM)] * (parts + 1),
+        scratch_shapes=[
+            pltpu.VMEM((height, width), f32),
+            pltpu.VMEM((blocks, width, LANES), f32),
+            pltpu.VMEM((blocks, width, LANES), f32),
+            pltpu.VMEM((blocks, width // 2, LANES), f32),
+        ],
         compiler_params=pltpu.CompilerParams(vmem_limit_bytes=32 * 2**20),
         cost_estimate=pl.CostEstimate(
-            flops=12 * height * height * width,
+            flops=64 * height * height * width,
             bytes_accessed=8 * height * width,
             transcendentals=height * width,
         ),
         name="paganin",
-    )(image, *[jnp.asarray(table) for table in tables])
+    )(rank.reshape(1), image, jnp.asarray(filter_tables(height)))
 
 
 def sirt_kernel(
@@ -170,17 +195,21 @@
     shift_x_ref,
     shift_y_ref,
     out_ref,
-    res_ref,
     weight_ref,
     acc_ref,
     along_ref,
     start_ref,
     update_ref,
     diff_ref,
+    res_ref,
     gain_ref,
     window_ref,
+    half_ref,
 ):
-    patches, slices, _ = vol_ref.shape
+    rays, held_rows, _ = vol_ref.shape
+    patches = slot_ref.shape[0]
+    slots = patches // rays
+    slices = held_rows // slots
     angles = sino_ref.shape[0]
     pairs = patches // 2
     both = 2 * slices
@@ -193,6 +222,19 @@
     def reversed_exact(values):
         return sum(dot(part, flip) for part in thirds(values))
 
+    def slot_rows(patch):
+        slot = slot_ref[patch]
+        return slot // slots, pl.ds(slot % slots, slices, stride=slots)
+
+    def slot_values(patch):
+        ray, rows = slot_rows(patch)
+        return jnp.concatenate(
+            [half_ref[0, ray, rows, :], half_ref[1, ray, rows, :]], axis=1
+        )
+
+    for part in range(2):
+        half_ref[part] = vol_ref[:, :, part * LANES : (part + 1) * LANES]
+
     def along_angle(t, carry):
         along_ref[t] = shift_x_ref[...] * cos_ref[t] + shift_y_ref[...] * sin_ref[t]
         return carry
@@ -200,7 +242,7 @@
     lax.fori_loop(0, angles, along_angle, 0)
 
     def first_order(q, carry):
-        diff_ref[q] = vol_ref[slot_ref[patches - 1 - q]]
+        diff_ref[q] = slot_values(patches - 1 - q)
         return carry
 
     lax.fori_loop(0, pairs, first_order, 0)
@@ -208,7 +250,7 @@
     start_ref[:, slices:both, :] = turned.reshape(pairs, slices, VOX)
 
     def second_order(q, carry):
-        start_ref[q, 0:slices, :] = vol_ref[slot_ref[q]]
+        start_ref[q, 0:slices, :] = slot_values(q)
         return carry
 
     lax.fori_loop(0, pairs, second_order, 0)
@@ -337,19 +379,30 @@
     diff_ref[0:pairs] = turned.reshape(pairs, slices, VOX)
 
     def finish(q, carry):
-        direct = slot_ref[q]
-        mirror = slot_ref[patches - 1 - q]
-        out_ref[direct] = vol_ref[direct] + step_size * update_ref[q, 0:slices, :]
-        out_ref[mirror] = vol_ref[mirror] + step_size * diff_ref[q]
+        for patch, update in (
+            (q, update_ref[q, 0:slices, :]),
+            (patches - 1 - q, diff_ref[q]),
+        ):
+            ray, rows = slot_rows(patch)
+            values = slot_values(patch) + step_size * update
+            half_ref[0, ray, rows, :] = values[:, 0:LANES]
+            half_ref[1, ray, rows, :] = values[:, LANES : 2 * LANES]
         return carry
 
     lax.fori_loop(0, pairs, finish, 0)
+    for part in range(2):
+        out_ref[:, 0:held_rows, part * LANES : (part + 1) * LANES] = half_ref[part]
+    for t in range(angles):
+        begin = held_rows + t // rays * slices
+        out_ref[t % rays, begin : begin + slices, :] = res_ref[t]
 
 
 def sirt(volume, sino, theta, vol_list, step_size):
-    patches, slices, _ = volume.shape
-    angles = sino.shape[0]
+    rays, held_rows, _ = volume.shape
+    patches = vol_list.shape[0]
+    angles, slices, _ = sino.shape
     pairs = patches // 2
+    sent_rows = held_rows + angles // rays * slices
     chunk = math.gcd(angles, 32)
     held = pairs if angles == chunk else 1
     centre = (ROI - 1) / 2.0
@@ -384,12 +437,9 @@
     macs = 3 * patches * VOX * angles * WIN * slices
     return pl.pallas_call(
         functools.partial(sirt_kernel, step_size, chunk),
-        out_shape=(
-            jax.ShapeDtypeStruct(volume.shape, f32),
-            jax.ShapeDtypeStruct(sino.shape, f32),
-        ),
+        out_shape=jax.ShapeDtypeStruct((rays, sent_rows, VOX), f32),
         in_specs=[smem] * 7 + [vmem] * 5,
-        out_specs=[vmem] * 2,
+        out_specs=vmem,
         scratch_shapes=[
             pltpu.VMEM((held, chunk * WIN, 2 * VOX), bf16),
             pltpu.VMEM((angles, ACTIVE, 3 * both), f32),
@@ -398,11 +448,13 @@
             pltpu.VMEM((pairs, both, VOX), f32),
             pltpu.VMEM((max(pairs, angles), slices, ACTIVE), f32),
             pltpu.VMEM((angles, slices, ACTIVE), f32),
+            pltpu.VMEM((angles, slices, ACTIVE), f32),
             pltpu.VMEM((angles, 3, both, LANES), f32),
+            pltpu.VMEM((2, rays, held_rows, LANES), f32),
         ],
         compiler_params=pltpu.CompilerParams(vmem_limit_bytes=56 * 2**20),
         cost_estimate=pl.CostEstimate(
-            flops=8 * macs, bytes_accessed=4 * volume.size * 4, transcendentals=0
+            flops=128 * macs, bytes_accessed=4 * volume.size * 4, transcendentals=0
         ),
         name="sirt",
     )(
@@ -421,6 +473,87 @@
     )
 
 
+def gather_kernel(rank_ref, *refs):
+    *part_refs, out_ref, sems = refs
+    rank = rank_ref[0]
+    copies = [
+        pltpu.make_async_copy(part_ref, out_ref.at[rank ^ d], sems.at[d])
+        for d, part_ref in enumerate(part_refs)
+    ]
+    for copy in copies:
+        copy.start()
+    for copy in copies:
+        copy.wait()
+
+
+def gather_parts(parts, rank):
+    count = len(parts)
+    return pl.pallas_call(
+        gather_kernel,
+        out_shape=jax.ShapeDtypeStruct((count,) + parts[0].shape, f32),
+        in_specs=[pl.BlockSpec(memory_space=pltpu.SMEM)]
+        + [pl.BlockSpec(memory_space=pl.ANY)] * count,
+        out_specs=pl.BlockSpec(memory_space=pl.ANY),
+        scratch_shapes=[pltpu.SemaphoreType.DMA((count,))],
+        cost_estimate=pl.CostEstimate(
+            flops=0, bytes_accessed=8 * count * parts[0].size, transcendentals=0
+        ),
+        name="gather_parts",
+    )(rank.reshape(1), *parts)
+
+
+def finish_kernel(slots, got_ref, sino_ref, rec_ref, out_ref, values_ref, active_ref, sems):
+    rays, rows, _ = got_ref.shape
+    slabs = active_ref.shape[0]
+    held = rows * slots // (slots + slabs)
+    slices = held // slots
+    for ray in range(rays):
+        values_ref[ray * slices : (ray + 1) * slices] = got_ref[ray, 0:held, :].reshape(
+            slices, slots, VOX
+        )
+        for k in range(slabs):
+            begin = held + k * slices
+            active_ref[k, ray * slices : (ray + 1) * slices, :] = got_ref[
+                ray, begin : begin + slices, :
+            ]
+    offset = (out_ref.shape[2] - ACTIVE) // 2
+    copies = [
+        pltpu.make_async_copy(values_ref, rec_ref, sems.at[0]),
+        pltpu.make_async_copy(
+            active_ref, out_ref.at[:, :, offset : offset + ACTIVE], sems.at[1]
+        ),
+    ]
+    for copy in copies:
+        copy.start()
+    for copy in copies:
+        copy.wait()
+
+
+def finish(got, sinogram, shape):
+    slabs, slab_rows, _ = sinogram.shape
+    any_space = pl.BlockSpec(memory_space=pl.ANY)
+    return pl.pallas_call(
+        functools.partial(finish_kernel, shape[1]),
+        out_shape=(
+            jax.ShapeDtypeStruct(shape, f32),
+            jax.ShapeDtypeStruct(sinogram.shape, f32),
+        ),
+        in_specs=[pl.BlockSpec(memory_space=pltpu.VMEM), any_space],
+        out_specs=[any_space, any_space],
+        scratch_shapes=[
+            pltpu.VMEM(shape, f32),
+            pltpu.VMEM((slabs, slab_rows, ACTIVE), f32),
+            pltpu.SemaphoreType.DMA((2,)),
+        ],
+        input_output_aliases={1: 1},
+        compiler_params=pltpu.CompilerParams(vmem_limit_bytes=32 * 2**20),
+        cost_estimate=pl.CostEstimate(
+            flops=0, bytes_accessed=8 * got.size, transcendentals=0
+        ),
+        name="finish",
+    )(got, sinogram)
+
+
 def local(intensity, angles, volume, vol_list):
     n_slab = lax.axis_size("slab")
     n_ray = lax.axis_size("ray")
@@ -432,12 +565,12 @@
     count = angles.shape[0] * angles.shape[1]
     step_size = relax * ROI / count
     theta = angles.reshape(-1)
-
-    spread = jnp.transpose(volume.reshape(n_ray, slices, slots, VOX), (0, 2, 1, 3))
-    spread = lax.all_to_all(spread, "ray", split_axis=0, concat_axis=0, tiled=True)
-    own_volume = spread.reshape(n_ray * slots, slices, VOX)
-
-    projected, active = paganin(intensity.reshape(height, band))
+    rank = lax.axis_index("slab")
+
+    spread = volume.reshape(n_ray, slices * slots, VOX)
+    own_volume = lax.all_to_all(spread, "ray", split_axis=0, concat_axis=0, tiled=True)
+
+    *parts, active = paganin(intensity.reshape(height, band), rank, n_slab)
     own_rays = lax.all_to_all(
         active.reshape(devices, slices, ACTIVE),
         ("slab", "ray"),
@@ -445,25 +578,25 @@
         concat_axis=0,
         tiled=True,
     )
-    pieces = projected.reshape(n_slab, slab_rows, band)
-    sinogram = lax.all_to_all(pieces, "slab", split_axis=0, concat_axis=0, tiled=True)
+    parts = [
+        lax.ppermute(part, "slab", [(i, i ^ d) for i in range(n_slab)]) if d else part
+        for d, part in enumerate(parts)
+    ]
 
     padded = -(-slices // ROWS) * ROWS
     if padded != slices:
         widen = ((0, 0), (0, padded - slices), (0, 0))
-        own_volume = jnp.pad(own_volume, widen)
+        own_volume = jnp.pad(own_volume, ((0, 0), (0, (padded - slices) * slots), (0, 0)))
         own_rays = jnp.pad(own_rays, widen)
-    result, residual = sirt(own_volume, own_rays, theta, vol_list, step_size)
-    result = result[:, :slices].reshape(n_ray, slots, slices, VOX)
-    residual = residual[:, :slices].reshape(n_slab, n_ray, slices, ACTIVE)
-
+    result = sirt(own_volume, own_rays, theta, vol_list, step_size)
+    if padded != slices:
+        lower = result[:, padded * slots :].reshape(n_ray, n_slab, padded, ACTIVE)
+        lower = lower[:, :, :slices].reshape(n_ray, n_slab * slices, ACTIVE)
+        result = jnp.concatenate([result[:, : slices * slots], lower], axis=1)
     result = lax.all_to_all(result, "ray", split_axis=0, concat_axis=0, tiled=True)
-    reconstruction = jnp.transpose(result, (0, 2, 1, 3)).reshape(volume.shape)
-    residual = lax.all_to_all(residual, "ray", split_axis=1, concat_axis=1, tiled=True)
-    residual = residual.reshape(n_slab, slab_rows, ACTIVE)
-    offset = (band - ACTIVE) // 2
-    residual_out = lax.dynamic_update_slice(sinogram, residual, (0, 0, offset))
-    return (reconstruction, residual_out[:, None])
+    sinogram = gather_parts(parts, rank)
+    reconstruction, residual = finish(result, sinogram, volume.shape)
+    return (reconstruction, residual[:, None])
 
 
 def solution(mesh):

time: 199 us -> 196 us (0.985)
  Pallas kernels: 92.1 us -> 125 us
  blocking collectives: 41.5 us -> 17.8 us
  local copies, waits for them, and re-layouts: 12.2 us -> 5.3 us
  starting transfers between devices: 14.4 us -> 9.03 us
    pallas_call x1 -> x3, Pallas kernels: 39 us -> 70.5 us  [the longest x1 64.7 us: gather_parts(): pl.pallas_call(gather_kernel, out_shape=jax.ShapeDtypeStruct((count,) + p...]
    all_to_all x2 -> x1, blocking collectives: 41.5 us -> 17.8 us  [local(): lax.all_to_all(active.reshape(devices, slices, ACTIVE), ('slab', 'ray'),...]
    ppermute x0 -> x3, waiting for transfers between devices: none -> 23.3 us  [local(): lax.ppermute(part, 'slab', [(i, i ^ d) for i in range(n_slab)])]
    all_to_all x1, waiting for transfers between devices: 13.5 us -> 0.01 us  [local(): lax.all_to_all(result, 'ray', split_axis=0, concat_axis=0, tiled=True)]
    all_to_all x1 -> x0, waiting for transfers between devices: 9.68 us -> none  [local(): lax.all_to_all(active.reshape(devices, slices, ACTIVE), ('slab', 'ray'),...]
    all_to_all x1 -> x0, starting transfers between devices: 7.3 us -> none  [local(): lax.all_to_all(active.reshape(devices, slices, ACTIVE), ('slab', 'ray'),...]
    unnamed x27 -> x26, local copies, waits for them, and re-layouts: 8.24 us -> 4.94 us
  transfers between devices with their start and end apart: 3 -> 5, of which waited for: 3 -> 3; matrix products, arithmetic and copies ran while one was open for 2% -> 1% of each run, Pallas kernels for 0% -> 33%
where the time goes in v2:
time: 196 us; the launch traced here: 195 us
  Pallas kernels  125 us (64%)
  waiting for transfers between devices  35.5 us (18%)
  blocking collectives  17.8 us (9%)
  starting transfers between devices  9.03 us (5%)
  local copies, waits for them, and re-layouts  5.3 us (3%)
  other arithmetic  1.99 us (1%)
    pallas_call x1, Pallas kernels, gather_parts(): pl.pallas_call(gather_kernel, out_shape=jax.ShapeDtypeStruct((count,) + p...  64.7 us
    pallas_call x1, Pallas kernels, sirt(): pl.pallas_call(functools.partial(sirt_kernel, step_size, chunk), out_shap...  54.3 us
    ppermute x3, waiting for transfers between devices, local(): lax.ppermute(part, 'slab', [(i, i ^ d) for i in range(n_slab)])  23.3 us
    all_to_all x1, blocking collectives, local(): lax.all_to_all(active.reshape(devices, slices, ACTIVE), ('slab', 'ray'),...  17.8 us
    all_to_all x1, waiting for transfers between devices, local(): lax.all_to_all(spread, 'ray', split_axis=0, concat_axis=0, tiled=True)  12.2 us
    unnamed x26, local copies, waits for them, and re-layouts  4.94 us
    pallas_call x1, Pallas kernels, paganin(): pl.pallas_call(filter_kernel, out_shape=[jax.ShapeDtypeStruct((height //...  4.91 us
  transfers between devices with their start and end apart: 5, of which 3 were waited for; matrix products, arithmetic and copies ran while one was open for 1% of the time, Pallas kernels for 33%

profile of v2, /device:TPU:0, one launch (start us, length us, event | category | flops | bytes accessed | tf_op | source)
XLA Modules:
  0.0 195.1 jit_solution(2397115176263565412)
XLA Ops:
  0.6 0.0 copy-start.1
  0.6 1.6 copy-done.1
  2.2 0.0 copy-start.2
  2.2 1.0 copy-done.2
  3.2 0.0 copy-start.7
  3.2 0.0 copy-start.10
  3.2 0.0 copy-start.11
  3.2 0.0 copy-start.12
  3.2 4.9 %paganin.1 = (f32[64,2048]{1,0:T(8,128)S(1)}, f32[64,2048]{1,0:T(8,128)S(1)}, f32[64,2048]{1,0:T(8,128)S(1)}, f32[64,2048]{1,0:T(8,128)S(1)}, f32[256,256]{1,0:T(8,128)S(1)}) custom-call(s32[1]{0:T(128)} %bitcast.1.rank_ref, f32[256,2048]{1,0:T(8,128)S(1)} %bitcast.8, f32[264,256]{1,0:T(8,128)S(1)} %copy-done.2), custom_call_target="tpu_custom_call" | custom-call | flops 8589934592 | bytes 4194304 | tf_op jit(solution)/shard_map/paganin/pallas_call | solution.py:159
  8.1 0.0 copy-start
  8.1 0.8 copy-done
  8.9 17.8 %all_to_all.15.sino_ref = f32[32,8,256]{2,1,0:T(8,128)} all-to-all(f32[32,8,256]{2,1,0:T(8,128)S(1)} %bitcast.7), channel_id=1, replica_groups=mesh['slab'=4,'ray'=8] {'slab','ray'}, dimensions={0} | all-to-all | bytes 524288 | tf_op jit(solution)/shard_map/all_to_all | solution.py:574
  26.8 3.5 %all-to-all-start = ((f32[8,64,256]{2,1,0:T(8,128)}), f32[8,64,256]{2,1,0:T(8,128)S(1)}, u32[]{:S(2)}, u32[]{:S(2)}) async-start(f32[8,64,256]{2,1,0:T(8,128)} %bitcast), calls=%async_computation | async-start | bytes 1048576 | tf_op jit(solution)/shard_map/all_to_all | solution.py:571
  30.3 0.0 copy-done.7
  30.3 0.1 cos.6.cos_ref
  30.4 0.0 copy-start.8
  30.4 0.1 sin.6.sin_ref
  30.5 0.0 copy-start.9
  30.5 0.1 sub.23
  30.6 0.0 copy-done.10
  30.6 0.0 copy-done.11
  30.6 0.1 add_add_fusion
  30.7 0.1 add.64
  30.7 0.0 copy-done.12
  30.7 0.7 select_reduce_fusion.slot_ref
  31.4 0.6 fusion.1.place_ref
  32.0 0.6 add_select_fusion
  32.6 12.2 %all-to-all-done.vol_ref = f32[8,64,256]{2,1,0:T(8,128)S(1)} async-done(((f32[8,64,256]{2,1,0:T(8,128)}), f32[8,64,256]{2,1,0:T(8,128)S(1)}, u32[]{:S(2)}, u32[]{:S(2)}) %all-to-all-start) | async-done | bytes 524320 | tf_op jit(solution)/shard_map/all_to_all | solution.py:571
  44.9 0.0 copy-start.6
  44.9 0.0 copy-done.8
  44.9 0.0 copy-done.9
  44.9 0.8 copy-done.6
  45.7 54.3 %sirt.1 = f32[8,96,256]{2,1,0:T(8,128)} custom-call(s32[1024]{0:T(1024)} %get-tuple-element.22.offset_ref, s32[1024]{0:T(1024)} %get-tuple-element.21.tile_ref, s32[1024]{0:T(1024)} %get-tuple-element.20.turn_ref, f32[1024]{0:T(1024)} %fusion.1.place_ref, s32[64]{0:T(128)} %select_reduce_fusion.slot_ref, f32[32]{0:T(128)} %copy-done.8, f32[32]{0:T(128)} %copy-done.9, ...), custom_call_target="tpu_custom_call" | custom-call | flops 38654705664 | bytes 2097152 | tf_op jit(solution)/shard_map/sirt/pallas_call | solution.py:438
  99.9 3.7 %all-to-all-start.2 = ((f32[8,96,256]{2,1,0:T(8,128)}), f32[8,96,256]{2,1,0:T(8,128)S(1)}, u32[]{:S(2)}, u32[]{:S(2)}) async-start(f32[8,96,256]{2,1,0:T(8,128)} %sirt.1), calls=%async_computation.2 | async-start | bytes 1572864 | tf_op jit(solution)/shard_map/all_to_all | solution.py:596
  103.6 0.0 collective-permute-start
  103.6 1.3 collective-permute-start.1
  104.9 0.6 collective-permute-start.2
  105.5 0.0 collective-permute-done.refs_1_
  105.5 0.0 copy-start.3
  105.5 12.9 %collective-permute-done.1.refs_2_ = f32[64,2048]{1,0:T(8,128)S(1)} collective-permute-done((f32[64,2048]{1,0:T(8,128)S(1)}, f32[64,2048]{1,0:T(8,128)S(1)}, u32[]{:S(2)}, u32[]{:S(2)}) %collective-permute-start.1) | collective-permute-done | bytes 524320 | tf_op jit(solution)/shard_map/ppermute | solution.py:582
  118.4 0.0 copy-start.4
  118.4 10.3 %collective-permute-done.2.refs_3_ = f32[64,2048]{1,0:T(8,128)S(1)} collective-permute-done((f32[64,2048]{1,0:T(8,128)S(1)}, f32[64,2048]{1,0:T(8,128)S(1)}, u32[]{:S(2)}, u32[]{:S(2)}) %collective-permute-start.2) | collective-permute-done | bytes 524320 | tf_op jit(solution)/shard_map/ppermute | solution.py:582
  128.7 0.8 copy-done.5
  129.5 0.0 copy-done.3
  129.5 0.0 copy-done.4
  129.5 64.7 %gather_parts.1.sino_ref = f32[4,64,2048]{2,1,0:T(8,128)} custom-call(s32[1]{0:T(128)} %bitcast.1.rank_ref, f32[64,2048]{1,0:T(8,128)} %copy-done, f32[64,2048]{1,0:T(8,128)} %copy-done.3, f32[64,2048]{1,0:T(8,128)} %copy-done.4, f32[64,2048]{1,0:T(8,128)} %copy-done.5), custom_call_target="tpu_custom_call" | custom-call | bytes 4194304 | tf_op jit(solution)/shard_map/gather_parts/pallas_call | solution.py:491
  194.2 0.0 all-to-all-done.2.got_ref
  194.2 0.9 finish.1
  (4 shorter events, 0.1 us)
Async XLA Ops:
  0.6 1.6 copy-start.1
  2.2 1.0 copy-start.2
  3.2 27.1 %copy-start.7 = (f32[4,8]{1,0:T(4,128)S(1)}, f32[4,8]{1,0:T(4,128)}, u32[]{:S(2)}) copy-start(f32[4,8]{1,0:T(4,128)} %param.11) | copy-start | bytes 388
  3.2 27.4 %copy-start.10 = (f32[32]{0:T(128)S(1)}, f32[32]{0:T(128)}, u32[]{:S(2)}) copy-start(f32[32]{0:T(128)} %constant.83) | copy-start | bytes 388
  3.2 27.4 %copy-start.11 = (f32[32]{0:T(128)S(1)}, f32[32]{0:T(128)}, u32[]{:S(2)}) copy-start(f32[32]{0:T(128)} %constant.82) | copy-start | bytes 388
  3.2 27.5 %copy-start.12 = (s32[64]{0:T(128)S(1)}, s32[64]{0:T(128)}, u32[]{:S(2)}) copy-start(s32[64]{0:T(128)} %param.13) | copy-start | bytes 772
  8.1 0.8 copy-start
  26.8 18.1 %all-to-all-start = ((f32[8,64,256]{2,1,0:T(8,128)}), f32[8,64,256]{2,1,0:T(8,128)S(1)}, u32[]{:S(2)}, u32[]{:S(2)}) async-start(f32[8,64,256]{2,1,0:T(8,128)} %bitcast), calls=%async_computation | async-start | bytes 1048576 | tf_op jit(solution)/shard_map/all_to_all | solution.py:571
  30.4 14.5 %copy-start.8 = (f32[32]{0:T(128)}, f32[32]{0:T(128)S(1)}, u32[]{:S(2)}) copy-start(f32[32]{0:T(128)S(1)} %cos.6.cos_ref) | copy-start | bytes 388
  30.5 14.4 %copy-start.9 = (f32[32]{0:T(128)}, f32[32]{0:T(128)S(1)}, u32[]{:S(2)}) copy-start(f32[32]{0:T(128)S(1)} %sin.6.sin_ref) | copy-start | bytes 388
  44.9 0.8 copy-start.6
  99.9 94.3 %all-to-all-start.2 = ((f32[8,96,256]{2,1,0:T(8,128)}), f32[8,96,256]{2,1,0:T(8,128)S(1)}, u32[]{:S(2)}, u32[]{:S(2)}) async-start(f32[8,96,256]{2,1,0:T(8,128)} %sirt.1), calls=%async_computation.2 | async-start | bytes 1572864 | tf_op jit(solution)/shard_map/all_to_all | solution.py:596
  103.6 1.9 collective-permute-start
  103.6 14.8 %collective-permute-start.1 = (f32[64,2048]{1,0:T(8,128)S(1)}, f32[64,2048]{1,0:T(8,128)S(1)}, u32[]{:S(2)}, u32[]{:S(2)}) collective-permute-start(f32[64,2048]{1,0:T(8,128)S(1)} %get-tuple-element.12), channel_id=1, source_target_pairs={{0,16},{8,24},{16,0},{24,8},{1,17},{9,25},{17,1},{25,9},{2,18},{10... | collective-permute-start | bytes 1572872 | tf_op jit(solution)/shard_map/ppermute | solution.py:582
  104.9 23.8 %collective-permute-start.2 = (f32[64,2048]{1,0:T(8,128)S(1)}, f32[64,2048]{1,0:T(8,128)S(1)}, u32[]{:S(2)}, u32[]{:S(2)}) collective-permute-start(f32[64,2048]{1,0:T(8,128)S(1)} %get-tuple-element.13), channel_id=1, source_target_pairs={{0,24},{8,16},{16,8},{24,0},{1,25},{9,17},{17,9},{25,1},{2,26},{10... | collective-permute-start | bytes 1572872 | tf_op jit(solution)/shard_map/ppermute | solution.py:582
  105.5 24.0 %copy-start.3 = (f32[64,2048]{1,0:T(8,128)}, f32[64,2048]{1,0:T(8,128)S(1)}, u32[]{:S(2)}) copy-start(f32[64,2048]{1,0:T(8,128)S(1)} %collective-permute-done.refs_1_) | copy-start | bytes 1572868
  118.4 11.1 %copy-start.4 = (f32[64,2048]{1,0:T(8,128)}, f32[64,2048]{1,0:T(8,128)S(1)}, u32[]{:S(2)}) copy-start(f32[64,2048]{1,0:T(8,128)S(1)} %collective-permute-done.1.refs_2_) | copy-start | bytes 1572868
  128.7 0.8 copy-start.5

commit v3 on v2

--- a/solution.py
+++ b/solution.py
@@ -20,6 +20,8 @@
 LANES = 128
 ROWS = 8
 SPLIT = 64
+GROUP = 8
+PAIR_UNROLL = 2
 
 paganin_strength = 10.0
 relax = 1.8
@@ -45,6 +47,17 @@
 
 def dot(left, right):
     return jnp.dot(left, right, preferred_element_type=f32)
+
+
+def repeat(count, body, unroll):
+    unroll = math.gcd(count, unroll)
+
+    def several(index, carry):
+        for step in range(unroll):
+            body(index * unroll + step)
+        return carry
+
+    lax.fori_loop(0, count // unroll, several, 0)
 
 
 def filter_tables(height):
@@ -235,25 +248,22 @@
     for part in range(2):
         half_ref[part] = vol_ref[:, :, part * LANES : (part + 1) * LANES]
 
-    def along_angle(t, carry):
+    def along_angle(t):
         along_ref[t] = shift_x_ref[...] * cos_ref[t] + shift_y_ref[...] * sin_ref[t]
-        return carry
-
-    lax.fori_loop(0, angles, along_angle, 0)
-
-    def first_order(q, carry):
+
+    repeat(angles, along_angle, 8)
+
+    def first_order(q):
         diff_ref[q] = slot_values(patches - 1 - q)
-        return carry
-
-    lax.fori_loop(0, pairs, first_order, 0)
+
+    repeat(pairs, first_order, 8)
     turned = reversed_exact(diff_ref[0:pairs].reshape(pairs * slices, VOX))
     start_ref[:, slices:both, :] = turned.reshape(pairs, slices, VOX)
 
-    def second_order(q, carry):
+    def second_order(q):
         start_ref[q, 0:slices, :] = slot_values(q)
-        return carry
-
-    lax.fori_loop(0, pairs, second_order, 0)
+
+    repeat(pairs, second_order, 8)
 
     ray = lax.broadcasted_iota(jnp.int32, (ROWS, VOX), 0).astype(f32)
 
@@ -274,7 +284,7 @@
     def forward(first):
         acc_ref[...] = jnp.zeros(acc_ref.shape, f32)
 
-        def pair(q, carry):
+        def pair(q):
             values = start_ref[q]
             if not first:
                 values = values + step_size * update_ref[q]
@@ -284,6 +294,7 @@
                     jnp.concatenate([high, high], axis=1),
                     jnp.concatenate([low, jnp.zeros_like(low)], axis=1),
                     jnp.ones((both, 2 * VOX), bf16),
+                    jnp.zeros((LANES - 3 * both, 2 * VOX), bf16),
                 ],
                 axis=0,
             )
@@ -297,25 +308,26 @@
                     (((1,), (1,)), ((), ())),
                     preferred_element_type=f32,
                 )
-                for t in range(chunk):
-                    angle = c * chunk + t
-                    rows = pl.ds(offset_ref[q * angles + angle], WIN)
-                    acc_ref[angle, rows, :] = (
-                        acc_ref[angle, rows, :] + sums[t * WIN : (t + 1) * WIN, :]
-                    )
-            return carry
-
-        lax.fori_loop(0, pairs, pair, 0)
-
-        def spread(t, carry):
+                for begin in range(0, chunk, GROUP):
+                    places = []
+                    for t in range(begin, min(begin + GROUP, chunk)):
+                        angle = c * chunk + t
+                        rows = pl.ds(offset_ref[q * angles + angle], WIN)
+                        values = acc_ref[angle, rows, :] + sums[t * WIN : (t + 1) * WIN, :]
+                        places.append((angle, rows, values))
+                    for angle, rows, values in places:
+                        acc_ref[angle, rows, :] = values
+
+        repeat(pairs, pair, PAIR_UNROLL)
+
+        def spread(t):
             rows = jnp.transpose(acc_ref[t]) * (1.0 / ROI)
             diff_ref[t] = rows[0:slices] + rows[both : both + slices]
             res_ref[t] = rows[slices:both] + rows[both + slices : 2 * both]
             if first:
                 gain_ref[t] = rows[2 * both : 2 * both + slices]
-            return carry
-
-        lax.fori_loop(0, angles, spread, 0)
+
+        repeat(angles, spread, 8)
         flat = (angles * slices, ACTIVE)
         full = (angles, slices, ACTIVE)
         mirrored = reversed_exact(res_ref[...].reshape(flat)).reshape(full)
@@ -341,7 +353,7 @@
             mixed = jnp.where(lane >= SPLIT, left, right)
             window_ref[:, 1, rows, :] = pltpu.roll(mixed, SPLIT, 2)
 
-        def pair(q, carry):
+        def pair(q):
             total = None
             for c in range(chunks):
                 if not cached:
@@ -367,9 +379,8 @@
                 piece = sums[0:both, 0:VOX] + sums[both:, 0:VOX] + sums[0:both, VOX:]
                 total = piece if total is None else total + piece
             update_ref[q] = total if first else update_ref[q] + total
-            return carry
-
-        lax.fori_loop(0, pairs, pair, 0)
+
+        repeat(pairs, pair, PAIR_UNROLL)
 
     forward(True)
     backward(True)
@@ -378,7 +389,7 @@
     turned = reversed_exact(update_ref[:, slices:both, :].reshape(pairs * slices, VOX))
     diff_ref[0:pairs] = turned.reshape(pairs, slices, VOX)
 
-    def finish(q, carry):
+    def finish(q):
         for patch, update in (
             (q, update_ref[q, 0:slices, :]),
             (patches - 1 - q, diff_ref[q]),
@@ -387,9 +398,8 @@
             values = slot_values(patch) + step_size * update
             half_ref[0, ray, rows, :] = values[:, 0:LANES]
             half_ref[1, ray, rows, :] = values[:, LANES : 2 * LANES]
-        return carry
-
-    lax.fori_loop(0, pairs, finish, 0)
+
+    repeat(pairs, finish, 8)
     for part in range(2):
         out_ref[:, 0:held_rows, part * LANES : (part + 1) * LANES] = half_ref[part]
     for t in range(angles):
@@ -442,7 +452,7 @@
         out_specs=vmem,
         scratch_shapes=[
             pltpu.VMEM((held, chunk * WIN, 2 * VOX), bf16),
-            pltpu.VMEM((angles, ACTIVE, 3 * both), f32),
+            pltpu.VMEM((angles, ACTIVE, LANES), f32),
             pltpu.VMEM((angles, ROWS, VOX), f32),
             pltpu.VMEM((pairs, both, VOX), f32),
             pltpu.VMEM((pairs, both, VOX), f32),
@@ -492,7 +502,7 @@
         gather_kernel,
         out_shape=jax.ShapeDtypeStruct((count,) + parts[0].shape, f32),
         in_specs=[pl.BlockSpec(memory_space=pltpu.SMEM)]
-        + [pl.BlockSpec(memory_space=pl.ANY)] * count,
+        + [pl.BlockSpec(memory_space=pltpu.VMEM)] * count,
         out_specs=pl.BlockSpec(memory_space=pl.ANY),
         scratch_shapes=[pltpu.SemaphoreType.DMA((count,))],
         cost_estimate=pl.CostEstimate(
@@ -571,6 +581,7 @@
     own_volume = lax.all_to_all(spread, "ray", split_axis=0, concat_axis=0, tiled=True)
 
     *parts, active = paganin(intensity.reshape(height, band), rank, n_slab)
+    active, own_volume = lax.optimization_barrier((active, own_volume))
     own_rays = lax.all_to_all(
         active.reshape(devices, slices, ACTIVE),
         ("slab", "ray"),
@@ -593,6 +604,7 @@
         lower = result[:, padded * slots :].reshape(n_ray, n_slab, padded, ACTIVE)
         lower = lower[:, :, :slices].reshape(n_ray, n_slab * slices, ACTIVE)
         result = jnp.concatenate([result[:, : slices * slots], lower], axis=1)
+    result, parts = lax.optimization_barrier((result, parts))
     result = lax.all_to_all(result, "ray", split_axis=0, concat_axis=0, tiled=True)
     sinogram = gather_parts(parts, rank)
     reconstruction, residual = finish(result, sinogram, volume.shape)

time: 196 us -> 115 us (0.59)
  Pallas kernels: 125 us -> 51.2 us
  blocking collectives: 17.8 us -> 0 us
  starting transfers between devices: 9.03 us -> 18.8 us
  waiting for transfers between devices: 35.5 us -> 37.8 us
    pallas_call x1, Pallas kernels: 64.7 us -> 2.87 us  [gather_parts(): pl.pallas_call(gather_kernel, out_shape=jax.ShapeDtypeStruct((count,) + p...]
    ppermute x3, waiting for transfers between devices: 23.3 us -> 0.01 us  [local(): lax.ppermute(part, 'slab', [(i, i ^ d) for i in range(n_slab)])]
    all_to_all x1 -> x0, blocking collectives: 17.8 us -> none  [local(): lax.all_to_all(active.reshape(devices, slices, ACTIVE), ('slab', 'ray'),...]
    all_to_all x1, waiting for transfers between devices: 0.01 us -> 17.2 us  [local(): lax.all_to_all(result, 'ray', split_axis=0, concat_axis=0, tiled=True)]
    all_to_all x0 -> x1, waiting for transfers between devices: none -> 17.2 us  [local(): lax.all_to_all(active.reshape(devices, slices, ACTIVE), ('slab', 'ray'),...]
    pallas_call x1, Pallas kernels: 54.3 us -> 41.8 us  [sirt(): pl.pallas_call(functools.partial(sirt_kernel, step_size, chunk), out_shap...]
    all_to_all x1, waiting for transfers between devices: 12.2 us -> 3.32 us  [local(): lax.all_to_all(spread, 'ray', split_axis=0, concat_axis=0, tiled=True)]
    all_to_all x1, starting transfers between devices: 3.5 us -> 7.26 us  [local(): lax.all_to_all(spread, 'ray', split_axis=0, concat_axis=0, tiled=True)]
  transfers between devices with their start and end apart: 5 -> 6, of which waited for: 3 -> 3; matrix products, arithmetic and copies ran while one was open for 1% -> 2% of each run, Pallas kernels for 33% -> 44%
where the time goes in v3:
time: 115 us
  Pallas kernels  51.2 us (45%)
  waiting for transfers between devices  37.8 us (33%)
  starting transfers between devices  18.8 us (16%)
  local copies, waits for them, and re-layouts  4.42 us (4%)
  other arithmetic  1.93 us (2%)
    pallas_call x1, Pallas kernels, sirt(): pl.pallas_call(functools.partial(sirt_kernel, step_size, chunk), out_shap...  41.8 us
    all_to_all x1, waiting for transfers between devices, local(): lax.all_to_all(result, 'ray', split_axis=0, concat_axis=0, tiled=True)  17.2 us
    all_to_all x1, waiting for transfers between devices, local(): lax.all_to_all(active.reshape(devices, slices, ACTIVE), ('slab', 'ray'),...  17.2 us
    all_to_all x1, starting transfers between devices, local(): lax.all_to_all(spread, 'ray', split_axis=0, concat_axis=0, tiled=True)  7.26 us
    all_to_all x1, starting transfers between devices, local(): lax.all_to_all(result, 'ray', split_axis=0, concat_axis=0, tiled=True)  6 us
    pallas_call x1, Pallas kernels, paganin(): pl.pallas_call(filter_kernel, out_shape=[jax.ShapeDtypeStruct((height //...  5.6 us
    unnamed x26, local copies, waits for them, and re-layouts  4.06 us
    all_to_all x1, starting transfers between devices, local(): lax.all_to_all(active.reshape(devices, slices, ACTIVE), ('slab', 'ray'),...  3.68 us
  transfers between devices with their start and end apart: 6, of which 3 were waited for; matrix products, arithmetic and copies ran while one was open for 2% of the time, Pallas kernels for 44%

profile of v3, /device:TPU:0, one launch (start us, length us, event | category | flops | bytes accessed | tf_op | source)
XLA Modules:
  0.0 114.9 jit_solution(8718743057843677690)
XLA Ops:
  0.6 7.3 %all-to-all-start = ((f32[8,64,256]{2,1,0:T(8,128)}), f32[8,64,256]{2,1,0:T(8,128)}, u32[]{:S(2)}, u32[]{:S(2)}) async-start(f32[8,64,256]{2,1,0:T(8,128)} %bitcast.9), calls=%async_computation | async-start | bytes 1048576 | tf_op jit(solution)/shard_map/all_to_all | solution.py:581
  7.9 0.0 copy-start.1
  7.9 1.6 %copy-done.1 = f32[1,1,256,2048]{3,2,1,0:T(8,128)S(1)} copy-done((f32[1,1,256,2048]{3,2,1,0:T(8,128)S(1)}, f32[1,1,256,2048]{3,2,1,0:T(8,128)}, u32[]{:S(2)}) %copy-start.1) | copy-done | bytes 2097176
  9.5 0.0 copy-start.2
  9.5 1.0 copy-done.2
  10.4 0.0 copy-start.7
  10.4 0.0 copy-start.10
  10.4 0.0 copy-start.11
  10.4 0.0 copy-start.12
  10.4 5.6 %paganin.1 = (f32[64,2048]{1,0:T(8,128)S(1)}, f32[64,2048]{1,0:T(8,128)S(1)}, f32[64,2048]{1,0:T(8,128)S(1)}, f32[64,2048]{1,0:T(8,128)S(1)}, f32[256,256]{1,0:T(8,128)}) custom-call(s32[1]{0:T(128)} %bitcast.rank_ref, f32[256,2048]{1,0:T(8,128)S(1)} %bitcast.7, f32[264,256]{1,0:T(8,128)S(1)} %copy-done.2), custom_call_target="tpu_custom_call" | custom-call | flops 8589934592 | bytes 4194304 | tf_op jit(solution)/shard_map/paganin/pallas_call | solution.py:172
  16.1 0.0 copy-start
  16.1 0.8 copy-done
  16.8 0.0 collective-permute-start
  16.9 1.5 %collective-permute-start.1 = (f32[64,2048]{1,0:T(8,128)S(1)}, f32[64,2048]{1,0:T(8,128)S(1)}, u32[]{:S(2)}, u32[]{:S(2)}) collective-permute-start(f32[64,2048]{1,0:T(8,128)S(1)} %get-tuple-element.21), channel_id=1, source_target_pairs={{0,16},{8,24},{16,0},{24,8},{1,17},{9,25},{17,1},{25,9},{2,18},{10... | collective-permute-start | bytes 1572872 | tf_op jit(solution)/shard_map/ppermute | solution.py:593
  18.4 0.3 collective-permute-start.2
  18.7 0.0 copy-done.7
  18.8 0.1 cos.6.cos_ref
  18.8 0.0 copy-start.8
  18.8 0.1 sin.6.sin_ref
  18.9 0.1 sub.23
  19.0 0.0 copy-done.10
  19.0 0.0 copy-done.11
  19.0 0.1 add_add_fusion
  19.1 0.1 add.64
  19.2 3.3 %all-to-all-done.vol_ref = f32[8,64,256]{2,1,0:T(8,128)} async-done(((f32[8,64,256]{2,1,0:T(8,128)}), f32[8,64,256]{2,1,0:T(8,128)}, u32[]{:S(2)}, u32[]{:S(2)}) %all-to-all-start) | async-done | bytes 524320 | tf_op jit(solution)/shard_map/all_to_all | solution.py:581
  22.5 3.7 %all-to-all-start.1 = ((f32[32,8,256]{2,1,0:T(8,128)}), f32[32,8,256]{2,1,0:T(8,128)S(1)}, u32[]{:S(2)}, u32[]{:S(2)}) async-start(f32[32,8,256]{2,1,0:T(8,128)} %bitcast.3), calls=%async_computation.1 | async-start | bytes 524288 | tf_op jit(solution)/shard_map/all_to_all | solution.py:585
  26.2 0.0 copy-done.12
  26.2 0.7 select_reduce_fusion.slot_ref
  26.8 0.6 fusion.1.place_ref
  27.4 0.6 add_select_fusion
  28.0 17.2 %all-to-all-done.1.sino_ref = f32[32,8,256]{2,1,0:T(8,128)S(1)} async-done(((f32[32,8,256]{2,1,0:T(8,128)}), f32[32,8,256]{2,1,0:T(8,128)S(1)}, u32[]{:S(2)}, u32[]{:S(2)}) %all-to-all-start.1) | async-done | bytes 262176 | tf_op jit(solution)/shard_map/all_to_all | solution.py:585
  45.2 0.0 copy-start.6
  45.2 0.0 copy-done.8
  45.2 0.0 copy-done.9
  45.2 0.7 copy-done.6
  45.9 41.8 %sirt.1 = f32[8,96,256]{2,1,0:T(8,128)} custom-call(s32[1024]{0:T(1024)} %get-tuple-element.36.offset_ref, s32[1024]{0:T(1024)} %get-tuple-element.35.tile_ref, s32[1024]{0:T(1024)} %get-tuple-element.34.turn_ref, f32[1024]{0:T(1024)} %fusion.1.place_ref, s32[64]{0:T(128)} %select_reduce_fusion.slot_ref, f32[32]{0:T(128)} %copy-done.8, f32[32]{0:T(128)} %copy-done.9, ...), custom_call_target="tpu_custom_call" | custom-call | flops 38654705664 | bytes 2097152 | tf_op jit(solution)/shard_map/sirt/pallas_call | solution.py:448
  87.8 0.0 collective-permute-done.refs_1_
  87.8 0.0 collective-permute-done.1.refs_2_
  87.8 0.0 copy-start.4
  87.8 0.0 collective-permute-done.2.refs_3_
  87.8 0.0 copy-start.5
  87.8 6.0 %all-to-all-start.2 = ((f32[8,96,256]{2,1,0:T(8,128)}), f32[8,96,256]{2,1,0:T(8,128)S(1)}, u32[]{:S(2)}, u32[]{:S(2)}) async-start(f32[8,96,256]{2,1,0:T(8,128)} %sirt.1), calls=%async_computation.2 | async-start | bytes 1572864 | tf_op jit(solution)/shard_map/all_to_all | solution.py:608
  93.8 0.0 copy-done.3
  93.8 0.0 copy-done.4
  93.8 0.0 copy-done.5
  93.9 2.9 %gather_parts.1.sino_ref = f32[4,64,2048]{2,1,0:T(8,128)} custom-call(s32[1]{0:T(128)} %bitcast.rank_ref, f32[64,2048]{1,0:T(8,128)} %copy-done, f32[64,2048]{1,0:T(8,128)} %copy-done.3, f32[64,2048]{1,0:T(8,128)} %copy-done.4, f32[64,2048]{1,0:T(8,128)} %copy-done.5), custom_call_target="tpu_custom_call" | custom-call | bytes 4194304 | tf_op jit(solution)/shard_map/gather_parts/pallas_call | solution.py:501
  96.7 17.2 %all-to-all-done.2.got_ref = f32[8,96,256]{2,1,0:T(8,128)S(1)} async-done(((f32[8,96,256]{2,1,0:T(8,128)}), f32[8,96,256]{2,1,0:T(8,128)S(1)}, u32[]{:S(2)}, u32[]{:S(2)}) %all-to-all-start.2) | async-done | bytes 786464 | tf_op jit(solution)/shard_map/all_to_all | solution.py:608
  114.0 0.9 finish.1
  (5 shorter events, 0.1 us)
Async XLA Ops:
  0.6 21.9 %all-to-all-start = ((f32[8,64,256]{2,1,0:T(8,128)}), f32[8,64,256]{2,1,0:T(8,128)}, u32[]{:S(2)}, u32[]{:S(2)}) async-start(f32[8,64,256]{2,1,0:T(8,128)} %bitcast.9), calls=%async_computation | async-start | bytes 1048576 | tf_op jit(solution)/shard_map/all_to_all | solution.py:581
  7.9 1.6 %copy-start.1 = (f32[1,1,256,2048]{3,2,1,0:T(8,128)S(1)}, f32[1,1,256,2048]{3,2,1,0:T(8,128)}, u32[]{:S(2)}) copy-start(f32[1,1,256,2048]{3,2,1,0:T(8,128)} %param.10) | copy-start | bytes 6291460
  9.5 1.0 copy-start.2
  10.4 8.3 %copy-start.7 = (f32[4,8]{1,0:T(4,128)S(1)}, f32[4,8]{1,0:T(4,128)}, u32[]{:S(2)}) copy-start(f32[4,8]{1,0:T(4,128)} %param.11) | copy-start | bytes 388
  10.4 8.6 %copy-start.10 = (f32[32]{0:T(128)S(1)}, f32[32]{0:T(128)}, u32[]{:S(2)}) copy-start(f32[32]{0:T(128)} %constant.83) | copy-start | bytes 388
  10.4 8.6 %copy-start.11 = (f32[32]{0:T(128)S(1)}, f32[32]{0:T(128)}, u32[]{:S(2)}) copy-start(f32[32]{0:T(128)} %constant.82) | copy-start | bytes 388
  10.4 15.7 %copy-start.12 = (s32[64]{0:T(128)S(1)}, s32[64]{0:T(128)}, u32[]{:S(2)}) copy-start(s32[64]{0:T(128)} %param.13) | copy-start | bytes 772
  16.1 0.8 copy-start
  16.8 70.9 %collective-permute-start = (f32[64,2048]{1,0:T(8,128)S(1)}, f32[64,2048]{1,0:T(8,128)S(1)}, u32[]{:S(2)}, u32[]{:S(2)}) collective-permute-start(f32[64,2048]{1,0:T(8,128)S(1)} %get-tuple-element.20), channel_id=1, source_target_pairs={{0,8},{8,0},{16,24},{24,16},{1,9},{9,1},{17,25},{25,17},{2,10},{10... | collective-permute-start | bytes 1572872 | tf_op jit(solution)/shard_map/ppermute | solution.py:593
  16.9 70.9 %collective-permute-start.1 = (f32[64,2048]{1,0:T(8,128)S(1)}, f32[64,2048]{1,0:T(8,128)S(1)}, u32[]{:S(2)}, u32[]{:S(2)}) collective-permute-start(f32[64,2048]{1,0:T(8,128)S(1)} %get-tuple-element.21), channel_id=1, source_target_pairs={{0,16},{8,24},{16,0},{24,8},{1,17},{9,25},{17,1},{25,9},{2,18},{10... | collective-permute-start | bytes 1572872 | tf_op jit(solution)/shard_map/ppermute | solution.py:593
  18.4 69.4 %collective-permute-start.2 = (f32[64,2048]{1,0:T(8,128)S(1)}, f32[64,2048]{1,0:T(8,128)S(1)}, u32[]{:S(2)}, u32[]{:S(2)}) collective-permute-start(f32[64,2048]{1,0:T(8,128)S(1)} %get-tuple-element.22), channel_id=1, source_target_pairs={{0,24},{8,16},{16,8},{24,0},{1,25},{9,17},{17,9},{25,1},{2,26},{10... | collective-permute-start | bytes 1572872 | tf_op jit(solution)/shard_map/ppermute | solution.py:593
  18.8 26.4 %copy-start.8 = (f32[32]{0:T(128)}, f32[32]{0:T(128)S(1)}, u32[]{:S(2)}) copy-start(f32[32]{0:T(128)S(1)} %cos.6.cos_ref) | copy-start | bytes 388
  18.9 26.3 %copy-start.9 = (f32[32]{0:T(128)}, f32[32]{0:T(128)S(1)}, u32[]{:S(2)}) copy-start(f32[32]{0:T(128)S(1)} %sin.6.sin_ref) | copy-start | bytes 388
  22.5 22.7 %all-to-all-start.1 = ((f32[32,8,256]{2,1,0:T(8,128)}), f32[32,8,256]{2,1,0:T(8,128)S(1)}, u32[]{:S(2)}, u32[]{:S(2)}) async-start(f32[32,8,256]{2,1,0:T(8,128)} %bitcast.3), calls=%async_computation.1 | async-start | bytes 524288 | tf_op jit(solution)/shard_map/all_to_all | solution.py:585
  45.2 0.7 copy-start.6
  87.8 6.0 %copy-start.3 = (f32[64,2048]{1,0:T(8,128)}, f32[64,2048]{1,0:T(8,128)S(1)}, u32[]{:S(2)}) copy-start(f32[64,2048]{1,0:T(8,128)S(1)} %collective-permute-done.refs_1_) | copy-start | bytes 1572868
  87.8 6.0 %copy-start.4 = (f32[64,2048]{1,0:T(8,128)}, f32[64,2048]{1,0:T(8,128)S(1)}, u32[]{:S(2)}) copy-start(f32[64,2048]{1,0:T(8,128)S(1)} %collective-permute-done.1.refs_2_) | copy-start | bytes 1572868
  87.8 6.0 %copy-start.5 = (f32[64,2048]{1,0:T(8,128)}, f32[64,2048]{1,0:T(8,128)S(1)}, u32[]{:S(2)}) copy-start(f32[64,2048]{1,0:T(8,128)S(1)} %collective-permute-done.2.refs_3_) | copy-start | bytes 1572868
  87.8 26.1 %all-to-all-start.2 = ((f32[8,96,256]{2,1,0:T(8,128)}), f32[8,96,256]{2,1,0:T(8,128)S(1)}, u32[]{:S(2)}, u32[]{:S(2)}) async-start(f32[8,96,256]{2,1,0:T(8,128)} %sirt.1), calls=%async_computation.2 | async-start | bytes 1572864 | tf_op jit(solution)/shard_map/all_to_all | solution.py:608

commit v4 on v3

v4 whole, which is shorter than its diff:
```python
import functools
import math

import jax
import jax.numpy as jnp
import ml_dtypes
import numpy as np
from jax import lax
from jax.experimental import pallas as pl
from jax.experimental.pallas import tpu as pltpu
from jax.sharding import PartitionSpec as P

BAND = 2048
PGRID = 8
ROI = 128
SIDE = 16
VOX = SIDE * SIDE
WIN = 24
ACTIVE = 256
LANES = 128
ROWS = 8
SPLIT = 64
GROUP = 8
PAIR_UNROLL = 2

paganin_strength = 10.0
relax = 1.8
row_floor = 0.25

bf16 = jnp.bfloat16
f32 = jnp.float32


def halves(values):
    high = values.astype(bf16)
    low = (values - high.astype(f32)).astype(bf16)
    return high, low


def thirds(values):
    high = values.astype(bf16)
    rest = values - high.astype(f32)
    middle = rest.astype(bf16)
    low = (rest - middle.astype(f32)).astype(bf16)
    return high, middle, low


def dot(left, right):
    return jnp.dot(left, right, preferred_element_type=f32)


def repeat(count, body, unroll):
    unroll = math.gcd(count, unroll)

    def several(index, carry):
        for step in range(unroll):
            body(index * unroll + step)
        return carry

    lax.fori_loop(0, count // unroll, several, 0)


def filter_tables(height):
    index = np.arange(height)
    phase = 2.0 * np.pi * (np.outer(index, index) % height) / height
    cas = (np.cos(phase) + np.sin(phase)) / math.sqrt(height)
    row_freq = 2.0 - 2.0 * np.cos(2.0 * np.pi * index / height)
    middle = (1.0 + paganin_strength * row_freq) / paganin_strength + 2.0
    rho = (middle - np.sqrt(middle * middle - 4.0)) / 2.0
    return np.concatenate([cas, np.repeat(rho[None, :], ROWS, axis=0)], axis=0).astype(np.float32)


def chunk_carry(ends, power, forward):
    shift = 1
    for _ in range(3):
        ends = ends + power * pltpu.roll(ends, shift if forward else ROWS - shift, 0)
        power = power * power
        shift *= 2
    return pltpu.roll(ends, 1 if forward else ROWS - 1, 0) / (1.0 - power)


def filter_kernel(rank_ref, image_ref, table_ref, *refs):
    *part_refs, active_ref, out_ref, spec_ref, up_ref, down_ref = refs
    height, width = image_ref.shape
    rank = rank_ref[0]
    share = height // len(part_refs)
    length = width // ROWS
    blocks = height // LANES
    unroll = 8
    cas_high, cas_low = halves(table_ref[0:height, :])
    rho_all = table_ref[height : height + ROWS, :]
    rhos = [rho_all[:, b * LANES : (b + 1) * LANES] for b in range(blocks)]
    zeros = [jnp.zeros((ROWS, LANES), f32)] * blocks

    def transform(values):
        high, low = halves(values)
        return dot(high, cas_high) + dot(low, cas_high) + dot(high, cas_low)

    for c in range(ROWS):
        image = 1.0 - image_ref[:, c * length : (c + 1) * length]
        spectrum = transform(jnp.transpose(image))
        for b in range(blocks):
            spec_ref[b, pl.ds(c, length, stride=ROWS), :] = spectrum[
                :, b * LANES : (b + 1) * LANES
            ]

    def rows(position):
        return pl.ds(pl.multiple_of(position * ROWS, ROWS), ROWS)

    def advance(position, ups, downs):
        ups = [spec_ref[b, rows(position), :] + rhos[b] * ups[b] for b in range(blocks)]
        back = length - 1 - position
        downs = [spec_ref[b, rows(back), :] + rhos[b] * downs[b] for b in range(blocks)]
        return ups, downs

    def sweep(index, carry):
        ups, downs = carry
        for step in range(unroll):
            ups, downs = advance(index * unroll + step, ups, downs)
        return ups, downs

    ups, downs = lax.fori_loop(0, length // unroll, sweep, (zeros, zeros))
    powers = list(rhos)
    for _ in range(int(math.log2(length))):
        powers = [power * power for power in powers]
    ups = [chunk_carry(ups[b], powers[b], True) for b in range(blocks)]
    downs = [chunk_carry(downs[b], powers[b], False) for b in range(blocks)]
    scales = [rho / (paganin_strength * (1.0 - rho * rho)) for rho in rhos]

    def outer(index, carry):
        ups, downs = carry
        for step in range(unroll):
            position = index * unroll + step
            ups, downs = advance(position, ups, downs)
            for b in range(blocks):
                up_ref[b, rows(position), :] = ups[b]
                down_ref[b, rows(position), :] = downs[b]
        return ups, downs

    def inner(index, carry):
        ups, downs = carry
        for step in range(unroll):
            position = index * unroll + step
            back = length - 1 - position
            ups, downs = advance(position, ups, downs)
            for b in range(blocks):
                here = ups[b] + down_ref[b, rows(back), :] - spec_ref[b, rows(position), :]
                there = downs[b] + up_ref[b, rows(back), :] - spec_ref[b, rows(back), :]
                up_ref[b, rows(position), :] = here * scales[b]
                up_ref[b, rows(back), :] = there * scales[b]
        return ups, downs

    half = length // 2 // unroll
    carry = lax.fori_loop(0, half, outer, (ups, downs))
    lax.fori_loop(half, 2 * half, inner, carry)

    offset = (width - ACTIVE) // 2
    for c in range(ROWS):
        spectrum = jnp.concatenate(
            [up_ref[b, pl.ds(c, length, stride=ROWS), :] for b in range(blocks)], axis=1
        )
        filtered = 1.0 - jnp.transpose(transform(spectrum))
        out_ref[:, c * length : (c + 1) * length] = -jnp.log(filtered)
    active_ref[...] = out_ref[:, offset : offset + ACTIVE]
    for d, part_ref in enumerate(part_refs):
        part_ref[...] = out_ref[pl.ds(pl.multiple_of((rank ^ d) * share, share), share), :]


def paganin(image, rank, parts):
    height, width = image.shape
    blocks = height // LANES
    return pl.pallas_call(
        filter_kernel,
        out_shape=[jax.ShapeDtypeStruct((height // parts, width), f32)] * parts
        + [jax.ShapeDtypeStruct((height, ACTIVE), f32)],
        in_specs=[pl.BlockSpec(memory_space=pltpu.SMEM)]
        + [pl.BlockSpec(memory_space=pltpu.VMEM)] * 2,
        out_specs=[pl.BlockSpec(memory_space=pltpu.VMEM)] * (parts + 1),
        scratch_shapes=[
            pltpu.VMEM((height, width), f32),
            pltpu.VMEM((blocks, width, LANES), f32),
            pltpu.VMEM((blocks, width, LANES), f32),
            pltpu.VMEM((blocks, width // 2, LANES), f32),
        ],
        compiler_params=pltpu.CompilerParams(vmem_limit_bytes=32 * 2**20),
        cost_estimate=pl.CostEstimate(
            flops=64 * height * height * width,
            bytes_accessed=8 * height * width,
            transcendentals=height * width,
        ),
        name="paganin",
    )(rank.reshape(1), image, jnp.asarray(filter_tables(height)))


def reversed_exact(values, flip):
    return sum(dot(part, flip) for part in thirds(values))


class Weights:
    def __init__(self, ref, along_ref, place_ref, angles, chunk, held):
        self.ref = ref
        self.along_ref = along_ref
        self.place_ref = place_ref
        self.angles = angles
        self.chunk = chunk
        self.held = held
        self.ray = lax.broadcasted_iota(jnp.int32, (ROWS, VOX), 0).astype(f32)

    def prepare(self, shift_x_ref, shift_y_ref, cos_ref, sin_ref):
        def along_angle(t):
            self.along_ref[t] = shift_x_ref[...] * cos_ref[t] + shift_y_ref[...] * sin_ref[t]

        repeat(self.angles, along_angle, 8)

    def make(self, q, c):
        place = q if self.held else 0
        for two in range(self.chunk // 2):
            pieces = []
            for t in (2 * two, 2 * two + 1):
                angle = c * self.chunk + t
                along = self.along_ref[angle] + self.place_ref[q * self.angles + angle]
                base = self.ray - along
                for group in range(WIN // ROWS):
                    distance = base + float(group * ROWS)
                    pieces.append(jnp.maximum(0.0, 1.0 - jnp.abs(distance)))
            high, low = halves(jnp.concatenate(pieces, axis=0))
            self.ref[place, 2 * two * WIN : (2 * two + 2) * WIN, 0:VOX] = high
            self.ref[place, 2 * two * WIN : (2 * two + 2) * WIN, VOX : 2 * VOX] = low

    def get(self, q):
        return self.ref[q if self.held else 0]


def project(weights, make, values_of, offset_ref, acc_ref, pairs, both):
    angles, chunk = weights.angles, weights.chunk
    acc_ref[...] = jnp.zeros(acc_ref.shape, f32)

    def pair(q):
        high, low = halves(values_of(q))
        operand = jnp.concatenate(
            [
                jnp.concatenate([high, high], axis=1),
                jnp.concatenate([low, jnp.zeros_like(low)], axis=1),
                jnp.ones((both, 2 * VOX), bf16),
                jnp.zeros((LANES - 3 * both, 2 * VOX), bf16),
            ],
            axis=0,
        )
        for c in range(angles // chunk):
            if make:
                weights.make(q, c)
            sums = lax.dot_general(
                weights.get(q),
                operand,
                (((1,), (1,)), ((), ())),
                preferred_element_type=f32,
            )
            for begin in range(0, chunk, GROUP):
                places = []
                for t in range(begin, min(begin + GROUP, chunk)):
                    angle = c * chunk + t
                    rows = pl.ds(offset_ref[q * angles + angle], WIN)
                    values = acc_ref[angle, rows, :] + sums[t * WIN : (t + 1) * WIN, :]
                    places.append((angle, rows, values))
                for angle, rows, values in places:
                    acc_ref[angle, rows, :] = values

    repeat(pairs, pair, PAIR_UNROLL)


def spread_rays(acc_ref, direct_ref, mirror_ref, total_ref, slices):
    both = 2 * slices

    def spread(t):
        rows = jnp.transpose(acc_ref[t]) * (1.0 / ROI)
        direct_ref[t] = rows[0:slices] + rows[both : both + slices]
        mirror_ref[t] = rows[slices:both] + rows[both + slices : 2 * both]
        if total_ref is not None:
            total_ref[t] = rows[2 * both : 2 * both + slices]

    repeat(acc_ref.shape[0], spread, 8)


def turn_rays(values, flip):
    shape = values.shape
    return reversed_exact(values.reshape(-1, shape[-1]), flip).reshape(shape)


def back_project(weights, weighted, flip, window_ref, tile_ref, turn_ref, store, pairs):
    angles, slices, _ = weighted.shape
    chunk = weights.chunk
    both = 2 * slices
    width = chunk * WIN
    high, low = halves(weighted.reshape(angles * slices, ACTIVE))
    mirrored = (dot(high, flip) + dot(low, flip)).reshape(weighted.shape)
    lane = lax.broadcasted_iota(jnp.int32, (angles, slices, LANES), 2)
    lane_rows = lax.broadcasted_iota(jnp.int32, (both, LANES), 1)
    for part, source in enumerate((weighted, mirrored)):
        rows = slice(part * slices, (part + 1) * slices)
        left = source[:, :, 0:LANES]
        right = source[:, :, LANES : 2 * LANES]
        window_ref[:, 0, rows, :] = left
        window_ref[:, 2, rows, :] = right
        mixed = jnp.where(lane >= SPLIT, left, right)
        window_ref[:, 1, rows, :] = pltpu.roll(mixed, SPLIT, 2)

    def pair(q):
        total = None
        for c in range(angles // chunk):
            if not weights.held:
                weights.make(q, c)
            tiles = [None] * (-(-width // LANES))
            for t in range(chunk):
                index = q * angles + c * chunk + t
                piece = pltpu.roll(
                    window_ref[c * chunk + t, tile_ref[index]], turn_ref[index], 1
                )
                begin = t * WIN
                for place in range(begin // LANES, (begin + WIN - 1) // LANES + 1):
                    if tiles[place] is None:
                        tiles[place] = piece
                    else:
                        tiles[place] = jnp.where(
                            lane_rows >= begin - place * LANES, piece, tiles[place]
                        )
            high, low = halves(jnp.concatenate(tiles, axis=1))
            sums = dot(jnp.concatenate([high, low], axis=0), weights.get(q))
            piece = sums[0:both, 0:VOX] + sums[both:, 0:VOX] + sums[0:both, VOX:]
            total = piece if total is None else total + piece
        store(q, total)

    repeat(pairs, pair, PAIR_UNROLL)


def first_kernel(
    sizes,
    offset_ref,
    place_ref,
    slot_ref,
    cos_ref,
    sin_ref,
    vol_ref,
    flip_ref,
    shift_x_ref,
    shift_y_ref,
    weight_ref,
    start_ref,
    predicted_ref,
    gain_ref,
    acc_ref,
    along_ref,
    half_ref,
    mirror_ref,
):
    angles, chunk, held, slots = sizes
    patches = slot_ref.shape[0]
    pairs, both, _ = start_ref.shape
    slices = both // 2
    flip = flip_ref[...]

    def slot_values(patch):
        slot = slot_ref[patch]
        rows = pl.ds(slot % slots, slices, stride=slots)
        return jnp.concatenate(
            [half_ref[part, slot // slots, rows, :] for part in range(2)], axis=1
        )

    weights = Weights(weight_ref, along_ref, place_ref, angles, chunk, held)
    weights.prepare(shift_x_ref, shift_y_ref, cos_ref, sin_ref)
    for part in range(2):
        half_ref[part] = vol_ref[:, :, part * LANES : (part + 1) * LANES]

    def order(q):
        start_ref[q, 0:slices, :] = slot_values(q)
        mirror_ref[q] = slot_values(patches - 1 - q)

    repeat(pairs, order, 8)
    start_ref[:, slices:both, :] = turn_rays(mirror_ref[0:pairs], flip)
    project(weights, True, lambda q: start_ref[q], offset_ref, acc_ref, pairs, both)
    spread_rays(acc_ref, predicted_ref, mirror_ref, gain_ref, slices)
    predicted_ref[...] = predicted_ref[...] + turn_rays(mirror_ref[0:angles], flip)
    direct = gain_ref[...]
    gain_ref[...] = 1.0 / jnp.maximum(direct + turn_rays(direct, flip), row_floor)


def second_kernel(
    sizes,
    step_size,
    offset_ref,
    place_ref,
    tile_ref,
    turn_ref,
    cos_ref,
    sin_ref,
    start_ref,
    predicted_ref,
    gain_ref,
    sino_ref,
    flip_ref,
    shift_x_ref,
    shift_y_ref,
    weight_ref,
    update_ref,
    res_ref,
    acc_ref,
    along_ref,
    direct_ref,
    mirror_ref,
    window_ref,
):
    angles, chunk, held, _ = sizes
    pairs, both, _ = start_ref.shape
    slices = both // 2
    rays = res_ref.shape[0]
    flip = flip_ref[...]
    weights = Weights(weight_ref, along_ref, place_ref, angles, chunk, held)
    if not held:
        weights.prepare(shift_x_ref, shift_y_ref, cos_ref, sin_ref)
    weighted = (sino_ref[...] - predicted_ref[...]) * gain_ref[...] * (1.0 / ROI)

    def store(q, total):
        update_ref[q] = total

    back_project(weights, weighted, flip, window_ref, tile_ref, turn_ref, store, pairs)

    def values_of(q):
        return start_ref[q] + step_size * update_ref[q]

    project(weights, not held, values_of, offset_ref, acc_ref, pairs, both)
    spread_rays(acc_ref, direct_ref, mirror_ref, None, slices)
    residual = sino_ref[...] - direct_ref[...] - turn_rays(mirror_ref[...], flip)
    for t in range(angles):
        begin = t // rays * slices
        res_ref[t % rays, begin : begin + slices, :] = residual[t]


def third_kernel(
    sizes,
    step_size,
    place_ref,
    tile_ref,
    turn_ref,
    slot_ref,
    cos_ref,
    sin_ref,
    update_ref,
    res_ref,
    gain_ref,
    vol_ref,
    flip_ref,
    shift_x_ref,
    shift_y_ref,
    weight_ref,
    out_ref,
    along_ref,
    total_ref,
    mirror_ref,
    window_ref,
    half_ref,
):
    angles, chunk, held, slots = sizes
    patches = slot_ref.shape[0]
    pairs, both, _ = update_ref.shape
    slices = both // 2
    rays = res_ref.shape[0]
    flip = flip_ref[...]
    weights = Weights(weight_ref, along_ref, place_ref, angles, chunk, held)
    if not held:
        weights.prepare(shift_x_ref, shift_y_ref, cos_ref, sin_ref)
    residual = [
        res_ref[t % rays, t // rays * slices : (t // rays + 1) * slices, :][None]
        for t in range(angles)
    ]
    weighted = jnp.concatenate(residual, axis=0) * gain_ref[...] * (1.0 / ROI)

    def store(q, total):
        total_ref[q] = (update_ref[q] + total) * step_size

    back_project(weights, weighted, flip, window_ref, tile_ref, turn_ref, store, pairs)
    mirror_ref[...] = turn_rays(total_ref[:, slices:both, :], flip)
    for part in range(2):
        half_ref[part] = vol_ref[:, :, part * LANES : (part + 1) * LANES]

    def finish(q):
        for patch, update in (
            (q, total_ref[q, 0:slices, :]),
            (patches - 1 - q, mirror_ref[q]),
        ):
            slot = slot_ref[patch]
            rows = pl.ds(slot % slots, slices, stride=slots)
            for part in range(2):
                half_ref[part, slot // slots, rows, :] = (
                    half_ref[part, slot // slots, rows, :]
                    + update[:, part * LANES : (part + 1) * LANES]
                )

    repeat(pairs, finish, 8)
    for part in range(2):
        out_ref[:, :, part * LANES : (part + 1) * LANES] = half_ref[part]


def call(kernel, name, inputs, outputs, scratch, micros, room):
    smem = pl.BlockSpec(memory_space=pltpu.SMEM)
    vmem = pl.BlockSpec(memory_space=pltpu.VMEM)
    return pl.pallas_call(
        kernel,
        out_shape=[jax.ShapeDtypeStruct(shape, dtype) for shape, dtype in outputs],
        in_specs=[smem if value.ndim == 1 else vmem for value in inputs],
        out_specs=[vmem] * len(outputs),
        scratch_shapes=[pltpu.VMEM(shape, dtype) for shape, dtype in scratch],
        compiler_params=pltpu.CompilerParams(vmem_limit_bytes=room * 2**20),
        cost_estimate=pl.CostEstimate(
            flops=int(micros * 1e9), bytes_accessed=4 * 2**20, transcendentals=0
        ),
        name=name,
    )(*inputs)


class Sirt:
    def __init__(self, theta, vol_list, slices, slots, rays, step_size):
        angles = theta.shape[0]
        patches = vol_list.shape[0]
        pairs = patches // 2
        both = 2 * slices
        chunk = math.gcd(angles, 32)
        self.held = angles == chunk
        self.room = 24 if self.held else 48
        self.sizes = (angles, chunk, self.held, slots)
        self.step_size = step_size
        self.rays = rays
        self.patches = patches
        centre = (ROI - 1) / 2.0
        ids = np.arange(pairs)
        centre_x = (ids // PGRID * float(SIDE) + (SIDE - 1) / 2.0 - centre).astype(np.float32)
        centre_y = (ids % PGRID * float(SIDE) + (SIDE - 1) / 2.0 - centre).astype(np.float32)
        self.cosine = jnp.cos(theta)
        self.sine = jnp.sin(theta)
        along = (
            centre_x[:, None] * self.cosine[None, :]
            + centre_y[:, None] * self.sine[None, :]
            + 0.5
        )
        whole = jnp.floor(along)
        lead = WIN // 2 - 1
        place = along - whole + float(lead)
        offset = whole.astype(jnp.int32) + (ACTIVE // 2 - 1 - lead)
        tile = jnp.minimum(offset // SPLIT, 2)
        local = jnp.arange(angles, dtype=jnp.int32) % chunk * WIN
        turn = (local[None, :] - offset + tile * SPLIT) % LANES
        self.offset = offset.reshape(-1)
        self.place = place.reshape(-1)
        self.tile = tile.reshape(-1)
        self.turn = turn.reshape(-1)
        ids = jnp.arange(patches, dtype=jnp.int32)
        self.slot = jnp.sum(
            jnp.where(vol_list[None, :] == ids[:, None], ids[None, :], 0), axis=1
        )
        voxel = np.arange(VOX)
        shift_x = np.repeat((voxel // SIDE - (SIDE - 1) / 2.0)[None, :], ROWS, axis=0)
        shift_y = np.repeat((voxel % SIDE - (SIDE - 1) / 2.0)[None, :], ROWS, axis=0)
        flip = np.eye(ACTIVE)[::-1].astype(ml_dtypes.bfloat16)
        self.fixed = [jnp.asarray(flip), jnp.asarray(shift_x, f32), jnp.asarray(shift_y, f32)]
        self.weight = ((pairs if self.held else 1, chunk * WIN, 2 * VOX), bf16)
        self.acc = ((angles, ACTIVE, LANES), f32)
        self.along = ((angles, ROWS, VOX), f32)
        self.by_ray = ((angles, slices, ACTIVE), f32)
        self.by_pair = ((pairs, both, VOX), f32)
        self.window = ((angles, 3, both, LANES), f32)
        self.half = ((2, rays, slices * slots, LANES), f32)
        self.mirror = ((max(pairs, angles), slices, ACTIVE), f32)
        self.sent = ((rays, angles // rays * slices, ACTIVE), f32)

    def first(self, volume):
        inputs = [self.offset, self.place, self.slot, self.cosine, self.sine, volume]
        outputs = [self.by_pair, self.by_ray, self.by_ray]
        scratch = [self.acc, self.along, self.half, self.mirror]
        held = [self.weight] if self.held else []
        spare = [] if self.held else [self.weight]

        def kernel(*refs):
            refs = list(refs)
            count = len(inputs) + len(self.fixed)
            if not self.held:
                refs.insert(count, refs.pop(count + len(outputs)))
            first_kernel(self.sizes, *refs)

        results = call(
            kernel, "first", inputs + self.fixed, held + outputs, spare + scratch, 16, self.room
        )
        return (results[:1], results[1:]) if self.held else ([], results)

    def second(self, weight, start, predicted, gain, sino):
        inputs = [self.offset, self.place, self.tile, self.turn, self.cosine, self.sine]
        inputs += [start, predicted, gain, sino] + self.fixed + list(weight)
        outputs = [self.by_pair, self.sent]
        scratch = [self.acc, self.along, self.by_ray, self.by_ray, self.window]
        spare = [] if self.held else [self.weight]

        def kernel(*refs):
            refs = list(refs)
            count = len(inputs)
            if not self.held:
                refs.insert(count, refs.pop(count + len(outputs)))
            second_kernel(self.sizes, self.step_size, *refs)

        return call(kernel, "second", inputs, outputs, spare + scratch, 20, self.room)

    def third(self, weight, update, residual, gain, volume):
        inputs = [self.place, self.tile, self.turn, self.slot, self.cosine, self.sine]
        inputs += [update, residual, gain, volume] + self.fixed + list(weight)
        outputs = [(volume.shape, f32)]
        pairs = self.patches // 2
        mirror = ((pairs,) + self.by_ray[0][1:], f32)
        scratch = [self.along, self.by_pair, mirror, self.window, self.half]
        spare = [] if self.held else [self.weight]

        def kernel(*refs):
            refs = list(refs)
            count = len(inputs)
            if not self.held:
                refs.insert(count, refs.pop(count + len(outputs)))
            third_kernel(self.sizes, self.step_size, *refs)

        return call(kernel, "third", inputs, outputs, spare + scratch, 10, self.room)[0]


def gather_kernel(rank_ref, *refs):
    *part_refs, out_ref, sems = refs
    rank = rank_ref[0]
    copies = [
        pltpu.make_async_copy(part_ref, out_ref.at[rank ^ d], sems.at[d])
        for d, part_ref in enumerate(part_refs)
    ]
    for copy in copies:
        copy.start()
    for copy in copies:
        copy.wait()


def gather_parts(parts, rank):
    count = len(parts)
    return pl.pallas_call(
        gather_kernel,
        out_shape=jax.ShapeDtypeStruct((count,) + parts[0].shape, f32),
        in_specs=[pl.BlockSpec(memory_space=pltpu.SMEM)]
        + [pl.BlockSpec(memory_space=pltpu.VMEM)] * count,
        out_specs=pl.BlockSpec(memory_space=pl.ANY),
        scratch_shapes=[pltpu.SemaphoreType.DMA((count,))],
        cost_estimate=pl.CostEstimate(
            flops=0, bytes_accessed=8 * count * parts[0].size, transcendentals=0
        ),
        name="gather_parts",
    )(rank.reshape(1), *parts)


def finish_kernel(got_ref, sino_ref, out_ref, active_ref, sem):
    rays, rows, _ = got_ref.shape
    slabs = active_ref.shape[0]
    slices = rows // slabs
    for ray in range(rays):
        for k in range(slabs):
            active_ref[k, ray * slices : (ray + 1) * slices, :] = got_ref[
                ray, k * slices : (k + 1) * slices, :
            ]
    offset = (out_ref.shape[2] - ACTIVE) // 2
    copy = pltpu.make_async_copy(
        active_ref, out_ref.at[:, :, offset : offset + ACTIVE], sem
    )
    copy.start()
    copy.wait()


def finish(got, sinogram):
    slabs, slab_rows, _ = sinogram.shape
    any_space = pl.BlockSpec(memory_space=pl.ANY)
    return pl.pallas_call(
        finish_kernel,
        out_shape=jax.ShapeDtypeStruct(sinogram.shape, f32),
        in_specs=[pl.BlockSpec(memory_space=pltpu.VMEM), any_space],
        out_specs=any_space,
        scratch_shapes=[
            pltpu.VMEM((slabs, slab_rows, ACTIVE), f32),
            pltpu.SemaphoreType.DMA,
        ],
        input_output_aliases={1: 0},
        cost_estimate=pl.CostEstimate(
            flops=0, bytes_accessed=8 * got.size, transcendentals=0
        ),
        name="finish",
    )(got, sinogram)


def local(intensity, angles, volume, vol_list):
    n_slab = lax.axis_size("slab")
    n_ray = lax.axis_size("ray")
    devices = n_slab * n_ray
    height, band = intensity.shape[2:]
    slices = height // devices
    slots = volume.shape[1]
    count = angles.shape[0] * angles.shape[1]
    step_size = relax * ROI / count
    rank = lax.axis_index("slab")
    padded = -(-slices // ROWS) * ROWS

    def to_all(values, axes):
        return lax.all_to_all(values, axes, split_axis=0, concat_axis=0, tiled=True)

    own_volume = to_all(volume.reshape(n_ray, slices * slots, VOX), "ray")
    *parts, active = paganin(intensity.reshape(height, band), rank, n_slab)
    active, own_volume = lax.optimization_barrier((active, own_volume))
    own_rays = to_all(active.reshape(devices, slices, ACTIVE), ("slab", "ray"))
    if padded != slices:
        widen = ((0, 0), (0, padded - slices), (0, 0))
        own_volume = jnp.pad(own_volume, ((0, 0), (0, (padded - slices) * slots), (0, 0)))
        own_rays = jnp.pad(own_rays, widen)

    sirt = Sirt(angles.reshape(-1), vol_list, padded, slots, n_ray, step_size)
    weight, (start, predicted, gain) = sirt.first(own_volume)
    own_rays, parts, start = lax.optimization_barrier((own_rays, parts, start))
    parts = [
        lax.ppermute(part, "slab", [(i, i ^ d) for i in range(n_slab)]) if d else part
        for d, part in enumerate(parts)
    ]
    update, residual = sirt.second(weight, start, predicted, gain, own_rays)
    sent = residual
    if padded != slices:
        sent = sent.reshape(n_ray, n_slab, padded, ACTIVE)[:, :, :slices]
        sent = sent.reshape(n_ray, n_slab * slices, ACTIVE)
    got = to_all(sent, "ray")
    result = sirt.third(weight, update, residual, gain, own_volume)
    result = result[:, : slices * slots]
    result, got, parts = lax.optimization_barrier((result, got, parts))
    reconstruction = to_all(result, "ray").reshape(volume.shape)
    sinogram = gather_parts(parts, rank)
    residual = finish(got, sinogram)
    return (reconstruction, residual[:, None])


def solution(mesh):
    placed = (P("slab", "ray", None, None), P(), P("slab", "ray", None), P())
    return jax.shard_map(
        local,
        mesh=mesh,
        in_specs=placed,
        out_specs=(P("slab", "ray", None), P(None, "ray", "slab", None)),
        check_vma=False,
    )
```

time: 115 us -> 133 us (1.16)
  local copies, waits for them, and re-layouts: 4.42 us -> 33.4 us
  waiting for transfers between devices: 37.8 us -> 18.1 us
  starting transfers between devices: 18.8 us -> 24.7 us
  Pallas kernels: 51.2 us -> 53.8 us
    unnamed x26 -> x29, local copies, waits for them, and re-layouts: 4.06 us -> 32.3 us
    all_to_all x3 -> x4, waiting for transfers between devices: 37.7 us -> 13.2 us  [to_all(): return lax.all_to_all(values, axes, split_axis=0, concat_axis=0, tiled=True)]
    all_to_all x3 -> x4, starting transfers between devices: 16.9 us -> 22.8 us  [to_all(): return lax.all_to_all(values, axes, split_axis=0, concat_axis=0, tiled=True)]
    ppermute x3, waiting for transfers between devices: 0.01 us -> 4.93 us  [local(): lax.ppermute(part, 'slab', [(i, i ^ d) for i in range(n_slab)])]
    pallas_call x2 -> x4, Pallas kernels: 42.8 us -> 45.3 us  [the longest x3 43.7 us: call(): pl.pallas_call(kernel, out_shape=[jax.ShapeDtypeStruct(shape, dtype) for...]
  transfers between devices with their start and end apart: 6 -> 7, of which waited for: 3 -> 3; matrix products, arithmetic and copies ran while one was open for 2% -> 2% of each run, Pallas kernels for 44% -> 26%
where the time goes in v4:
time: 133 us; the launch traced here: 132 us
  Pallas kernels  53.8 us (40%)
  local copies, waits for them, and re-layouts  33.4 us (25%)
  starting transfers between devices  24.7 us (19%)
  waiting for transfers between devices  18.1 us (14%)
  other arithmetic  1.55 us (1%)
    pallas_call x3, Pallas kernels, call(): pl.pallas_call(kernel, out_shape=[jax.ShapeDtypeStruct(shape, dtype) for...  43.7 us
    unnamed x29, local copies, waits for them, and re-layouts  32.3 us
    all_to_all x4, starting transfers between devices, to_all(): return lax.all_to_all(values, axes, split_axis=0, concat_axis=0, tiled=True)  22.8 us
    all_to_all x4, waiting for transfers between devices, to_all(): return lax.all_to_all(values, axes, split_axis=0, concat_axis=0, tiled=True)  13.2 us
    pallas_call x1, Pallas kernels, paganin(): pl.pallas_call(filter_kernel, out_shape=[jax.ShapeDtypeStruct((height //...  5.59 us
    ppermute x3, waiting for transfers between devices, local(): lax.ppermute(part, 'slab', [(i, i ^ d) for i in range(n_slab)])  4.93 us
    pallas_call x1, Pallas kernels, gather_parts(): pl.pallas_call(gather_kernel, out_shape=jax.ShapeDtypeStruct((count,) + p...  2.86 us
  transfers between devices with their start and end apart: 7, of which 3 were waited for; matrix products, arithmetic and copies ran while one was open for 2% of the time, Pallas kernels for 26%

profile of v4, /device:TPU:0, one launch (start us, length us, event | category | flops | bytes accessed | tf_op | source)
XLA Modules:
  0.0 132.2 jit_solution(371481479348692184)
XLA Ops:
  0.6 7.3 %all-to-all-start = ((f32[8,64,256]{2,1,0:T(8,128)}), f32[8,64,256]{2,1,0:T(8,128)S(1)}, u32[]{:S(2)}, u32[]{:S(2)}) async-start(f32[8,64,256]{2,1,0:T(8,128)} %bitcast.11), calls=%async_computation | async-start | bytes 1048576 | tf_op jit(solution)/shard_map/all_to_all | solution.py:706
  7.9 0.7 fusion.8
  8.6 0.1 cos.6.refs_3_.refs_4_
  8.7 0.1 sin.6.refs_4_.refs_5_
  8.8 0.1 sub.24
  8.9 0.8 add_add_fusion
  9.6 0.1 add.64
  9.7 0.8 select_reduce_fusion.refs_2_.refs_3_
  10.5 0.0 copy-start.1
  10.5 1.6 %copy-done.1 = f32[1,1,256,2048]{3,2,1,0:T(8,128)S(1)} copy-done((f32[1,1,256,2048]{3,2,1,0:T(8,128)S(1)}, f32[1,1,256,2048]{3,2,1,0:T(8,128)}, u32[]{:S(2)}) %copy-start.1) | copy-done | bytes 2097176
  12.1 0.0 copy-start.2
  12.1 1.0 copy-done.2
  13.1 0.0 copy-start.3
  13.1 0.0 copy-start.5
  13.1 5.6 %paganin.1 = (f32[64,2048]{1,0:T(8,128)S(1)}, f32[64,2048]{1,0:T(8,128)S(1)}, f32[64,2048]{1,0:T(8,128)S(1)}, f32[64,2048]{1,0:T(8,128)S(1)}, f32[256,256]{1,0:T(8,128)}) custom-call(s32[1]{0:T(128)} %bitcast.rank_ref, f32[256,2048]{1,0:T(8,128)S(1)} %bitcast.8, f32[264,256]{1,0:T(8,128)S(1)} %copy-done.2), custom_call_target="tpu_custom_call" | custom-call | flops 8589934592 | bytes 4194304 | tf_op jit(solution)/shard_map/paganin/pallas_call | solution.py:172
  18.7 0.0 copy-start
  18.7 0.9 copy-done
  19.5 2.9 %all-to-all-done.refs_5_.refs_9_ = f32[8,64,256]{2,1,0:T(8,128)S(1)} async-done(((f32[8,64,256]{2,1,0:T(8,128)}), f32[8,64,256]{2,1,0:T(8,128)S(1)}, u32[]{:S(2)}, u32[]{:S(2)}) %all-to-all-start) | async-done | bytes 524320 | tf_op jit(solution)/shard_map/all_to_all | solution.py:706
  22.4 3.7 %all-to-all-start.1 = ((f32[32,8,256]{2,1,0:T(8,128)}), f32[32,8,256]{2,1,0:T(8,128)S(1)}, u32[]{:S(2)}, u32[]{:S(2)}) async-start(f32[32,8,256]{2,1,0:T(8,128)} %bitcast.3), calls=%async_computation.1 | async-start | bytes 524288 | tf_op jit(solution)/shard_map/all_to_all | solution.py:706
  26.1 0.0 copy-done.3
  26.1 0.0 copy-done.4
  26.1 0.0 copy-done.5
  26.1 13.5 %first.1 = (bf16[32,768,512]{2,1,0:T(8,128)(2,1)S(1)}, f32[32,16,256]{2,1,0:T(8,128)S(1)}, f32[32,8,256]{2,1,0:T(8,128)S(1)}, f32[32,8,256]{2,1,0:T(8,128)S(1)}) custom-call(s32[1024]{0:T(1024)S(1)} %get-tuple-element.56.refs_0_, f32[1024]{0:T(1024)S(1)} %fusion.refs_1_.refs_0_, s32[64]{0:T(128)S(1)} %select_reduce_fusion.refs_2_.refs_3_, ...), custom_call_target="tpu_custom_call" | custom-call | flops 16000000000 | bytes 4194304 | tf_op jit(solution)/shard_map/first/pallas_call | solution.py:505
  39.6 0.0 copy-start.6
  39.6 8.3 %copy-done.6 = bf16[32,768,512]{2,1,0:T(8,128)(2,1)} copy-done((bf16[32,768,512]{2,1,0:T(8,128)(2,1)}, bf16[32,768,512]{2,1,0:T(8,128)(2,1)S(1)}, u32[]{:S(2)}) %copy-start.6) | copy-done | bytes 25165848
  47.9 0.8 copy-done.9
  48.7 0.7 copy-done.11
  49.4 0.0 all-to-all-done.1.refs_9_
  49.4 8.2 %copy-done.7 = bf16[32,768,512]{2,1,0:T(8,128)(2,1)S(1)} copy-done((bf16[32,768,512]{2,1,0:T(8,128)(2,1)S(1)}, bf16[32,768,512]{2,1,0:T(8,128)(2,1)}, u32[]{:S(2)}) %copy-start.7) | copy-done | bytes 25165848
  57.6 1.0 copy-done.10
  58.6 0.9 copy-done.12
  59.6 19.9 %second.1 = (f32[32,16,256]{2,1,0:T(8,128)S(1)}, f32[8,32,256]{2,1,0:T(8,128)}) custom-call(s32[1024]{0:T(1024)S(1)} %get-tuple-element.56.refs_0_, f32[1024]{0:T(1024)S(1)} %fusion.refs_1_.refs_0_, s32[1024]{0:T(1024)S(1)} %get-tuple-element.57.refs_2_.refs_1_, s32[1024]{0:T(1024)S(1)} %get-tuple-element.58.refs_3_.refs_2_, f32[32]{0:T(128)S(1)} %cos.6.refs_3_.refs_4_, ...), custom_call_target="tpu_custom_call" | custom-call | flops 20000000000 | bytes 4194304 | tf_op jit(solution)/shard_map/second/pallas_call | solution.py:505
  79.5 5.8 %all-to-all-start.2 = ((f32[8,32,256]{2,1,0:T(8,128)}), f32[8,32,256]{2,1,0:T(8,128)S(1)}, u32[]{:S(2)}, u32[]{:S(2)}) async-start(f32[8,32,256]{2,1,0:T(8,128)} %get-tuple-element.41.refs_7_), calls=%async_computation.2 | async-start | bytes 524288 | tf_op jit(solution)/shard_map/all_to_all | solution.py:706
  85.3 0.0 collective-permute-start
  85.3 1.6 %collective-permute-start.1 = (f32[64,2048]{1,0:T(8,128)S(1)}, f32[64,2048]{1,0:T(8,128)}, u32[]{:S(2)}, u32[]{:S(2)}) collective-permute-start(f32[64,2048]{1,0:T(8,128)S(1)} %get-tuple-element.44), channel_id=1, source_target_pairs={{0,16},{8,24},{16,0},{24,8},{1,17},{9,25},{17,1},{25,9},{2,18},{10... | collective-permute-start | bytes 1572872 | tf_op jit(solution)/shard_map/ppermute | solution.py:721
  86.9 0.3 collective-permute-start.2
  87.2 8.2 %copy-done.8 = bf16[32,768,512]{2,1,0:T(8,128)(2,1)S(1)} copy-done((bf16[32,768,512]{2,1,0:T(8,128)(2,1)S(1)}, bf16[32,768,512]{2,1,0:T(8,128)(2,1)}, u32[]{:S(2)}) %copy-start.8) | copy-done | bytes 25165848
  95.3 10.2 %third.1 = f32[8,64,256]{2,1,0:T(8,128)} custom-call(f32[1024]{0:T(1024)S(1)} %fusion.refs_1_.refs_0_, s32[1024]{0:T(1024)S(1)} %get-tuple-element.57.refs_2_.refs_1_, s32[1024]{0:T(1024)S(1)} %get-tuple-element.58.refs_3_.refs_2_, s32[64]{0:T(128)S(1)} %select_reduce_fusion.refs_2_.refs_3_, f32[32]{0:T(128)S(1)} %cos.6.refs_3_.refs_4_, ...), custom_call_target="tpu_custom_call" | custom-call | flops 10000000000 | bytes 4194304 | tf_op jit(solution)/shard_map/third/pallas_call | solution.py:505
  105.6 0.0 all-to-all-done.2.got_ref
  105.6 0.0 collective-permute-done.refs_1_
  105.6 0.0 collective-permute-done.1.refs_2_
  105.6 4.9 %collective-permute-done.2.refs_3_ = f32[64,2048]{1,0:T(8,128)} collective-permute-done((f32[64,2048]{1,0:T(8,128)S(1)}, f32[64,2048]{1,0:T(8,128)}, u32[]{:S(2)}, u32[]{:S(2)}) %collective-permute-start.2) | collective-permute-done | bytes 524320 | tf_op jit(solution)/shard_map/ppermute | solution.py:721
  110.5 6.1 %all-to-all-start.3 = ((f32[8,64,256]{2,1,0:T(8,128)}), f32[8,64,256]{2,1,0:T(8,128)S(1)}, u32[]{:S(2)}, u32[]{:S(2)}) async-start(f32[8,64,256]{2,1,0:T(8,128)} %third.1), calls=%async_computation.3 | async-start | bytes 1048576 | tf_op jit(solution)/shard_map/all_to_all | solution.py:706
  116.6 2.9 %gather_parts.1.sino_ref = f32[4,64,2048]{2,1,0:T(8,128)} custom-call(s32[1]{0:T(128)} %bitcast.rank_ref, f32[64,2048]{1,0:T(8,128)} %copy-done, f32[64,2048]{1,0:T(8,128)} %collective-permute-done.refs_1_, f32[64,2048]{1,0:T(8,128)} %collective-permute-done.1.refs_2_, f32[64,2048]{1,0:T(8,128)} %collective-permute-done.2.refs_3_), custom_call_target="tpu_custom_call" | custom-call | bytes 4194304 | tf_op jit(solution)/shard_map/gather_parts/pallas_call | solution.py:642
  119.4 0.0 copy-done.13
  119.5 1.7 %finish.1 = f32[4,64,2048]{2,1,0:T(8,128)} custom-call(f32[8,32,256]{2,1,0:T(8,128)} %copy-done.13, f32[4,64,2048]{2,1,0:T(8,128)} %gather_parts.1.sino_ref), custom_call_target="tpu_custom_call", output_to_operand_aliasing={{}: (1, {})} | custom-call | bytes 524288 | tf_op jit(solution)/shard_map/finish/pallas_call | solution.py:676
  121.1 10.3 %all-to-all-done.3 = f32[8,64,256]{2,1,0:T(8,128)S(1)} async-done(((f32[8,64,256]{2,1,0:T(8,128)}), f32[8,64,256]{2,1,0:T(8,128)S(1)}, u32[]{:S(2)}, u32[]{:S(2)}) %all-to-all-start.3) | async-done | bytes 524320 | tf_op jit(solution)/shard_map/all_to_all | solution.py:706
  131.4 0.8 copy.17
  (12 shorter events, 0.1 us)
Async XLA Ops:
  0.6 21.8 %all-to-all-start = ((f32[8,64,256]{2,1,0:T(8,128)}), f32[8,64,256]{2,1,0:T(8,128)S(1)}, u32[]{:S(2)}, u32[]{:S(2)}) async-start(f32[8,64,256]{2,1,0:T(8,128)} %bitcast.11), calls=%async_computation | async-start | bytes 1048576 | tf_op jit(solution)/shard_map/all_to_all | solution.py:706
  10.5 1.6 %copy-start.1 = (f32[1,1,256,2048]{3,2,1,0:T(8,128)S(1)}, f32[1,1,256,2048]{3,2,1,0:T(8,128)}, u32[]{:S(2)}) copy-start(f32[1,1,256,2048]{3,2,1,0:T(8,128)} %param.10) | copy-start | bytes 6291460
  12.1 1.0 copy-start.2
  13.1 13.0 %copy-start.3 = (bf16[256,256]{1,0:T(8,128)(2,1)S(1)}, bf16[256,256]{1,0:T(8,128)(2,1)}, u32[]{:S(2)}) copy-start(bf16[256,256]{1,0:T(8,128)(2,1)} %constant.78.clone.refs_6_.refs_10_) | copy-start | bytes 393220
  13.1 13.0 %copy-start.4 = (f32[8,256]{1,0:T(8,128)S(1)}, f32[8,256]{1,0:T(8,128)}, u32[]{:S(2)}) copy-start(f32[8,256]{1,0:T(8,128)} %constant.80.clone.refs_8_.refs_12_) | copy-start | bytes 24580
  13.1 13.0 %copy-start.5 = (f32[8,256]{1,0:T(8,128)S(1)}, f32[8,256]{1,0:T(8,128)}, u32[]{:S(2)}) copy-start(f32[8,256]{1,0:T(8,128)} %constant.79.clone.refs_7_.refs_11_) | copy-start | bytes 24580
  18.7 0.9 copy-start
  22.4 27.0 %all-to-all-start.1 = ((f32[32,8,256]{2,1,0:T(8,128)}), f32[32,8,256]{2,1,0:T(8,128)S(1)}, u32[]{:S(2)}, u32[]{:S(2)}) async-start(f32[32,8,256]{2,1,0:T(8,128)} %bitcast.3), calls=%async_computation.1 | async-start | bytes 524288 | tf_op jit(solution)/shard_map/all_to_all | solution.py:706
  39.6 8.3 %copy-start.6 = (bf16[32,768,512]{2,1,0:T(8,128)(2,1)}, bf16[32,768,512]{2,1,0:T(8,128)(2,1)S(1)}, u32[]{:S(2)}) copy-start(bf16[32,768,512]{2,1,0:T(8,128)(2,1)S(1)} %get-tuple-element.39.refs_13_) | copy-start | bytes 75497472
  47.9 0.8 copy-start.9
  48.7 0.7 copy-start.11
  49.4 8.2 %copy-start.7 = (bf16[32,768,512]{2,1,0:T(8,128)(2,1)S(1)}, bf16[32,768,512]{2,1,0:T(8,128)(2,1)}, u32[]{:S(2)}) copy-start(bf16[32,768,512]{2,1,0:T(8,128)(2,1)} %copy-done.6) | copy-start | bytes 75497472
  57.6 1.0 copy-start.10
  58.6 0.9 copy-start.12
  79.5 26.1 %all-to-all-start.2 = ((f32[8,32,256]{2,1,0:T(8,128)}), f32[8,32,256]{2,1,0:T(8,128)S(1)}, u32[]{:S(2)}, u32[]{:S(2)}) async-start(f32[8,32,256]{2,1,0:T(8,128)} %get-tuple-element.41.refs_7_), calls=%async_computation.2 | async-start | bytes 524288 | tf_op jit(solution)/shard_map/all_to_all | solution.py:706
  85.3 20.3 %collective-permute-start = (f32[64,2048]{1,0:T(8,128)S(1)}, f32[64,2048]{1,0:T(8,128)}, u32[]{:S(2)}, u32[]{:S(2)}) collective-permute-start(f32[64,2048]{1,0:T(8,128)S(1)} %get-tuple-element.43), channel_id=1, source_target_pairs={{0,8},{8,0},{16,24},{24,16},{1,9},{9,1},{17,25},{25,17},{2,10},{10... | collective-permute-start | bytes 1572872 | tf_op jit(solution)/shard_map/ppermute | solution.py:721
  85.3 20.3 %collective-permute-start.1 = (f32[64,2048]{1,0:T(8,128)S(1)}, f32[64,2048]{1,0:T(8,128)}, u32[]{:S(2)}, u32[]{:S(2)}) collective-permute-start(f32[64,2048]{1,0:T(8,128)S(1)} %get-tuple-element.44), channel_id=1, source_target_pairs={{0,16},{8,24},{16,0},{24,8},{1,17},{9,25},{17,1},{25,9},{2,18},{10... | collective-permute-start | bytes 1572872 | tf_op jit(solution)/shard_map/ppermute | solution.py:721
  86.9 23.6 %collective-permute-start.2 = (f32[64,2048]{1,0:T(8,128)S(1)}, f32[64,2048]{1,0:T(8,128)}, u32[]{:S(2)}, u32[]{:S(2)}) collective-permute-start(f32[64,2048]{1,0:T(8,128)S(1)} %get-tuple-element.45), channel_id=1, source_target_pairs={{0,24},{8,16},{16,8},{24,0},{1,25},{9,17},{17,9},{25,1},{2,26},{10... | collective-permute-start | bytes 1572872 | tf_op jit(solution)/shard_map/ppermute | solution.py:721
  87.1 8.2 %copy-start.8 = (bf16[32,768,512]{2,1,0:T(8,128)(2,1)S(1)}, bf16[32,768,512]{2,1,0:T(8,128)(2,1)}, u32[]{:S(2)}) copy-start(bf16[32,768,512]{2,1,0:T(8,128)(2,1)} %copy-done.6) | copy-start | bytes 75497472
  105.6 13.9 %copy-start.13 = (f32[8,32,256]{2,1,0:T(8,128)}, f32[8,32,256]{2,1,0:T(8,128)S(1)}, u32[]{:S(2)}) copy-start(f32[8,32,256]{2,1,0:T(8,128)S(1)} %all-to-all-done.2.got_ref) | copy-start | bytes 786436
  110.5 20.9 %all-to-all-start.3 = ((f32[8,64,256]{2,1,0:T(8,128)}), f32[8,64,256]{2,1,0:T(8,128)S(1)}, u32[]{:S(2)}, u32[]{:S(2)}) async-start(f32[8,64,256]{2,1,0:T(8,128)} %third.1), calls=%async_computation.3 | async-start | bytes 1048576 | tf_op jit(solution)/shard_map/all_to_all | solution.py:706

commit v5 on v4

--- a/solution.py
+++ b/solution.py
@@ -21,7 +21,6 @@
 ROWS = 8
 SPLIT = 64
 GROUP = 8
-PAIR_UNROLL = 2
 
 paganin_strength = 10.0
 relax = 1.8
@@ -79,14 +78,27 @@
     return pltpu.roll(ends, 1 if forward else ROWS - 1, 0) / (1.0 - power)
 
 
-def filter_kernel(rank_ref, image_ref, table_ref, *refs):
-    *part_refs, active_ref, out_ref, spec_ref, up_ref, down_ref = refs
+def filter_kernel(rank_ref, source_ref, given_ref, *refs):
+    *part_refs, active_ref, image_ref, table_ref, out_ref, spec_ref, up_ref, down_ref, sems = refs
     height, width = image_ref.shape
     rank = rank_ref[0]
     share = height // len(part_refs)
     length = width // ROWS
     blocks = height // LANES
     unroll = 8
+    copies = []
+    for c in range(ROWS):
+        columns = slice(c * length, (c + 1) * length)
+        copies.append(
+            pltpu.make_async_copy(
+                source_ref.at[:, columns], image_ref.at[:, columns], sems.at[c]
+            )
+        )
+    given = pltpu.make_async_copy(given_ref, table_ref, sems.at[ROWS])
+    given.start()
+    for copy in copies:
+        copy.start()
+    given.wait()
     cas_high, cas_low = halves(table_ref[0:height, :])
     rho_all = table_ref[height : height + ROWS, :]
     rhos = [rho_all[:, b * LANES : (b + 1) * LANES] for b in range(blocks)]
@@ -97,6 +109,7 @@
         return dot(high, cas_high) + dot(low, cas_high) + dot(high, cas_low)
 
     for c in range(ROWS):
+        copies[c].wait()
         image = 1.0 - image_ref[:, c * length : (c + 1) * length]
         spectrum = transform(jnp.transpose(image))
         for b in range(blocks):
@@ -174,15 +187,18 @@
         out_shape=[jax.ShapeDtypeStruct((height // parts, width), f32)] * parts
         + [jax.ShapeDtypeStruct((height, ACTIVE), f32)],
         in_specs=[pl.BlockSpec(memory_space=pltpu.SMEM)]
-        + [pl.BlockSpec(memory_space=pltpu.VMEM)] * 2,
+        + [pl.BlockSpec(memory_space=pltpu.HBM)] * 2,
         out_specs=[pl.BlockSpec(memory_space=pltpu.VMEM)] * (parts + 1),
         scratch_shapes=[
+            pltpu.VMEM((height, width), f32),
+            pltpu.VMEM((height + ROWS, height), f32),
             pltpu.VMEM((height, width), f32),
             pltpu.VMEM((blocks, width, LANES), f32),
             pltpu.VMEM((blocks, width, LANES), f32),
             pltpu.VMEM((blocks, width // 2, LANES), f32),
+            pltpu.SemaphoreType.DMA((ROWS + 1,)),
         ],
-        compiler_params=pltpu.CompilerParams(vmem_limit_bytes=32 * 2**20),
+        compiler_params=pltpu.CompilerParams(vmem_limit_bytes=58 * 2**20),
         cost_estimate=pl.CostEstimate(
             flops=64 * height * height * width,
             bytes_accessed=8 * height * width,
@@ -197,13 +213,13 @@
 
 
 class Weights:
-    def __init__(self, ref, along_ref, place_ref, angles, chunk, held):
+    def __init__(self, ref, along_ref, place_ref, angles, chunk, count):
         self.ref = ref
         self.along_ref = along_ref
         self.place_ref = place_ref
         self.angles = angles
         self.chunk = chunk
-        self.held = held
+        self.count = count
         self.ray = lax.broadcasted_iota(jnp.int32, (ROWS, VOX), 0).astype(f32)
 
     def prepare(self, shift_x_ref, shift_y_ref, cos_ref, sin_ref):
@@ -213,7 +229,7 @@
         repeat(self.angles, along_angle, 8)
 
     def make(self, q, c):
-        place = q if self.held else 0
+        place = q % self.count
         for two in range(self.chunk // 2):
             pieces = []
             for t in (2 * two, 2 * two + 1):
@@ -228,10 +244,26 @@
             self.ref[place, 2 * two * WIN : (2 * two + 2) * WIN, VOX : 2 * VOX] = low
 
     def get(self, q):
-        return self.ref[q if self.held else 0]
-
-
-def project(weights, make, values_of, offset_ref, acc_ref, pairs, both):
+        return self.ref[q % self.count]
+
+
+class Stream:
+    def __init__(self, hbm_ref, vmem_ref, sems, outward):
+        self.hbm_ref = hbm_ref
+        self.vmem_ref = vmem_ref
+        self.sems = sems
+        self.outward = outward
+        self.count = vmem_ref.shape[0]
+
+    def copy(self, q):
+        place = q % self.count
+        here, there = self.vmem_ref.at[place], self.hbm_ref.at[q]
+        if self.outward:
+            return pltpu.make_async_copy(here, there, self.sems.at[place])
+        return pltpu.make_async_copy(there, here, self.sems.at[place])
+
+
+def project(weights, make, values_of, offset_ref, acc_ref, pairs, both, stream, unroll):
     angles, chunk = weights.angles, weights.chunk
     acc_ref[...] = jnp.zeros(acc_ref.shape, f32)
 
@@ -246,9 +278,17 @@
             ],
             axis=0,
         )
+        if stream is not None:
+
+            @pl.when(q >= stream.count)
+            def _():
+                stream.copy(q - stream.count).wait()
+
         for c in range(angles // chunk):
             if make:
                 weights.make(q, c)
+            if stream is not None:
+                stream.copy(q).start()
             sums = lax.dot_general(
                 weights.get(q),
                 operand,
@@ -265,7 +305,10 @@
                 for angle, rows, values in places:
                     acc_ref[angle, rows, :] = values
 
-    repeat(pairs, pair, PAIR_UNROLL)
+    repeat(pairs, pair, unroll)
+    if stream is not None:
+        for q in range(pairs - stream.count, pairs):
+            stream.copy(q).wait()
 
 
 def spread_rays(acc_ref, direct_ref, mirror_ref, total_ref, slices):
@@ -286,7 +329,9 @@
     return reversed_exact(values.reshape(-1, shape[-1]), flip).reshape(shape)
 
 
-def back_project(weights, weighted, flip, window_ref, tile_ref, turn_ref, store, pairs):
+def back_project(
+    weights, weighted, flip, window_ref, tile_ref, turn_ref, store, pairs, stream, unroll
+):
     angles, slices, _ = weighted.shape
     chunk = weights.chunk
     both = 2 * slices
@@ -307,8 +352,10 @@
     def pair(q):
         total = None
         for c in range(angles // chunk):
-            if not weights.held:
+            if stream is None:
                 weights.make(q, c)
+            else:
+                stream.copy(q).wait()
             tiles = [None] * (-(-width // LANES))
             for t in range(chunk):
                 index = q * angles + c * chunk + t
@@ -329,7 +376,7 @@
             total = piece if total is None else total + piece
         store(q, total)
 
-    repeat(pairs, pair, PAIR_UNROLL)
+    repeat(pairs, pair, unroll)
 
 
 def first_kernel(
@@ -343,10 +390,12 @@
     flip_ref,
     shift_x_ref,
     shift_y_ref,
-    weight_ref,
+    held_ref,
     start_ref,
     predicted_ref,
     gain_ref,
+    weight_ref,
+    sems,
     acc_ref,
     along_ref,
     half_ref,
@@ -365,7 +414,10 @@
             [half_ref[part, slot // slots, rows, :] for part in range(2)], axis=1
         )
 
-    weights = Weights(weight_ref, along_ref, place_ref, angles, chunk, held)
+    weights = Weights(
+        weight_ref, along_ref, place_ref, angles, chunk, weight_ref.shape[0]
+    )
+    stream = Stream(held_ref, weight_ref, sems, True) if held else None
     weights.prepare(shift_x_ref, shift_y_ref, cos_ref, sin_ref)
     for part in range(2):
         half_ref[part] = vol_ref[:, :, part * LANES : (part + 1) * LANES]
@@ -376,7 +428,9 @@
 
     repeat(pairs, order, 8)
     start_ref[:, slices:both, :] = turn_rays(mirror_ref[0:pairs], flip)
-    project(weights, True, lambda q: start_ref[q], offset_ref, acc_ref, pairs, both)
+    project(
+        weights, True, lambda q: start_ref[q], offset_ref, acc_ref, pairs, both, stream, 2
+    )
     spread_rays(acc_ref, predicted_ref, mirror_ref, gain_ref, slices)
     predicted_ref[...] = predicted_ref[...] + turn_rays(mirror_ref[0:angles], flip)
     direct = gain_ref[...]
@@ -399,9 +453,11 @@
     flip_ref,
     shift_x_ref,
     shift_y_ref,
-    weight_ref,
+    held_ref,
     update_ref,
     res_ref,
+    weight_ref,
+    sems,
     acc_ref,
     along_ref,
     direct_ref,
@@ -413,20 +469,27 @@
     slices = both // 2
     rays = res_ref.shape[0]
     flip = flip_ref[...]
-    weights = Weights(weight_ref, along_ref, place_ref, angles, chunk, held)
-    if not held:
+    weights = Weights(
+        weight_ref, along_ref, place_ref, angles, chunk, weight_ref.shape[0]
+    )
+    stream = Stream(held_ref, weight_ref, sems, False) if held else None
+    if held:
+        repeat(pairs, lambda q: stream.copy(q).start(), 8)
+    else:
         weights.prepare(shift_x_ref, shift_y_ref, cos_ref, sin_ref)
     weighted = (sino_ref[...] - predicted_ref[...]) * gain_ref[...] * (1.0 / ROI)
 
     def store(q, total):
         update_ref[q] = total
 
-    back_project(weights, weighted, flip, window_ref, tile_ref, turn_ref, store, pairs)
+    back_project(
+        weights, weighted, flip, window_ref, tile_ref, turn_ref, store, pairs, stream, 4
+    )
 
     def values_of(q):
         return start_ref[q] + step_size * update_ref[q]
 
-    project(weights, not held, values_of, offset_ref, acc_ref, pairs, both)
+    project(weights, not held, values_of, offset_ref, acc_ref, pairs, both, None, 4)
     spread_rays(acc_ref, direct_ref, mirror_ref, None, slices)
     residual = sino_ref[...] - direct_ref[...] - turn_rays(mirror_ref[...], flip)
     for t in range(angles):
@@ -450,8 +513,10 @@
     flip_ref,
     shift_x_ref,
     shift_y_ref,
+    held_ref,
+    out_ref,
     weight_ref,
-    out_ref,
+    sems,
     along_ref,
     total_ref,
     mirror_ref,
@@ -464,8 +529,13 @@
     slices = both // 2
     rays = res_ref.shape[0]
     flip = flip_ref[...]
-    weights = Weights(weight_ref, along_ref, place_ref, angles, chunk, held)
-    if not held:
+    weights = Weights(
+        weight_ref, along_ref, place_ref, angles, chunk, weight_ref.shape[0]
+    )
+    stream = Stream(held_ref, weight_ref, sems, False) if held else None
+    if held:
+        repeat(pairs, lambda q: stream.copy(q).start(), 8)
+    else:
         weights.prepare(shift_x_ref, shift_y_ref, cos_ref, sin_ref)
     residual = [
         res_ref[t % rays, t // rays * slices : (t // rays + 1) * slices, :][None]
@@ -476,7 +546,9 @@
     def store(q, total):
         total_ref[q] = (update_ref[q] + total) * step_size
 
-    back_project(weights, weighted, flip, window_ref, tile_ref, turn_ref, store, pairs)
+    back_project(
+        weights, weighted, flip, window_ref, tile_ref, turn_ref, store, pairs, stream, 4
+    )
     mirror_ref[...] = turn_rays(total_ref[:, slices:both, :], flip)
     for part in range(2):
         half_ref[part] = vol_ref[:, :, part * LANES : (part + 1) * LANES]
@@ -499,21 +571,30 @@
         out_ref[:, :, part * LANES : (part + 1) * LANES] = half_ref[part]
 
 
-def call(kernel, name, inputs, outputs, scratch, micros, room):
+def call(kernel, name, inputs, held_in, outputs, held_out, scratch, micros, room):
     smem = pl.BlockSpec(memory_space=pltpu.SMEM)
     vmem = pl.BlockSpec(memory_space=pltpu.VMEM)
+    hbm = [pl.BlockSpec(memory_space=pltpu.HBM)]
+    before = len(inputs)
+
+    def body(*refs):
+        refs = list(refs)
+        if not held_in and not held_out:
+            refs.insert(before, None)
+        kernel(*refs)
+
     return pl.pallas_call(
-        kernel,
-        out_shape=[jax.ShapeDtypeStruct(shape, dtype) for shape, dtype in outputs],
-        in_specs=[smem if value.ndim == 1 else vmem for value in inputs],
-        out_specs=[vmem] * len(outputs),
-        scratch_shapes=[pltpu.VMEM(shape, dtype) for shape, dtype in scratch],
+        body,
+        out_shape=[jax.ShapeDtypeStruct(*value) for value in held_out + outputs],
+        in_specs=[smem if value.ndim == 1 else vmem for value in inputs] + hbm * len(held_in),
+        out_specs=hbm * len(held_out) + [vmem] * len(outputs),
+        scratch_shapes=scratch,
         compiler_params=pltpu.CompilerParams(vmem_limit_bytes=room * 2**20),
         cost_estimate=pl.CostEstimate(
             flops=int(micros * 1e9), bytes_accessed=4 * 2**20, transcendentals=0
         ),
         name=name,
-    )(*inputs)
+    )(*inputs, *held_in)
 
 
 class Sirt:
@@ -524,7 +605,7 @@
         both = 2 * slices
         chunk = math.gcd(angles, 32)
         self.held = angles == chunk
-        self.room = 24 if self.held else 48
+        self.room = 52
         self.sizes = (angles, chunk, self.held, slots)
         self.step_size = step_size
         self.rays = rays
@@ -560,7 +641,7 @@
         shift_y = np.repeat((voxel % SIDE - (SIDE - 1) / 2.0)[None, :], ROWS, axis=0)
         flip = np.eye(ACTIVE)[::-1].astype(ml_dtypes.bfloat16)
         self.fixed = [jnp.asarray(flip), jnp.asarray(shift_x, f32), jnp.asarray(shift_y, f32)]
-        self.weight = ((pairs if self.held else 1, chunk * WIN, 2 * VOX), bf16)
+        self.held_weight = ((pairs, chunk * WIN, 2 * VOX), bf16)
         self.acc = ((angles, ACTIVE, LANES), f32)
         self.along = ((angles, ROWS, VOX), f32)
         self.by_ray = ((angles, slices, ACTIVE), f32)
@@ -570,58 +651,61 @@
         self.mirror = ((max(pairs, angles), slices, ACTIVE), f32)
         self.sent = ((rays, angles // rays * slices, ACTIVE), f32)
 
+    def scratch(self, held, *shapes):
+        count = held if self.held else 1
+        shape, dtype = self.held_weight
+        weight = pltpu.VMEM((count,) + shape[1:], dtype)
+        rest = [pltpu.VMEM(*shape) for shape in shapes]
+        return [weight, pltpu.SemaphoreType.DMA((count,))] + rest
+
     def first(self, volume):
         inputs = [self.offset, self.place, self.slot, self.cosine, self.sine, volume]
-        outputs = [self.by_pair, self.by_ray, self.by_ray]
-        scratch = [self.acc, self.along, self.half, self.mirror]
-        held = [self.weight] if self.held else []
-        spare = [] if self.held else [self.weight]
-
-        def kernel(*refs):
-            refs = list(refs)
-            count = len(inputs) + len(self.fixed)
-            if not self.held:
-                refs.insert(count, refs.pop(count + len(outputs)))
-            first_kernel(self.sizes, *refs)
-
         results = call(
-            kernel, "first", inputs + self.fixed, held + outputs, spare + scratch, 16, self.room
+            functools.partial(first_kernel, self.sizes),
+            "first",
+            inputs + self.fixed,
+            [],
+            [self.by_pair, self.by_ray, self.by_ray],
+            [self.held_weight] if self.held else [],
+            self.scratch(4, self.acc, self.along, self.half, self.mirror),
+            16,
+            self.room,
         )
         return (results[:1], results[1:]) if self.held else ([], results)
 
     def second(self, weight, start, predicted, gain, sino):
         inputs = [self.offset, self.place, self.tile, self.turn, self.cosine, self.sine]
-        inputs += [start, predicted, gain, sino] + self.fixed + list(weight)
-        outputs = [self.by_pair, self.sent]
-        scratch = [self.acc, self.along, self.by_ray, self.by_ray, self.window]
-        spare = [] if self.held else [self.weight]
-
-        def kernel(*refs):
-            refs = list(refs)
-            count = len(inputs)
-            if not self.held:
-                refs.insert(count, refs.pop(count + len(outputs)))
-            second_kernel(self.sizes, self.step_size, *refs)
-
-        return call(kernel, "second", inputs, outputs, spare + scratch, 20, self.room)
+        inputs += [start, predicted, gain, sino]
+        return call(
+            functools.partial(second_kernel, self.sizes, self.step_size),
+            "second",
+            inputs + self.fixed,
+            list(weight),
+            [self.by_pair, self.sent],
+            [],
+            self.scratch(
+                self.patches // 2, self.acc, self.along, self.by_ray, self.by_ray, self.window
+            ),
+            20,
+            self.room,
+        )
 
     def third(self, weight, update, residual, gain, volume):
         inputs = [self.place, self.tile, self.turn, self.slot, self.cosine, self.sine]
-        inputs += [update, residual, gain, volume] + self.fixed + list(weight)
-        outputs = [(volume.shape, f32)]
+        inputs += [update, residual, gain, volume]
         pairs = self.patches // 2
         mirror = ((pairs,) + self.by_ray[0][1:], f32)
-        scratch = [self.along, self.by_pair, mirror, self.window, self.half]
-        spare = [] if self.held else [self.weight]
-
-        def kernel(*refs):
-            refs = list(refs)
-            count = len(inputs)
-            if not self.held:
-                refs.insert(count, refs.pop(count + len(outputs)))
-            third_kernel(self.sizes, self.step_size, *refs)
-
-        return call(kernel, "third", inputs, outputs, spare + scratch, 10, self.room)[0]
+        return call(
+            functools.partial(third_kernel, self.sizes, self.step_size),
+            "third",
+            inputs + self.fixed,
+            list(weight),
+            [(volume.shape, f32)],
+            [],
+            self.scratch(pairs, self.along, self.by_pair, mirror, self.window, self.half),
+            10,
+            self.room,
+        )[0]
 
 
 def gather_kernel(rank_ref, *refs):
@@ -714,7 +798,10 @@
         own_volume = jnp.pad(own_volume, ((0, 0), (0, (padded - slices) * slots), (0, 0)))
         own_rays = jnp.pad(own_rays, widen)
 
-    sirt = Sirt(angles.reshape(-1), vol_list, padded, slots, n_ray, step_size)
+    theta, vol_list, own_volume, parts = lax.optimization_barrier(
+        (angles.reshape(-1), vol_list, own_volume, parts)
+    )
+    sirt = Sirt(theta, vol_list, padded, slots, n_ray, step_size)
     weight, (start, predicted, gain) = sirt.first(own_volume)
     own_rays, parts, start = lax.optimization_barrier((own_rays, parts, start))
     parts = [
@@ -727,6 +814,10 @@
         sent = sent.reshape(n_ray, n_slab, padded, ACTIVE)[:, :, :slices]
         sent = sent.reshape(n_ray, n_slab * slices, ACTIVE)
     got = to_all(sent, "ray")
+    ready = [d for d in range(n_slab) if d != n_slab // 2]
+    update, *early = lax.optimization_barrier((update, *[parts[d] for d in ready]))
+    for d, part in zip(ready, early):
+        parts[d] = part
     result = sirt.third(weight, update, residual, gain, own_volume)
     result = result[:, : slices * slots]
     result, got, parts = lax.optimization_barrier((result, got, parts))

time: 133 us -> 116 us (0.87)
  local copies, waits for them, and re-layouts: 33.4 us -> 2.59 us
  Pallas kernels: 53.8 us -> 72.7 us
  waiting for transfers between devices: 18.1 us -> 13.7 us
  other arithmetic: 1.55 us -> 0.22 us
    unnamed x29 -> x27, local copies, waits for them, and re-layouts: 32.3 us -> 1.63 us
    pallas_call x3, Pallas kernels: 43.7 us -> 58.8 us  [call(): pl.pallas_call(body, out_shape=[jax.ShapeDtypeStruct(*value) for value in...]
    ppermute x3, waiting for transfers between devices: 4.93 us -> 0.01 us  [local(): lax.ppermute(part, 'slab', [(i, i ^ d) for i in range(n_slab)])]
    pallas_call x1, Pallas kernels: 5.59 us -> 9.34 us  [paganin(): pl.pallas_call(filter_kernel, out_shape=[jax.ShapeDtypeStruct((height //...]
  transfers between devices with their start and end apart: 7 -> 7, of which waited for: 3 -> 2; matrix products, arithmetic and copies ran while one was open for 2% -> 1% of each run, Pallas kernels for 26% -> 63%
where the time goes in v5:
time: 116 us; the launch traced here: 115 us
  Pallas kernels  72.7 us (63%)
  starting transfers between devices  24.9 us (21%)
  waiting for transfers between devices  13.7 us (12%)
  local copies, waits for them, and re-layouts  2.59 us (2%)
    pallas_call x3, Pallas kernels, call(): pl.pallas_call(body, out_shape=[jax.ShapeDtypeStruct(*value) for value in...  58.8 us
    all_to_all x4, starting transfers between devices, to_all(): return lax.all_to_all(values, axes, split_axis=0, concat_axis=0, tiled=True)  22.4 us
    all_to_all x4, waiting for transfers between devices, to_all(): return lax.all_to_all(values, axes, split_axis=0, concat_axis=0, tiled=True)  13.7 us
    pallas_call x1, Pallas kernels, paganin(): pl.pallas_call(filter_kernel, out_shape=[jax.ShapeDtypeStruct((height //...  9.34 us
    pallas_call x1, Pallas kernels, gather_parts(): pl.pallas_call(gather_kernel, out_shape=jax.ShapeDtypeStruct((count,) + p...  2.87 us
    ppermute x3, starting transfers between devices, local(): lax.ppermute(part, 'slab', [(i, i ^ d) for i in range(n_slab)])  2.46 us
  transfers between devices with their start and end apart: 7, of which 2 were waited for; matrix products, arithmetic and copies ran while one was open for 1% of the time, Pallas kernels for 63%

profile of v5, /device:TPU:0, one launch (start us, length us, event | category | flops | bytes accessed | tf_op | source)
XLA Modules:
  0.0 115.0 jit_solution(3994154408191943240)
XLA Ops:
  0.6 7.3 %all-to-all-start = ((f32[8,64,256]{2,1,0:T(8,128)}), f32[8,64,256]{2,1,0:T(8,128)S(1)}, u32[]{:S(2)}, u32[]{:S(2)}) async-start(f32[8,64,256]{2,1,0:T(8,128)} %bitcast.10), calls=%async_computation | async-start | bytes 1048576 | tf_op jit(solution)/shard_map/all_to_all | solution.py:790
  7.9 0.8 reshape.62
  8.7 0.1 sub.24
  8.7 0.0 copy-start.12
  8.7 0.0 copy-start.9
  8.7 0.0 copy-start.10
  8.8 0.0 copy-start.2
  8.8 0.0 copy-start.3
  8.8 9.3 %paganin.1 = (f32[64,2048]{1,0:T(8,128)}, f32[64,2048]{1,0:T(8,128)}, f32[64,2048]{1,0:T(8,128)}, f32[64,2048]{1,0:T(8,128)}, f32[256,256]{1,0:T(8,128)}) custom-call(s32[1]{0:T(128)} %bitcast.rank_ref, f32[256,2048]{1,0:T(8,128)} %bitcast.12, f32[264,256]{1,0:T(8,128)} %constant.75.clone.given_ref), custom_call_target="tpu_custom_call" | custom-call | flops 8589934592 | bytes 4194304 | tf_op jit(solution)/shard_map/paganin/pallas_call | solution.py:185
  18.1 4.3 %all-to-all-done.refs_5_.refs_9_ = f32[8,64,256]{2,1,0:T(8,128)S(1)} async-done(((f32[8,64,256]{2,1,0:T(8,128)}), f32[8,64,256]{2,1,0:T(8,128)S(1)}, u32[]{:S(2)}, u32[]{:S(2)}) %all-to-all-start) | async-done | bytes 524320 | tf_op jit(solution)/shard_map/all_to_all | solution.py:790
  22.4 0.0 copy-done.12
  22.4 0.1 select_reduce_fusion.refs_2_.refs_3_
  22.5 3.7 %all-to-all-start.1 = ((f32[32,8,256]{2,1,0:T(8,128)}), f32[32,8,256]{2,1,0:T(8,128)S(1)}, u32[]{:S(2)}, u32[]{:S(2)}) async-start(f32[32,8,256]{2,1,0:T(8,128)} %bitcast.11), calls=%async_computation.1 | async-start | bytes 524288 | tf_op jit(solution)/shard_map/all_to_all | solution.py:790
  26.2 0.0 copy-done.9
  26.2 0.0 copy-done.10
  26.3 0.1 add_add_fusion
  26.3 0.1 add.64
  26.4 0.0 copy-done.1
  26.5 0.0 copy-done.2
  26.5 0.0 copy-done.3
  26.5 16.7 %first.1 = (bf16[32,768,512]{2,1,0:T(8,128)(2,1)}, f32[32,16,256]{2,1,0:T(8,128)S(1)}, f32[32,8,256]{2,1,0:T(8,128)S(1)}, f32[32,8,256]{2,1,0:T(8,128)S(1)}) custom-call(s32[1024]{0:T(1024)S(1)} %get-tuple-element.78.refs_0_, f32[1024]{0:T(1024)S(1)} %fusion.refs_1_.refs_0_, s32[64]{0:T(128)S(1)} %select_reduce_fusion.refs_2_.refs_3_, ...), custom_call_target="tpu_custom_call" | custom-call | flops 16000000000 | bytes 4194304 | tf_op jit(solution)/shard_map/first/pallas_call | solution.py:586
  43.2 0.0 copy-done
  43.2 0.0 copy-start.4
  43.3 0.8 copy-done.4
  44.0 0.0 all-to-all-done.1.refs_9_
  44.0 0.2 collective-permute-start
  44.3 1.6 %collective-permute-start.1 = (f32[64,2048]{1,0:T(8,128)}, f32[64,2048]{1,0:T(8,128)S(1)}, u32[]{:S(2)}, u32[]{:S(2)}) collective-permute-start(f32[64,2048]{1,0:T(8,128)} %get-tuple-element.61), channel_id=1, source_target_pairs={{0,24},{8,16},{16,8},{24,0},{1,25},{9,17},{17,9},{25,1},{2,26},{10... | collective-permute-start | bytes 1572872 | tf_op jit(solution)/shard_map/ppermute | solution.py:808
  45.9 25.2 %second.1 = (f32[32,16,256]{2,1,0:T(8,128)S(1)}, f32[8,32,256]{2,1,0:T(8,128)}) custom-call(s32[1024]{0:T(1024)S(1)} %get-tuple-element.78.refs_0_, f32[1024]{0:T(1024)S(1)} %fusion.refs_1_.refs_0_, s32[1024]{0:T(1024)S(1)} %get-tuple-element.79.refs_2_.refs_1_, s32[1024]{0:T(1024)S(1)} %get-tuple-element.80.refs_3_.refs_2_, ...), custom_call_target="tpu_custom_call" | custom-call | flops 20000000000 | bytes 4194304 | tf_op jit(solution)/shard_map/second/pallas_call | solution.py:586
  71.1 5.6 %all-to-all-start.2 = ((f32[8,32,256]{2,1,0:T(8,128)}), f32[8,32,256]{2,1,0:T(8,128)S(1)}, u32[]{:S(2)}, u32[]{:S(2)}) async-start(f32[8,32,256]{2,1,0:T(8,128)} %get-tuple-element.63.refs_7_), calls=%async_computation.2 | async-start | bytes 524288 | tf_op jit(solution)/shard_map/all_to_all | solution.py:790
  76.7 0.0 copy-done.11
  76.7 0.6 collective-permute-start.2
  77.2 0.0 collective-permute-done.refs_1_
  77.2 0.0 collective-permute-done.1.refs_3_
  77.2 0.0 copy-start.7
  77.3 16.9 %third.1 = f32[8,64,256]{2,1,0:T(8,128)} custom-call(f32[1024]{0:T(1024)S(1)} %fusion.refs_1_.refs_0_, s32[1024]{0:T(1024)S(1)} %get-tuple-element.79.refs_2_.refs_1_, s32[1024]{0:T(1024)S(1)} %get-tuple-element.80.refs_3_.refs_2_, s32[64]{0:T(128)S(1)} %select_reduce_fusion.refs_2_.refs_3_, f32[32]{0:T(128)S(1)} %get-tuple-element.81.refs_3_.refs_4_, ...), custom_call_target="tpu_custom_call" | custom-call | flops 10000000000 | bytes 4194304 | tf_op jit(solution)/shard_map/third/pallas_call | solution.py:586
  94.2 0.0 copy-done.6
  94.2 0.0 copy-done.7
  94.2 0.0 all-to-all-done.2.got_ref
  94.2 0.0 copy-start.5
  94.2 0.0 collective-permute-done.2.refs_2_
  94.2 0.0 copy-start.8
  94.2 5.9 %all-to-all-start.3 = ((f32[8,64,256]{2,1,0:T(8,128)}), f32[8,64,256]{2,1,0:T(8,128)S(1)}, u32[]{:S(2)}, u32[]{:S(2)}) async-start(f32[8,64,256]{2,1,0:T(8,128)} %third.1), calls=%async_computation.3 | async-start | bytes 1048576 | tf_op jit(solution)/shard_map/all_to_all | solution.py:790
  100.2 0.0 copy-done.8
  100.2 2.9 %gather_parts.1.sino_ref = f32[4,64,2048]{2,1,0:T(8,128)} custom-call(s32[1]{0:T(128)} %bitcast.rank_ref, f32[64,2048]{1,0:T(8,128)} %get-tuple-element.70.refs_0_, f32[64,2048]{1,0:T(8,128)} %copy-done.6, f32[64,2048]{1,0:T(8,128)} %copy-done.8, f32[64,2048]{1,0:T(8,128)} %copy-done.7), custom_call_target="tpu_custom_call" | custom-call | bytes 4194304 | tf_op jit(solution)/shard_map/gather_parts/pallas_call | solution.py:726
  103.0 0.0 copy-done.5
  103.1 1.7 %finish.1 = f32[4,64,2048]{2,1,0:T(8,128)} custom-call(f32[8,32,256]{2,1,0:T(8,128)} %copy-done.5, f32[4,64,2048]{2,1,0:T(8,128)} %gather_parts.1.sino_ref), custom_call_target="tpu_custom_call", output_to_operand_aliasing={{}: (1, {})} | custom-call | bytes 524288 | tf_op jit(solution)/shard_map/finish/pallas_call | solution.py:760
  104.7 9.4 %all-to-all-done.3 = f32[8,64,256]{2,1,0:T(8,128)S(1)} async-done(((f32[8,64,256]{2,1,0:T(8,128)}), f32[8,64,256]{2,1,0:T(8,128)S(1)}, u32[]{:S(2)}, u32[]{:S(2)}) %all-to-all-start.3) | async-done | bytes 524320 | tf_op jit(solution)/shard_map/all_to_all | solution.py:790
  114.2 0.8 copy.17
  (9 shorter events, 0.1 us)
Async XLA Ops:
  0.6 21.8 %all-to-all-start = ((f32[8,64,256]{2,1,0:T(8,128)}), f32[8,64,256]{2,1,0:T(8,128)S(1)}, u32[]{:S(2)}, u32[]{:S(2)}) async-start(f32[8,64,256]{2,1,0:T(8,128)} %bitcast.10), calls=%async_computation | async-start | bytes 1048576 | tf_op jit(solution)/shard_map/all_to_all | solution.py:790
  8.7 13.6 %copy-start.12 = (s32[64]{0:T(128)S(1)}, s32[64]{0:T(128)}, u32[]{:S(2)}) copy-start(s32[64]{0:T(128)} %param.13) | copy-start | bytes 772
  8.7 17.5 %copy-start.9 = (f32[32]{0:T(128)S(1)}, f32[32]{0:T(128)}, u32[]{:S(2)}) copy-start(f32[32]{0:T(128)} %constant.83) | copy-start | bytes 388
  8.7 17.5 %copy-start.10 = (f32[32]{0:T(128)S(1)}, f32[32]{0:T(128)}, u32[]{:S(2)}) copy-start(f32[32]{0:T(128)} %constant.82) | copy-start | bytes 388
  8.7 17.7 %copy-start.1 = (bf16[256,256]{1,0:T(8,128)(2,1)S(1)}, bf16[256,256]{1,0:T(8,128)(2,1)}, u32[]{:S(2)}) copy-start(bf16[256,256]{1,0:T(8,128)(2,1)} %constant.78.clone.refs_6_.refs_10_) | copy-start | bytes 393220
  8.8 17.7 %copy-start.2 = (f32[8,256]{1,0:T(8,128)S(1)}, f32[8,256]{1,0:T(8,128)}, u32[]{:S(2)}) copy-start(f32[8,256]{1,0:T(8,128)} %constant.80.clone.refs_8_.refs_12_) | copy-start | bytes 24580
  8.8 17.7 %copy-start.3 = (f32[8,256]{1,0:T(8,128)S(1)}, f32[8,256]{1,0:T(8,128)}, u32[]{:S(2)}) copy-start(f32[8,256]{1,0:T(8,128)} %constant.79.clone.refs_7_.refs_11_) | copy-start | bytes 24580
  22.4 20.9 %copy-start = (f32[8,64,256]{2,1,0:T(8,128)}, f32[8,64,256]{2,1,0:T(8,128)S(1)}, u32[]{:S(2)}) copy-start(f32[8,64,256]{2,1,0:T(8,128)S(1)} %all-to-all-done.refs_5_.refs_9_) | copy-start | bytes 1572868
  22.5 21.5 %all-to-all-start.1 = ((f32[32,8,256]{2,1,0:T(8,128)}), f32[32,8,256]{2,1,0:T(8,128)S(1)}, u32[]{:S(2)}, u32[]{:S(2)}) async-start(f32[32,8,256]{2,1,0:T(8,128)} %bitcast.11), calls=%async_computation.1 | async-start | bytes 524288 | tf_op jit(solution)/shard_map/all_to_all | solution.py:790
  43.2 0.8 copy-start.4
  44.0 33.2 %collective-permute-start = (f32[64,2048]{1,0:T(8,128)}, f32[64,2048]{1,0:T(8,128)S(1)}, u32[]{:S(2)}, u32[]{:S(2)}) collective-permute-start(f32[64,2048]{1,0:T(8,128)} %get-tuple-element.60), channel_id=1, source_target_pairs={{0,8},{8,0},{16,24},{24,16},{1,9},{9,1},{17,25},{25,17},{2,10},{10... | collective-permute-start | bytes 1572872 | tf_op jit(solution)/shard_map/ppermute | solution.py:808
  44.3 33.0 %collective-permute-start.1 = (f32[64,2048]{1,0:T(8,128)}, f32[64,2048]{1,0:T(8,128)S(1)}, u32[]{:S(2)}, u32[]{:S(2)}) collective-permute-start(f32[64,2048]{1,0:T(8,128)} %get-tuple-element.61), channel_id=1, source_target_pairs={{0,24},{8,16},{16,8},{24,0},{1,25},{9,17},{17,9},{25,1},{2,26},{10... | collective-permute-start | bytes 1572872 | tf_op jit(solution)/shard_map/ppermute | solution.py:808
  45.9 30.7 %copy-start.11 = (f32[64,2048]{1,0:T(8,128)S(1)}, f32[64,2048]{1,0:T(8,128)}, u32[]{:S(2)}) copy-start(f32[64,2048]{1,0:T(8,128)} %get-tuple-element.66) | copy-start | bytes 1572868
  71.1 23.1 %all-to-all-start.2 = ((f32[8,32,256]{2,1,0:T(8,128)}), f32[8,32,256]{2,1,0:T(8,128)S(1)}, u32[]{:S(2)}, u32[]{:S(2)}) async-start(f32[8,32,256]{2,1,0:T(8,128)} %get-tuple-element.63.refs_7_), calls=%async_computation.2 | async-start | bytes 524288 | tf_op jit(solution)/shard_map/all_to_all | solution.py:790
  76.7 17.6 %collective-permute-start.2 = (f32[64,2048]{1,0:T(8,128)S(1)}, f32[64,2048]{1,0:T(8,128)S(1)}, u32[]{:S(2)}, u32[]{:S(2)}) collective-permute-start(f32[64,2048]{1,0:T(8,128)S(1)} %copy-done.11), channel_id=1, source_target_pairs={{0,16},{8,24},{16,0},{24,8},{1,17},{9,25},{17,1},{25,9},{2,18},{10... | collective-permute-start | bytes 1572872 | tf_op jit(solution)/shard_map/ppermute | solution.py:808
  77.2 16.9 %copy-start.6 = (f32[64,2048]{1,0:T(8,128)}, f32[64,2048]{1,0:T(8,128)S(1)}, u32[]{:S(2)}) copy-start(f32[64,2048]{1,0:T(8,128)S(1)} %collective-permute-done.refs_1_) | copy-start | bytes 1572868
  77.2 16.9 %copy-start.7 = (f32[64,2048]{1,0:T(8,128)}, f32[64,2048]{1,0:T(8,128)S(1)}, u32[]{:S(2)}) copy-start(f32[64,2048]{1,0:T(8,128)S(1)} %collective-permute-done.1.refs_3_) | copy-start | bytes 1572868
  94.2 8.9 %copy-start.5 = (f32[8,32,256]{2,1,0:T(8,128)}, f32[8,32,256]{2,1,0:T(8,128)S(1)}, u32[]{:S(2)}) copy-start(f32[8,32,256]{2,1,0:T(8,128)S(1)} %all-to-all-done.2.got_ref) | copy-start | bytes 786436
  94.2 6.0 %copy-start.8 = (f32[64,2048]{1,0:T(8,128)}, f32[64,2048]{1,0:T(8,128)S(1)}, u32[]{:S(2)}) copy-start(f32[64,2048]{1,0:T(8,128)S(1)} %collective-permute-done.2.refs_2_) | copy-start | bytes 1572868
  94.2 20.0 %all-to-all-start.3 = ((f32[8,64,256]{2,1,0:T(8,128)}), f32[8,64,256]{2,1,0:T(8,128)S(1)}, u32[]{:S(2)}, u32[]{:S(2)}) async-start(f32[8,64,256]{2,1,0:T(8,128)} %third.1), calls=%async_computation.3 | async-start | bytes 1048576 | tf_op jit(solution)/shard_map/all_to_all | solution.py:790

commit v6 on v5

--- a/solution.py
+++ b/solution.py
@@ -79,7 +79,8 @@
 
 
 def filter_kernel(rank_ref, source_ref, given_ref, *refs):
-    *part_refs, active_ref, image_ref, table_ref, out_ref, spec_ref, up_ref, down_ref, sems = refs
+    *part_refs, active_ref, image_ref, table_ref, out_ref, spec_ref, up_ref, down_ref = refs[:-2]
+    sems, out_sems = refs[-2:]
     height, width = image_ref.shape
     rank = rank_ref[0]
     share = height // len(part_refs)
@@ -168,15 +169,25 @@
     lax.fori_loop(half, 2 * half, inner, carry)
 
     offset = (width - ACTIVE) // 2
+    sent = []
     for c in range(ROWS):
         spectrum = jnp.concatenate(
             [up_ref[b, pl.ds(c, length, stride=ROWS), :] for b in range(blocks)], axis=1
         )
         filtered = 1.0 - jnp.transpose(transform(spectrum))
-        out_ref[:, c * length : (c + 1) * length] = -jnp.log(filtered)
+        columns = slice(c * length, (c + 1) * length)
+        out_ref[:, columns] = -jnp.log(filtered)
+        for d, part_ref in enumerate(part_refs):
+            rows = pl.ds(pl.multiple_of((rank ^ d) * share, share), share)
+            sent.append(
+                pltpu.make_async_copy(
+                    out_ref.at[rows, columns], part_ref.at[:, columns], out_sems.at[c, d]
+                )
+            )
+            sent[-1].start()
     active_ref[...] = out_ref[:, offset : offset + ACTIVE]
-    for d, part_ref in enumerate(part_refs):
-        part_ref[...] = out_ref[pl.ds(pl.multiple_of((rank ^ d) * share, share), share), :]
+    for copy in sent:
+        copy.wait()
 
 
 def paganin(image, rank, parts):
@@ -188,7 +199,8 @@
         + [jax.ShapeDtypeStruct((height, ACTIVE), f32)],
         in_specs=[pl.BlockSpec(memory_space=pltpu.SMEM)]
         + [pl.BlockSpec(memory_space=pltpu.HBM)] * 2,
-        out_specs=[pl.BlockSpec(memory_space=pltpu.VMEM)] * (parts + 1),
+        out_specs=[pl.BlockSpec(memory_space=pltpu.HBM)] * parts
+        + [pl.BlockSpec(memory_space=pltpu.VMEM)],
         scratch_shapes=[
             pltpu.VMEM((height, width), f32),
             pltpu.VMEM((height + ROWS, height), f32),
@@ -197,6 +209,7 @@
             pltpu.VMEM((blocks, width, LANES), f32),
             pltpu.VMEM((blocks, width // 2, LANES), f32),
             pltpu.SemaphoreType.DMA((ROWS + 1,)),
+            pltpu.SemaphoreType.DMA((ROWS, parts)),
         ],
         compiler_params=pltpu.CompilerParams(vmem_limit_bytes=58 * 2**20),
         cost_estimate=pl.CostEstimate(
@@ -213,13 +226,12 @@
 
 
 class Weights:
-    def __init__(self, ref, along_ref, place_ref, angles, chunk, count):
+    def __init__(self, ref, along_ref, place_ref, angles, chunk):
         self.ref = ref
         self.along_ref = along_ref
         self.place_ref = place_ref
         self.angles = angles
         self.chunk = chunk
-        self.count = count
         self.ray = lax.broadcasted_iota(jnp.int32, (ROWS, VOX), 0).astype(f32)
 
     def prepare(self, shift_x_ref, shift_y_ref, cos_ref, sin_ref):
@@ -228,8 +240,8 @@
 
         repeat(self.angles, along_angle, 8)
 
-    def make(self, q, c):
-        place = q % self.count
+    def make(self, q, c, place):
+        ref = self.ref.at[place]
         for two in range(self.chunk // 2):
             pieces = []
             for t in (2 * two, 2 * two + 1):
@@ -240,34 +252,15 @@
                     distance = base + float(group * ROWS)
                     pieces.append(jnp.maximum(0.0, 1.0 - jnp.abs(distance)))
             high, low = halves(jnp.concatenate(pieces, axis=0))
-            self.ref[place, 2 * two * WIN : (2 * two + 2) * WIN, 0:VOX] = high
-            self.ref[place, 2 * two * WIN : (2 * two + 2) * WIN, VOX : 2 * VOX] = low
-
-    def get(self, q):
-        return self.ref[q % self.count]
-
-
-class Stream:
-    def __init__(self, hbm_ref, vmem_ref, sems, outward):
-        self.hbm_ref = hbm_ref
-        self.vmem_ref = vmem_ref
-        self.sems = sems
-        self.outward = outward
-        self.count = vmem_ref.shape[0]
-
-    def copy(self, q):
-        place = q % self.count
-        here, there = self.vmem_ref.at[place], self.hbm_ref.at[q]
-        if self.outward:
-            return pltpu.make_async_copy(here, there, self.sems.at[place])
-        return pltpu.make_async_copy(there, here, self.sems.at[place])
-
-
-def project(weights, make, values_of, offset_ref, acc_ref, pairs, both, stream, unroll):
+            ref[2 * two * WIN : (2 * two + 2) * WIN, 0:VOX] = high
+            ref[2 * two * WIN : (2 * two + 2) * WIN, VOX : 2 * VOX] = low
+
+
+def project(weights, values_of, weights_of, offset_ref, acc_ref, pairs, both, unroll):
     angles, chunk = weights.angles, weights.chunk
     acc_ref[...] = jnp.zeros(acc_ref.shape, f32)
 
-    def pair(q):
+    def pair(q, step):
         high, low = halves(values_of(q))
         operand = jnp.concatenate(
             [
@@ -278,19 +271,9 @@
             ],
             axis=0,
         )
-        if stream is not None:
-
-            @pl.when(q >= stream.count)
-            def _():
-                stream.copy(q - stream.count).wait()
-
         for c in range(angles // chunk):
-            if make:
-                weights.make(q, c)
-            if stream is not None:
-                stream.copy(q).start()
             sums = lax.dot_general(
-                weights.get(q),
+                weights_of(q, c, step),
                 operand,
                 (((1,), (1,)), ((), ())),
                 preferred_element_type=f32,
@@ -305,10 +288,12 @@
                 for angle, rows, values in places:
                     acc_ref[angle, rows, :] = values
 
-    repeat(pairs, pair, unroll)
-    if stream is not None:
-        for q in range(pairs - stream.count, pairs):
-            stream.copy(q).wait()
+    def several(index, carry):
+        for step in range(unroll):
+            pair(index * unroll + step, step)
+        return carry
+
+    lax.fori_loop(0, pairs // unroll, several, 0)
 
 
 def spread_rays(acc_ref, direct_ref, mirror_ref, total_ref, slices):
@@ -330,7 +315,7 @@
 
 
 def back_project(
-    weights, weighted, flip, window_ref, tile_ref, turn_ref, store, pairs, stream, unroll
+    weights, weights_of, weighted, flip, window_ref, tile_ref, turn_ref, store, pairs, unroll
 ):
     angles, slices, _ = weighted.shape
     chunk = weights.chunk
@@ -352,10 +337,7 @@
     def pair(q):
         total = None
         for c in range(angles // chunk):
-            if stream is None:
-                weights.make(q, c)
-            else:
-                stream.copy(q).wait()
+            held = weights_of(q, c)
             tiles = [None] * (-(-width // LANES))
             for t in range(chunk):
                 index = q * angles + c * chunk + t
@@ -371,7 +353,7 @@
                             lane_rows >= begin - place * LANES, piece, tiles[place]
                         )
             high, low = halves(jnp.concatenate(tiles, axis=1))
-            sums = dot(jnp.concatenate([high, low], axis=0), weights.get(q))
+            sums = dot(jnp.concatenate([high, low], axis=0), held)
             piece = sums[0:both, 0:VOX] + sums[both:, 0:VOX] + sums[0:both, VOX:]
             total = piece if total is None else total + piece
         store(q, total)
@@ -381,30 +363,26 @@
 
 def first_kernel(
     sizes,
+    rank_ref,
     offset_ref,
     place_ref,
     slot_ref,
     cos_ref,
     sin_ref,
-    vol_ref,
     flip_ref,
     shift_x_ref,
     shift_y_ref,
-    held_ref,
-    start_ref,
-    predicted_ref,
-    gain_ref,
-    weight_ref,
-    sems,
-    acc_ref,
-    along_ref,
-    half_ref,
-    mirror_ref,
+    *refs,
 ):
-    angles, chunk, held, slots = sizes
+    angles, chunk, held, slots, rays = sizes
+    vol_refs, refs = refs[:rays], list(refs[rays:])
+    held_ref = refs.pop(0) if held else None
+    half_ref, start_ref, predicted_ref, gain_ref = refs[:4]
+    weight_a_ref, weight_b_ref, sems, acc_ref, along_ref, mirror_ref = refs[4:]
     patches = slot_ref.shape[0]
     pairs, both, _ = start_ref.shape
     slices = both // 2
+    rank = rank_ref[0]
     flip = flip_ref[...]
 
     def slot_values(patch):
@@ -414,13 +392,9 @@
             [half_ref[part, slot // slots, rows, :] for part in range(2)], axis=1
         )
 
-    weights = Weights(
-        weight_ref, along_ref, place_ref, angles, chunk, weight_ref.shape[0]
-    )
-    stream = Stream(held_ref, weight_ref, sems, True) if held else None
-    weights.prepare(shift_x_ref, shift_y_ref, cos_ref, sin_ref)
-    for part in range(2):
-        half_ref[part] = vol_ref[:, :, part * LANES : (part + 1) * LANES]
+    for d, vol_ref in enumerate(vol_refs):
+        for part in range(2):
+            half_ref[part, rank ^ d] = vol_ref[:, part * LANES : (part + 1) * LANES]
 
     def order(q):
         start_ref[q, 0:slices, :] = slot_values(q)
@@ -428,9 +402,36 @@
 
     repeat(pairs, order, 8)
     start_ref[:, slices:both, :] = turn_rays(mirror_ref[0:pairs], flip)
+    both_weights = [
+        Weights(ref, along_ref, place_ref, angles, chunk) for ref in (weight_a_ref, weight_b_ref)
+    ]
+    both_weights[0].prepare(shift_x_ref, shift_y_ref, cos_ref, sin_ref)
+
+    def outward(q, step):
+        place = q // 2 % 2
+        return pltpu.make_async_copy(
+            both_weights[step].ref.at[place], held_ref.at[q], sems.at[step, place]
+        )
+
+    def weights_of(q, c, step):
+        if held:
+
+            @pl.when(q >= 4)
+            def _():
+                outward(q - 4, step).wait()
+
+        place = q // 2 % 2
+        both_weights[step].make(q, c, place)
+        if held:
+            outward(q, step).start()
+        return both_weights[step].ref[place]
+
     project(
-        weights, True, lambda q: start_ref[q], offset_ref, acc_ref, pairs, both, stream, 2
+        both_weights[0], lambda q: start_ref[q], weights_of, offset_ref, acc_ref, pairs, both, 2
     )
+    if held:
+        for q in range(pairs - 4, pairs):
+            outward(q, q % 2).wait()
     spread_rays(acc_ref, predicted_ref, mirror_ref, gain_ref, slices)
     predicted_ref[...] = predicted_ref[...] + turn_rays(mirror_ref[0:angles], flip)
     direct = gain_ref[...]
@@ -440,122 +441,91 @@
 def second_kernel(
     sizes,
     step_size,
+    rank_ref,
     offset_ref,
-    place_ref,
-    tile_ref,
-    turn_ref,
-    cos_ref,
-    sin_ref,
-    start_ref,
-    predicted_ref,
-    gain_ref,
-    sino_ref,
-    flip_ref,
-    shift_x_ref,
-    shift_y_ref,
-    held_ref,
-    update_ref,
-    res_ref,
-    weight_ref,
-    sems,
-    acc_ref,
-    along_ref,
-    direct_ref,
-    mirror_ref,
-    window_ref,
-):
-    angles, chunk, held, _ = sizes
-    pairs, both, _ = start_ref.shape
-    slices = both // 2
-    rays = res_ref.shape[0]
-    flip = flip_ref[...]
-    weights = Weights(
-        weight_ref, along_ref, place_ref, angles, chunk, weight_ref.shape[0]
-    )
-    stream = Stream(held_ref, weight_ref, sems, False) if held else None
-    if held:
-        repeat(pairs, lambda q: stream.copy(q).start(), 8)
-    else:
-        weights.prepare(shift_x_ref, shift_y_ref, cos_ref, sin_ref)
-    weighted = (sino_ref[...] - predicted_ref[...]) * gain_ref[...] * (1.0 / ROI)
-
-    def store(q, total):
-        update_ref[q] = total
-
-    back_project(
-        weights, weighted, flip, window_ref, tile_ref, turn_ref, store, pairs, stream, 4
-    )
-
-    def values_of(q):
-        return start_ref[q] + step_size * update_ref[q]
-
-    project(weights, not held, values_of, offset_ref, acc_ref, pairs, both, None, 4)
-    spread_rays(acc_ref, direct_ref, mirror_ref, None, slices)
-    residual = sino_ref[...] - direct_ref[...] - turn_rays(mirror_ref[...], flip)
-    for t in range(angles):
-        begin = t // rays * slices
-        res_ref[t % rays, begin : begin + slices, :] = residual[t]
-
-
-def third_kernel(
-    sizes,
-    step_size,
     place_ref,
     tile_ref,
     turn_ref,
     slot_ref,
     cos_ref,
     sin_ref,
-    update_ref,
-    res_ref,
-    gain_ref,
-    vol_ref,
     flip_ref,
     shift_x_ref,
     shift_y_ref,
-    held_ref,
-    out_ref,
-    weight_ref,
-    sems,
-    along_ref,
-    total_ref,
-    mirror_ref,
-    window_ref,
-    half_ref,
+    half_in_ref,
+    start_ref,
+    predicted_ref,
+    gain_ref,
+    sino_ref,
+    *refs,
 ):
-    angles, chunk, held, slots = sizes
+    angles, chunk, held, slots, rays = sizes
+    refs = list(refs)
+    held_ref = refs.pop(0) if held else None
+    out_refs, refs = refs[:rays], refs[rays:]
+    weight_ref, sems, acc_ref, along_ref, direct_ref, mirror_ref, window_ref = refs[:7]
+    update_ref, half_ref = refs[7:]
     patches = slot_ref.shape[0]
-    pairs, both, _ = update_ref.shape
+    pairs, both, _ = start_ref.shape
     slices = both // 2
-    rays = res_ref.shape[0]
+    rank = rank_ref[0]
     flip = flip_ref[...]
-    weights = Weights(
-        weight_ref, along_ref, place_ref, angles, chunk, weight_ref.shape[0]
-    )
-    stream = Stream(held_ref, weight_ref, sems, False) if held else None
+    weights = Weights(weight_ref, along_ref, place_ref, angles, chunk)
+    ahead = 4
+
+    def inward(q):
+        return pltpu.make_async_copy(held_ref.at[q], weight_ref.at[q], sems.at[q])
+
     if held:
-        repeat(pairs, lambda q: stream.copy(q).start(), 8)
+        for q in range(ahead):
+            inward(q).start()
     else:
         weights.prepare(shift_x_ref, shift_y_ref, cos_ref, sin_ref)
-    residual = [
-        res_ref[t % rays, t // rays * slices : (t // rays + 1) * slices, :][None]
-        for t in range(angles)
-    ]
-    weighted = jnp.concatenate(residual, axis=0) * gain_ref[...] * (1.0 / ROI)
-
-    def store(q, total):
-        total_ref[q] = (update_ref[q] + total) * step_size
-
-    back_project(
-        weights, weighted, flip, window_ref, tile_ref, turn_ref, store, pairs, stream, 4
-    )
-    mirror_ref[...] = turn_rays(total_ref[:, slices:both, :], flip)
-    for part in range(2):
-        half_ref[part] = vol_ref[:, :, part * LANES : (part + 1) * LANES]
+
+    def arriving(q, c):
+        if not held:
+            weights.make(q, c, 0)
+            return weight_ref[0]
+
+        @pl.when(q + ahead < pairs)
+        def _():
+            inward(q + ahead).start()
+
+        inward(q).wait()
+        return weight_ref[q]
+
+    def ready(q, c, step=0):
+        if not held:
+            weights.make(q, c, 0)
+            return weight_ref[0]
+        return weight_ref[q]
+
+    def first_update(q, total):
+        update_ref[q] = total
+
+    def second_update(q, total):
+        update_ref[q] = (update_ref[q] + total) * step_size
+
+    rest = (flip, window_ref, tile_ref, turn_ref)
+    weighted = (sino_ref[...] - predicted_ref[...]) * gain_ref[...] * (1.0 / ROI)
+    back_project(weights, arriving, weighted, *rest, first_update, pairs, 2)
+
+    def values_of(q):
+        return start_ref[q] + step_size * update_ref[q]
+
+    project(weights, values_of, ready, offset_ref, acc_ref, pairs, both, 2)
+    spread_rays(acc_ref, direct_ref, mirror_ref, None, slices)
+    turned = turn_rays(mirror_ref[0:angles], flip)
+    direct_ref[...] = sino_ref[...] - direct_ref[...] - turned
+    weighted = direct_ref[...] * gain_ref[...] * (1.0 / ROI)
+    back_project(weights, ready, weighted, *rest, second_update, pairs, 2)
+
+    mirror_ref[0:pairs] = turn_rays(update_ref[:, slices:both, :], flip)
+    half_ref[...] = half_in_ref[...]
 
     def finish(q):
         for patch, update in (
-            (q, total_ref[q, 0:slices, :]),
+            (q, update_ref[q, 0:slices, :]),
             (patches - 1 - q, mirror_ref[q]),
         ):
             slot = slot_ref[patch]
@@ -567,29 +537,27 @@
                 )
 
     repeat(pairs, finish, 8)
-    for part in range(2):
-        out_ref[:, :, part * LANES : (part + 1) * LANES] = half_ref[part]
-
-
-def call(kernel, name, inputs, held_in, outputs, held_out, scratch, micros, room):
+    lead = slices * slots
+    for d, out_ref in enumerate(out_refs):
+        ray = rank ^ d
+        for part in range(2):
+            out_ref[0:lead, part * LANES : (part + 1) * LANES] = half_ref[part, ray]
+        for k in range(angles // rays):
+            begin = lead + k * slices
+            out_ref[begin : begin + slices, :] = direct_ref[k * rays + ray]
+
+
+def call(kernel, name, inputs, held_in, held_out, outputs, scratch, micros):
     smem = pl.BlockSpec(memory_space=pltpu.SMEM)
     vmem = pl.BlockSpec(memory_space=pltpu.VMEM)
     hbm = [pl.BlockSpec(memory_space=pltpu.HBM)]
-    before = len(inputs)
-
-    def body(*refs):
-        refs = list(refs)
-        if not held_in and not held_out:
-            refs.insert(before, None)
-        kernel(*refs)
-
     return pl.pallas_call(
-        body,
+        kernel,
         out_shape=[jax.ShapeDtypeStruct(*value) for value in held_out + outputs],
         in_specs=[smem if value.ndim == 1 else vmem for value in inputs] + hbm * len(held_in),
         out_specs=hbm * len(held_out) + [vmem] * len(outputs),
         scratch_shapes=scratch,
-        compiler_params=pltpu.CompilerParams(vmem_limit_bytes=room * 2**20),
+        compiler_params=pltpu.CompilerParams(vmem_limit_bytes=52 * 2**20),
         cost_estimate=pl.CostEstimate(
             flops=int(micros * 1e9), bytes_accessed=4 * 2**20, transcendentals=0
         ),
@@ -598,15 +566,15 @@
 
 
 class Sirt:
-    def __init__(self, theta, vol_list, slices, slots, rays, step_size):
+    def __init__(self, rank, theta, vol_list, slices, slots, rays, step_size):
         angles = theta.shape[0]
         patches = vol_list.shape[0]
         pairs = patches // 2
         both = 2 * slices
         chunk = math.gcd(angles, 32)
         self.held = angles == chunk
-        self.room = 52
-        self.sizes = (angles, chunk, self.held, slots)
+        self.sizes = (angles, chunk, self.held, slots, rays)
+        self.rank = rank.reshape(1)
         self.step_size = step_size
         self.rays = rays
         self.patches = patches
@@ -649,63 +617,46 @@
         self.window = ((angles, 3, both, LANES), f32)
         self.half = ((2, rays, slices * slots, LANES), f32)
         self.mirror = ((max(pairs, angles), slices, ACTIVE), f32)
-        self.sent = ((rays, angles // rays * slices, ACTIVE), f32)
-
-    def scratch(self, held, *shapes):
-        count = held if self.held else 1
+        self.sent = ((slices * (slots + angles // rays), ACTIVE), f32)
+
+    def weight(self, count):
         shape, dtype = self.held_weight
-        weight = pltpu.VMEM((count,) + shape[1:], dtype)
-        rest = [pltpu.VMEM(*shape) for shape in shapes]
-        return [weight, pltpu.SemaphoreType.DMA((count,))] + rest
-
-    def first(self, volume):
-        inputs = [self.offset, self.place, self.slot, self.cosine, self.sine, volume]
+        return pltpu.VMEM((count,) + shape[1:], dtype)
+
+    def first(self, volumes):
+        inputs = [self.rank, self.offset, self.place, self.slot, self.cosine, self.sine]
+        shapes = (self.acc, self.along, self.mirror)
         results = call(
             functools.partial(first_kernel, self.sizes),
             "first",
-            inputs + self.fixed,
+            inputs + self.fixed + volumes,
             [],
-            [self.by_pair, self.by_ray, self.by_ray],
             [self.held_weight] if self.held else [],
-            self.scratch(4, self.acc, self.along, self.half, self.mirror),
+            [self.half, self.by_pair, self.by_ray, self.by_ray],
+            [self.weight(2), self.weight(2), pltpu.SemaphoreType.DMA((2, 2))]
+            + [pltpu.VMEM(*shape) for shape in shapes],
             16,
-            self.room,
         )
         return (results[:1], results[1:]) if self.held else ([], results)
 
-    def second(self, weight, start, predicted, gain, sino):
-        inputs = [self.offset, self.place, self.tile, self.turn, self.cosine, self.sine]
-        inputs += [start, predicted, gain, sino]
+    def second(self, weight, half, start, predicted, gain, sino):
+        inputs = [self.rank, self.offset, self.place, self.tile, self.turn, self.slot]
+        inputs += [self.cosine, self.sine] + self.fixed
+        inputs += [half, start, predicted, gain, sino]
+        count = self.patches // 2 if self.held else 1
+        shapes = (self.acc, self.along, self.by_ray, self.mirror, self.window)
+        shapes += (self.by_pair, self.half)
         return call(
             functools.partial(second_kernel, self.sizes, self.step_size),
             "second",
-            inputs + self.fixed,
+            inputs,
             list(weight),
-            [self.by_pair, self.sent],
             [],
-            self.scratch(
-                self.patches // 2, self.acc, self.along, self.by_ray, self.by_ray, self.window
-            ),
-            20,
-            self.room,
+            [self.sent] * self.rays,
+            [self.weight(count), pltpu.SemaphoreType.DMA((count,))]
+            + [pltpu.VMEM(*shape) for shape in shapes],
+            30,
         )
-
-    def third(self, weight, update, residual, gain, volume):
-        inputs = [self.place, self.tile, self.turn, self.slot, self.cosine, self.sine]
-        inputs += [update, residual, gain, volume]
-        pairs = self.patches // 2
-        mirror = ((pairs,) + self.by_ray[0][1:], f32)
-        return call(
-            functools.partial(third_kernel, self.sizes, self.step_size),
-            "third",
-            inputs + self.fixed,
-            list(weight),
-            [(volume.shape, f32)],
-            [],
-            self.scratch(pairs, self.along, self.by_pair, mirror, self.window, self.half),
-            10,
-            self.room,
-        )[0]
 
 
 def gather_kernel(rank_ref, *refs):
@@ -737,41 +688,85 @@
     )(rank.reshape(1), *parts)
 
 
-def finish_kernel(got_ref, sino_ref, out_ref, active_ref, sem):
-    rays, rows, _ = got_ref.shape
+def finish_kernel(rank_ref, *refs):
+    *got_refs, _, rec_ref, out_ref, values_ref, active_ref, sems = refs
+    rank = rank_ref[0]
+    rays = len(got_refs)
+    slots = values_ref.shape[1]
     slabs = active_ref.shape[0]
-    slices = rows // slabs
-    for ray in range(rays):
+    slices = values_ref.shape[0] // rays
+    lead = slices * slots
+    for d, got_ref in enumerate(got_refs):
+        rows = pl.ds(pl.multiple_of((rank ^ d) * slices, slices), slices)
+        values_ref[rows] = got_ref[0:lead, :].reshape(slices, slots, VOX)
         for k in range(slabs):
-            active_ref[k, ray * slices : (ray + 1) * slices, :] = got_ref[
-                ray, k * slices : (k + 1) * slices, :
-            ]
+            begin = lead + k * slices
+            active_ref[k, rows, :] = got_ref[begin : begin + slices, :]
     offset = (out_ref.shape[2] - ACTIVE) // 2
-    copy = pltpu.make_async_copy(
-        active_ref, out_ref.at[:, :, offset : offset + ACTIVE], sem
-    )
-    copy.start()
-    copy.wait()
-
-
-def finish(got, sinogram):
+    copies = [
+        pltpu.make_async_copy(values_ref, rec_ref, sems.at[0]),
+        pltpu.make_async_copy(
+            active_ref, out_ref.at[:, :, offset : offset + ACTIVE], sems.at[1]
+        ),
+    ]
+    for copy in copies:
+        copy.start()
+    for copy in copies:
+        copy.wait()
+
+
+def finish(pieces, sinogram, rank, shape):
     slabs, slab_rows, _ = sinogram.shape
     any_space = pl.BlockSpec(memory_space=pl.ANY)
     return pl.pallas_call(
         finish_kernel,
-        out_shape=jax.ShapeDtypeStruct(sinogram.shape, f32),
-        in_specs=[pl.BlockSpec(memory_space=pltpu.VMEM), any_space],
-        out_specs=any_space,
+        out_shape=(
+            jax.ShapeDtypeStruct(shape, f32),
+            jax.ShapeDtypeStruct(sinogram.shape, f32),
+        ),
+        in_specs=[pl.BlockSpec(memory_space=pltpu.SMEM)]
+        + [pl.BlockSpec(memory_space=pltpu.VMEM)] * len(pieces)
+        + [any_space],
+        out_specs=[any_space, any_space],
         scratch_shapes=[
+            pltpu.VMEM(shape, f32),
             pltpu.VMEM((slabs, slab_rows, ACTIVE), f32),
-            pltpu.SemaphoreType.DMA,
+            pltpu.SemaphoreType.DMA((2,)),
         ],
-        input_output_aliases={1: 0},
+        input_output_aliases={len(pieces) + 1: 1},
         cost_estimate=pl.CostEstimate(
-            flops=0, bytes_accessed=8 * got.size, transcendentals=0
+            flops=0, bytes_accessed=8 * len(pieces) * pieces[0].size, transcendentals=0
         ),
         name="finish",
-    )(got, sinogram)
+    )(rank.reshape(1), *pieces, sinogram)
+
+
+def split_kernel(rank_ref, source_ref, *piece_refs):
+    for d, piece_ref in enumerate(piece_refs):
+        piece_ref[...] = source_ref[rank_ref[0] ^ d]
+
+
+def split(values, rank):
+    vmem = pl.BlockSpec(memory_space=pltpu.VMEM)
+    count = values.shape[0]
+    return pl.pallas_call(
+        split_kernel,
+        out_shape=[jax.ShapeDtypeStruct(values.shape[1:], f32)] * count,
+        in_specs=[pl.BlockSpec(memory_space=pltpu.SMEM), vmem],
+        out_specs=[vmem] * count,
+        cost_estimate=pl.CostEstimate(
+            flops=0, bytes_accessed=8 * values.size, transcendentals=0
+        ),
+        name="split",
+    )(rank.reshape(1), values)
+
+
+def exchange(pieces, axis):
+    count = len(pieces)
+    return [
+        lax.ppermute(piece, axis, [(i, i ^ d) for i in range(count)]) if d else piece
+        for d, piece in enumerate(pieces)
+    ]
 
 
 def local(intensity, angles, volume, vol_list):
@@ -784,46 +779,52 @@
     count = angles.shape[0] * angles.shape[1]
     step_size = relax * ROI / count
     rank = lax.axis_index("slab")
+    ray_rank = lax.axis_index("ray")
     padded = -(-slices // ROWS) * ROWS
 
-    def to_all(values, axes):
-        return lax.all_to_all(values, axes, split_axis=0, concat_axis=0, tiled=True)
-
-    own_volume = to_all(volume.reshape(n_ray, slices * slots, VOX), "ray")
+    volumes = exchange(split(volume.reshape(n_ray, slices * slots, VOX), ray_rank), "ray")
     *parts, active = paganin(intensity.reshape(height, band), rank, n_slab)
-    active, own_volume = lax.optimization_barrier((active, own_volume))
-    own_rays = to_all(active.reshape(devices, slices, ACTIVE), ("slab", "ray"))
+    active, volumes = lax.optimization_barrier((active, volumes))
+    own_rays = lax.all_to_all(
+        active.reshape(devices, slices, ACTIVE),
+        ("slab", "ray"),
+        split_axis=0,
+        concat_axis=0,
+        tiled=True,
+    )
     if padded != slices:
-        widen = ((0, 0), (0, padded - slices), (0, 0))
-        own_volume = jnp.pad(own_volume, ((0, 0), (0, (padded - slices) * slots), (0, 0)))
-        own_rays = jnp.pad(own_rays, widen)
-
-    theta, vol_list, own_volume, parts = lax.optimization_barrier(
-        (angles.reshape(-1), vol_list, own_volume, parts)
+        more = padded - slices
+        volumes = [jnp.pad(value, ((0, more * slots), (0, 0))) for value in volumes]
+        own_rays = jnp.pad(own_rays, ((0, 0), (0, more), (0, 0)))
+
+    theta, vol_list, volumes, parts = lax.optimization_barrier(
+        (angles.reshape(-1), vol_list, volumes, parts)
     )
-    sirt = Sirt(theta, vol_list, padded, slots, n_ray, step_size)
-    weight, (start, predicted, gain) = sirt.first(own_volume)
+    sirt = Sirt(ray_rank, theta, vol_list, padded, slots, n_ray, step_size)
+    weight, (half, start, predicted, gain) = sirt.first(volumes)
     own_rays, parts, start = lax.optimization_barrier((own_rays, parts, start))
-    parts = [
-        lax.ppermute(part, "slab", [(i, i ^ d) for i in range(n_slab)]) if d else part
-        for d, part in enumerate(parts)
-    ]
-    update, residual = sirt.second(weight, start, predicted, gain, own_rays)
-    sent = residual
+    parts = exchange(parts, "slab")
+    pieces = sirt.second(weight, half, start, predicted, gain, own_rays)
+    pieces, parts = lax.optimization_barrier((pieces, parts))
     if padded != slices:
-        sent = sent.reshape(n_ray, n_slab, padded, ACTIVE)[:, :, :slices]
-        sent = sent.reshape(n_ray, n_slab * slices, ACTIVE)
-    got = to_all(sent, "ray")
-    ready = [d for d in range(n_slab) if d != n_slab // 2]
-    update, *early = lax.optimization_barrier((update, *[parts[d] for d in ready]))
-    for d, part in zip(ready, early):
-        parts[d] = part
-    result = sirt.third(weight, update, residual, gain, own_volume)
-    result = result[:, : slices * slots]
-    result, got, parts = lax.optimization_barrier((result, got, parts))
-    reconstruction = to_all(result, "ray").reshape(volume.shape)
+        narrow = []
+        for piece in pieces:
+            lower = piece[padded * slots :].reshape(n_slab, padded, ACTIVE)[:, :slices]
+            lower = lower.reshape(n_slab * slices, ACTIVE)
+            narrow.append(jnp.concatenate([piece[: slices * slots], lower], axis=0))
+        pieces = narrow
+    pieces = exchange(pieces, "ray")
     sinogram = gather_parts(parts, rank)
-    residual = finish(got, sinogram)
+    if padded == slices:
+        reconstruction, residual = finish(pieces, sinogram, ray_rank, volume.shape)
+    else:
+        order = ray_rank ^ jnp.arange(n_ray, dtype=jnp.int32)
+        pieces = jnp.take(jnp.stack(pieces), order, axis=0)
+        reconstruction = pieces[:, : slices * slots].reshape(volume.shape)
+        lower = pieces[:, slices * slots :].reshape(n_ray, n_slab, slices, ACTIVE)
+        lower = jnp.transpose(lower, (1, 0, 2, 3)).reshape(n_slab, n_ray * slices, ACTIVE)
+        begin = (band - ACTIVE) // 2
+        residual = lax.dynamic_update_slice(sinogram, lower, (0, 0, begin))
     return (reconstruction, residual[:, None])
 
 

time: 116 us -> 116 us (level)
  Pallas kernels: 72.7 us -> 68 us
  starting transfers between devices: 24.9 us -> 28.2 us
    ppermute x3 -> x17, starting transfers between devices: 2.46 us -> 25.6 us  [exchange(): lax.ppermute(piece, axis, [(i, i ^ d) for i in range(count)])]
    all_to_all x4 -> x1, starting transfers between devices: 22.4 us -> 2.6 us  [local(): lax.all_to_all(active.reshape(devices, slices, ACTIVE), ('slab', 'ray'),...]
    ppermute x3 -> x17, waiting for transfers between devices: 0.01 us -> 13.8 us  [exchange(): lax.ppermute(piece, axis, [(i, i ^ d) for i in range(count)])]
    all_to_all x4 -> x1, waiting for transfers between devices: 13.7 us -> 0.01 us  [local(): lax.all_to_all(active.reshape(devices, slices, ACTIVE), ('slab', 'ray'),...]
    pallas_call x4, Pallas kernels: 60.5 us -> 55.3 us  [the longest x2 51.3 us: call(): pl.pallas_call(kernel, out_shape=[jax.ShapeDtypeStruct(*value) for value...]
    unnamed x27 -> x44, local copies, waits for them, and re-layouts: 1.63 us -> 2.79 us
  transfers between devices with their start and end apart: 7 -> 18, of which waited for: 2 -> 3; matrix products, arithmetic and copies ran while one was open for 1% -> 0% of each run, Pallas kernels for 63% -> 56%
where the time goes in v6:
time: 116 us; the launch traced here: 114 us
  Pallas kernels  68 us (59%)
  starting transfers between devices  28.2 us (24%)
  waiting for transfers between devices  13.8 us (12%)
  local copies, waits for them, and re-layouts  3.07 us (3%)
    pallas_call x2, Pallas kernels, call(): pl.pallas_call(kernel, out_shape=[jax.ShapeDtypeStruct(*value) for value...  51.3 us
    ppermute x17, starting transfers between devices, exchange(): lax.ppermute(piece, axis, [(i, i ^ d) for i in range(count)])  25.6 us
    ppermute x17, waiting for transfers between devices, exchange(): lax.ppermute(piece, axis, [(i, i ^ d) for i in range(count)])  13.8 us
    pallas_call x1, Pallas kernels, paganin(): pl.pallas_call(filter_kernel, out_shape=[jax.ShapeDtypeStruct((height //...  9.82 us
    pallas_call x1, Pallas kernels, gather_parts(): pl.pallas_call(gather_kernel, out_shape=jax.ShapeDtypeStruct((count,) + p...  2.86 us
    unnamed x44, local copies, waits for them, and re-layouts  2.79 us
    all_to_all x1, starting transfers between devices, local(): lax.all_to_all(active.reshape(devices, slices, ACTIVE), ('slab', 'ray'),...  2.6 us
  transfers between devices with their start and end apart: 18, of which 3 were waited for; matrix products, arithmetic and copies ran while one was open for 0% of the time, Pallas kernels for 56%

profile of v6, /device:TPU:0, one launch (start us, length us, event | category | flops | bytes accessed | tf_op | source)
XLA Modules:
  0.0 114.2 jit_solution(1009688643337970168)
XLA Ops:
  0.6 1.9 %split.1 = (f32[64,256]{1,0:T(8,128)}, f32[64,256]{1,0:T(8,128)}, f32[64,256]{1,0:T(8,128)}, f32[64,256]{1,0:T(8,128)}, f32[64,256]{1,0:T(8,128)}, /*index=5*/f3...) custom-call(s32[1]{0:T(128)} %bitcast.rank_ref, f32[8,64,256]{2,1,0:T(8,128)} %bitcast.9), custom_call_target="tpu_custom_call" | custom-call | bytes 1048576 | tf_op jit(solution)/shard_map/split/pallas_call | solution.py:752
  2.5 2.9 %collective-permute-start = (f32[64,256]{1,0:T(8,128)}, f32[64,256]{1,0:T(8,128)S(1)}, u32[]{:S(2)}, u32[]{:S(2)}) collective-permute-start(f32[64,256]{1,0:T(8,128)} %get-tuple-element.73), channel_id=1, source_target_pairs={{0,1},{1,0},{2,3},{3,2},{4,5},{5,4},{6,7},{7,6},{8,9},{9,8},{10,11... | collective-permute-start | bytes 196616 | tf_op jit(solution)/shard_map/ppermute | solution.py:767
  5.4 1.6 %collective-permute-start.1 = (f32[64,256]{1,0:T(8,128)}, f32[64,256]{1,0:T(8,128)S(1)}, u32[]{:S(2)}, u32[]{:S(2)}) collective-permute-start(f32[64,256]{1,0:T(8,128)} %get-tuple-element.74), channel_id=1, source_target_pairs={{0,2},{1,3},{2,0},{3,1},{4,6},{5,7},{6,4},{7,5},{8,10},{9,11},{10,... | collective-permute-start | bytes 196616 | tf_op jit(solution)/shard_map/ppermute | solution.py:767
  7.0 0.0 collective-permute-start.2
  7.0 3.0 %collective-permute-start.3 = (f32[64,256]{1,0:T(8,128)}, f32[64,256]{1,0:T(8,128)S(1)}, u32[]{:S(2)}, u32[]{:S(2)}) collective-permute-start(f32[64,256]{1,0:T(8,128)} %get-tuple-element.76), channel_id=1, source_target_pairs={{0,4},{1,5},{2,6},{3,7},{4,0},{5,1},{6,2},{7,3},{8,12},{9,13},{10,... | collective-permute-start | bytes 196616 | tf_op jit(solution)/shard_map/ppermute | solution.py:767
  10.0 1.3 %collective-permute-start.4 = (f32[64,256]{1,0:T(8,128)}, f32[64,256]{1,0:T(8,128)S(1)}, u32[]{:S(2)}, u32[]{:S(2)}) collective-permute-start(f32[64,256]{1,0:T(8,128)} %get-tuple-element.77), channel_id=1, source_target_pairs={{0,5},{1,4},{2,7},{3,6},{4,1},{5,0},{6,3},{7,2},{8,13},{9,12},{10,... | collective-permute-start | bytes 196616 | tf_op jit(solution)/shard_map/ppermute | solution.py:767
  11.3 0.0 copy-start.17
  11.3 0.0 copy-start.18
  11.3 0.0 copy-start.1
  11.3 0.0 copy-start.2
  11.3 0.0 copy-start.3
  11.4 0.0 copy-start.4
  11.4 9.8 %paganin.1 = (f32[64,2048]{1,0:T(8,128)}, f32[64,2048]{1,0:T(8,128)}, f32[64,2048]{1,0:T(8,128)}, f32[64,2048]{1,0:T(8,128)}, f32[256,256]{1,0:T(8,128)}) custom-call(s32[1]{0:T(128)} %bitcast.1.rank_ref, f32[256,2048]{1,0:T(8,128)} %bitcast.11, f32[264,256]{1,0:T(8,128)} %constant.78.clone.given_ref), custom_call_target="tpu_custom_call" | custom-call | flops 8589934592 | bytes 4194304 | tf_op jit(solution)/shard_map/paganin/pallas_call | solution.py:196
  21.2 0.1 reshape.65
  21.3 0.0 collective-permute-done.refs_1_
  21.3 3.7 %collective-permute-start.5 = (f32[64,256]{1,0:T(8,128)S(1)}, f32[64,256]{1,0:T(8,128)S(1)}, u32[]{:S(2)}, u32[]{:S(2)}) collective-permute-start(f32[64,256]{1,0:T(8,128)S(1)} %copy-done.20), channel_id=1, source_target_pairs={{0,6},{1,7},{2,4},{3,5},{4,2},{5,3},{6,0},{7,1},{8,14},{9,15},{10,... | collective-permute-start | bytes 196616 | tf_op jit(solution)/shard_map/ppermute | solution.py:767
  25.0 0.1 collective-permute-start.6
  25.0 0.1 sub.24
  25.1 0.0 collective-permute-done.2.refs_3_
  25.1 0.0 collective-permute-done.3.refs_4_
  25.1 0.0 collective-permute-done.4.refs_5_
  25.1 2.3 %collective-permute-done.5.refs_6_ = f32[64,256]{1,0:T(8,128)S(1)} collective-permute-done((f32[64,256]{1,0:T(8,128)S(1)}, f32[64,256]{1,0:T(8,128)S(1)}, u32[]{:S(2)}, u32[]{:S(2)}) %collective-permute-start.5) | collective-permute-done | bytes 65568 | tf_op jit(solution)/shard_map/ppermute | solution.py:767
  27.4 4.5 %collective-permute-done.6.refs_7_ = f32[64,256]{1,0:T(8,128)S(1)} collective-permute-done((f32[64,256]{1,0:T(8,128)S(1)}, f32[64,256]{1,0:T(8,128)S(1)}, u32[]{:S(2)}, u32[]{:S(2)}) %collective-permute-start.6) | collective-permute-done | bytes 65568 | tf_op jit(solution)/shard_map/ppermute | solution.py:767
  31.9 0.1 select_reduce_fusion.slot_ref
  32.1 2.6 %all-to-all-start = ((f32[32,8,256]{2,1,0:T(8,128)}), f32[32,8,256]{2,1,0:T(8,128)S(1)}, u32[]{:S(2)}, u32[]{:S(2)}) async-start(f32[32,8,256]{2,1,0:T(8,128)} %bitcast.10), calls=%async_computation | async-start | bytes 524288 | tf_op jit(solution)/shard_map/all_to_all | solution.py:788
  34.7 0.1 add_add_fusion
  34.8 0.1 add.64
  34.9 17.1 %first.1 = (bf16[32,768,512]{2,1,0:T(8,128)(2,1)}, f32[2,8,64,128]{3,2,1,0:T(8,128)S(1)}, f32[32,16,256]{2,1,0:T(8,128)}, f32[32,8,256]{2,1,0:T(8,128)S(1)}, f32[32,8,256]{2,1,0:T(8,128)S(1)}) custom-call(s32[1]{0:T(128)} %bitcast.rank_ref, s32[1024]{0:T(1024)S(1)} %get-tuple-element.146.offset_ref, f32[1024]{0:T(1024)S(1)} %fusion.1.place_ref, ...), custom_call_target="tpu_custom_call" | custom-call | flops 16000000000 | bytes 4194304 | tf_op jit(solution)/shard_map/first/pallas_call | solution.py:554
  52.0 0.0 copy-start.5
  52.0 0.8 copy-done.5
  52.8 0.1 collective-permute-start.7
  52.9 1.7 %collective-permute-start.8 = (f32[64,2048]{1,0:T(8,128)}, f32[64,2048]{1,0:T(8,128)S(1)}, u32[]{:S(2)}, u32[]{:S(2)}) collective-permute-start(f32[64,2048]{1,0:T(8,128)} %get-tuple-element.124), channel_id=1, source_target_pairs={{0,16},{8,24},{16,0},{24,8},{1,17},{9,25},{17,1},{25,9},{2,18},{10... | collective-permute-start | bytes 1572872 | tf_op jit(solution)/shard_map/ppermute | solution.py:767
  54.6 0.1 collective-permute-start.9
  54.7 34.2 %second.1 = (f32[96,256]{1,0:T(8,128)S(1)}, f32[96,256]{1,0:T(8,128)S(1)}, f32[96,256]{1,0:T(8,128)S(1)}, f32[96,256]{1,0:T(8,128)S(1)}, f32[96,256]{1,0:T(8,128...) custom-call(s32[1]{0:T(128)} %bitcast.rank_ref, ...), custom_call_target="tpu_custom_call" | custom-call | flops 30000001024 | bytes 4194304 | tf_op jit(solution)/shard_map/second/pallas_call | solution.py:554
  88.9 0.6 copy-done
  89.6 1.7 %collective-permute-start.10 = (f32[96,256]{1,0:T(8,128)S(1)}, f32[96,256]{1,0:T(8,128)S(1)}, u32[]{:S(2)}, u32[]{:S(2)}) collective-permute-start(f32[96,256]{1,0:T(8,128)S(1)} %get-tuple-element.127), channel_id=1, source_target_pairs={{0,1},{1,0},{2,3},{3,2},{4,5},{5,4},{6,7},{7,6},{8,9},{9,8},{10,11... | collective-permute-start | bytes 294920 | tf_op jit(solution)/shard_map/ppermute | solution.py:767
  91.3 1.5 %collective-permute-start.11 = (f32[96,256]{1,0:T(8,128)S(1)}, f32[96,256]{1,0:T(8,128)S(1)}, u32[]{:S(2)}, u32[]{:S(2)}) collective-permute-start(f32[96,256]{1,0:T(8,128)S(1)} %get-tuple-element.128), channel_id=1, source_target_pairs={{0,2},{1,3},{2,0},{3,1},{4,6},{5,7},{6,4},{7,5},{8,10},{9,11},{10,... | collective-permute-start | bytes 294920 | tf_op jit(solution)/shard_map/ppermute | solution.py:767
  92.8 0.4 collective-permute-start.12
  93.2 2.6 %collective-permute-start.13 = (f32[96,256]{1,0:T(8,128)S(1)}, f32[96,256]{1,0:T(8,128)S(1)}, u32[]{:S(2)}, u32[]{:S(2)}) collective-permute-start(f32[96,256]{1,0:T(8,128)S(1)} %get-tuple-element.130), channel_id=1, source_target_pairs={{0,4},{1,5},{2,6},{3,7},{4,0},{5,1},{6,2},{7,3},{8,12},{9,13},{10,... | collective-permute-start | bytes 294920 | tf_op jit(solution)/shard_map/ppermute | solution.py:767
  95.8 1.3 %collective-permute-start.14 = (f32[96,256]{1,0:T(8,128)S(1)}, f32[96,256]{1,0:T(8,128)S(1)}, u32[]{:S(2)}, u32[]{:S(2)}) collective-permute-start(f32[96,256]{1,0:T(8,128)S(1)} %get-tuple-element.131), channel_id=1, source_target_pairs={{0,5},{1,4},{2,7},{3,6},{4,1},{5,0},{6,3},{7,2},{8,13},{9,12},{10,... | collective-permute-start | bytes 294920 | tf_op jit(solution)/shard_map/ppermute | solution.py:767
  97.1 3.5 %collective-permute-start.15 = (f32[96,256]{1,0:T(8,128)S(1)}, f32[96,256]{1,0:T(8,128)S(1)}, u32[]{:S(2)}, u32[]{:S(2)}) collective-permute-start(f32[96,256]{1,0:T(8,128)S(1)} %get-tuple-element.132), channel_id=1, source_target_pairs={{0,6},{1,7},{2,4},{3,5},{4,2},{5,3},{6,0},{7,1},{8,14},{9,15},{10,... | collective-permute-start | bytes 294920 | tf_op jit(solution)/shard_map/ppermute | solution.py:767
  100.6 0.3 collective-permute-start.16
  100.9 2.9 %gather_parts.1.refs_8_ = f32[4,64,2048]{2,1,0:T(8,128)} custom-call(s32[1]{0:T(128)} %bitcast.1.rank_ref, f32[64,2048]{1,0:T(8,128)} %get-tuple-element.134.refs_0_, f32[64,2048]{1,0:T(8,128)} %copy-done.6, f32[64,2048]{1,0:T(8,128)} %copy-done.7, f32[64,2048]{1,0:T(8,128)} %copy-done.8), custom_call_target="tpu_custom_call" | custom-call | bytes 4194304 | tf_op jit(solution)/shard_map/gather_parts/pallas_call | solution.py:677
  103.8 7.0 %collective-permute-done.14.refs_5_ = f32[96,256]{1,0:T(8,128)S(1)} collective-permute-done((f32[96,256]{1,0:T(8,128)S(1)}, f32[96,256]{1,0:T(8,128)S(1)}, u32[]{:S(2)}, u32[]{:S(2)}) %collective-permute-start.14) | collective-permute-done | bytes 98336 | tf_op jit(solution)/shard_map/ppermute | solution.py:767
  110.8 0.6 copy-done.13
  111.4 0.0 copy-done.14
  111.4 0.6 copy-done.15
  112.1 2.2 %finish.1 = (f32[64,8,256]{2,1,0:T(8,128)}, f32[4,64,2048]{2,1,0:T(8,128)}) custom-call(s32[1]{0:T(128)} %bitcast.rank_ref, f32[96,256]{1,0:T(8,128)} %copy-done, f32[96,256]{1,0:T(8,128)} %copy-done.9, f32[96,256]{1,0:T(8,128)} %copy-done.10, f32[96,256]{1,0:T(8,128)} %copy-done.11, f32[96,256]{1,0:T(8,128)} %copy-done.12, ...), custom_call_target="tpu_custom_call", output_to_operand_aliasing={{1}: (9, {})} | custom-call | bytes 1572864 | tf_op jit(solution)/shard_map/finish/pallas_call | solution.py:721
  (48 shorter events, 0.2 us)
Async XLA Ops:
  2.5 18.8 %collective-permute-start = (f32[64,256]{1,0:T(8,128)}, f32[64,256]{1,0:T(8,128)S(1)}, u32[]{:S(2)}, u32[]{:S(2)}) collective-permute-start(f32[64,256]{1,0:T(8,128)} %get-tuple-element.73), channel_id=1, source_target_pairs={{0,1},{1,0},{2,3},{3,2},{4,5},{5,4},{6,7},{7,6},{8,9},{9,8},{10,11... | collective-permute-start | bytes 196616 | tf_op jit(solution)/shard_map/ppermute | solution.py:767
  5.4 19.5 %collective-permute-start.1 = (f32[64,256]{1,0:T(8,128)}, f32[64,256]{1,0:T(8,128)S(1)}, u32[]{:S(2)}, u32[]{:S(2)}) collective-permute-start(f32[64,256]{1,0:T(8,128)} %get-tuple-element.74), channel_id=1, source_target_pairs={{0,2},{1,3},{2,0},{3,1},{4,6},{5,7},{6,4},{7,5},{8,10},{9,11},{10,... | collective-permute-start | bytes 196616 | tf_op jit(solution)/shard_map/ppermute | solution.py:767
  7.0 18.1 %collective-permute-start.2 = (f32[64,256]{1,0:T(8,128)}, f32[64,256]{1,0:T(8,128)S(1)}, u32[]{:S(2)}, u32[]{:S(2)}) collective-permute-start(f32[64,256]{1,0:T(8,128)} %get-tuple-element.75), channel_id=1, source_target_pairs={{0,3},{1,2},{2,1},{3,0},{4,7},{5,6},{6,5},{7,4},{8,11},{9,10},{10,... | collective-permute-start | bytes 196616 | tf_op jit(solution)/shard_map/ppermute | solution.py:767
  7.0 18.1 %collective-permute-start.3 = (f32[64,256]{1,0:T(8,128)}, f32[64,256]{1,0:T(8,128)S(1)}, u32[]{:S(2)}, u32[]{:S(2)}) collective-permute-start(f32[64,256]{1,0:T(8,128)} %get-tuple-element.76), channel_id=1, source_target_pairs={{0,4},{1,5},{2,6},{3,7},{4,0},{5,1},{6,2},{7,3},{8,12},{9,13},{10,... | collective-permute-start | bytes 196616 | tf_op jit(solution)/shard_map/ppermute | solution.py:767
  10.0 15.1 %collective-permute-start.4 = (f32[64,256]{1,0:T(8,128)}, f32[64,256]{1,0:T(8,128)S(1)}, u32[]{:S(2)}, u32[]{:S(2)}) collective-permute-start(f32[64,256]{1,0:T(8,128)} %get-tuple-element.77), channel_id=1, source_target_pairs={{0,5},{1,4},{2,7},{3,6},{4,1},{5,0},{6,3},{7,2},{8,13},{9,12},{10,... | collective-permute-start | bytes 196616 | tf_op jit(solution)/shard_map/ppermute | solution.py:767
  11.3 9.9 %copy-start.16 = (f32[4,8]{1,0:T(4,128)S(1)}, f32[4,8]{1,0:T(4,128)}, u32[]{:S(2)}) copy-start(f32[4,8]{1,0:T(4,128)} %param.11) | copy-start | bytes 388
  11.3 10.0 %copy-start.20 = (f32[64,256]{1,0:T(8,128)S(1)}, f32[64,256]{1,0:T(8,128)}, u32[]{:S(2)}) copy-start(f32[64,256]{1,0:T(8,128)} %get-tuple-element.78) | copy-start | bytes 196612
  11.3 13.7 %copy-start.19 = (f32[64,256]{1,0:T(8,128)S(1)}, f32[64,256]{1,0:T(8,128)}, u32[]{:S(2)}) copy-start(f32[64,256]{1,0:T(8,128)} %get-tuple-element.79) | copy-start | bytes 196612
  11.3 20.6 %copy-start.21 = (s32[64]{0:T(128)S(1)}, s32[64]{0:T(128)}, u32[]{:S(2)}) copy-start(s32[64]{0:T(128)} %param.13) | copy-start | bytes 772
  11.3 23.4 %copy-start.17 = (f32[32]{0:T(128)S(1)}, f32[32]{0:T(128)}, u32[]{:S(2)}) copy-start(f32[32]{0:T(128)} %constant.86) | copy-start | bytes 388
  11.3 23.4 %copy-start.18 = (f32[32]{0:T(128)S(1)}, f32[32]{0:T(128)}, u32[]{:S(2)}) copy-start(f32[32]{0:T(128)} %constant.85) | copy-start | bytes 388
  11.3 23.6 %copy-start.1 = (f32[64,256]{1,0:T(8,128)S(1)}, f32[64,256]{1,0:T(8,128)}, u32[]{:S(2)}) copy-start(f32[64,256]{1,0:T(8,128)} %get-tuple-element.94.refs_0_) | copy-start | bytes 196612
  11.3 23.6 %copy-start.2 = (bf16[256,256]{1,0:T(8,128)(2,1)S(1)}, bf16[256,256]{1,0:T(8,128)(2,1)}, u32[]{:S(2)}) copy-start(bf16[256,256]{1,0:T(8,128)(2,1)} %constant.81.clone.flip_ref) | copy-start | bytes 393220
  11.3 23.6 %copy-start.3 = (f32[8,256]{1,0:T(8,128)S(1)}, f32[8,256]{1,0:T(8,128)}, u32[]{:S(2)}) copy-start(f32[8,256]{1,0:T(8,128)} %constant.83.clone.shift_y_ref) | copy-start | bytes 24580
  11.4 23.6 %copy-start.4 = (f32[8,256]{1,0:T(8,128)S(1)}, f32[8,256]{1,0:T(8,128)}, u32[]{:S(2)}) copy-start(f32[8,256]{1,0:T(8,128)} %constant.82.clone.shift_x_ref) | copy-start | bytes 24580
  21.3 6.1 %collective-permute-start.5 = (f32[64,256]{1,0:T(8,128)S(1)}, f32[64,256]{1,0:T(8,128)S(1)}, u32[]{:S(2)}, u32[]{:S(2)}) collective-permute-start(f32[64,256]{1,0:T(8,128)S(1)} %copy-done.20), channel_id=1, source_target_pairs={{0,6},{1,7},{2,4},{3,5},{4,2},{5,3},{6,0},{7,1},{8,14},{9,15},{10,... | collective-permute-start | bytes 196616 | tf_op jit(solution)/shard_map/ppermute | solution.py:767
  25.0 7.0 %collective-permute-start.6 = (f32[64,256]{1,0:T(8,128)S(1)}, f32[64,256]{1,0:T(8,128)S(1)}, u32[]{:S(2)}, u32[]{:S(2)}) collective-permute-start(f32[64,256]{1,0:T(8,128)S(1)} %copy-done.19), channel_id=1, source_target_pairs={{0,7},{1,6},{2,5},{3,4},{4,3},{5,2},{6,1},{7,0},{8,15},{9,14},{10,... | collective-permute-start | bytes 196616 | tf_op jit(solution)/shard_map/ppermute | solution.py:767
  32.1 20.7 %all-to-all-start = ((f32[32,8,256]{2,1,0:T(8,128)}), f32[32,8,256]{2,1,0:T(8,128)S(1)}, u32[]{:S(2)}, u32[]{:S(2)}) async-start(f32[32,8,256]{2,1,0:T(8,128)} %bitcast.10), calls=%async_computation | async-start | bytes 524288 | tf_op jit(solution)/shard_map/all_to_all | solution.py:788
  52.0 0.8 copy-start.5
  52.8 36.8 %collective-permute-start.7 = (f32[64,2048]{1,0:T(8,128)}, f32[64,2048]{1,0:T(8,128)S(1)}, u32[]{:S(2)}, u32[]{:S(2)}) collective-permute-start(f32[64,2048]{1,0:T(8,128)} %get-tuple-element.123), channel_id=1, source_target_pairs={{0,8},{8,0},{16,24},{24,16},{1,9},{9,1},{17,25},{25,17},{2,10},{10... | collective-permute-start | bytes 1572872 | tf_op jit(solution)/shard_map/ppermute | solution.py:767
  52.9 36.7 %collective-permute-start.8 = (f32[64,2048]{1,0:T(8,128)}, f32[64,2048]{1,0:T(8,128)S(1)}, u32[]{:S(2)}, u32[]{:S(2)}) collective-permute-start(f32[64,2048]{1,0:T(8,128)} %get-tuple-element.124), channel_id=1, source_target_pairs={{0,16},{8,24},{16,0},{24,8},{1,17},{9,25},{17,1},{25,9},{2,18},{10... | collective-permute-start | bytes 1572872 | tf_op jit(solution)/shard_map/ppermute | solution.py:767
  54.6 35.0 %collective-permute-start.9 = (f32[64,2048]{1,0:T(8,128)}, f32[64,2048]{1,0:T(8,128)S(1)}, u32[]{:S(2)}, u32[]{:S(2)}) collective-permute-start(f32[64,2048]{1,0:T(8,128)} %get-tuple-element.125), channel_id=1, source_target_pairs={{0,24},{8,16},{16,8},{24,0},{1,25},{9,17},{17,9},{25,1},{2,26},{10... | collective-permute-start | bytes 1572872 | tf_op jit(solution)/shard_map/ppermute | solution.py:767
  88.9 0.6 copy-start
  89.6 11.3 %copy-start.6 = (f32[64,2048]{1,0:T(8,128)}, f32[64,2048]{1,0:T(8,128)S(1)}, u32[]{:S(2)}) copy-start(f32[64,2048]{1,0:T(8,128)S(1)} %collective-permute-done.7.refs_1_) | copy-start | bytes 1572868
  89.6 11.3 %copy-start.7 = (f32[64,2048]{1,0:T(8,128)}, f32[64,2048]{1,0:T(8,128)S(1)}, u32[]{:S(2)}) copy-start(f32[64,2048]{1,0:T(8,128)S(1)} %collective-permute-done.8.refs_2_) | copy-start | bytes 1572868
  89.6 11.3 %copy-start.8 = (f32[64,2048]{1,0:T(8,128)}, f32[64,2048]{1,0:T(8,128)S(1)}, u32[]{:S(2)}) copy-start(f32[64,2048]{1,0:T(8,128)S(1)} %collective-permute-done.9.refs_3_) | copy-start | bytes 1572868
  89.6 7.5 %collective-permute-start.10 = (f32[96,256]{1,0:T(8,128)S(1)}, f32[96,256]{1,0:T(8,128)S(1)}, u32[]{:S(2)}, u32[]{:S(2)}) collective-permute-start(f32[96,256]{1,0:T(8,128)S(1)} %get-tuple-element.127), channel_id=1, source_target_pairs={{0,1},{1,0},{2,3},{3,2},{4,5},{5,4},{6,7},{7,6},{8,9},{9,8},{10,11... | collective-permute-start | bytes 294920 | tf_op jit(solution)/shard_map/ppermute | solution.py:767
  91.3 9.3 %collective-permute-start.11 = (f32[96,256]{1,0:T(8,128)S(1)}, f32[96,256]{1,0:T(8,128)S(1)}, u32[]{:S(2)}, u32[]{:S(2)}) collective-permute-start(f32[96,256]{1,0:T(8,128)S(1)} %get-tuple-element.128), channel_id=1, source_target_pairs={{0,2},{1,3},{2,0},{3,1},{4,6},{5,7},{6,4},{7,5},{8,10},{9,11},{10,... | collective-permute-start | bytes 294920 | tf_op jit(solution)/shard_map/ppermute | solution.py:767
  92.8 11.0 %collective-permute-start.12 = (f32[96,256]{1,0:T(8,128)S(1)}, f32[96,256]{1,0:T(8,128)S(1)}, u32[]{:S(2)}, u32[]{:S(2)}) collective-permute-start(f32[96,256]{1,0:T(8,128)S(1)} %get-tuple-element.129), channel_id=1, source_target_pairs={{0,3},{1,2},{2,1},{3,0},{4,7},{5,6},{6,5},{7,4},{8,11},{9,10},{10,... | collective-permute-start | bytes 294920 | tf_op jit(solution)/shard_map/ppermute | solution.py:767
  93.2 10.6 %collective-permute-start.13 = (f32[96,256]{1,0:T(8,128)S(1)}, f32[96,256]{1,0:T(8,128)S(1)}, u32[]{:S(2)}, u32[]{:S(2)}) collective-permute-start(f32[96,256]{1,0:T(8,128)S(1)} %get-tuple-element.130), channel_id=1, source_target_pairs={{0,4},{1,5},{2,6},{3,7},{4,0},{5,1},{6,2},{7,3},{8,12},{9,13},{10,... | collective-permute-start | bytes 294920 | tf_op jit(solution)/shard_map/ppermute | solution.py:767
  95.8 15.0 %collective-permute-start.14 = (f32[96,256]{1,0:T(8,128)S(1)}, f32[96,256]{1,0:T(8,128)S(1)}, u32[]{:S(2)}, u32[]{:S(2)}) collective-permute-start(f32[96,256]{1,0:T(8,128)S(1)} %get-tuple-element.131), channel_id=1, source_target_pairs={{0,5},{1,4},{2,7},{3,6},{4,1},{5,0},{6,3},{7,2},{8,13},{9,12},{10,... | collective-permute-start | bytes 294920 | tf_op jit(solution)/shard_map/ppermute | solution.py:767
  97.1 6.6 %copy-start.9 = (f32[96,256]{1,0:T(8,128)}, f32[96,256]{1,0:T(8,128)S(1)}, u32[]{:S(2)}) copy-start(f32[96,256]{1,0:T(8,128)S(1)} %collective-permute-done.10.refs_1_) | copy-start | bytes 294916
  97.1 13.6 %collective-permute-start.15 = (f32[96,256]{1,0:T(8,128)S(1)}, f32[96,256]{1,0:T(8,128)S(1)}, u32[]{:S(2)}, u32[]{:S(2)}) collective-permute-start(f32[96,256]{1,0:T(8,128)S(1)} %get-tuple-element.132), channel_id=1, source_target_pairs={{0,6},{1,7},{2,4},{3,5},{4,2},{5,3},{6,0},{7,1},{8,14},{9,15},{10,... | collective-permute-start | bytes 294920 | tf_op jit(solution)/shard_map/ppermute | solution.py:767
  100.6 3.2 %copy-start.10 = (f32[96,256]{1,0:T(8,128)}, f32[96,256]{1,0:T(8,128)S(1)}, u32[]{:S(2)}) copy-start(f32[96,256]{1,0:T(8,128)S(1)} %collective-permute-done.11.refs_2_) | copy-start | bytes 294916
  100.6 10.2 %collective-permute-start.16 = (f32[96,256]{1,0:T(8,128)S(1)}, f32[96,256]{1,0:T(8,128)S(1)}, u32[]{:S(2)}, u32[]{:S(2)}) collective-permute-start(f32[96,256]{1,0:T(8,128)S(1)} %get-tuple-element.133), channel_id=1, source_target_pairs={{0,7},{1,6},{2,5},{3,4},{4,3},{5,2},{6,1},{7,0},{8,15},{9,14},{10,... | collective-permute-start | bytes 294920 | tf_op jit(solution)/shard_map/ppermute | solution.py:767
  103.8 7.0 %copy-start.11 = (f32[96,256]{1,0:T(8,128)}, f32[96,256]{1,0:T(8,128)S(1)}, u32[]{:S(2)}) copy-start(f32[96,256]{1,0:T(8,128)S(1)} %collective-permute-done.12.refs_3_) | copy-start | bytes 294916
  103.8 7.0 %copy-start.12 = (f32[96,256]{1,0:T(8,128)}, f32[96,256]{1,0:T(8,128)S(1)}, u32[]{:S(2)}) copy-start(f32[96,256]{1,0:T(8,128)S(1)} %collective-permute-done.13.refs_4_) | copy-start | bytes 294916
  110.8 0.7 copy-start.13
  110.8 0.7 copy-start.14
  111.4 0.6 copy-start.15

commit v7 on v6

v7 whole, which is shorter than its diff:
```python
import functools
import math

import jax
import jax.numpy as jnp
import ml_dtypes
import numpy as np
from jax import lax
from jax.experimental import pallas as pl
from jax.experimental.pallas import tpu as pltpu
from jax.sharding import PartitionSpec as P

BAND = 2048
PGRID = 8
ROI = 128
SIDE = 16
VOX = SIDE * SIDE
WIN = 24
ACTIVE = 256
LANES = 128
ROWS = 8
SPLIT = 64
GROUP = 8
CYCLE = 4

paganin_strength = 10.0
relax = 1.8
row_floor = 0.25

bf16 = jnp.bfloat16
f32 = jnp.float32


def halves(values):
    high = values.astype(bf16)
    low = (values - high.astype(f32)).astype(bf16)
    return high, low


def thirds(values):
    high = values.astype(bf16)
    rest = values - high.astype(f32)
    middle = rest.astype(bf16)
    low = (rest - middle.astype(f32)).astype(bf16)
    return high, middle, low


def dot(left, right):
    return jnp.dot(left, right, preferred_element_type=f32)


def repeat(count, body, unroll):
    unroll = math.gcd(count, unroll)

    def several(index, carry):
        for step in range(unroll):
            body(index * unroll + step)
        return carry

    lax.fori_loop(0, count // unroll, several, 0)


def filter_tables(height):
    index = np.arange(height)
    phase = 2.0 * np.pi * (np.outer(index, index) % height) / height
    cas = (np.cos(phase) + np.sin(phase)) / math.sqrt(height)
    row_freq = 2.0 - 2.0 * np.cos(2.0 * np.pi * index / height)
    middle = (1.0 + paganin_strength * row_freq) / paganin_strength + 2.0
    rho = (middle - np.sqrt(middle * middle - 4.0)) / 2.0
    return np.concatenate([cas, np.repeat(rho[None, :], ROWS, axis=0)], axis=0).astype(np.float32)


def chunk_carry(ends, power, forward):
    shift = 1
    for _ in range(3):
        ends = ends + power * pltpu.roll(ends, shift if forward else ROWS - shift, 0)
        power = power * power
        shift *= 2
    return pltpu.roll(ends, 1 if forward else ROWS - 1, 0) / (1.0 - power)


def filter_kernel(rank_ref, source_ref, given_ref, *refs):
    *part_refs, active_ref, image_ref, table_ref, out_ref, spec_ref, up_ref, down_ref = refs[:-2]
    sems, out_sems = refs[-2:]
    height, width = image_ref.shape
    rank = rank_ref[0]
    share = height // len(part_refs)
    length = width // ROWS
    blocks = height // LANES
    unroll = 8
    copies = []
    for c in range(ROWS):
        columns = slice(c * length, (c + 1) * length)
        copies.append(
            pltpu.make_async_copy(
                source_ref.at[:, columns], image_ref.at[:, columns], sems.at[c]
            )
        )
    given = pltpu.make_async_copy(given_ref, table_ref, sems.at[ROWS])
    given.start()
    for copy in copies:
        copy.start()
    given.wait()
    cas_high, cas_low = halves(table_ref[0:height, :])
    rho_all = table_ref[height : height + ROWS, :]
    rhos = [rho_all[:, b * LANES : (b + 1) * LANES] for b in range(blocks)]
    zeros = [jnp.zeros((ROWS, LANES), f32)] * blocks

    def transform(values):
        high, low = halves(values)
        return dot(high, cas_high) + dot(low, cas_high) + dot(high, cas_low)

    for c in range(ROWS):
        copies[c].wait()
        image = 1.0 - image_ref[:, c * length : (c + 1) * length]
        spectrum = transform(jnp.transpose(image))
        for b in range(blocks):
            spec_ref[b, pl.ds(c, length, stride=ROWS), :] = spectrum[
                :, b * LANES : (b + 1) * LANES
            ]

    def rows(position):
        return pl.ds(pl.multiple_of(position * ROWS, ROWS), ROWS)

    def advance(position, ups, downs):
        ups = [spec_ref[b, rows(position), :] + rhos[b] * ups[b] for b in range(blocks)]
        back = length - 1 - position
        downs = [spec_ref[b, rows(back), :] + rhos[b] * downs[b] for b in range(blocks)]
        return ups, downs

    def sweep(index, carry):
        ups, downs = carry
        for step in range(unroll):
            ups, downs = advance(index * unroll + step, ups, downs)
        return ups, downs

    ups, downs = lax.fori_loop(0, length // unroll, sweep, (zeros, zeros))
    powers = list(rhos)
    for _ in range(int(math.log2(length))):
        powers = [power * power for power in powers]
    ups = [chunk_carry(ups[b], powers[b], True) for b in range(blocks)]
    downs = [chunk_carry(downs[b], powers[b], False) for b in range(blocks)]
    scales = [rho / (paganin_strength * (1.0 - rho * rho)) for rho in rhos]

    def outer(index, carry):
        ups, downs = carry
        for step in range(unroll):
            position = index * unroll + step
            ups, downs = advance(position, ups, downs)
            for b in range(blocks):
                up_ref[b, rows(position), :] = ups[b]
                down_ref[b, rows(position), :] = downs[b]
        return ups, downs

    def inner(index, carry):
        ups, downs = carry
        for step in range(unroll):
            position = index * unroll + step
            back = length - 1 - position
            ups, downs = advance(position, ups, downs)
            for b in range(blocks):
                here = ups[b] + down_ref[b, rows(back), :] - spec_ref[b, rows(position), :]
                there = downs[b] + up_ref[b, rows(back), :] - spec_ref[b, rows(back), :]
                up_ref[b, rows(position), :] = here * scales[b]
                up_ref[b, rows(back), :] = there * scales[b]
        return ups, downs

    half = length // 2 // unroll
    carry = lax.fori_loop(0, half, outer, (ups, downs))
    lax.fori_loop(half, 2 * half, inner, carry)

    offset = (width - ACTIVE) // 2
    sent = []
    for c in range(ROWS):
        spectrum = jnp.concatenate(
            [up_ref[b, pl.ds(c, length, stride=ROWS), :] for b in range(blocks)], axis=1
        )
        filtered = 1.0 - jnp.transpose(transform(spectrum))
        columns = slice(c * length, (c + 1) * length)
        out_ref[:, columns] = -jnp.log(filtered)
        for d, part_ref in enumerate(part_refs):
            rows = pl.ds(pl.multiple_of((rank ^ d) * share, share), share)
            sent.append(
                pltpu.make_async_copy(
                    out_ref.at[rows, columns], part_ref.at[:, columns], out_sems.at[c, d]
                )
            )
            sent[-1].start()
    active_ref[...] = out_ref[:, offset : offset + ACTIVE]
    for copy in sent:
        copy.wait()


def paganin(image, rank, parts):
    height, width = image.shape
    blocks = height // LANES
    return pl.pallas_call(
        filter_kernel,
        out_shape=[jax.ShapeDtypeStruct((height // parts, width), f32)] * parts
        + [jax.ShapeDtypeStruct((height, ACTIVE), f32)],
        in_specs=[pl.BlockSpec(memory_space=pltpu.SMEM)]
        + [pl.BlockSpec(memory_space=pltpu.HBM)] * 2,
        out_specs=[pl.BlockSpec(memory_space=pltpu.HBM)] * parts
        + [pl.BlockSpec(memory_space=pltpu.VMEM)],
        scratch_shapes=[
            pltpu.VMEM((height, width), f32),
            pltpu.VMEM((height + ROWS, height), f32),
            pltpu.VMEM((height, width), f32),
            pltpu.VMEM((blocks, width, LANES), f32),
            pltpu.VMEM((blocks, width, LANES), f32),
            pltpu.VMEM((blocks, width // 2, LANES), f32),
            pltpu.SemaphoreType.DMA((ROWS + 1,)),
            pltpu.SemaphoreType.DMA((ROWS, parts)),
        ],
        compiler_params=pltpu.CompilerParams(vmem_limit_bytes=58 * 2**20),
        cost_estimate=pl.CostEstimate(
            flops=64 * height * height * width,
            bytes_accessed=8 * height * width,
            transcendentals=height * width,
        ),
        name="paganin",
    )(rank.reshape(1), image, jnp.asarray(filter_tables(height)))


def reversed_exact(values, flip):
    return sum(dot(part, flip) for part in thirds(values))


class Weights:
    def __init__(self, along_ref, place_ref, angles, chunk):
        self.along_ref = along_ref
        self.place_ref = place_ref
        self.angles = angles
        self.chunk = chunk
        self.ray = lax.broadcasted_iota(jnp.int32, (ROWS, VOX), 0).astype(f32)

    def prepare(self, shift_x_ref, shift_y_ref, cos_ref, sin_ref):
        def along_angle(t):
            self.along_ref[t] = shift_x_ref[...] * cos_ref[t] + shift_y_ref[...] * sin_ref[t]

        repeat(self.angles, along_angle, 8)

    def make(self, q, c, ref):
        for two in range(self.chunk // 2):
            pieces = []
            for t in (2 * two, 2 * two + 1):
                angle = c * self.chunk + t
                along = self.along_ref[angle] + self.place_ref[q * self.angles + angle]
                base = self.ray - along
                for group in range(WIN // ROWS):
                    distance = base + float(group * ROWS)
                    pieces.append(jnp.maximum(0.0, 1.0 - jnp.abs(distance)))
            high, low = halves(jnp.concatenate(pieces, axis=0))
            ref[2 * two * WIN : (2 * two + 2) * WIN, 0:VOX] = high
            ref[2 * two * WIN : (2 * two + 2) * WIN, VOX : 2 * VOX] = low


def ray_operand(values, sums_too):
    high, low = halves(values)
    both = values.shape[0]
    rows = [
        jnp.concatenate([high, high], axis=1),
        jnp.concatenate([low, jnp.zeros_like(low)], axis=1),
    ]
    if sums_too:
        rows.append(jnp.ones((both, 2 * VOX), bf16))
    rows.append(jnp.zeros((LANES - len(rows) * both, 2 * VOX), bf16))
    return jnp.concatenate(rows, axis=0)


def project_pair(held, operand, q, c, sizes, offset_ref, acc_ref):
    angles, chunk = sizes[:2]
    sums = lax.dot_general(
        held, operand, (((1,), (1,)), ((), ())), preferred_element_type=f32
    )
    for begin in range(0, chunk, GROUP):
        places = []
        for t in range(begin, min(begin + GROUP, chunk)):
            angle = c * chunk + t
            rows = pl.ds(offset_ref[q * angles + angle], WIN)
            values = acc_ref[angle, rows, :] + sums[t * WIN : (t + 1) * WIN, :]
            places.append((angle, rows, values))
        for angle, rows, values in places:
            acc_ref[angle, rows, :] = values


def spread_rays(acc_ref, direct_ref, mirror_ref, total_ref, slices):
    both = 2 * slices

    def spread(t):
        rows = jnp.transpose(acc_ref[t]) * (1.0 / ROI)
        direct_ref[t] = rows[0:slices] + rows[both : both + slices]
        mirror_ref[t] = rows[slices:both] + rows[both + slices : 2 * both]
        if total_ref is not None:
            total_ref[t] = rows[2 * both : 2 * both + slices]

    repeat(acc_ref.shape[0], spread, 8)


def turn_rays(values, flip):
    shape = values.shape
    return reversed_exact(values.reshape(-1, shape[-1]), flip).reshape(shape)


def fill_windows(weighted, flip, window_ref):
    angles, slices, _ = weighted.shape
    high, low = halves(weighted.reshape(angles * slices, ACTIVE))
    mirrored = (dot(high, flip) + dot(low, flip)).reshape(weighted.shape)
    lane = lax.broadcasted_iota(jnp.int32, (angles, slices, LANES), 2)
    for part, source in enumerate((weighted, mirrored)):
        rows = slice(part * slices, (part + 1) * slices)
        left = source[:, :, 0:LANES]
        right = source[:, :, LANES : 2 * LANES]
        window_ref[:, 0, rows, :] = left
        window_ref[:, 2, rows, :] = right
        mixed = jnp.where(lane >= SPLIT, left, right)
        window_ref[:, 1, rows, :] = pltpu.roll(mixed, SPLIT, 2)


def update_pair(held, q, c, sizes, window_ref, tile_ref, turn_ref):
    angles, chunk = sizes[:2]
    both = window_ref.shape[2]
    lane_rows = lax.broadcasted_iota(jnp.int32, (both, LANES), 1)
    tiles = [None] * (-(-chunk * WIN // LANES))
    for t in range(chunk):
        index = q * angles + c * chunk + t
        piece = pltpu.roll(window_ref[c * chunk + t, tile_ref[index]], turn_ref[index], 1)
        begin = t * WIN
        for place in range(begin // LANES, (begin + WIN - 1) // LANES + 1):
            if tiles[place] is None:
                tiles[place] = piece
            else:
                tiles[place] = jnp.where(
                    lane_rows >= begin - place * LANES, piece, tiles[place]
                )
    high, low = halves(jnp.concatenate(tiles, axis=1))
    sums = dot(jnp.concatenate([high, low], axis=0), held)
    return sums[0:both, 0:VOX] + sums[both:, 0:VOX] + sums[0:both, VOX:]


def first_kernel(
    sizes,
    offset_ref,
    place_ref,
    slot_ref,
    cos_ref,
    sin_ref,
    vol_ref,
    flip_ref,
    shift_x_ref,
    shift_y_ref,
    start_ref,
    predicted_ref,
    gain_ref,
    even_ref,
    odd_ref,
    acc_ref,
    along_ref,
    half_ref,
    mirror_ref,
):
    angles, chunk, slots = sizes
    patches = slot_ref.shape[0]
    pairs, both, _ = start_ref.shape
    slices = both // 2
    flip = flip_ref[...]

    def slot_values(patch):
        slot = slot_ref[patch]
        rows = pl.ds(slot % slots, slices, stride=slots)
        return jnp.concatenate(
            [half_ref[part, slot // slots, rows, :] for part in range(2)], axis=1
        )

    for part in range(2):
        half_ref[part] = vol_ref[:, :, part * LANES : (part + 1) * LANES]

    def order(q):
        start_ref[q, 0:slices, :] = slot_values(q)
        mirror_ref[q] = slot_values(patches - 1 - q)

    repeat(pairs, order, 8)
    start_ref[:, slices:both, :] = turn_rays(mirror_ref[0:pairs], flip)
    weights = Weights(along_ref, place_ref, angles, chunk)
    weights.prepare(shift_x_ref, shift_y_ref, cos_ref, sin_ref)
    acc_ref[...] = jnp.zeros(acc_ref.shape, f32)

    def two(index, carry):
        q = 2 * index
        for c in range(angles // chunk):
            weights.make(q, c, even_ref)
            operand = ray_operand(start_ref[q], True)
            project_pair(even_ref[...], operand, q, c, sizes, offset_ref, acc_ref)
            weights.make(q + 1, c, odd_ref)
            operand = ray_operand(start_ref[q + 1], True)
            project_pair(odd_ref[...], operand, q + 1, c, sizes, offset_ref, acc_ref)
        return carry

    lax.fori_loop(0, pairs // 2, two, 0)
    spread_rays(acc_ref, predicted_ref, mirror_ref, gain_ref, slices)
    predicted_ref[...] = predicted_ref[...] + turn_rays(mirror_ref[0:angles], flip)
    direct = gain_ref[...]
    gain_ref[...] = 1.0 / jnp.maximum(direct + turn_rays(direct, flip), row_floor)


def second_kernel(
    sizes,
    step_size,
    offset_ref,
    place_ref,
    tile_ref,
    turn_ref,
    slot_ref,
    cos_ref,
    sin_ref,
    vol_ref,
    start_ref,
    predicted_ref,
    gain_ref,
    sino_ref,
    flip_ref,
    shift_x_ref,
    shift_y_ref,
    out_ref,
    *refs,
):
    angles, chunk, slots = sizes
    held_refs = refs[:CYCLE]
    acc_ref, along_ref, direct_ref, mirror_ref, window_ref, update_ref, half_ref = refs[CYCLE:]
    patches = slot_ref.shape[0]
    pairs, both, _ = start_ref.shape
    slices = both // 2
    rays = out_ref.shape[0]
    flip = flip_ref[...]
    weights = Weights(along_ref, place_ref, angles, chunk)
    weights.prepare(shift_x_ref, shift_y_ref, cos_ref, sin_ref)
    chunks = angles // chunk
    windows = (sizes, window_ref, tile_ref, turn_ref)
    fill_windows(
        (sino_ref[...] - predicted_ref[...]) * gain_ref[...] * (1.0 / ROI), flip, window_ref
    )
    acc_ref[...] = jnp.zeros(acc_ref.shape, f32)

    def advance(q, held):
        total = update_pair(held, q, 0, *windows)
        update_ref[q] = total
        return start_ref[q] + step_size * total

    def forward(values, q, held):
        project_pair(held, ray_operand(values, False), q, 0, sizes, offset_ref, acc_ref)

    def cycle(index, values):
        for step in range(CYCLE):
            q = index * CYCLE + step
            after = (step + 1) % CYCLE
            before = (step - 1) % CYCLE
            later = index + (step + 1) // CYCLE
            earlier = index if step else jnp.maximum(index - 1, 0)
            weights.make(jnp.minimum(q + 1, pairs - 1), 0, held_refs[after].at[later])
            new_values = advance(q, held_refs[step][index])
            forward(values, jnp.maximum(q - 1, 0), held_refs[before][earlier])
            values = new_values
        return values

    def all_chunks(q, body):
        for c in range(chunks):
            weights.make(q, c, held_refs[0].at[0])
            body(c, held_refs[0][0])

    def plain_update(q, carry):
        update_ref[q] = jnp.zeros(update_ref.shape[1:], f32)

        def add(c, held):
            update_ref[q] = update_ref[q] + update_pair(held, q, c, *windows)

        all_chunks(q, add)
        return carry

    def plain_forward(q, carry):
        operand = ray_operand(start_ref[q] + step_size * update_ref[q], False)
        all_chunks(
            q,
            lambda c, held: project_pair(held, operand, q, c, sizes, offset_ref, acc_ref),
        )
        return carry

    if chunks == 1:
        held_refs[CYCLE - 1][0] = jnp.zeros(held_refs[CYCLE - 1].shape[1:], bf16)
        weights.make(0, 0, held_refs[0].at[0])
        values = lax.fori_loop(0, pairs // CYCLE, cycle, jnp.zeros((both, VOX), f32))
        forward(values, pairs - 1, held_refs[CYCLE - 1][pairs // CYCLE - 1])
    else:
        lax.fori_loop(0, pairs, plain_update, 0)
        lax.fori_loop(0, pairs, plain_forward, 0)

    spread_rays(acc_ref, direct_ref, mirror_ref, None, slices)
    turned = turn_rays(mirror_ref[0:angles], flip)
    direct_ref[...] = sino_ref[...] - direct_ref[...] - turned
    fill_windows(direct_ref[...] * gain_ref[...] * (1.0 / ROI), flip, window_ref)

    def last_cycle(index, carry):
        for step in range(CYCLE):
            q = index * CYCLE + step
            total = update_pair(held_refs[step][index], q, 0, *windows)
            update_ref[q] = (update_ref[q] + total) * step_size
        return carry

    def plain_last(q, carry):
        def add(c, held):
            update_ref[q] = update_ref[q] + update_pair(held, q, c, *windows)

        all_chunks(q, add)
        update_ref[q] = update_ref[q] * step_size
        return carry

    if chunks == 1:
        lax.fori_loop(0, pairs // CYCLE, last_cycle, 0)
    else:
        lax.fori_loop(0, pairs, plain_last, 0)

    mirror_ref[0:pairs] = turn_rays(update_ref[:, slices:both, :], flip)
    for part in range(2):
        half_ref[part] = vol_ref[:, :, part * LANES : (part + 1) * LANES]

    def finish(q):
        for patch, update in (
            (q, update_ref[q, 0:slices, :]),
            (patches - 1 - q, mirror_ref[q]),
        ):
            slot = slot_ref[patch]
            rows = pl.ds(slot % slots, slices, stride=slots)
            for part in range(2):
                half_ref[part, slot // slots, rows, :] = (
                    half_ref[part, slot // slots, rows, :]
                    + update[:, part * LANES : (part + 1) * LANES]
                )

    repeat(pairs, finish, 8)
    lead = slices * slots
    for part in range(2):
        out_ref[:, 0:lead, part * LANES : (part + 1) * LANES] = half_ref[part]
    for t in range(angles):
        begin = lead + t // rays * slices
        out_ref[t % rays, begin : begin + slices, :] = direct_ref[t]


def call(kernel, name, inputs, outputs, scratch, micros):
    smem = pl.BlockSpec(memory_space=pltpu.SMEM)
    vmem = pl.BlockSpec(memory_space=pltpu.VMEM)
    return pl.pallas_call(
        kernel,
        out_shape=[jax.ShapeDtypeStruct(*value) for value in outputs],
        in_specs=[smem if value.ndim == 1 else vmem for value in inputs],
        out_specs=[vmem] * len(outputs),
        scratch_shapes=[pltpu.VMEM(*value) for value in scratch],
        compiler_params=pltpu.CompilerParams(vmem_limit_bytes=52 * 2**20),
        cost_estimate=pl.CostEstimate(
            flops=int(micros * 1e9), bytes_accessed=4 * 2**20, transcendentals=0
        ),
        name=name,
    )(*inputs)


class Sirt:
    def __init__(self, theta, vol_list, slices, slots, rays, step_size):
        angles = theta.shape[0]
        patches = vol_list.shape[0]
        pairs = patches // 2
        both = 2 * slices
        chunk = math.gcd(angles, 32)
        self.sizes = (angles, chunk, slots)
        self.step_size = step_size
        self.rays = rays
        self.patches = patches
        centre = (ROI - 1) / 2.0
        ids = np.arange(pairs)
        centre_x = (ids // PGRID * float(SIDE) + (SIDE - 1) / 2.0 - centre).astype(np.float32)
        centre_y = (ids % PGRID * float(SIDE) + (SIDE - 1) / 2.0 - centre).astype(np.float32)
        self.cosine = jnp.cos(theta)
        self.sine = jnp.sin(theta)
        along = (
            centre_x[:, None] * self.cosine[None, :]
            + centre_y[:, None] * self.sine[None, :]
            + 0.5
        )
        whole = jnp.floor(along)
        lead = WIN // 2 - 1
        place = along - whole + float(lead)
        offset = whole.astype(jnp.int32) + (ACTIVE // 2 - 1 - lead)
        tile = jnp.minimum(offset // SPLIT, 2)
        local = jnp.arange(angles, dtype=jnp.int32) % chunk * WIN
        turn = (local[None, :] - offset + tile * SPLIT) % LANES
        self.offset = offset.reshape(-1)
        self.place = place.reshape(-1)
        self.tile = tile.reshape(-1)
        self.turn = turn.reshape(-1)
        ids = jnp.arange(patches, dtype=jnp.int32)
        self.slot = jnp.sum(
            jnp.where(vol_list[None, :] == ids[:, None], ids[None, :], 0), axis=1
        )
        voxel = np.arange(VOX)
        shift_x = np.repeat((voxel // SIDE - (SIDE - 1) / 2.0)[None, :], ROWS, axis=0)
        shift_y = np.repeat((voxel % SIDE - (SIDE - 1) / 2.0)[None, :], ROWS, axis=0)
        flip = np.eye(ACTIVE)[::-1].astype(ml_dtypes.bfloat16)
        self.fixed = [jnp.asarray(flip), jnp.asarray(shift_x, f32), jnp.asarray(shift_y, f32)]
        self.weight = ((chunk * WIN, 2 * VOX), bf16)
        self.held = (pairs // CYCLE + 1 if angles == chunk else 1,) + self.weight[0]
        self.acc = ((angles, ACTIVE, LANES), f32)
        self.along = ((angles, ROWS, VOX), f32)
        self.by_ray = ((angles, slices, ACTIVE), f32)
        self.by_pair = ((pairs, both, VOX), f32)
        self.window = ((angles, 3, both, LANES), f32)
        self.half = ((2, rays, slices * slots, LANES), f32)
        self.mirror = ((max(pairs, angles), slices, ACTIVE), f32)
        self.sent = ((rays, slices * (slots + angles // rays), ACTIVE), f32)

    def first(self, volume):
        inputs = [self.offset, self.place, self.slot, self.cosine, self.sine, volume]
        return call(
            functools.partial(first_kernel, self.sizes),
            "first",
            inputs + self.fixed,
            [self.by_pair, self.by_ray, self.by_ray],
            [self.weight, self.weight, self.acc, self.along, self.half, self.mirror],
            14,
        )

    def second(self, volume, start, predicted, gain, sino):
        inputs = [self.offset, self.place, self.tile, self.turn, self.slot]
        inputs += [self.cosine, self.sine, volume, start, predicted, gain, sino]
        scratch = [(self.held, bf16)] * CYCLE
        scratch += [self.acc, self.along, self.by_ray, self.mirror, self.window]
        return call(
            functools.partial(second_kernel, self.sizes, self.step_size),
            "second",
            inputs + self.fixed,
            [self.sent],
            scratch + [self.by_pair, self.half],
            26,
        )[0]


def gather_kernel(rank_ref, *refs):
    *part_refs, out_ref, sems = refs
    rank = rank_ref[0]
    copies = [
        pltpu.make_async_copy(part_ref, out_ref.at[rank ^ d], sems.at[d])
        for d, part_ref in enumerate(part_refs)
    ]
    for copy in copies:
        copy.start()
    for copy in copies:
        copy.wait()


def gather_parts(parts, rank):
    count = len(parts)
    return pl.pallas_call(
        gather_kernel,
        out_shape=jax.ShapeDtypeStruct((count,) + parts[0].shape, f32),
        in_specs=[pl.BlockSpec(memory_space=pltpu.SMEM)]
        + [pl.BlockSpec(memory_space=pltpu.VMEM)] * count,
        out_specs=pl.BlockSpec(memory_space=pl.ANY),
        scratch_shapes=[pltpu.SemaphoreType.DMA((count,))],
        cost_estimate=pl.CostEstimate(
            flops=0, bytes_accessed=8 * count * parts[0].size, transcendentals=0
        ),
        name="gather_parts",
    )(rank.reshape(1), *parts)


def finish_kernel(got_ref, _, rec_ref, out_ref, values_ref, active_ref, sems):
    rays = got_ref.shape[0]
    slots = values_ref.shape[1]
    slabs = active_ref.shape[0]
    slices = values_ref.shape[0] // rays
    lead = slices * slots
    for ray in range(rays):
        rows = slice(ray * slices, (ray + 1) * slices)
        values_ref[rows] = got_ref[ray, 0:lead, :].reshape(slices, slots, VOX)
        for k in range(slabs):
            begin = lead + k * slices
            active_ref[k, rows, :] = got_ref[ray, begin : begin + slices, :]
    offset = (out_ref.shape[2] - ACTIVE) // 2
    copies = [
        pltpu.make_async_copy(values_ref, rec_ref, sems.at[0]),
        pltpu.make_async_copy(
            active_ref, out_ref.at[:, :, offset : offset + ACTIVE], sems.at[1]
        ),
    ]
    for copy in copies:
        copy.start()
    for copy in copies:
        copy.wait()


def finish(got, sinogram, shape):
    slabs, slab_rows, _ = sinogram.shape
    any_space = pl.BlockSpec(memory_space=pl.ANY)
    return pl.pallas_call(
        finish_kernel,
        out_shape=(
            jax.ShapeDtypeStruct(shape, f32),
            jax.ShapeDtypeStruct(sinogram.shape, f32),
        ),
        in_specs=[pl.BlockSpec(memory_space=pltpu.VMEM), any_space],
        out_specs=[any_space, any_space],
        scratch_shapes=[
            pltpu.VMEM(shape, f32),
            pltpu.VMEM((slabs, slab_rows, ACTIVE), f32),
            pltpu.SemaphoreType.DMA((2,)),
        ],
        input_output_aliases={1: 1},
        cost_estimate=pl.CostEstimate(
            flops=0, bytes_accessed=8 * got.size, transcendentals=0
        ),
        name="finish",
    )(got, sinogram)


def local(intensity, angles, volume, vol_list):
    n_slab = lax.axis_size("slab")
    n_ray = lax.axis_size("ray")
    devices = n_slab * n_ray
    height, band = intensity.shape[2:]
    slices = height // devices
    slots = volume.shape[1]
    count = angles.shape[0] * angles.shape[1]
    step_size = relax * ROI / count
    rank = lax.axis_index("slab")
    padded = -(-slices // ROWS) * ROWS

    def to_all(values, axes):
        return lax.all_to_all(values, axes, split_axis=0, concat_axis=0, tiled=True)

    own_volume = to_all(volume.reshape(n_ray, slices * slots, VOX), "ray")
    *parts, active = paganin(intensity.reshape(height, band), rank, n_slab)
    active, own_volume = lax.optimization_barrier((active, own_volume))
    own_rays = to_all(active.reshape(devices, slices, ACTIVE), ("slab", "ray"))
    if padded != slices:
        more = padded - slices
        own_volume = jnp.pad(own_volume, ((0, 0), (0, more * slots), (0, 0)))
        own_rays = jnp.pad(own_rays, ((0, 0), (0, more), (0, 0)))

    theta, vol_list, own_volume, parts = lax.optimization_barrier(
        (angles.reshape(-1), vol_list, own_volume, parts)
    )
    sirt = Sirt(theta, vol_list, padded, slots, n_ray, step_size)
    start, predicted, gain = sirt.first(own_volume)
    own_rays, parts, start = lax.optimization_barrier((own_rays, parts, start))
    parts = [
        lax.ppermute(part, "slab", [(i, i ^ d) for i in range(n_slab)]) if d else part
        for d, part in enumerate(parts)
    ]
    result = sirt.second(own_volume, start, predicted, gain, own_rays)
    result, parts = lax.optimization_barrier((result, parts))
    if padded != slices:
        lower = result[:, padded * slots :].reshape(n_ray, n_slab, padded, ACTIVE)
        lower = lower[:, :, :slices].reshape(n_ray, n_slab * slices, ACTIVE)
        result = jnp.concatenate([result[:, : slices * slots], lower], axis=1)
    got = to_all(result, "ray")
    sinogram = gather_parts(parts, rank)
    reconstruction, residual = finish(got, sinogram, volume.shape)
    return (reconstruction, residual[:, None])


def solution(mesh):
    placed = (P("slab", "ray", None, None), P(), P("slab", "ray", None), P())
    return jax.shard_map(
        local,
        mesh=mesh,
        in_specs=placed,
        out_specs=(P("slab", "ray", None), P(None, "ray", "slab", None)),
        check_vma=False,
    )
```

time: 116 us -> 96.4 us (0.83); the launches traced: 114 us -> 95.9 us
  Pallas kernels: 68 us -> 52.6 us
  starting transfers between devices: 28.2 us -> 18.7 us
  waiting for transfers between devices: 13.8 us -> 21.7 us
  local copies, waits for them, and re-layouts: 3.07 us -> 1.88 us
    ppermute x17 -> x3, starting transfers between devices: 25.6 us -> 2.01 us  [local(): lax.ppermute(part, 'slab', [(i, i ^ d) for i in range(n_slab)])]
    all_to_all x1 -> x3, waiting for transfers between devices: 0.01 us -> 21.7 us  [to_all(): return lax.all_to_all(values, axes, split_axis=0, concat_axis=0, tiled=True)]
    all_to_all x1 -> x3, starting transfers between devices: 2.6 us -> 16.7 us  [to_all(): return lax.all_to_all(values, axes, split_axis=0, concat_axis=0, tiled=True)]
    ppermute x17 -> x3, waiting for transfers between devices: 13.8 us -> 0.01 us  [local(): lax.ppermute(part, 'slab', [(i, i ^ d) for i in range(n_slab)])]
    pallas_call x2, Pallas kernels: 51.3 us -> 37.9 us  [call(): pl.pallas_call(kernel, out_shape=[jax.ShapeDtypeStruct(*value) for value...]
    unnamed x44 -> x18, local copies, waits for them, and re-layouts: 2.79 us -> 0.92 us
    pallas_call x1 -> x0, Pallas kernels: 1.86 us -> none  [split(): pl.pallas_call(split_kernel, out_shape=[jax.ShapeDtypeStruct(values.shape...]
  transfers between devices with their start and end apart: 18 -> 6, of which waited for: 3 -> 2; matrix products, arithmetic and copies ran while one was open for 0% -> 1% of each run, Pallas kernels for 56% -> 53%
where the time goes in v7:
time: 96.4 us; the launch traced here: 95.9 us
  Pallas kernels  52.6 us (55%)
  waiting for transfers between devices  21.7 us (23%)
  starting transfers between devices  18.7 us (19%)
  local copies, waits for them, and re-layouts  1.88 us (2%)
    pallas_call x2, Pallas kernels, call(): pl.pallas_call(kernel, out_shape=[jax.ShapeDtypeStruct(*value) for value...  37.9 us
    all_to_all x3, waiting for transfers between devices, to_all(): return lax.all_to_all(values, axes, split_axis=0, concat_axis=0, tiled=True)  21.7 us
    all_to_all x3, starting transfers between devices, to_all(): return lax.all_to_all(values, axes, split_axis=0, concat_axis=0, tiled=True)  16.7 us
    pallas_call x1, Pallas kernels, paganin(): pl.pallas_call(filter_kernel, out_shape=[jax.ShapeDtypeStruct((height //...  9.72 us
    pallas_call x1, Pallas kernels, gather_parts(): pl.pallas_call(gather_kernel, out_shape=jax.ShapeDtypeStruct((count,) + p...  2.87 us
    pallas_call x1, Pallas kernels, finish(): pl.pallas_call(finish_kernel, out_shape=(jax.ShapeDtypeStruct(shape, f32)...  2.06 us
    ppermute x3, starting transfers between devices, local(): lax.ppermute(part, 'slab', [(i, i ^ d) for i in range(n_slab)])  2.01 us
  transfers between devices with their start and end apart: 6, of which 2 were waited for; matrix products, arithmetic and copies ran while one was open for 1% of the time, Pallas kernels for 53%

profile of v7, /device:TPU:0, one launch (start us, length us, event | category | flops | bytes accessed | tf_op | source)
XLA Modules:
  0.0 95.9 jit_solution(10277531175949971340)
XLA Ops:
  0.6 7.3 %all-to-all-start = ((f32[8,64,256]{2,1,0:T(8,128)}), f32[8,64,256]{2,1,0:T(8,128)S(1)}, u32[]{:S(2)}, u32[]{:S(2)}) async-start(f32[8,64,256]{2,1,0:T(8,128)} %bitcast.8), calls=%async_computation | async-start | bytes 1048576 | tf_op jit(solution)/shard_map/all_to_all | solution.py:734
  7.9 0.8 reshape.59
  8.7 0.1 sub.24
  8.7 0.0 copy-start.8
  8.7 0.0 copy-start.6
  8.7 0.0 copy-start.7
  8.7 0.0 copy-start
  8.8 0.0 copy-start.1
  8.8 0.0 copy-start.2
  8.8 9.7 %paganin.1 = (f32[64,2048]{1,0:T(8,128)}, f32[64,2048]{1,0:T(8,128)}, f32[64,2048]{1,0:T(8,128)}, f32[64,2048]{1,0:T(8,128)}, f32[256,256]{1,0:T(8,128)}) custom-call(s32[1]{0:T(128)} %bitcast.rank_ref, f32[256,2048]{1,0:T(8,128)} %bitcast.10, f32[264,256]{1,0:T(8,128)} %constant.75.clone.given_ref), custom_call_target="tpu_custom_call" | custom-call | flops 8589934592 | bytes 4194304 | tf_op jit(solution)/shard_map/paganin/pallas_call | solution.py:197
  18.5 3.9 %all-to-all-done.vol_ref = f32[8,64,256]{2,1,0:T(8,128)S(1)} async-done(((f32[8,64,256]{2,1,0:T(8,128)}), f32[8,64,256]{2,1,0:T(8,128)S(1)}, u32[]{:S(2)}, u32[]{:S(2)}) %all-to-all-start) | async-done | bytes 524320 | tf_op jit(solution)/shard_map/all_to_all | solution.py:734
  22.4 0.0 copy-done.8
  22.4 0.1 select_reduce_fusion.slot_ref
  22.5 3.7 %all-to-all-start.1 = ((f32[32,8,256]{2,1,0:T(8,128)}), f32[32,8,256]{2,1,0:T(8,128)S(1)}, u32[]{:S(2)}, u32[]{:S(2)}) async-start(f32[32,8,256]{2,1,0:T(8,128)} %bitcast.9), calls=%async_computation.1 | async-start | bytes 524288 | tf_op jit(solution)/shard_map/all_to_all | solution.py:734
  26.2 0.0 copy-done.6
  26.2 0.0 copy-done.7
  26.3 0.1 add_add_fusion
  26.3 0.1 add.64
  26.4 0.0 copy-done
  26.5 0.0 copy-done.1
  26.5 0.0 copy-done.2
  26.5 12.9 %first.1 = (f32[32,16,256]{2,1,0:T(8,128)S(1)}, f32[32,8,256]{2,1,0:T(8,128)S(1)}, f32[32,8,256]{2,1,0:T(8,128)S(1)}) custom-call(s32[1024]{0:T(1024)S(1)} %get-tuple-element.68.offset_ref, f32[1024]{0:T(1024)S(1)} %fusion.1.place_ref, s32[64]{0:T(128)S(1)} %select_reduce_fusion.slot_ref, f32[32]{0:T(128)S(1)} %get-tuple-element.69.cos_ref, ...), custom_call_target="tpu_custom_call" | custom-call | flops 14000000000 | bytes 4194304 | tf_op jit(solution)/shard_map/first/pallas_call | solution.py:550
  39.4 0.0 all-to-all-done.1.sino_ref
  39.4 0.3 collective-permute-start
  39.8 1.7 %collective-permute-start.1 = (f32[64,2048]{1,0:T(8,128)}, f32[64,2048]{1,0:T(8,128)S(1)}, u32[]{:S(2)}, u32[]{:S(2)}) collective-permute-start(f32[64,2048]{1,0:T(8,128)} %get-tuple-element.53), channel_id=1, source_target_pairs={{0,16},{8,24},{16,0},{24,8},{1,17},{9,25},{17,1},{25,9},{2,18},{10... | collective-permute-start | bytes 1572872 | tf_op jit(solution)/shard_map/ppermute | solution.py:752
  41.4 0.0 collective-permute-start.2
  41.4 25.0 %second.1 = f32[8,96,256]{2,1,0:T(8,128)} custom-call(s32[1024]{0:T(1024)S(1)} %get-tuple-element.68.offset_ref, f32[1024]{0:T(1024)S(1)} %fusion.1.place_ref, s32[1024]{0:T(1024)S(1)} %get-tuple-element.67.tile_ref, s32[1024]{0:T(1024)S(1)} %get-tuple-element.66.turn_ref, s32[64]{0:T(128)S(1)} %select_reduce_fusion.slot_ref, ...), custom_call_target="tpu_custom_call" | custom-call | flops 25999998976 | bytes 4194304 | tf_op jit(solution)/shard_map/second/pallas_call | solution.py:550
  66.4 0.0 collective-permute-done.refs_1_
  66.5 0.0 copy-start.4
  66.5 0.0 collective-permute-done.1.refs_2_
  66.5 0.0 copy-start.5
  66.5 0.0 collective-permute-done.2.refs_3_
  66.5 5.7 %all-to-all-start.2 = ((f32[8,96,256]{2,1,0:T(8,128)}), f32[8,96,256]{2,1,0:T(8,128)S(1)}, u32[]{:S(2)}, u32[]{:S(2)}) async-start(f32[8,96,256]{2,1,0:T(8,128)} %second.1), calls=%async_computation.2 | async-start | bytes 1572864 | tf_op jit(solution)/shard_map/all_to_all | solution.py:734
  72.2 0.0 copy-done.4
  72.2 0.0 copy-done.5
  72.2 2.9 %gather_parts.1._ = f32[4,64,2048]{2,1,0:T(8,128)} custom-call(s32[1]{0:T(128)} %bitcast.rank_ref, f32[64,2048]{1,0:T(8,128)} %get-tuple-element.56.refs_0_, f32[64,2048]{1,0:T(8,128)} %copy-done.4, f32[64,2048]{1,0:T(8,128)} %copy-done.5, f32[64,2048]{1,0:T(8,128)} %collective-permute-done.2.refs_3_), custom_call_target="tpu_custom_call" | custom-call | bytes 4194304 | tf_op jit(solution)/shard_map/gather_parts/pallas_call | solution.py:658
  75.1 17.9 %all-to-all-done.2.got_ref = f32[8,96,256]{2,1,0:T(8,128)S(1)} async-done(((f32[8,96,256]{2,1,0:T(8,128)}), f32[8,96,256]{2,1,0:T(8,128)S(1)}, u32[]{:S(2)}, u32[]{:S(2)}) %all-to-all-start.2) | async-done | bytes 786464 | tf_op jit(solution)/shard_map/all_to_all | solution.py:734
  93.0 0.0 copy-start.3
  93.0 0.9 copy-done.3
  93.9 2.1 %finish.1 = (f32[64,8,256]{2,1,0:T(8,128)}, f32[4,64,2048]{2,1,0:T(8,128)}) custom-call(f32[8,96,256]{2,1,0:T(8,128)} %copy-done.3, f32[4,64,2048]{2,1,0:T(8,128)} %gather_parts.1._), custom_call_target="tpu_custom_call", output_to_operand_aliasing={{1}: (1, {})} | custom-call | bytes 1572864 | tf_op jit(solution)/shard_map/finish/pallas_call | solution.py:700
  (5 shorter events, 0.1 us)
Async XLA Ops:
  0.6 21.8 %all-to-all-start = ((f32[8,64,256]{2,1,0:T(8,128)}), f32[8,64,256]{2,1,0:T(8,128)S(1)}, u32[]{:S(2)}, u32[]{:S(2)}) async-start(f32[8,64,256]{2,1,0:T(8,128)} %bitcast.8), calls=%async_computation | async-start | bytes 1048576 | tf_op jit(solution)/shard_map/all_to_all | solution.py:734
  8.7 13.6 %copy-start.8 = (s32[64]{0:T(128)S(1)}, s32[64]{0:T(128)}, u32[]{:S(2)}) copy-start(s32[64]{0:T(128)} %param.13) | copy-start | bytes 772
  8.7 17.5 %copy-start.6 = (f32[32]{0:T(128)S(1)}, f32[32]{0:T(128)}, u32[]{:S(2)}) copy-start(f32[32]{0:T(128)} %constant.83) | copy-start | bytes 388
  8.7 17.5 %copy-start.7 = (f32[32]{0:T(128)S(1)}, f32[32]{0:T(128)}, u32[]{:S(2)}) copy-start(f32[32]{0:T(128)} %constant.82) | copy-start | bytes 388
  8.7 17.7 %copy-start = (bf16[256,256]{1,0:T(8,128)(2,1)S(1)}, bf16[256,256]{1,0:T(8,128)(2,1)}, u32[]{:S(2)}) copy-start(bf16[256,256]{1,0:T(8,128)(2,1)} %constant.78.clone.flip_ref) | copy-start | bytes 393220
  8.8 17.7 %copy-start.1 = (f32[8,256]{1,0:T(8,128)S(1)}, f32[8,256]{1,0:T(8,128)}, u32[]{:S(2)}) copy-start(f32[8,256]{1,0:T(8,128)} %constant.80.clone.shift_y_ref) | copy-start | bytes 24580
  8.8 17.7 %copy-start.2 = (f32[8,256]{1,0:T(8,128)S(1)}, f32[8,256]{1,0:T(8,128)}, u32[]{:S(2)}) copy-start(f32[8,256]{1,0:T(8,128)} %constant.79.clone.shift_x_ref) | copy-start | bytes 24580
  22.5 16.9 %all-to-all-start.1 = ((f32[32,8,256]{2,1,0:T(8,128)}), f32[32,8,256]{2,1,0:T(8,128)S(1)}, u32[]{:S(2)}, u32[]{:S(2)}) async-start(f32[32,8,256]{2,1,0:T(8,128)} %bitcast.9), calls=%async_computation.1 | async-start | bytes 524288 | tf_op jit(solution)/shard_map/all_to_all | solution.py:734
  39.4 27.0 %collective-permute-start = (f32[64,2048]{1,0:T(8,128)}, f32[64,2048]{1,0:T(8,128)S(1)}, u32[]{:S(2)}, u32[]{:S(2)}) collective-permute-start(f32[64,2048]{1,0:T(8,128)} %get-tuple-element.52), channel_id=1, source_target_pairs={{0,8},{8,0},{16,24},{24,16},{1,9},{9,1},{17,25},{25,17},{2,10},{10... | collective-permute-start | bytes 1572872 | tf_op jit(solution)/shard_map/ppermute | solution.py:752
  39.8 26.7 %collective-permute-start.1 = (f32[64,2048]{1,0:T(8,128)}, f32[64,2048]{1,0:T(8,128)S(1)}, u32[]{:S(2)}, u32[]{:S(2)}) collective-permute-start(f32[64,2048]{1,0:T(8,128)} %get-tuple-element.53), channel_id=1, source_target_pairs={{0,16},{8,24},{16,0},{24,8},{1,17},{9,25},{17,1},{25,9},{2,18},{10... | collective-permute-start | bytes 1572872 | tf_op jit(solution)/shard_map/ppermute | solution.py:752
  41.4 25.0 %collective-permute-start.2 = (f32[64,2048]{1,0:T(8,128)}, f32[64,2048]{1,0:T(8,128)}, u32[]{:S(2)}, u32[]{:S(2)}) collective-permute-start(f32[64,2048]{1,0:T(8,128)} %get-tuple-element.54), channel_id=1, source_target_pairs={{0,24},{8,16},{16,8},{24,0},{1,25},{9,17},{17,9},{25,1},{2,26},{10... | collective-permute-start | bytes 1572872 | tf_op jit(solution)/shard_map/ppermute | solution.py:752
  66.5 5.8 %copy-start.4 = (f32[64,2048]{1,0:T(8,128)}, f32[64,2048]{1,0:T(8,128)S(1)}, u32[]{:S(2)}) copy-start(f32[64,2048]{1,0:T(8,128)S(1)} %collective-permute-done.refs_1_) | copy-start | bytes 1572868
  66.5 5.8 %copy-start.5 = (f32[64,2048]{1,0:T(8,128)}, f32[64,2048]{1,0:T(8,128)S(1)}, u32[]{:S(2)}) copy-start(f32[64,2048]{1,0:T(8,128)S(1)} %collective-permute-done.1.refs_2_) | copy-start | bytes 1572868
  66.5 26.5 %all-to-all-start.2 = ((f32[8,96,256]{2,1,0:T(8,128)}), f32[8,96,256]{2,1,0:T(8,128)S(1)}, u32[]{:S(2)}, u32[]{:S(2)}) async-start(f32[8,96,256]{2,1,0:T(8,128)} %second.1), calls=%async_computation.2 | async-start | bytes 1572864 | tf_op jit(solution)/shard_map/all_to_all | solution.py:734
  93.0 0.9 copy-start.3

commit v8 on v7

--- a/solution.py
+++ b/solution.py
@@ -406,6 +406,7 @@
 def second_kernel(
     sizes,
     step_size,
+    rank_ref,
     offset_ref,
     place_ref,
     tile_ref,
@@ -421,16 +422,16 @@
     flip_ref,
     shift_x_ref,
     shift_y_ref,
-    out_ref,
     *refs,
 ):
     angles, chunk, slots = sizes
+    rays = vol_ref.shape[0]
+    out_refs, refs = refs[:rays], refs[rays:]
     held_refs = refs[:CYCLE]
     acc_ref, along_ref, direct_ref, mirror_ref, window_ref, update_ref, half_ref = refs[CYCLE:]
     patches = slot_ref.shape[0]
     pairs, both, _ = start_ref.shape
     slices = both // 2
-    rays = out_ref.shape[0]
     flip = flip_ref[...]
     weights = Weights(along_ref, place_ref, angles, chunk)
     weights.prepare(shift_x_ref, shift_y_ref, cos_ref, sin_ref)
@@ -537,11 +538,13 @@
 
     repeat(pairs, finish, 8)
     lead = slices * slots
-    for part in range(2):
-        out_ref[:, 0:lead, part * LANES : (part + 1) * LANES] = half_ref[part]
-    for t in range(angles):
-        begin = lead + t // rays * slices
-        out_ref[t % rays, begin : begin + slices, :] = direct_ref[t]
+    for d, out_ref in enumerate(out_refs):
+        ray = rank_ref[0] ^ d
+        for part in range(2):
+            out_ref[0:lead, part * LANES : (part + 1) * LANES] = half_ref[part, ray]
+        for k in range(angles // rays):
+            begin = lead + k * slices
+            out_ref[begin : begin + slices, :] = direct_ref[k * rays + ray]
 
 
 def call(kernel, name, inputs, outputs, scratch, micros):
@@ -612,7 +615,7 @@
         self.window = ((angles, 3, both, LANES), f32)
         self.half = ((2, rays, slices * slots, LANES), f32)
         self.mirror = ((max(pairs, angles), slices, ACTIVE), f32)
-        self.sent = ((rays, slices * (slots + angles // rays), ACTIVE), f32)
+        self.sent = [((slices * (slots + angles // rays), ACTIVE), f32)] * rays
 
     def first(self, volume):
         inputs = [self.offset, self.place, self.slot, self.cosine, self.sine, volume]
@@ -625,8 +628,8 @@
             14,
         )
 
-    def second(self, volume, start, predicted, gain, sino):
-        inputs = [self.offset, self.place, self.tile, self.turn, self.slot]
+    def second(self, rank, volume, start, predicted, gain, sino):
+        inputs = [rank.reshape(1), self.offset, self.place, self.tile, self.turn, self.slot]
         inputs += [self.cosine, self.sine, volume, start, predicted, gain, sino]
         scratch = [(self.held, bf16)] * CYCLE
         scratch += [self.acc, self.along, self.by_ray, self.mirror, self.window]
@@ -634,10 +637,10 @@
             functools.partial(second_kernel, self.sizes, self.step_size),
             "second",
             inputs + self.fixed,
-            [self.sent],
+            self.sent,
             scratch + [self.by_pair, self.half],
             26,
-        )[0]
+        )
 
 
 def gather_kernel(rank_ref, *refs):
@@ -662,6 +665,7 @@
         + [pl.BlockSpec(memory_space=pltpu.VMEM)] * count,
         out_specs=pl.BlockSpec(memory_space=pl.ANY),
         scratch_shapes=[pltpu.SemaphoreType.DMA((count,))],
+        compiler_params=pltpu.CompilerParams(vmem_limit_bytes=8 * 2**20),
         cost_estimate=pl.CostEstimate(
             flops=0, bytes_accessed=8 * count * parts[0].size, transcendentals=0
         ),
@@ -669,18 +673,19 @@
     )(rank.reshape(1), *parts)
 
 
-def finish_kernel(got_ref, _, rec_ref, out_ref, values_ref, active_ref, sems):
-    rays = got_ref.shape[0]
+def finish_kernel(rank_ref, *refs):
+    *got_refs, _, rec_ref, out_ref, values_ref, active_ref, sems = refs
+    rays = len(got_refs)
     slots = values_ref.shape[1]
     slabs = active_ref.shape[0]
     slices = values_ref.shape[0] // rays
     lead = slices * slots
-    for ray in range(rays):
-        rows = slice(ray * slices, (ray + 1) * slices)
-        values_ref[rows] = got_ref[ray, 0:lead, :].reshape(slices, slots, VOX)
+    for d, got_ref in enumerate(reversed(got_refs)):
+        rows = pl.ds(pl.multiple_of((rank_ref[0] ^ d) * slices, slices), slices)
+        values_ref[rows] = got_ref[0:lead, :].reshape(slices, slots, VOX)
         for k in range(slabs):
             begin = lead + k * slices
-            active_ref[k, rows, :] = got_ref[ray, begin : begin + slices, :]
+            active_ref[k, rows, :] = got_ref[begin : begin + slices, :]
     offset = (out_ref.shape[2] - ACTIVE) // 2
     copies = [
         pltpu.make_async_copy(values_ref, rec_ref, sems.at[0]),
@@ -694,28 +699,39 @@
         copy.wait()
 
 
-def finish(got, sinogram, shape):
+def finish(pieces, sinogram, rank, shape):
     slabs, slab_rows, _ = sinogram.shape
-    any_space = pl.BlockSpec(memory_space=pl.ANY)
+    hbm = pl.BlockSpec(memory_space=pltpu.HBM)
     return pl.pallas_call(
         finish_kernel,
         out_shape=(
             jax.ShapeDtypeStruct(shape, f32),
             jax.ShapeDtypeStruct(sinogram.shape, f32),
         ),
-        in_specs=[pl.BlockSpec(memory_space=pltpu.VMEM), any_space],
-        out_specs=[any_space, any_space],
+        in_specs=[pl.BlockSpec(memory_space=pltpu.SMEM)]
+        + [pl.BlockSpec(memory_space=pltpu.VMEM)] * len(pieces)
+        + [hbm],
+        out_specs=[hbm, hbm],
         scratch_shapes=[
             pltpu.VMEM(shape, f32),
             pltpu.VMEM((slabs, slab_rows, ACTIVE), f32),
             pltpu.SemaphoreType.DMA((2,)),
         ],
-        input_output_aliases={1: 1},
+        input_output_aliases={len(pieces) + 1: 1},
+        compiler_params=pltpu.CompilerParams(vmem_limit_bytes=8 * 2**20),
         cost_estimate=pl.CostEstimate(
-            flops=0, bytes_accessed=8 * got.size, transcendentals=0
+            flops=0, bytes_accessed=8 * len(pieces) * pieces[0].size, transcendentals=0
         ),
         name="finish",
-    )(got, sinogram)
+    )(rank.reshape(1), *reversed(pieces), sinogram)
+
+
+def exchange(pieces, axis):
+    count = len(pieces)
+    results = list(pieces)
+    for d in range(count - 1, 0, -1):
+        results[d] = lax.ppermute(pieces[d], axis, [(i, i ^ d) for i in range(count)])
+    return results
 
 
 def local(intensity, angles, volume, vol_list):
@@ -728,6 +744,7 @@
     count = angles.shape[0] * angles.shape[1]
     step_size = relax * ROI / count
     rank = lax.axis_index("slab")
+    ray_rank = lax.axis_index("ray")
     padded = -(-slices // ROWS) * ROWS
 
     def to_all(values, axes):
@@ -748,19 +765,28 @@
     sirt = Sirt(theta, vol_list, padded, slots, n_ray, step_size)
     start, predicted, gain = sirt.first(own_volume)
     own_rays, parts, start = lax.optimization_barrier((own_rays, parts, start))
-    parts = [
-        lax.ppermute(part, "slab", [(i, i ^ d) for i in range(n_slab)]) if d else part
-        for d, part in enumerate(parts)
-    ]
-    result = sirt.second(own_volume, start, predicted, gain, own_rays)
-    result, parts = lax.optimization_barrier((result, parts))
+    parts = exchange(parts, "slab")
+    pieces = sirt.second(ray_rank, own_volume, start, predicted, gain, own_rays)
+    pieces, parts = lax.optimization_barrier((pieces, parts))
     if padded != slices:
-        lower = result[:, padded * slots :].reshape(n_ray, n_slab, padded, ACTIVE)
-        lower = lower[:, :, :slices].reshape(n_ray, n_slab * slices, ACTIVE)
-        result = jnp.concatenate([result[:, : slices * slots], lower], axis=1)
-    got = to_all(result, "ray")
+        narrow = []
+        for piece in pieces:
+            lower = piece[padded * slots :].reshape(n_slab, padded, ACTIVE)[:, :slices]
+            lower = lower.reshape(n_slab * slices, ACTIVE)
+            narrow.append(jnp.concatenate([piece[: slices * slots], lower], axis=0))
+        pieces = narrow
+    pieces = exchange(pieces, "ray")
     sinogram = gather_parts(parts, rank)
-    reconstruction, residual = finish(got, sinogram, volume.shape)
+    if padded == slices:
+        reconstruction, residual = finish(pieces, sinogram, ray_rank, volume.shape)
+    else:
+        order = ray_rank ^ jnp.arange(n_ray, dtype=jnp.int32)
+        pieces = jnp.take(jnp.stack(pieces), order, axis=0)
+        reconstruction = pieces[:, : slices * slots].reshape(volume.shape)
+        lower = pieces[:, slices * slots :].reshape(n_ray, n_slab, slices, ACTIVE)
+        lower = jnp.transpose(lower, (1, 0, 2, 3)).reshape(n_slab, n_ray * slices, ACTIVE)
+        begin = (band - ACTIVE) // 2
+        residual = lax.dynamic_update_slice(sinogram, lower, (0, 0, begin))
     return (reconstruction, residual[:, None])
 
 

time: 96.4 us -> 91.1 us (0.945)
  waiting for transfers between devices: 21.7 us -> 7.46 us
  starting transfers between devices: 18.7 us -> 31 us
  Pallas kernels: 52.6 us -> 49.6 us
    ppermute x3 -> x10, starting transfers between devices: 2.01 us -> 20 us  [exchange(): lax.ppermute(pieces[d], axis, [(i, i ^ d) for i in range(count)])]
    all_to_all x3 -> x2, waiting for transfers between devices: 21.7 us -> 3.86 us  [to_all(): return lax.all_to_all(values, axes, split_axis=0, concat_axis=0, tiled=True)]
    all_to_all x3 -> x2, starting transfers between devices: 16.7 us -> 11 us  [to_all(): return lax.all_to_all(values, axes, split_axis=0, concat_axis=0, tiled=True)]
    ppermute x3 -> x10, waiting for transfers between devices: 0.01 us -> 3.6 us  [exchange(): lax.ppermute(pieces[d], axis, [(i, i ^ d) for i in range(count)])]
    pallas_call x1, Pallas kernels: 2.87 us -> 1.34 us  [gather_parts(): pl.pallas_call(gather_kernel, out_shape=jax.ShapeDtypeStruct((count,) + p...]
    pallas_call x1, Pallas kernels: 2.06 us -> 0.95 us  [finish(): pl.pallas_call(finish_kernel, out_shape=(jax.ShapeDtypeStruct(shape, f32)...]
  transfers between devices with their start and end apart: 6 -> 12, of which waited for: 2 -> 4; matrix products, arithmetic and copies ran while one was open for 1% -> 1% of each run, Pallas kernels for 53% -> 54%
where the time goes in v8:
time: 91.1 us; the launch traced here: 90.8 us
  Pallas kernels  49.6 us (54%)
  starting transfers between devices  31 us (34%)
  waiting for transfers between devices  7.46 us (8%)
  local copies, waits for them, and re-layouts  1.8 us (2%)
    pallas_call x2, Pallas kernels, call(): pl.pallas_call(kernel, out_shape=[jax.ShapeDtypeStruct(*value) for value...  37.5 us
    ppermute x10, starting transfers between devices, exchange(): lax.ppermute(pieces[d], axis, [(i, i ^ d) for i in range(count)])  20 us
    all_to_all x2, starting transfers between devices, to_all(): return lax.all_to_all(values, axes, split_axis=0, concat_axis=0, tiled=True)  11 us
    pallas_call x1, Pallas kernels, paganin(): pl.pallas_call(filter_kernel, out_shape=[jax.ShapeDtypeStruct((height //...  9.74 us
    all_to_all x2, waiting for transfers between devices, to_all(): return lax.all_to_all(values, axes, split_axis=0, concat_axis=0, tiled=True)  3.86 us
    ppermute x10, waiting for transfers between devices, exchange(): lax.ppermute(pieces[d], axis, [(i, i ^ d) for i in range(count)])  3.6 us
  transfers between devices with their start and end apart: 12, of which 4 were waited for; matrix products, arithmetic and copies ran while one was open for 1% of the time, Pallas kernels for 54%

profile of v8, /device:TPU:0, one launch (start us, length us, event | category | flops | bytes accessed | tf_op | source)
XLA Modules:
  0.0 90.8 jit_solution(11109815585919887276)
XLA Ops:
  0.6 7.3 %all-to-all-start = ((f32[8,64,256]{2,1,0:T(8,128)}), f32[8,64,256]{2,1,0:T(8,128)S(1)}, u32[]{:S(2)}, u32[]{:S(2)}) async-start(f32[8,64,256]{2,1,0:T(8,128)} %bitcast.9), calls=%async_computation | async-start | bytes 1048576 | tf_op jit(solution)/shard_map/all_to_all | solution.py:751
  7.9 0.8 reshape.64
  8.7 0.1 sub.24
  8.8 0.0 copy-start.3
  8.8 0.0 copy-start.4
  8.8 9.7 %paganin.1 = (f32[64,2048]{1,0:T(8,128)}, f32[64,2048]{1,0:T(8,128)}, f32[64,2048]{1,0:T(8,128)}, f32[64,2048]{1,0:T(8,128)}, f32[256,256]{1,0:T(8,128)}) custom-call(s32[1]{0:T(128)} %bitcast.1.rank_ref, f32[256,2048]{1,0:T(8,128)} %bitcast.11, f32[264,256]{1,0:T(8,128)} %constant.78.clone.given_ref), custom_call_target="tpu_custom_call" | custom-call | flops 8589934592 | bytes 4194304 | tf_op jit(solution)/shard_map/paganin/pallas_call | solution.py:197
  18.5 3.9 %all-to-all-done.vol_ref = f32[8,64,256]{2,1,0:T(8,128)S(1)} async-done(((f32[8,64,256]{2,1,0:T(8,128)}), f32[8,64,256]{2,1,0:T(8,128)S(1)}, u32[]{:S(2)}, u32[]{:S(2)}) %all-to-all-start) | async-done | bytes 524320 | tf_op jit(solution)/shard_map/all_to_all | solution.py:751
  22.4 0.0 copy-done.11
  22.4 0.1 select_reduce_fusion.slot_ref
  22.5 3.7 %all-to-all-start.1 = ((f32[32,8,256]{2,1,0:T(8,128)}), f32[32,8,256]{2,1,0:T(8,128)S(1)}, u32[]{:S(2)}, u32[]{:S(2)}) async-start(f32[32,8,256]{2,1,0:T(8,128)} %bitcast.10), calls=%async_computation.1 | async-start | bytes 524288 | tf_op jit(solution)/shard_map/all_to_all | solution.py:751
  26.2 0.0 copy-done.6
  26.2 0.0 copy-done.7
  26.3 0.1 add_add_fusion
  26.3 0.1 add.64
  26.4 0.0 copy-done.2
  26.5 0.0 copy-done.3
  26.5 0.0 copy-done.4
  26.5 0.0 copy-start.10
  26.5 12.9 %first.1 = (f32[32,16,256]{2,1,0:T(8,128)S(1)}, f32[32,8,256]{2,1,0:T(8,128)S(1)}, f32[32,8,256]{2,1,0:T(8,128)S(1)}) custom-call(s32[1024]{0:T(1024)S(1)} %get-tuple-element.98.offset_ref, f32[1024]{0:T(1024)S(1)} %fusion.1.place_ref, s32[64]{0:T(128)S(1)} %select_reduce_fusion.slot_ref, f32[32]{0:T(128)S(1)} %get-tuple-element.99.cos_ref, ...), custom_call_target="tpu_custom_call" | custom-call | flops 14000000000 | bytes 4194304 | tf_op jit(solution)/shard_map/first/pallas_call | solution.py:553
  39.5 0.0 copy-start.5
  39.5 0.8 copy-done.5
  40.3 0.0 all-to-all-done.1.sino_ref
  40.3 0.0 copy-done.10
  40.3 0.3 collective-permute-start
  40.5 0.0 copy-done.9
  40.5 1.7 %collective-permute-start.1 = (f32[64,2048]{1,0:T(8,128)S(1)}, f32[64,2048]{1,0:T(8,128)S(1)}, u32[]{:S(2)}, u32[]{:S(2)}) collective-permute-start(f32[64,2048]{1,0:T(8,128)S(1)} %copy-done.9), channel_id=1, source_target_pairs={{0,16},{8,24},{16,0},{24,8},{1,17},{9,25},{17,1},{25,9},{2,18},{10... | collective-permute-start | bytes 1572872 | tf_op jit(solution)/shard_map/ppermute | solution.py:733
  42.2 0.0 collective-permute-start.2
  42.2 24.6 %second.1 = (f32[96,256]{1,0:T(8,128)S(1)}, f32[96,256]{1,0:T(8,128)S(1)}, f32[96,256]{1,0:T(8,128)S(1)}, f32[96,256]{1,0:T(8,128)S(1)}, f32[96,256]{1,0:T(8,128...) custom-call(s32[1]{0:T(128)} %bitcast.rank_ref, ...), custom_call_target="tpu_custom_call" | custom-call | flops 25999998976 | bytes 4194304 | tf_op jit(solution)/shard_map/second/pallas_call | solution.py:553
  66.8 0.0 collective-permute-done.refs_1_
  66.8 0.0 collective-permute-done.1.refs_2_
  66.9 0.0 collective-permute-done.2.refs_3_
  66.9 4.5 %collective-permute-start.3 = (f32[96,256]{1,0:T(8,128)S(1)}, f32[96,256]{1,0:T(8,128)S(1)}, u32[]{:S(2)}, u32[]{:S(2)}) collective-permute-start(f32[96,256]{1,0:T(8,128)S(1)} %get-tuple-element.78), channel_id=1, source_target_pairs={{0,7},{1,6},{2,5},{3,4},{4,3},{5,2},{6,1},{7,0},{8,15},{9,14},{10,... | collective-permute-start | bytes 294920 | tf_op jit(solution)/shard_map/ppermute | solution.py:733
  71.4 0.5 collective-permute-start.4
  71.9 0.6 collective-permute-start.5
  72.4 2.1 %collective-permute-start.6 = (f32[96,256]{1,0:T(8,128)S(1)}, f32[96,256]{1,0:T(8,128)S(1)}, u32[]{:S(2)}, u32[]{:S(2)}) collective-permute-start(f32[96,256]{1,0:T(8,128)S(1)} %get-tuple-element.81), channel_id=1, source_target_pairs={{0,4},{1,5},{2,6},{3,7},{4,0},{5,1},{6,2},{7,3},{8,12},{9,13},{10,... | collective-permute-start | bytes 294920 | tf_op jit(solution)/shard_map/ppermute | solution.py:733
  74.6 2.1 %collective-permute-start.7 = (f32[96,256]{1,0:T(8,128)S(1)}, f32[96,256]{1,0:T(8,128)S(1)}, u32[]{:S(2)}, u32[]{:S(2)}) collective-permute-start(f32[96,256]{1,0:T(8,128)S(1)} %get-tuple-element.82), channel_id=1, source_target_pairs={{0,3},{1,2},{2,1},{3,0},{4,7},{5,6},{6,5},{7,4},{8,11},{9,10},{10,... | collective-permute-start | bytes 294920 | tf_op jit(solution)/shard_map/ppermute | solution.py:733
  76.7 0.0 collective-permute-done.3.refs_0_
  76.7 6.8 %collective-permute-start.8 = (f32[96,256]{1,0:T(8,128)S(1)}, f32[96,256]{1,0:T(8,128)S(1)}, u32[]{:S(2)}, u32[]{:S(2)}) collective-permute-start(f32[96,256]{1,0:T(8,128)S(1)} %get-tuple-element.83), channel_id=1, source_target_pairs={{0,2},{1,3},{2,0},{3,1},{4,6},{5,7},{6,4},{7,5},{8,10},{9,11},{10,... | collective-permute-start | bytes 294920 | tf_op jit(solution)/shard_map/ppermute | solution.py:733
  83.5 0.0 collective-permute-done.4.refs_1_
  83.5 1.4 %collective-permute-start.9 = (f32[96,256]{1,0:T(8,128)S(1)}, f32[96,256]{1,0:T(8,128)S(1)}, u32[]{:S(2)}, u32[]{:S(2)}) collective-permute-start(f32[96,256]{1,0:T(8,128)S(1)} %get-tuple-element.84), channel_id=1, source_target_pairs={{0,1},{1,0},{2,3},{3,2},{4,5},{5,4},{6,7},{7,6},{8,9},{9,8},{10,11... | collective-permute-start | bytes 294920 | tf_op jit(solution)/shard_map/ppermute | solution.py:733
  84.9 0.0 copy-done
  84.9 1.3 %gather_parts.1.refs_8_ = f32[4,64,2048]{2,1,0:T(8,128)} custom-call(s32[1]{0:T(128)} %bitcast.1.rank_ref, f32[64,2048]{1,0:T(8,128)S(1)} %copy-done, f32[64,2048]{1,0:T(8,128)S(1)} %collective-permute-done.refs_1_, f32[64,2048]{1,0:T(8,128)S(1)} %collective-permute-done.1.refs_2_, f32[64,2048]{1,0:T(8,128)S(1)} %collective-permute-done.2.refs_3_), custom_call_target="tpu_custom_call" | custom-call | bytes 4194304 | tf_op jit(solution)/shard_map/gather_parts/pallas_call | solution.py:661
  86.3 1.0 %collective-permute-done.5.refs_2_ = f32[96,256]{1,0:T(8,128)S(1)} collective-permute-done((f32[96,256]{1,0:T(8,128)S(1)}, f32[96,256]{1,0:T(8,128)S(1)}, u32[]{:S(2)}, u32[]{:S(2)}) %collective-permute-start.5) | collective-permute-done | bytes 98336 | tf_op jit(solution)/shard_map/ppermute | solution.py:733
  87.3 1.7 %collective-permute-done.6.refs_3_ = f32[96,256]{1,0:T(8,128)S(1)} collective-permute-done((f32[96,256]{1,0:T(8,128)S(1)}, f32[96,256]{1,0:T(8,128)S(1)}, u32[]{:S(2)}, u32[]{:S(2)}) %collective-permute-start.6) | collective-permute-done | bytes 98336 | tf_op jit(solution)/shard_map/ppermute | solution.py:733
  89.0 0.0 collective-permute-done.7.refs_4_
  89.0 0.9 %collective-permute-done.8.refs_5_ = f32[96,256]{1,0:T(8,128)S(1)} collective-permute-done((f32[96,256]{1,0:T(8,128)S(1)}, f32[96,256]{1,0:T(8,128)S(1)}, u32[]{:S(2)}, u32[]{:S(2)}) %collective-permute-start.8) | collective-permute-done | bytes 98336 | tf_op jit(solution)/shard_map/ppermute | solution.py:733
  89.9 0.0 collective-permute-done.9.refs_6_
  89.9 0.9 %finish.1 = (f32[64,8,256]{2,1,0:T(8,128)}, f32[4,64,2048]{2,1,0:T(8,128)}) custom-call(s32[1]{0:T(128)} %bitcast.rank_ref, f32[96,256]{1,0:T(8,128)S(1)} %collective-permute-done.3.refs_0_, f32[96,256]{1,0:T(8,128)S(1)} %collective-permute-done.4.refs_1_, f32[96,256]{1,0:T(8,128)S(1)} %collective-permute-done.5.refs_2_, ...), custom_call_target="tpu_custom_call", output_to_operand_aliasing={{1}: (9, {})} | custom-call | bytes 1572864 | tf_op jit(solution)/shard_map/finish/pallas_call | solution.py:705
  (15 shorter events, 0.1 us)
Async XLA Ops:
  0.6 21.8 %all-to-all-start = ((f32[8,64,256]{2,1,0:T(8,128)}), f32[8,64,256]{2,1,0:T(8,128)S(1)}, u32[]{:S(2)}, u32[]{:S(2)}) async-start(f32[8,64,256]{2,1,0:T(8,128)} %bitcast.9), calls=%async_computation | async-start | bytes 1048576 | tf_op jit(solution)/shard_map/all_to_all | solution.py:751
  8.7 13.6 %copy-start.11 = (s32[64]{0:T(128)S(1)}, s32[64]{0:T(128)}, u32[]{:S(2)}) copy-start(s32[64]{0:T(128)} %param.13) | copy-start | bytes 772
  8.7 17.5 %copy-start.6 = (f32[32]{0:T(128)S(1)}, f32[32]{0:T(128)}, u32[]{:S(2)}) copy-start(f32[32]{0:T(128)} %constant.86) | copy-start | bytes 388
  8.7 17.5 %copy-start.7 = (f32[32]{0:T(128)S(1)}, f32[32]{0:T(128)}, u32[]{:S(2)}) copy-start(f32[32]{0:T(128)} %constant.85) | copy-start | bytes 388
  8.7 17.7 %copy-start.2 = (bf16[256,256]{1,0:T(8,128)(2,1)S(1)}, bf16[256,256]{1,0:T(8,128)(2,1)}, u32[]{:S(2)}) copy-start(bf16[256,256]{1,0:T(8,128)(2,1)} %constant.81.clone.flip_ref) | copy-start | bytes 393220
  8.8 17.7 %copy-start.3 = (f32[8,256]{1,0:T(8,128)S(1)}, f32[8,256]{1,0:T(8,128)}, u32[]{:S(2)}) copy-start(f32[8,256]{1,0:T(8,128)} %constant.83.clone.shift_y_ref) | copy-start | bytes 24580
  8.8 17.7 %copy-start.4 = (f32[8,256]{1,0:T(8,128)S(1)}, f32[8,256]{1,0:T(8,128)}, u32[]{:S(2)}) copy-start(f32[8,256]{1,0:T(8,128)} %constant.82.clone.shift_x_ref) | copy-start | bytes 24580
  22.4 17.1 %copy-start.1 = (f32[8,64,256]{2,1,0:T(8,128)}, f32[8,64,256]{2,1,0:T(8,128)S(1)}, u32[]{:S(2)}) copy-start(f32[8,64,256]{2,1,0:T(8,128)S(1)} %all-to-all-done.vol_ref) | copy-start | bytes 1572868
  22.5 17.7 %all-to-all-start.1 = ((f32[32,8,256]{2,1,0:T(8,128)}), f32[32,8,256]{2,1,0:T(8,128)S(1)}, u32[]{:S(2)}, u32[]{:S(2)}) async-start(f32[32,8,256]{2,1,0:T(8,128)} %bitcast.10), calls=%async_computation.1 | async-start | bytes 524288 | tf_op jit(solution)/shard_map/all_to_all | solution.py:751
  26.5 13.8 %copy-start.10 = (f32[64,2048]{1,0:T(8,128)S(1)}, f32[64,2048]{1,0:T(8,128)}, u32[]{:S(2)}) copy-start(f32[64,2048]{1,0:T(8,128)} %get-tuple-element.75) | copy-start | bytes 1572868
  26.5 14.0 %copy-start.9 = (f32[64,2048]{1,0:T(8,128)S(1)}, f32[64,2048]{1,0:T(8,128)}, u32[]{:S(2)}) copy-start(f32[64,2048]{1,0:T(8,128)} %get-tuple-element.76) | copy-start | bytes 1572868
  26.5 15.7 %copy-start.8 = (f32[64,2048]{1,0:T(8,128)S(1)}, f32[64,2048]{1,0:T(8,128)}, u32[]{:S(2)}) copy-start(f32[64,2048]{1,0:T(8,128)} %get-tuple-element.77) | copy-start | bytes 1572868
  39.5 0.8 copy-start.5
  40.3 26.6 %collective-permute-start = (f32[64,2048]{1,0:T(8,128)S(1)}, f32[64,2048]{1,0:T(8,128)S(1)}, u32[]{:S(2)}, u32[]{:S(2)}) collective-permute-start(f32[64,2048]{1,0:T(8,128)S(1)} %copy-done.10), channel_id=1, source_target_pairs={{0,8},{8,0},{16,24},{24,16},{1,9},{9,1},{17,25},{25,17},{2,10},{10... | collective-permute-start | bytes 1572872 | tf_op jit(solution)/shard_map/ppermute | solution.py:733
  40.5 26.3 %collective-permute-start.1 = (f32[64,2048]{1,0:T(8,128)S(1)}, f32[64,2048]{1,0:T(8,128)S(1)}, u32[]{:S(2)}, u32[]{:S(2)}) collective-permute-start(f32[64,2048]{1,0:T(8,128)S(1)} %copy-done.9), channel_id=1, source_target_pairs={{0,16},{8,24},{16,0},{24,8},{1,17},{9,25},{17,1},{25,9},{2,18},{10... | collective-permute-start | bytes 1572872 | tf_op jit(solution)/shard_map/ppermute | solution.py:733
  42.2 24.7 %collective-permute-start.2 = (f32[64,2048]{1,0:T(8,128)S(1)}, f32[64,2048]{1,0:T(8,128)S(1)}, u32[]{:S(2)}, u32[]{:S(2)}) collective-permute-start(f32[64,2048]{1,0:T(8,128)S(1)} %copy-done.8), channel_id=1, source_target_pairs={{0,24},{8,16},{16,8},{24,0},{1,25},{9,17},{17,9},{25,1},{2,26},{10... | collective-permute-start | bytes 1572872 | tf_op jit(solution)/shard_map/ppermute | solution.py:733
  42.2 42.7 %copy-start = (f32[64,2048]{1,0:T(8,128)S(1)}, f32[64,2048]{1,0:T(8,128)}, u32[]{:S(2)}) copy-start(f32[64,2048]{1,0:T(8,128)} %get-tuple-element.86.refs_0_) | copy-start | bytes 1572868
  66.9 9.8 %collective-permute-start.3 = (f32[96,256]{1,0:T(8,128)S(1)}, f32[96,256]{1,0:T(8,128)S(1)}, u32[]{:S(2)}, u32[]{:S(2)}) collective-permute-start(f32[96,256]{1,0:T(8,128)S(1)} %get-tuple-element.78), channel_id=1, source_target_pairs={{0,7},{1,6},{2,5},{3,4},{4,3},{5,2},{6,1},{7,0},{8,15},{9,14},{10,... | collective-permute-start | bytes 294920 | tf_op jit(solution)/shard_map/ppermute | solution.py:733
  71.4 12.1 %collective-permute-start.4 = (f32[96,256]{1,0:T(8,128)S(1)}, f32[96,256]{1,0:T(8,128)S(1)}, u32[]{:S(2)}, u32[]{:S(2)}) collective-permute-start(f32[96,256]{1,0:T(8,128)S(1)} %get-tuple-element.79), channel_id=1, source_target_pairs={{0,6},{1,7},{2,4},{3,5},{4,2},{5,3},{6,0},{7,1},{8,14},{9,15},{10,... | collective-permute-start | bytes 294920 | tf_op jit(solution)/shard_map/ppermute | solution.py:733
  71.9 15.4 %collective-permute-start.5 = (f32[96,256]{1,0:T(8,128)S(1)}, f32[96,256]{1,0:T(8,128)S(1)}, u32[]{:S(2)}, u32[]{:S(2)}) collective-permute-start(f32[96,256]{1,0:T(8,128)S(1)} %get-tuple-element.80), channel_id=1, source_target_pairs={{0,5},{1,4},{2,7},{3,6},{4,1},{5,0},{6,3},{7,2},{8,13},{9,12},{10,... | collective-permute-start | bytes 294920 | tf_op jit(solution)/shard_map/ppermute | solution.py:733
  72.4 16.5 %collective-permute-start.6 = (f32[96,256]{1,0:T(8,128)S(1)}, f32[96,256]{1,0:T(8,128)S(1)}, u32[]{:S(2)}, u32[]{:S(2)}) collective-permute-start(f32[96,256]{1,0:T(8,128)S(1)} %get-tuple-element.81), channel_id=1, source_target_pairs={{0,4},{1,5},{2,6},{3,7},{4,0},{5,1},{6,2},{7,3},{8,12},{9,13},{10,... | collective-permute-start | bytes 294920 | tf_op jit(solution)/shard_map/ppermute | solution.py:733
  74.6 14.4 %collective-permute-start.7 = (f32[96,256]{1,0:T(8,128)S(1)}, f32[96,256]{1,0:T(8,128)S(1)}, u32[]{:S(2)}, u32[]{:S(2)}) collective-permute-start(f32[96,256]{1,0:T(8,128)S(1)} %get-tuple-element.82), channel_id=1, source_target_pairs={{0,3},{1,2},{2,1},{3,0},{4,7},{5,6},{6,5},{7,4},{8,11},{9,10},{10,... | collective-permute-start | bytes 294920 | tf_op jit(solution)/shard_map/ppermute | solution.py:733
  76.7 13.2 %collective-permute-start.8 = (f32[96,256]{1,0:T(8,128)S(1)}, f32[96,256]{1,0:T(8,128)S(1)}, u32[]{:S(2)}, u32[]{:S(2)}) collective-permute-start(f32[96,256]{1,0:T(8,128)S(1)} %get-tuple-element.83), channel_id=1, source_target_pairs={{0,2},{1,3},{2,0},{3,1},{4,6},{5,7},{6,4},{7,5},{8,10},{9,11},{10,... | collective-permute-start | bytes 294920 | tf_op jit(solution)/shard_map/ppermute | solution.py:733
  83.5 6.4 %collective-permute-start.9 = (f32[96,256]{1,0:T(8,128)S(1)}, f32[96,256]{1,0:T(8,128)S(1)}, u32[]{:S(2)}, u32[]{:S(2)}) collective-permute-start(f32[96,256]{1,0:T(8,128)S(1)} %get-tuple-element.84), channel_id=1, source_target_pairs={{0,1},{1,0},{2,3},{3,2},{4,5},{5,4},{6,7},{7,6},{8,9},{9,8},{10,11... | collective-permute-start | bytes 294920 | tf_op jit(solution)/shard_map/ppermute | solution.py:733

commit v9 on v8

--- a/solution.py
+++ b/solution.py
@@ -257,44 +257,55 @@
 
 def ray_operand(values, sums_too):
     high, low = halves(values)
-    both = values.shape[0]
     rows = [
         jnp.concatenate([high, high], axis=1),
         jnp.concatenate([low, jnp.zeros_like(low)], axis=1),
     ]
     if sums_too:
-        rows.append(jnp.ones((both, 2 * VOX), bf16))
-    rows.append(jnp.zeros((LANES - len(rows) * both, 2 * VOX), bf16))
+        rows.append(jnp.ones((values.shape[0], 2 * VOX), bf16))
     return jnp.concatenate(rows, axis=0)
 
 
-def project_pair(held, operand, q, c, sizes, offset_ref, acc_ref):
+def project_pair(held, operand, q, c, both, sizes, tile_ref, turn_ref, acc_ref):
     angles, chunk = sizes[:2]
+    rows = acc_ref.shape[2]
     sums = lax.dot_general(
-        held, operand, (((1,), (1,)), ((), ())), preferred_element_type=f32
+        operand, held, (((1,), (1,)), ((), ())), preferred_element_type=f32
     )
+    total = sums[0:both] + sums[both : 2 * both]
+    if rows != both:
+        total = jnp.concatenate([total, sums[2 * both : 2 * both + ROWS]], axis=0)
+    lane = lax.broadcasted_iota(jnp.int32, (rows, LANES), 1)
     for begin in range(0, chunk, GROUP):
         places = []
         for t in range(begin, min(begin + GROUP, chunk)):
+            index = q * angles + c * chunk + t
+            first = t * WIN // LANES
+            last = (t * WIN + WIN - 1) // LANES
+            low = t * WIN - first * LANES
+            high = low + WIN
+            piece = total[:, first * LANES : (first + 1) * LANES]
+            if first == last:
+                piece = jnp.where((lane >= low) & (lane < high), piece, 0.0)
+            else:
+                other = total[:, last * LANES : (last + 1) * LANES]
+                piece = jnp.where(
+                    lane >= low, piece, jnp.where(lane < high - LANES, other, 0.0)
+                )
+            tile = tile_ref[index]
             angle = c * chunk + t
-            rows = pl.ds(offset_ref[q * angles + angle], WIN)
-            values = acc_ref[angle, rows, :] + sums[t * WIN : (t + 1) * WIN, :]
-            places.append((angle, rows, values))
-        for angle, rows, values in places:
-            acc_ref[angle, rows, :] = values
-
-
-def spread_rays(acc_ref, direct_ref, mirror_ref, total_ref, slices):
-    both = 2 * slices
-
-    def spread(t):
-        rows = jnp.transpose(acc_ref[t]) * (1.0 / ROI)
-        direct_ref[t] = rows[0:slices] + rows[both : both + slices]
-        mirror_ref[t] = rows[slices:both] + rows[both + slices : 2 * both]
-        if total_ref is not None:
-            total_ref[t] = rows[2 * both : 2 * both + slices]
-
-    repeat(acc_ref.shape[0], spread, 8)
+            piece = pltpu.roll(piece, (LANES - turn_ref[index]) % LANES, 1)
+            places.append((angle, tile, acc_ref[angle, tile] + piece))
+        for angle, tile, values in places:
+            acc_ref[angle, tile] = values
+
+
+def join_tiles(acc_ref, rows):
+    lane = lax.broadcasted_iota(jnp.int32, (acc_ref.shape[0], ROWS, LANES), 2)
+    middle = pltpu.roll(acc_ref[:, 1, rows, :], SPLIT, 2)
+    left = acc_ref[:, 0, rows, :] + jnp.where(lane >= SPLIT, middle, 0.0)
+    right = acc_ref[:, 2, rows, :] + jnp.where(lane < SPLIT, middle, 0.0)
+    return jnp.concatenate([left, right], axis=2) * (1.0 / ROI)
 
 
 def turn_rays(values, flip):
@@ -340,8 +351,9 @@
 
 def first_kernel(
     sizes,
-    offset_ref,
     place_ref,
+    tile_ref,
+    turn_ref,
     slot_ref,
     cos_ref,
     sin_ref,
@@ -385,21 +397,25 @@
     weights.prepare(shift_x_ref, shift_y_ref, cos_ref, sin_ref)
     acc_ref[...] = jnp.zeros(acc_ref.shape, f32)
 
+    rest = (both, sizes, tile_ref, turn_ref, acc_ref)
+
     def two(index, carry):
         q = 2 * index
         for c in range(angles // chunk):
             weights.make(q, c, even_ref)
             operand = ray_operand(start_ref[q], True)
-            project_pair(even_ref[...], operand, q, c, sizes, offset_ref, acc_ref)
+            project_pair(even_ref[...], operand, q, c, *rest)
             weights.make(q + 1, c, odd_ref)
             operand = ray_operand(start_ref[q + 1], True)
-            project_pair(odd_ref[...], operand, q + 1, c, sizes, offset_ref, acc_ref)
+            project_pair(odd_ref[...], operand, q + 1, c, *rest)
         return carry
 
     lax.fori_loop(0, pairs // 2, two, 0)
-    spread_rays(acc_ref, predicted_ref, mirror_ref, gain_ref, slices)
-    predicted_ref[...] = predicted_ref[...] + turn_rays(mirror_ref[0:angles], flip)
-    direct = gain_ref[...]
+    direct, mirror, weight_sums = (
+        join_tiles(acc_ref, slice(part * ROWS, (part + 1) * ROWS)) for part in range(3)
+    )
+    predicted_ref[...] = direct + turn_rays(mirror, flip)
+    direct = weight_sums
     gain_ref[...] = 1.0 / jnp.maximum(direct + turn_rays(direct, flip), row_floor)
 
 
@@ -407,7 +423,6 @@
     sizes,
     step_size,
     rank_ref,
-    offset_ref,
     place_ref,
     tile_ref,
     turn_ref,
@@ -437,6 +452,7 @@
     weights.prepare(shift_x_ref, shift_y_ref, cos_ref, sin_ref)
     chunks = angles // chunk
     windows = (sizes, window_ref, tile_ref, turn_ref)
+    windows_out = (both, sizes, tile_ref, turn_ref, acc_ref)
     fill_windows(
         (sino_ref[...] - predicted_ref[...]) * gain_ref[...] * (1.0 / ROI), flip, window_ref
     )
@@ -448,7 +464,7 @@
         return start_ref[q] + step_size * total
 
     def forward(values, q, held):
-        project_pair(held, ray_operand(values, False), q, 0, sizes, offset_ref, acc_ref)
+        project_pair(held, ray_operand(values, False), q, 0, *windows_out)
 
     def cycle(index, values):
         for step in range(CYCLE):
@@ -481,7 +497,7 @@
         operand = ray_operand(start_ref[q] + step_size * update_ref[q], False)
         all_chunks(
             q,
-            lambda c, held: project_pair(held, operand, q, c, sizes, offset_ref, acc_ref),
+            lambda c, held: project_pair(held, operand, q, c, *windows_out),
         )
         return carry
 
@@ -494,9 +510,10 @@
         lax.fori_loop(0, pairs, plain_update, 0)
         lax.fori_loop(0, pairs, plain_forward, 0)
 
-    spread_rays(acc_ref, direct_ref, mirror_ref, None, slices)
-    turned = turn_rays(mirror_ref[0:angles], flip)
-    direct_ref[...] = sino_ref[...] - direct_ref[...] - turned
+    direct, mirror = (
+        join_tiles(acc_ref, slice(part * ROWS, (part + 1) * ROWS)) for part in range(2)
+    )
+    direct_ref[...] = sino_ref[...] - direct - turn_rays(mirror, flip)
     fill_windows(direct_ref[...] * gain_ref[...] * (1.0 / ROI), flip, window_ref)
 
     def last_cycle(index, carry):
@@ -593,7 +610,6 @@
         tile = jnp.minimum(offset // SPLIT, 2)
         local = jnp.arange(angles, dtype=jnp.int32) % chunk * WIN
         turn = (local[None, :] - offset + tile * SPLIT) % LANES
-        self.offset = offset.reshape(-1)
         self.place = place.reshape(-1)
         self.tile = tile.reshape(-1)
         self.turn = turn.reshape(-1)
@@ -608,7 +624,8 @@
         self.fixed = [jnp.asarray(flip), jnp.asarray(shift_x, f32), jnp.asarray(shift_y, f32)]
         self.weight = ((chunk * WIN, 2 * VOX), bf16)
         self.held = (pairs // CYCLE + 1 if angles == chunk else 1,) + self.weight[0]
-        self.acc = ((angles, ACTIVE, LANES), f32)
+        self.acc = ((angles, 3, both, LANES), f32)
+        self.acc_sums = ((angles, 3, both + ROWS, LANES), f32)
         self.along = ((angles, ROWS, VOX), f32)
         self.by_ray = ((angles, slices, ACTIVE), f32)
         self.by_pair = ((pairs, both, VOX), f32)
@@ -618,18 +635,18 @@
         self.sent = [((slices * (slots + angles // rays), ACTIVE), f32)] * rays
 
     def first(self, volume):
-        inputs = [self.offset, self.place, self.slot, self.cosine, self.sine, volume]
+        inputs = [self.place, self.tile, self.turn, self.slot, self.cosine, self.sine, volume]
         return call(
             functools.partial(first_kernel, self.sizes),
             "first",
             inputs + self.fixed,
             [self.by_pair, self.by_ray, self.by_ray],
-            [self.weight, self.weight, self.acc, self.along, self.half, self.mirror],
+            [self.weight, self.weight, self.acc_sums, self.along, self.half, self.mirror],
             14,
         )
 
     def second(self, rank, volume, start, predicted, gain, sino):
-        inputs = [rank.reshape(1), self.offset, self.place, self.tile, self.turn, self.slot]
+        inputs = [rank.reshape(1), self.place, self.tile, self.turn, self.slot]
         inputs += [self.cosine, self.sine, volume, start, predicted, gain, sino]
         scratch = [(self.held, bf16)] * CYCLE
         scratch += [self.acc, self.along, self.by_ray, self.mirror, self.window]
@@ -759,10 +776,10 @@
         own_volume = jnp.pad(own_volume, ((0, 0), (0, more * slots), (0, 0)))
         own_rays = jnp.pad(own_rays, ((0, 0), (0, more), (0, 0)))
 
-    theta, vol_list, own_volume, parts = lax.optimization_barrier(
-        (angles.reshape(-1), vol_list, own_volume, parts)
+    angles, vol_list, own_volume, parts = lax.optimization_barrier(
+        (angles, vol_list, own_volume, parts)
     )
-    sirt = Sirt(theta, vol_list, padded, slots, n_ray, step_size)
+    sirt = Sirt(angles.reshape(-1), vol_list, padded, slots, n_ray, step_size)
     start, predicted, gain = sirt.first(own_volume)
     own_rays, parts, start = lax.optimization_barrier((own_rays, parts, start))
     parts = exchange(parts, "slab")

time: 91.1 us -> 92.8 us (1.019)
  Pallas kernels: 49.6 us -> 51.1 us
    pallas_call x2, Pallas kernels: 37.5 us -> 39 us  [call(): pl.pallas_call(kernel, out_shape=[jax.ShapeDtypeStruct(*value) for value...]
  transfers between devices with their start and end apart: 12 -> 12, of which waited for: 4 -> 4; matrix products, arithmetic and copies ran while one was open for 1% -> 0% of each run, Pallas kernels for 54% -> 54%
where the time goes in v9:
time: 92.8 us; the launch traced here: 92.5 us
  Pallas kernels  51.1 us (55%)
  starting transfers between devices  30.9 us (33%)
  waiting for transfers between devices  8.15 us (9%)
  local copies, waits for them, and re-layouts  1.2 us (1%)
    pallas_call x2, Pallas kernels, call(): pl.pallas_call(kernel, out_shape=[jax.ShapeDtypeStruct(*value) for value...  39 us
    ppermute x10, starting transfers between devices, exchange(): lax.ppermute(pieces[d], axis, [(i, i ^ d) for i in range(count)])  20 us
    all_to_all x2, starting transfers between devices, to_all(): return lax.all_to_all(values, axes, split_axis=0, concat_axis=0, tiled=True)  11 us
    pallas_call x1, Pallas kernels, paganin(): pl.pallas_call(filter_kernel, out_shape=[jax.ShapeDtypeStruct((height //...  9.78 us
    all_to_all x2, waiting for transfers between devices, to_all(): return lax.all_to_all(values, axes, split_axis=0, concat_axis=0, tiled=True)  4.56 us
    ppermute x10, waiting for transfers between devices, exchange(): lax.ppermute(pieces[d], axis, [(i, i ^ d) for i in range(count)])  3.59 us
  transfers between devices with their start and end apart: 12, of which 4 were waited for; matrix products, arithmetic and copies ran while one was open for 0% of the time, Pallas kernels for 54%

profile of v9, /device:TPU:0, one launch (start us, length us, event | category | flops | bytes accessed | tf_op | source)
XLA Modules:
  0.0 92.5 jit_solution(2398442604525551604)
XLA Ops:
  0.6 7.3 %all-to-all-start = ((f32[8,64,256]{2,1,0:T(8,128)}), f32[8,64,256]{2,1,0:T(8,128)S(1)}, u32[]{:S(2)}, u32[]{:S(2)}) async-start(f32[8,64,256]{2,1,0:T(8,128)} %bitcast.9), calls=%async_computation | async-start | bytes 1048576 | tf_op jit(solution)/shard_map/all_to_all | solution.py:768
  7.9 0.1 sub.24
  8.0 0.0 copy-start.2
  8.0 0.0 copy-start.3
  8.0 0.0 copy-start.4
  8.0 9.8 %paganin.1 = (f32[64,2048]{1,0:T(8,128)}, f32[64,2048]{1,0:T(8,128)}, f32[64,2048]{1,0:T(8,128)}, f32[64,2048]{1,0:T(8,128)}, f32[256,256]{1,0:T(8,128)}) custom-call(s32[1]{0:T(128)} %bitcast.1.rank_ref, f32[256,2048]{1,0:T(8,128)} %bitcast.11, f32[264,256]{1,0:T(8,128)} %constant.78.clone.given_ref), custom_call_target="tpu_custom_call" | custom-call | flops 8589934592 | bytes 4194304 | tf_op jit(solution)/shard_map/paganin/pallas_call | solution.py:197
  17.8 4.6 %all-to-all-done.vol_ref = f32[8,64,256]{2,1,0:T(8,128)S(1)} async-done(((f32[8,64,256]{2,1,0:T(8,128)}), f32[8,64,256]{2,1,0:T(8,128)S(1)}, u32[]{:S(2)}, u32[]{:S(2)}) %all-to-all-start) | async-done | bytes 524320 | tf_op jit(solution)/shard_map/all_to_all | solution.py:768
  22.4 0.1 select_reduce_fusion.slot_ref
  22.5 0.1 cos.6.cos_ref
  22.6 0.1 sin.6.sin_ref
  22.7 3.7 %all-to-all-start.1 = ((f32[32,8,256]{2,1,0:T(8,128)}), f32[32,8,256]{2,1,0:T(8,128)S(1)}, u32[]{:S(2)}, u32[]{:S(2)}) async-start(f32[32,8,256]{2,1,0:T(8,128)} %bitcast.10), calls=%async_computation.1 | async-start | bytes 524288 | tf_op jit(solution)/shard_map/all_to_all | solution.py:768
  26.4 0.1 add_add_fusion
  26.5 0.1 add.61
  26.6 0.0 copy-done.2
  26.6 0.0 copy-done.3
  26.6 0.0 copy-done.4
  26.6 0.0 copy-start.11
  26.7 0.0 copy-start.10
  26.7 0.0 copy-start.9
  26.7 14.8 %first.1 = (f32[32,16,256]{2,1,0:T(8,128)S(1)}, f32[32,8,256]{2,1,0:T(8,128)S(1)}, f32[32,8,256]{2,1,0:T(8,128)S(1)}) custom-call(f32[1024]{0:T(1024)S(1)} %fusion.place_ref, s32[1024]{0:T(1024)S(1)} %get-tuple-element.97.tile_ref, s32[1024]{0:T(1024)S(1)} %get-tuple-element.96.turn_ref, s32[64]{0:T(128)S(1)} %select_reduce_fusion.slot_ref, ...), custom_call_target="tpu_custom_call" | custom-call | flops 14000000000 | bytes 4194304 | tf_op jit(solution)/shard_map/first/pallas_call | solution.py:570
  41.5 0.0 copy-start.5
  41.5 0.8 copy-done.5
  42.3 0.0 all-to-all-done.1.sino_ref
  42.3 0.3 collective-permute-start
  42.5 0.0 copy-done.10
  42.6 1.7 %collective-permute-start.1 = (f32[64,2048]{1,0:T(8,128)S(1)}, f32[64,2048]{1,0:T(8,128)S(1)}, u32[]{:S(2)}, u32[]{:S(2)}) collective-permute-start(f32[64,2048]{1,0:T(8,128)S(1)} %copy-done.10), channel_id=1, source_target_pairs={{0,16},{8,24},{16,0},{24,8},{1,17},{9,25},{17,1},{25,9},{2,18},{10... | collective-permute-start | bytes 1572872 | tf_op jit(solution)/shard_map/ppermute | solution.py:750
  44.2 0.0 collective-permute-start.2
  44.3 24.3 %second.1 = (f32[96,256]{1,0:T(8,128)S(1)}, f32[96,256]{1,0:T(8,128)S(1)}, f32[96,256]{1,0:T(8,128)S(1)}, f32[96,256]{1,0:T(8,128)S(1)}, f32[96,256]{1,0:T(8,128...) custom-call(s32[1]{0:T(128)} %bitcast.rank_ref, f32[1024]{0:T(1024)S(1)} %fusion.place_ref, ...), custom_call_target="tpu_custom_call" | custom-call | flops 25999998976 | bytes 4194304 | tf_op jit(solution)/shard_map/second/pallas_call | solution.py:570
  68.5 0.0 collective-permute-done.refs_1_
  68.5 0.0 collective-permute-done.1.refs_2_
  68.5 0.0 collective-permute-done.2.refs_3_
  68.6 4.5 %collective-permute-start.3 = (f32[96,256]{1,0:T(8,128)S(1)}, f32[96,256]{1,0:T(8,128)S(1)}, u32[]{:S(2)}, u32[]{:S(2)}) collective-permute-start(f32[96,256]{1,0:T(8,128)S(1)} %get-tuple-element.78), channel_id=1, source_target_pairs={{0,7},{1,6},{2,5},{3,4},{4,3},{5,2},{6,1},{7,0},{8,15},{9,14},{10,... | collective-permute-start | bytes 294920 | tf_op jit(solution)/shard_map/ppermute | solution.py:750
  73.0 0.5 collective-permute-start.4
  73.5 0.6 collective-permute-start.5
  74.1 2.2 %collective-permute-start.6 = (f32[96,256]{1,0:T(8,128)S(1)}, f32[96,256]{1,0:T(8,128)S(1)}, u32[]{:S(2)}, u32[]{:S(2)}) collective-permute-start(f32[96,256]{1,0:T(8,128)S(1)} %get-tuple-element.81), channel_id=1, source_target_pairs={{0,4},{1,5},{2,6},{3,7},{4,0},{5,1},{6,2},{7,3},{8,12},{9,13},{10,... | collective-permute-start | bytes 294920 | tf_op jit(solution)/shard_map/ppermute | solution.py:750
  76.3 2.1 %collective-permute-start.7 = (f32[96,256]{1,0:T(8,128)S(1)}, f32[96,256]{1,0:T(8,128)S(1)}, u32[]{:S(2)}, u32[]{:S(2)}) collective-permute-start(f32[96,256]{1,0:T(8,128)S(1)} %get-tuple-element.82), channel_id=1, source_target_pairs={{0,3},{1,2},{2,1},{3,0},{4,7},{5,6},{6,5},{7,4},{8,11},{9,10},{10,... | collective-permute-start | bytes 294920 | tf_op jit(solution)/shard_map/ppermute | solution.py:750
  78.3 0.0 collective-permute-done.3.refs_0_
  78.3 6.8 %collective-permute-start.8 = (f32[96,256]{1,0:T(8,128)S(1)}, f32[96,256]{1,0:T(8,128)S(1)}, u32[]{:S(2)}, u32[]{:S(2)}) collective-permute-start(f32[96,256]{1,0:T(8,128)S(1)} %get-tuple-element.83), channel_id=1, source_target_pairs={{0,2},{1,3},{2,0},{3,1},{4,6},{5,7},{6,4},{7,5},{8,10},{9,11},{10,... | collective-permute-start | bytes 294920 | tf_op jit(solution)/shard_map/ppermute | solution.py:750
  85.2 0.0 collective-permute-done.4.refs_1_
  85.2 1.4 %collective-permute-start.9 = (f32[96,256]{1,0:T(8,128)S(1)}, f32[96,256]{1,0:T(8,128)S(1)}, u32[]{:S(2)}, u32[]{:S(2)}) collective-permute-start(f32[96,256]{1,0:T(8,128)S(1)} %get-tuple-element.84), channel_id=1, source_target_pairs={{0,1},{1,0},{2,3},{3,2},{4,5},{5,4},{6,7},{7,6},{8,9},{9,8},{10,11... | collective-permute-start | bytes 294920 | tf_op jit(solution)/shard_map/ppermute | solution.py:750
  86.6 0.0 copy-done
  86.6 1.3 %gather_parts.1.refs_8_ = f32[4,64,2048]{2,1,0:T(8,128)} custom-call(s32[1]{0:T(128)} %bitcast.1.rank_ref, f32[64,2048]{1,0:T(8,128)S(1)} %copy-done, f32[64,2048]{1,0:T(8,128)S(1)} %collective-permute-done.refs_1_, f32[64,2048]{1,0:T(8,128)S(1)} %collective-permute-done.1.refs_2_, f32[64,2048]{1,0:T(8,128)S(1)} %collective-permute-done.2.refs_3_), custom_call_target="tpu_custom_call" | custom-call | bytes 4194304 | tf_op jit(solution)/shard_map/gather_parts/pallas_call | solution.py:678
  88.0 1.0 %collective-permute-done.5.refs_2_ = f32[96,256]{1,0:T(8,128)S(1)} collective-permute-done((f32[96,256]{1,0:T(8,128)S(1)}, f32[96,256]{1,0:T(8,128)S(1)}, u32[]{:S(2)}, u32[]{:S(2)}) %collective-permute-start.5) | collective-permute-done | bytes 98336 | tf_op jit(solution)/shard_map/ppermute | solution.py:750
  89.0 1.7 %collective-permute-done.6.refs_3_ = f32[96,256]{1,0:T(8,128)S(1)} collective-permute-done((f32[96,256]{1,0:T(8,128)S(1)}, f32[96,256]{1,0:T(8,128)S(1)}, u32[]{:S(2)}, u32[]{:S(2)}) %collective-permute-start.6) | collective-permute-done | bytes 98336 | tf_op jit(solution)/shard_map/ppermute | solution.py:750
  90.6 0.0 collective-permute-done.7.refs_4_
  90.6 0.9 collective-permute-done.8.refs_5_
  91.5 0.0 collective-permute-done.9.refs_6_
  91.5 0.9 %finish.1 = (f32[64,8,256]{2,1,0:T(8,128)}, f32[4,64,2048]{2,1,0:T(8,128)}) custom-call(s32[1]{0:T(128)} %bitcast.rank_ref, f32[96,256]{1,0:T(8,128)S(1)} %collective-permute-done.3.refs_0_, f32[96,256]{1,0:T(8,128)S(1)} %collective-permute-done.4.refs_1_, f32[96,256]{1,0:T(8,128)S(1)} %collective-permute-done.5.refs_2_, ...), custom_call_target="tpu_custom_call", output_to_operand_aliasing={{1}: (9, {})} | custom-call | bytes 1572864 | tf_op jit(solution)/shard_map/finish/pallas_call | solution.py:722
  (18 shorter events, 0.1 us)
Async XLA Ops:
  0.6 21.8 %all-to-all-start = ((f32[8,64,256]{2,1,0:T(8,128)}), f32[8,64,256]{2,1,0:T(8,128)S(1)}, u32[]{:S(2)}, u32[]{:S(2)}) async-start(f32[8,64,256]{2,1,0:T(8,128)} %bitcast.9), calls=%async_computation | async-start | bytes 1048576 | tf_op jit(solution)/shard_map/all_to_all | solution.py:768
  8.0 14.4 %copy-start.12 = (s32[64]{0:T(128)S(1)}, s32[64]{0:T(128)}, u32[]{:S(2)}) copy-start(s32[64]{0:T(128)} %param.13) | copy-start | bytes 772
  8.0 14.5 %copy-start.6 = (f32[4,8]{1,0:T(4,128)S(1)}, f32[4,8]{1,0:T(4,128)}, u32[]{:S(2)}) copy-start(f32[4,8]{1,0:T(4,128)} %param.11) | copy-start | bytes 388
  8.0 18.4 %copy-start.7 = (f32[32]{0:T(128)S(1)}, f32[32]{0:T(128)}, u32[]{:S(2)}) copy-start(f32[32]{0:T(128)} %constant.86) | copy-start | bytes 388
  8.0 18.4 %copy-start.8 = (f32[32]{0:T(128)S(1)}, f32[32]{0:T(128)}, u32[]{:S(2)}) copy-start(f32[32]{0:T(128)} %constant.85) | copy-start | bytes 388
  8.0 18.6 %copy-start.2 = (bf16[256,256]{1,0:T(8,128)(2,1)S(1)}, bf16[256,256]{1,0:T(8,128)(2,1)}, u32[]{:S(2)}) copy-start(bf16[256,256]{1,0:T(8,128)(2,1)} %constant.81.clone.flip_ref) | copy-start | bytes 393220
  8.0 18.6 %copy-start.3 = (f32[8,256]{1,0:T(8,128)S(1)}, f32[8,256]{1,0:T(8,128)}, u32[]{:S(2)}) copy-start(f32[8,256]{1,0:T(8,128)} %constant.83.clone.shift_y_ref) | copy-start | bytes 24580
  8.0 18.6 %copy-start.4 = (f32[8,256]{1,0:T(8,128)S(1)}, f32[8,256]{1,0:T(8,128)}, u32[]{:S(2)}) copy-start(f32[8,256]{1,0:T(8,128)} %constant.82.clone.shift_x_ref) | copy-start | bytes 24580
  22.4 19.1 %copy-start.1 = (f32[8,64,256]{2,1,0:T(8,128)}, f32[8,64,256]{2,1,0:T(8,128)S(1)}, u32[]{:S(2)}) copy-start(f32[8,64,256]{2,1,0:T(8,128)S(1)} %all-to-all-done.vol_ref) | copy-start | bytes 1572868
  22.7 19.6 %all-to-all-start.1 = ((f32[32,8,256]{2,1,0:T(8,128)}), f32[32,8,256]{2,1,0:T(8,128)S(1)}, u32[]{:S(2)}, u32[]{:S(2)}) async-start(f32[32,8,256]{2,1,0:T(8,128)} %bitcast.10), calls=%async_computation.1 | async-start | bytes 524288 | tf_op jit(solution)/shard_map/all_to_all | solution.py:768
  26.6 15.6 %copy-start.11 = (f32[64,2048]{1,0:T(8,128)S(1)}, f32[64,2048]{1,0:T(8,128)}, u32[]{:S(2)}) copy-start(f32[64,2048]{1,0:T(8,128)} %get-tuple-element.75) | copy-start | bytes 1572868
  26.7 15.9 %copy-start.10 = (f32[64,2048]{1,0:T(8,128)S(1)}, f32[64,2048]{1,0:T(8,128)}, u32[]{:S(2)}) copy-start(f32[64,2048]{1,0:T(8,128)} %get-tuple-element.76) | copy-start | bytes 1572868
  26.7 17.6 %copy-start.9 = (f32[64,2048]{1,0:T(8,128)S(1)}, f32[64,2048]{1,0:T(8,128)}, u32[]{:S(2)}) copy-start(f32[64,2048]{1,0:T(8,128)} %get-tuple-element.77) | copy-start | bytes 1572868
  41.5 0.8 copy-start.5
  42.3 26.2 %collective-permute-start = (f32[64,2048]{1,0:T(8,128)S(1)}, f32[64,2048]{1,0:T(8,128)S(1)}, u32[]{:S(2)}, u32[]{:S(2)}) collective-permute-start(f32[64,2048]{1,0:T(8,128)S(1)} %copy-done.11), channel_id=1, source_target_pairs={{0,8},{8,0},{16,24},{24,16},{1,9},{9,1},{17,25},{25,17},{2,10},{10... | collective-permute-start | bytes 1572872 | tf_op jit(solution)/shard_map/ppermute | solution.py:750
  42.6 26.0 %collective-permute-start.1 = (f32[64,2048]{1,0:T(8,128)S(1)}, f32[64,2048]{1,0:T(8,128)S(1)}, u32[]{:S(2)}, u32[]{:S(2)}) collective-permute-start(f32[64,2048]{1,0:T(8,128)S(1)} %copy-done.10), channel_id=1, source_target_pairs={{0,16},{8,24},{16,0},{24,8},{1,17},{9,25},{17,1},{25,9},{2,18},{10... | collective-permute-start | bytes 1572872 | tf_op jit(solution)/shard_map/ppermute | solution.py:750
  44.2 24.3 %collective-permute-start.2 = (f32[64,2048]{1,0:T(8,128)S(1)}, f32[64,2048]{1,0:T(8,128)S(1)}, u32[]{:S(2)}, u32[]{:S(2)}) collective-permute-start(f32[64,2048]{1,0:T(8,128)S(1)} %copy-done.9), channel_id=1, source_target_pairs={{0,24},{8,16},{16,8},{24,0},{1,25},{9,17},{17,9},{25,1},{2,26},{10... | collective-permute-start | bytes 1572872 | tf_op jit(solution)/shard_map/ppermute | solution.py:750
  44.3 42.3 %copy-start = (f32[64,2048]{1,0:T(8,128)S(1)}, f32[64,2048]{1,0:T(8,128)}, u32[]{:S(2)}) copy-start(f32[64,2048]{1,0:T(8,128)} %get-tuple-element.86.refs_0_) | copy-start | bytes 1572868
  68.6 9.8 %collective-permute-start.3 = (f32[96,256]{1,0:T(8,128)S(1)}, f32[96,256]{1,0:T(8,128)S(1)}, u32[]{:S(2)}, u32[]{:S(2)}) collective-permute-start(f32[96,256]{1,0:T(8,128)S(1)} %get-tuple-element.78), channel_id=1, source_target_pairs={{0,7},{1,6},{2,5},{3,4},{4,3},{5,2},{6,1},{7,0},{8,15},{9,14},{10,... | collective-permute-start | bytes 294920 | tf_op jit(solution)/shard_map/ppermute | solution.py:750
  73.0 12.1 %collective-permute-start.4 = (f32[96,256]{1,0:T(8,128)S(1)}, f32[96,256]{1,0:T(8,128)S(1)}, u32[]{:S(2)}, u32[]{:S(2)}) collective-permute-start(f32[96,256]{1,0:T(8,128)S(1)} %get-tuple-element.79), channel_id=1, source_target_pairs={{0,6},{1,7},{2,4},{3,5},{4,2},{5,3},{6,0},{7,1},{8,14},{9,15},{10,... | collective-permute-start | bytes 294920 | tf_op jit(solution)/shard_map/ppermute | solution.py:750
  73.5 15.4 %collective-permute-start.5 = (f32[96,256]{1,0:T(8,128)S(1)}, f32[96,256]{1,0:T(8,128)S(1)}, u32[]{:S(2)}, u32[]{:S(2)}) collective-permute-start(f32[96,256]{1,0:T(8,128)S(1)} %get-tuple-element.80), channel_id=1, source_target_pairs={{0,5},{1,4},{2,7},{3,6},{4,1},{5,0},{6,3},{7,2},{8,13},{9,12},{10,... | collective-permute-start | bytes 294920 | tf_op jit(solution)/shard_map/ppermute | solution.py:750
  74.1 16.5 %collective-permute-start.6 = (f32[96,256]{1,0:T(8,128)S(1)}, f32[96,256]{1,0:T(8,128)S(1)}, u32[]{:S(2)}, u32[]{:S(2)}) collective-permute-start(f32[96,256]{1,0:T(8,128)S(1)} %get-tuple-element.81), channel_id=1, source_target_pairs={{0,4},{1,5},{2,6},{3,7},{4,0},{5,1},{6,2},{7,3},{8,12},{9,13},{10,... | collective-permute-start | bytes 294920 | tf_op jit(solution)/shard_map/ppermute | solution.py:750
  76.3 14.3 %collective-permute-start.7 = (f32[96,256]{1,0:T(8,128)S(1)}, f32[96,256]{1,0:T(8,128)S(1)}, u32[]{:S(2)}, u32[]{:S(2)}) collective-permute-start(f32[96,256]{1,0:T(8,128)S(1)} %get-tuple-element.82), channel_id=1, source_target_pairs={{0,3},{1,2},{2,1},{3,0},{4,7},{5,6},{6,5},{7,4},{8,11},{9,10},{10,... | collective-permute-start | bytes 294920 | tf_op jit(solution)/shard_map/ppermute | solution.py:750
  78.3 13.2 %collective-permute-start.8 = (f32[96,256]{1,0:T(8,128)S(1)}, f32[96,256]{1,0:T(8,128)S(1)}, u32[]{:S(2)}, u32[]{:S(2)}) collective-permute-start(f32[96,256]{1,0:T(8,128)S(1)} %get-tuple-element.83), channel_id=1, source_target_pairs={{0,2},{1,3},{2,0},{3,1},{4,6},{5,7},{6,4},{7,5},{8,10},{9,11},{10,... | collective-permute-start | bytes 294920 | tf_op jit(solution)/shard_map/ppermute | solution.py:750
  85.2 6.4 %collective-permute-start.9 = (f32[96,256]{1,0:T(8,128)S(1)}, f32[96,256]{1,0:T(8,128)S(1)}, u32[]{:S(2)}, u32[]{:S(2)}) collective-permute-start(f32[96,256]{1,0:T(8,128)S(1)} %get-tuple-element.84), channel_id=1, source_target_pairs={{0,1},{1,0},{2,3},{3,2},{4,5},{5,4},{6,7},{7,6},{8,9},{9,8},{10,11... | collective-permute-start | bytes 294920 | tf_op jit(solution)/shard_map/ppermute | solution.py:750

commit v10 on v9

--- a/solution.py
+++ b/solution.py
@@ -97,9 +97,9 @@
             )
         )
     given = pltpu.make_async_copy(given_ref, table_ref, sems.at[ROWS])
+    copies[0].start()
     given.start()
-    for copy in copies:
-        copy.start()
+    copies[1].start()
     given.wait()
     cas_high, cas_low = halves(table_ref[0:height, :])
     rho_all = table_ref[height : height + ROWS, :]
@@ -112,6 +112,8 @@
 
     for c in range(ROWS):
         copies[c].wait()
+        if c + 2 < ROWS:
+            copies[c + 2].start()
         image = 1.0 - image_ref[:, c * length : (c + 1) * length]
         spectrum = transform(jnp.transpose(image))
         for b in range(blocks):
@@ -300,6 +302,37 @@
             acc_ref[angle, tile] = values
 
 
+def project_rows(held, operand, q, c, sizes, offset_ref, acc_ref):
+    angles, chunk = sizes[:2]
+    spare = jnp.zeros((LANES - operand.shape[0], operand.shape[1]), bf16)
+    operand = jnp.concatenate([operand, spare], axis=0)
+    sums = lax.dot_general(
+        held, operand, (((1,), (1,)), ((), ())), preferred_element_type=f32
+    )
+    for begin in range(0, chunk, GROUP):
+        places = []
+        for t in range(begin, min(begin + GROUP, chunk)):
+            angle = c * chunk + t
+            rows = pl.ds(offset_ref[q * angles + angle], WIN)
+            values = acc_ref[angle, rows, :] + sums[t * WIN : (t + 1) * WIN, :]
+            places.append((angle, rows, values))
+        for angle, rows, values in places:
+            acc_ref[angle, rows, :] = values
+
+
+def spread_rays(acc_ref, direct_ref, mirror_ref, total_ref, slices):
+    both = 2 * slices
+
+    def spread(t):
+        rows = jnp.transpose(acc_ref[t]) * (1.0 / ROI)
+        direct_ref[t] = rows[0:slices] + rows[both : both + slices]
+        mirror_ref[t] = rows[slices:both] + rows[both + slices : 2 * both]
+        if total_ref is not None:
+            total_ref[t] = rows[2 * both : 2 * both + slices]
+
+    repeat(acc_ref.shape[0], spread, 8)
+
+
 def join_tiles(acc_ref, rows):
     lane = lax.broadcasted_iota(jnp.int32, (acc_ref.shape[0], ROWS, LANES), 2)
     middle = pltpu.roll(acc_ref[:, 1, rows, :], SPLIT, 2)
@@ -352,8 +385,7 @@
 def first_kernel(
     sizes,
     place_ref,
-    tile_ref,
-    turn_ref,
+    offset_ref,
     slot_ref,
     cos_ref,
     sin_ref,
@@ -361,16 +393,13 @@
     flip_ref,
     shift_x_ref,
     shift_y_ref,
-    start_ref,
+    kept_ref,
     predicted_ref,
     gain_ref,
-    even_ref,
-    odd_ref,
-    acc_ref,
-    along_ref,
-    half_ref,
-    mirror_ref,
+    *refs,
 ):
+    held_refs = refs[:CYCLE]
+    acc_ref, along_ref, half_ref, mirror_ref, start_ref, sem = refs[CYCLE:]
     angles, chunk, slots = sizes
     patches = slot_ref.shape[0]
     pairs, both, _ = start_ref.shape
@@ -397,26 +426,30 @@
     weights.prepare(shift_x_ref, shift_y_ref, cos_ref, sin_ref)
     acc_ref[...] = jnp.zeros(acc_ref.shape, f32)
 
-    rest = (both, sizes, tile_ref, turn_ref, acc_ref)
-
-    def two(index, carry):
-        q = 2 * index
-        for c in range(angles // chunk):
-            weights.make(q, c, even_ref)
+    kept = pltpu.make_async_copy(start_ref, kept_ref, sem)
+    kept.start()
+    chunks = angles // chunk
+
+    def cycle(index, carry):
+        for step in range(CYCLE):
+            q = index * CYCLE + step
             operand = ray_operand(start_ref[q], True)
-            project_pair(even_ref[...], operand, q, c, *rest)
-            weights.make(q + 1, c, odd_ref)
-            operand = ray_operand(start_ref[q + 1], True)
-            project_pair(odd_ref[...], operand, q + 1, c, *rest)
+            for c in range(chunks):
+                more = jnp.minimum(q + (c + 1) // chunks, pairs - 1)
+                after = (step * chunks + c + 1) % CYCLE
+                weights.make(more, (c + 1) % chunks, held_refs[after])
+                here = held_refs[(step * chunks + c) % CYCLE][...]
+                project_rows(here, operand, q, c, sizes, offset_ref, acc_ref)
         return carry
 
-    lax.fori_loop(0, pairs // 2, two, 0)
-    direct, mirror, weight_sums = (
-        join_tiles(acc_ref, slice(part * ROWS, (part + 1) * ROWS)) for part in range(3)
-    )
+    weights.make(0, 0, held_refs[0])
+    lax.fori_loop(0, pairs // CYCLE, cycle, 0)
+    spread_rays(acc_ref, predicted_ref, mirror_ref, gain_ref, slices)
+    direct, mirror, weight_sums = predicted_ref[...], mirror_ref[0:angles], gain_ref[...]
     predicted_ref[...] = direct + turn_rays(mirror, flip)
     direct = weight_sums
     gain_ref[...] = 1.0 / jnp.maximum(direct + turn_rays(direct, flip), row_floor)
+    kept.wait()
 
 
 def second_kernel(
@@ -430,20 +463,25 @@
     cos_ref,
     sin_ref,
     vol_ref,
-    start_ref,
     predicted_ref,
     gain_ref,
     sino_ref,
     flip_ref,
     shift_x_ref,
     shift_y_ref,
+    kept_ref,
     *refs,
 ):
     angles, chunk, slots = sizes
     rays = vol_ref.shape[0]
     out_refs, refs = refs[:rays], refs[rays:]
     held_refs = refs[:CYCLE]
-    acc_ref, along_ref, direct_ref, mirror_ref, window_ref, update_ref, half_ref = refs[CYCLE:]
+    acc_ref, along_ref, direct_ref, mirror_ref, window_ref, update_ref, half_ref = refs[
+        CYCLE:-2
+    ]
+    start_ref, sem = refs[-2:]
+    kept = pltpu.make_async_copy(kept_ref, start_ref, sem)
+    kept.start()
     patches = slot_ref.shape[0]
     pairs, both, _ = start_ref.shape
     slices = both // 2
@@ -457,6 +495,7 @@
         (sino_ref[...] - predicted_ref[...]) * gain_ref[...] * (1.0 / ROI), flip, window_ref
     )
     acc_ref[...] = jnp.zeros(acc_ref.shape, f32)
+    kept.wait()
 
     def advance(q, held):
         total = update_pair(held, q, 0, *windows)
@@ -564,21 +603,23 @@
             out_ref[begin : begin + slices, :] = direct_ref[k * rays + ray]
 
 
-def call(kernel, name, inputs, outputs, scratch, micros):
+def call(kernel, name, inputs, held_in, held_out, outputs, scratch, micros):
     smem = pl.BlockSpec(memory_space=pltpu.SMEM)
     vmem = pl.BlockSpec(memory_space=pltpu.VMEM)
+    hbm = pl.BlockSpec(memory_space=pltpu.HBM)
     return pl.pallas_call(
         kernel,
-        out_shape=[jax.ShapeDtypeStruct(*value) for value in outputs],
-        in_specs=[smem if value.ndim == 1 else vmem for value in inputs],
-        out_specs=[vmem] * len(outputs),
-        scratch_shapes=[pltpu.VMEM(*value) for value in scratch],
+        out_shape=[jax.ShapeDtypeStruct(*value) for value in held_out + outputs],
+        in_specs=[smem if value.ndim == 1 else vmem for value in inputs] + [hbm] * len(held_in),
+        out_specs=[hbm] * len(held_out) + [vmem] * len(outputs),
+        scratch_shapes=[pltpu.VMEM(*value) for value in scratch]
+        + [pltpu.SemaphoreType.DMA],
         compiler_params=pltpu.CompilerParams(vmem_limit_bytes=52 * 2**20),
         cost_estimate=pl.CostEstimate(
             flops=int(micros * 1e9), bytes_accessed=4 * 2**20, transcendentals=0
         ),
         name=name,
-    )(*inputs)
+    )(*inputs, *held_in)
 
 
 class Sirt:
@@ -610,6 +651,7 @@
         tile = jnp.minimum(offset // SPLIT, 2)
         local = jnp.arange(angles, dtype=jnp.int32) % chunk * WIN
         turn = (local[None, :] - offset + tile * SPLIT) % LANES
+        self.offset = offset.reshape(-1)
         self.place = place.reshape(-1)
         self.tile = tile.reshape(-1)
         self.turn = turn.reshape(-1)
@@ -625,7 +667,7 @@
         self.weight = ((chunk * WIN, 2 * VOX), bf16)
         self.held = (pairs // CYCLE + 1 if angles == chunk else 1,) + self.weight[0]
         self.acc = ((angles, 3, both, LANES), f32)
-        self.acc_sums = ((angles, 3, both + ROWS, LANES), f32)
+        self.acc_rows = ((angles, ACTIVE, LANES), f32)
         self.along = ((angles, ROWS, VOX), f32)
         self.by_ray = ((angles, slices, ACTIVE), f32)
         self.by_pair = ((pairs, both, VOX), f32)
@@ -635,27 +677,32 @@
         self.sent = [((slices * (slots + angles // rays), ACTIVE), f32)] * rays
 
     def first(self, volume):
-        inputs = [self.place, self.tile, self.turn, self.slot, self.cosine, self.sine, volume]
+        inputs = [self.place, self.offset, self.slot, self.cosine, self.sine, volume]
         return call(
             functools.partial(first_kernel, self.sizes),
             "first",
             inputs + self.fixed,
-            [self.by_pair, self.by_ray, self.by_ray],
-            [self.weight, self.weight, self.acc_sums, self.along, self.half, self.mirror],
+            [],
+            [self.by_pair],
+            [self.by_ray, self.by_ray],
+            [self.weight] * CYCLE
+            + [self.acc_rows, self.along, self.half, self.mirror, self.by_pair],
             14,
         )
 
     def second(self, rank, volume, start, predicted, gain, sino):
         inputs = [rank.reshape(1), self.place, self.tile, self.turn, self.slot]
-        inputs += [self.cosine, self.sine, volume, start, predicted, gain, sino]
+        inputs += [self.cosine, self.sine, volume, predicted, gain, sino]
         scratch = [(self.held, bf16)] * CYCLE
         scratch += [self.acc, self.along, self.by_ray, self.mirror, self.window]
         return call(
             functools.partial(second_kernel, self.sizes, self.step_size),
             "second",
             inputs + self.fixed,
+            [start],
+            [],
             self.sent,
-            scratch + [self.by_pair, self.half],
+            scratch + [self.by_pair, self.half, self.by_pair],
             26,
         )
 

time: 92.8 us -> 90.9 us (0.980)
  Pallas kernels: 51.1 us -> 49.7 us
    pallas_call x2, Pallas kernels: 39 us -> 37.1 us  [call(): pl.pallas_call(kernel, out_shape=[jax.ShapeDtypeStruct(*value) for value...]
where the time goes in v10:
time: 90.9 us; the launch traced here: 90.5 us
  Pallas kernels  49.7 us (55%)
  starting transfers between devices  30.9 us (34%)
  waiting for transfers between devices  7.65 us (8%)
  local copies, waits for them, and re-layouts  1.2 us (1%)
    pallas_call x2, Pallas kernels, call(): pl.pallas_call(kernel, out_shape=[jax.ShapeDtypeStruct(*value) for value...  37.1 us
    ppermute x10, starting transfers between devices, exchange(): lax.ppermute(pieces[d], axis, [(i, i ^ d) for i in range(count)])  20 us
    all_to_all x2, starting transfers between devices, to_all(): return lax.all_to_all(values, axes, split_axis=0, concat_axis=0, tiled=True)  11 us
    pallas_call x1, Pallas kernels, paganin(): pl.pallas_call(filter_kernel, out_shape=[jax.ShapeDtypeStruct((height //...  10.3 us
    all_to_all x2, waiting for transfers between devices, to_all(): return lax.all_to_all(values, axes, split_axis=0, concat_axis=0, tiled=True)  4.04 us
    ppermute x10, waiting for transfers between devices, exchange(): lax.ppermute(pieces[d], axis, [(i, i ^ d) for i in range(count)])  3.61 us
  transfers between devices with their start and end apart: 12, of which 4 were waited for; matrix products, arithmetic and copies ran while one was open for 0% of the time, Pallas kernels for 54%

profile of v10, /device:TPU:0, one launch (start us, length us, event | category | flops | bytes accessed | tf_op | source)
XLA Modules:
  0.0 90.5 jit_solution(12007529317080817935)
XLA Ops:
  0.6 7.3 %all-to-all-start = ((f32[8,64,256]{2,1,0:T(8,128)}), f32[8,64,256]{2,1,0:T(8,128)S(1)}, u32[]{:S(2)}, u32[]{:S(2)}) async-start(f32[8,64,256]{2,1,0:T(8,128)} %bitcast.9), calls=%async_computation | async-start | bytes 1048576 | tf_op jit(solution)/shard_map/all_to_all | solution.py:815
  7.9 0.1 sub.24
  8.0 0.0 copy-start.2
  8.0 0.0 copy-start.3
  8.0 0.0 copy-start.4
  8.0 10.3 %paganin.1 = (f32[64,2048]{1,0:T(8,128)}, f32[64,2048]{1,0:T(8,128)}, f32[64,2048]{1,0:T(8,128)}, f32[64,2048]{1,0:T(8,128)}, f32[256,256]{1,0:T(8,128)}) custom-call(s32[1]{0:T(128)} %bitcast.1.rank_ref, f32[256,2048]{1,0:T(8,128)} %bitcast.11, f32[264,256]{1,0:T(8,128)} %constant.78.clone.given_ref), custom_call_target="tpu_custom_call" | custom-call | flops 8589934592 | bytes 4194304 | tf_op jit(solution)/shard_map/paganin/pallas_call | solution.py:199
  18.3 4.0 %all-to-all-done.vol_ref = f32[8,64,256]{2,1,0:T(8,128)S(1)} async-done(((f32[8,64,256]{2,1,0:T(8,128)}), f32[8,64,256]{2,1,0:T(8,128)S(1)}, u32[]{:S(2)}, u32[]{:S(2)}) %all-to-all-start) | async-done | bytes 524320 | tf_op jit(solution)/shard_map/all_to_all | solution.py:815
  22.4 0.0 copy-done.12
  22.4 0.1 select_reduce_fusion.slot_ref
  22.5 0.0 copy-done.6
  22.5 0.1 cos.6.cos_ref
  22.6 0.1 sin.6.sin_ref
  22.7 3.7 %all-to-all-start.1 = ((f32[32,8,256]{2,1,0:T(8,128)}), f32[32,8,256]{2,1,0:T(8,128)S(1)}, u32[]{:S(2)}, u32[]{:S(2)}) async-start(f32[32,8,256]{2,1,0:T(8,128)} %bitcast.10), calls=%async_computation.1 | async-start | bytes 524288 | tf_op jit(solution)/shard_map/all_to_all | solution.py:815
  26.4 0.0 copy-done.7
  26.4 0.1 add_add_fusion
  26.5 0.1 add.64
  26.6 0.0 copy-done.2
  26.6 0.0 copy-done.3
  26.6 0.0 copy-done.4
  26.6 0.0 copy-start.11
  26.7 0.0 copy-start.10
  26.7 0.0 copy-start.9
  26.7 12.3 %first.1 = (f32[32,16,256]{2,1,0:T(8,128)S(1)}, f32[32,8,256]{2,1,0:T(8,128)S(1)}, f32[32,8,256]{2,1,0:T(8,128)S(1)}) custom-call(f32[1024]{0:T(1024)S(1)} %fusion.place_ref, s32[1024]{0:T(1024)S(1)} %get-tuple-element.96.offset_ref, s32[64]{0:T(128)S(1)} %select_reduce_fusion.slot_ref, f32[32]{0:T(128)S(1)} %cos.6.cos_ref, f32[32]{0:T(128)S(1)} %sin.6.sin_ref, ...), custom_call_target="tpu_custom_call" | custom-call | flops 14000000000 | bytes 4194304 | tf_op jit(solution)/shard_map/first/pallas_call | solution.py:610
  39.0 0.8 copy-done.5
  39.8 0.0 all-to-all-done.1.sino_ref
  39.8 0.3 collective-permute-start
  40.1 1.7 %collective-permute-start.1 = (f32[64,2048]{1,0:T(8,128)S(1)}, f32[64,2048]{1,0:T(8,128)S(1)}, u32[]{:S(2)}, u32[]{:S(2)}) collective-permute-start(f32[64,2048]{1,0:T(8,128)S(1)} %copy-done.10), channel_id=1, source_target_pairs={{0,16},{8,24},{16,0},{24,8},{1,17},{9,25},{17,1},{25,9},{2,18},{10... | collective-permute-start | bytes 1572872 | tf_op jit(solution)/shard_map/ppermute | solution.py:797
  41.8 0.0 collective-permute-start.2
  41.8 24.8 %second.1 = (f32[96,256]{1,0:T(8,128)S(1)}, f32[96,256]{1,0:T(8,128)S(1)}, f32[96,256]{1,0:T(8,128)S(1)}, f32[96,256]{1,0:T(8,128)S(1)}, f32[96,256]{1,0:T(8,128...) custom-call(s32[1]{0:T(128)} %bitcast.rank_ref, f32[1024]{0:T(1024)S(1)} %fusion.place_ref, ...), custom_call_target="tpu_custom_call" | custom-call | flops 25999998976 | bytes 4194304 | tf_op jit(solution)/shard_map/second/pallas_call | solution.py:610
  66.6 0.0 collective-permute-done.refs_1_
  66.6 0.0 collective-permute-done.1.refs_2_
  66.6 0.0 collective-permute-done.2.refs_3_
  66.6 4.5 %collective-permute-start.3 = (f32[96,256]{1,0:T(8,128)S(1)}, f32[96,256]{1,0:T(8,128)S(1)}, u32[]{:S(2)}, u32[]{:S(2)}) collective-permute-start(f32[96,256]{1,0:T(8,128)S(1)} %get-tuple-element.78), channel_id=1, source_target_pairs={{0,7},{1,6},{2,5},{3,4},{4,3},{5,2},{6,1},{7,0},{8,15},{9,14},{10,... | collective-permute-start | bytes 294920 | tf_op jit(solution)/shard_map/ppermute | solution.py:797
  71.1 0.5 collective-permute-start.4
  71.6 0.6 collective-permute-start.5
  72.2 2.1 %collective-permute-start.6 = (f32[96,256]{1,0:T(8,128)S(1)}, f32[96,256]{1,0:T(8,128)S(1)}, u32[]{:S(2)}, u32[]{:S(2)}) collective-permute-start(f32[96,256]{1,0:T(8,128)S(1)} %get-tuple-element.81), channel_id=1, source_target_pairs={{0,4},{1,5},{2,6},{3,7},{4,0},{5,1},{6,2},{7,3},{8,12},{9,13},{10,... | collective-permute-start | bytes 294920 | tf_op jit(solution)/shard_map/ppermute | solution.py:797
  74.3 2.1 %collective-permute-start.7 = (f32[96,256]{1,0:T(8,128)S(1)}, f32[96,256]{1,0:T(8,128)S(1)}, u32[]{:S(2)}, u32[]{:S(2)}) collective-permute-start(f32[96,256]{1,0:T(8,128)S(1)} %get-tuple-element.82), channel_id=1, source_target_pairs={{0,3},{1,2},{2,1},{3,0},{4,7},{5,6},{6,5},{7,4},{8,11},{9,10},{10,... | collective-permute-start | bytes 294920 | tf_op jit(solution)/shard_map/ppermute | solution.py:797
  76.4 0.0 collective-permute-done.3.refs_0_
  76.4 6.8 %collective-permute-start.8 = (f32[96,256]{1,0:T(8,128)S(1)}, f32[96,256]{1,0:T(8,128)S(1)}, u32[]{:S(2)}, u32[]{:S(2)}) collective-permute-start(f32[96,256]{1,0:T(8,128)S(1)} %get-tuple-element.83), channel_id=1, source_target_pairs={{0,2},{1,3},{2,0},{3,1},{4,6},{5,7},{6,4},{7,5},{8,10},{9,11},{10,... | collective-permute-start | bytes 294920 | tf_op jit(solution)/shard_map/ppermute | solution.py:797
  83.2 0.0 collective-permute-done.4.refs_1_
  83.2 1.4 %collective-permute-start.9 = (f32[96,256]{1,0:T(8,128)S(1)}, f32[96,256]{1,0:T(8,128)S(1)}, u32[]{:S(2)}, u32[]{:S(2)}) collective-permute-start(f32[96,256]{1,0:T(8,128)S(1)} %get-tuple-element.84), channel_id=1, source_target_pairs={{0,1},{1,0},{2,3},{3,2},{4,5},{5,4},{6,7},{7,6},{8,9},{9,8},{10,11... | collective-permute-start | bytes 294920 | tf_op jit(solution)/shard_map/ppermute | solution.py:797
  84.6 1.3 %gather_parts.1.refs_8_ = f32[4,64,2048]{2,1,0:T(8,128)} custom-call(s32[1]{0:T(128)} %bitcast.1.rank_ref, f32[64,2048]{1,0:T(8,128)S(1)} %copy-done, f32[64,2048]{1,0:T(8,128)S(1)} %collective-permute-done.refs_1_, f32[64,2048]{1,0:T(8,128)S(1)} %collective-permute-done.1.refs_2_, f32[64,2048]{1,0:T(8,128)S(1)} %collective-permute-done.2.refs_3_), custom_call_target="tpu_custom_call" | custom-call | bytes 4194304 | tf_op jit(solution)/shard_map/gather_parts/pallas_call | solution.py:725
  86.0 1.0 %collective-permute-done.5.refs_2_ = f32[96,256]{1,0:T(8,128)S(1)} collective-permute-done((f32[96,256]{1,0:T(8,128)S(1)}, f32[96,256]{1,0:T(8,128)S(1)}, u32[]{:S(2)}, u32[]{:S(2)}) %collective-permute-start.5) | collective-permute-done | bytes 98336 | tf_op jit(solution)/shard_map/ppermute | solution.py:797
  87.0 1.7 %collective-permute-done.6.refs_3_ = f32[96,256]{1,0:T(8,128)S(1)} collective-permute-done((f32[96,256]{1,0:T(8,128)S(1)}, f32[96,256]{1,0:T(8,128)S(1)}, u32[]{:S(2)}, u32[]{:S(2)}) %collective-permute-start.6) | collective-permute-done | bytes 98336 | tf_op jit(solution)/shard_map/ppermute | solution.py:797
  88.7 0.0 collective-permute-done.7.refs_4_
  88.7 0.9 collective-permute-done.8.refs_5_
  89.6 0.0 collective-permute-done.9.refs_6_
  89.6 0.9 %finish.1 = (f32[64,8,256]{2,1,0:T(8,128)}, f32[4,64,2048]{2,1,0:T(8,128)}) custom-call(s32[1]{0:T(128)} %bitcast.rank_ref, f32[96,256]{1,0:T(8,128)S(1)} %collective-permute-done.3.refs_0_, f32[96,256]{1,0:T(8,128)S(1)} %collective-permute-done.4.refs_1_, f32[96,256]{1,0:T(8,128)S(1)} %collective-permute-done.5.refs_2_, ...), custom_call_target="tpu_custom_call", output_to_operand_aliasing={{1}: (9, {})} | custom-call | bytes 1572864 | tf_op jit(solution)/shard_map/finish/pallas_call | solution.py:769
  (18 shorter events, 0.1 us)
Async XLA Ops:
  0.6 21.8 %all-to-all-start = ((f32[8,64,256]{2,1,0:T(8,128)}), f32[8,64,256]{2,1,0:T(8,128)S(1)}, u32[]{:S(2)}, u32[]{:S(2)}) async-start(f32[8,64,256]{2,1,0:T(8,128)} %bitcast.9), calls=%async_computation | async-start | bytes 1048576 | tf_op jit(solution)/shard_map/all_to_all | solution.py:815
  8.0 14.4 %copy-start.12 = (s32[64]{0:T(128)S(1)}, s32[64]{0:T(128)}, u32[]{:S(2)}) copy-start(s32[64]{0:T(128)} %param.13) | copy-start | bytes 772
  8.0 14.5 %copy-start.6 = (f32[4,8]{1,0:T(4,128)S(1)}, f32[4,8]{1,0:T(4,128)}, u32[]{:S(2)}) copy-start(f32[4,8]{1,0:T(4,128)} %param.11) | copy-start | bytes 388
  8.0 18.4 %copy-start.7 = (f32[32]{0:T(128)S(1)}, f32[32]{0:T(128)}, u32[]{:S(2)}) copy-start(f32[32]{0:T(128)} %constant.86) | copy-start | bytes 388
  8.0 18.4 %copy-start.8 = (f32[32]{0:T(128)S(1)}, f32[32]{0:T(128)}, u32[]{:S(2)}) copy-start(f32[32]{0:T(128)} %constant.85) | copy-start | bytes 388
  8.0 18.6 %copy-start.2 = (bf16[256,256]{1,0:T(8,128)(2,1)S(1)}, bf16[256,256]{1,0:T(8,128)(2,1)}, u32[]{:S(2)}) copy-start(bf16[256,256]{1,0:T(8,128)(2,1)} %constant.81.clone.flip_ref) | copy-start | bytes 393220
  8.0 18.6 %copy-start.3 = (f32[8,256]{1,0:T(8,128)S(1)}, f32[8,256]{1,0:T(8,128)}, u32[]{:S(2)}) copy-start(f32[8,256]{1,0:T(8,128)} %constant.83.clone.shift_y_ref) | copy-start | bytes 24580
  8.0 18.6 %copy-start.4 = (f32[8,256]{1,0:T(8,128)S(1)}, f32[8,256]{1,0:T(8,128)}, u32[]{:S(2)}) copy-start(f32[8,256]{1,0:T(8,128)} %constant.82.clone.shift_x_ref) | copy-start | bytes 24580
  22.4 16.6 %copy-start.1 = (f32[8,64,256]{2,1,0:T(8,128)}, f32[8,64,256]{2,1,0:T(8,128)S(1)}, u32[]{:S(2)}) copy-start(f32[8,64,256]{2,1,0:T(8,128)S(1)} %all-to-all-done.vol_ref) | copy-start | bytes 1572868
  22.7 17.1 %all-to-all-start.1 = ((f32[32,8,256]{2,1,0:T(8,128)}), f32[32,8,256]{2,1,0:T(8,128)S(1)}, u32[]{:S(2)}, u32[]{:S(2)}) async-start(f32[32,8,256]{2,1,0:T(8,128)} %bitcast.10), calls=%async_computation.1 | async-start | bytes 524288 | tf_op jit(solution)/shard_map/all_to_all | solution.py:815
  26.6 13.2 %copy-start.11 = (f32[64,2048]{1,0:T(8,128)S(1)}, f32[64,2048]{1,0:T(8,128)}, u32[]{:S(2)}) copy-start(f32[64,2048]{1,0:T(8,128)} %get-tuple-element.75) | copy-start | bytes 1572868
  26.7 13.4 %copy-start.10 = (f32[64,2048]{1,0:T(8,128)S(1)}, f32[64,2048]{1,0:T(8,128)}, u32[]{:S(2)}) copy-start(f32[64,2048]{1,0:T(8,128)} %get-tuple-element.76) | copy-start | bytes 1572868
  26.7 15.1 %copy-start.9 = (f32[64,2048]{1,0:T(8,128)S(1)}, f32[64,2048]{1,0:T(8,128)}, u32[]{:S(2)}) copy-start(f32[64,2048]{1,0:T(8,128)} %get-tuple-element.77) | copy-start | bytes 1572868
  39.0 0.8 copy-start.5
  39.8 26.8 %collective-permute-start = (f32[64,2048]{1,0:T(8,128)S(1)}, f32[64,2048]{1,0:T(8,128)S(1)}, u32[]{:S(2)}, u32[]{:S(2)}) collective-permute-start(f32[64,2048]{1,0:T(8,128)S(1)} %copy-done.11), channel_id=1, source_target_pairs={{0,8},{8,0},{16,24},{24,16},{1,9},{9,1},{17,25},{25,17},{2,10},{10... | collective-permute-start | bytes 1572872 | tf_op jit(solution)/shard_map/ppermute | solution.py:797
  40.1 26.5 %collective-permute-start.1 = (f32[64,2048]{1,0:T(8,128)S(1)}, f32[64,2048]{1,0:T(8,128)S(1)}, u32[]{:S(2)}, u32[]{:S(2)}) collective-permute-start(f32[64,2048]{1,0:T(8,128)S(1)} %copy-done.10), channel_id=1, source_target_pairs={{0,16},{8,24},{16,0},{24,8},{1,17},{9,25},{17,1},{25,9},{2,18},{10... | collective-permute-start | bytes 1572872 | tf_op jit(solution)/shard_map/ppermute | solution.py:797
  41.8 24.8 %collective-permute-start.2 = (f32[64,2048]{1,0:T(8,128)S(1)}, f32[64,2048]{1,0:T(8,128)S(1)}, u32[]{:S(2)}, u32[]{:S(2)}) collective-permute-start(f32[64,2048]{1,0:T(8,128)S(1)} %copy-done.9), channel_id=1, source_target_pairs={{0,24},{8,16},{16,8},{24,0},{1,25},{9,17},{17,9},{25,1},{2,26},{10... | collective-permute-start | bytes 1572872 | tf_op jit(solution)/shard_map/ppermute | solution.py:797
  41.8 42.8 %copy-start = (f32[64,2048]{1,0:T(8,128)S(1)}, f32[64,2048]{1,0:T(8,128)}, u32[]{:S(2)}) copy-start(f32[64,2048]{1,0:T(8,128)} %get-tuple-element.86.refs_0_) | copy-start | bytes 1572868
  66.6 9.8 %collective-permute-start.3 = (f32[96,256]{1,0:T(8,128)S(1)}, f32[96,256]{1,0:T(8,128)S(1)}, u32[]{:S(2)}, u32[]{:S(2)}) collective-permute-start(f32[96,256]{1,0:T(8,128)S(1)} %get-tuple-element.78), channel_id=1, source_target_pairs={{0,7},{1,6},{2,5},{3,4},{4,3},{5,2},{6,1},{7,0},{8,15},{9,14},{10,... | collective-permute-start | bytes 294920 | tf_op jit(solution)/shard_map/ppermute | solution.py:797
  71.1 12.1 %collective-permute-start.4 = (f32[96,256]{1,0:T(8,128)S(1)}, f32[96,256]{1,0:T(8,128)S(1)}, u32[]{:S(2)}, u32[]{:S(2)}) collective-permute-start(f32[96,256]{1,0:T(8,128)S(1)} %get-tuple-element.79), channel_id=1, source_target_pairs={{0,6},{1,7},{2,4},{3,5},{4,2},{5,3},{6,0},{7,1},{8,14},{9,15},{10,... | collective-permute-start | bytes 294920 | tf_op jit(solution)/shard_map/ppermute | solution.py:797
  71.6 15.4 %collective-permute-start.5 = (f32[96,256]{1,0:T(8,128)S(1)}, f32[96,256]{1,0:T(8,128)S(1)}, u32[]{:S(2)}, u32[]{:S(2)}) collective-permute-start(f32[96,256]{1,0:T(8,128)S(1)} %get-tuple-element.80), channel_id=1, source_target_pairs={{0,5},{1,4},{2,7},{3,6},{4,1},{5,0},{6,3},{7,2},{8,13},{9,12},{10,... | collective-permute-start | bytes 294920 | tf_op jit(solution)/shard_map/ppermute | solution.py:797
  72.2 16.5 %collective-permute-start.6 = (f32[96,256]{1,0:T(8,128)S(1)}, f32[96,256]{1,0:T(8,128)S(1)}, u32[]{:S(2)}, u32[]{:S(2)}) collective-permute-start(f32[96,256]{1,0:T(8,128)S(1)} %get-tuple-element.81), channel_id=1, source_target_pairs={{0,4},{1,5},{2,6},{3,7},{4,0},{5,1},{6,2},{7,3},{8,12},{9,13},{10,... | collective-permute-start | bytes 294920 | tf_op jit(solution)/shard_map/ppermute | solution.py:797
  74.3 14.3 %collective-permute-start.7 = (f32[96,256]{1,0:T(8,128)S(1)}, f32[96,256]{1,0:T(8,128)S(1)}, u32[]{:S(2)}, u32[]{:S(2)}) collective-permute-start(f32[96,256]{1,0:T(8,128)S(1)} %get-tuple-element.82), channel_id=1, source_target_pairs={{0,3},{1,2},{2,1},{3,0},{4,7},{5,6},{6,5},{7,4},{8,11},{9,10},{10,... | collective-permute-start | bytes 294920 | tf_op jit(solution)/shard_map/ppermute | solution.py:797
  76.4 13.2 %collective-permute-start.8 = (f32[96,256]{1,0:T(8,128)S(1)}, f32[96,256]{1,0:T(8,128)S(1)}, u32[]{:S(2)}, u32[]{:S(2)}) collective-permute-start(f32[96,256]{1,0:T(8,128)S(1)} %get-tuple-element.83), channel_id=1, source_target_pairs={{0,2},{1,3},{2,0},{3,1},{4,6},{5,7},{6,4},{7,5},{8,10},{9,11},{10,... | collective-permute-start | bytes 294920 | tf_op jit(solution)/shard_map/ppermute | solution.py:797
  83.2 6.4 %collective-permute-start.9 = (f32[96,256]{1,0:T(8,128)S(1)}, f32[96,256]{1,0:T(8,128)S(1)}, u32[]{:S(2)}, u32[]{:S(2)}) collective-permute-start(f32[96,256]{1,0:T(8,128)S(1)} %get-tuple-element.84), channel_id=1, source_target_pairs={{0,1},{1,0},{2,3},{3,2},{4,5},{5,4},{6,7},{7,6},{8,9},{9,8},{10,11... | collective-permute-start | bytes 294920 | tf_op jit(solution)/shard_map/ppermute | solution.py:797

commit v11 on v10

--- a/solution.py
+++ b/solution.py
@@ -20,6 +20,7 @@
 LANES = 128
 ROWS = 8
 SPLIT = 64
+EDGE = 32
 GROUP = 8
 CYCLE = 4
 
@@ -97,9 +98,9 @@
             )
         )
     given = pltpu.make_async_copy(given_ref, table_ref, sems.at[ROWS])
-    copies[0].start()
     given.start()
-    copies[1].start()
+    for copy in copies:
+        copy.start()
     given.wait()
     cas_high, cas_low = halves(table_ref[0:height, :])
     rho_all = table_ref[height : height + ROWS, :]
@@ -112,8 +113,6 @@
 
     for c in range(ROWS):
         copies[c].wait()
-        if c + 2 < ROWS:
-            copies[c + 2].start()
         image = 1.0 - image_ref[:, c * length : (c + 1) * length]
         spectrum = transform(jnp.transpose(image))
         for b in range(blocks):
@@ -188,7 +187,12 @@
                 )
             )
             sent[-1].start()
-    active_ref[...] = out_ref[:, offset : offset + ACTIVE]
+        if c == (offset + ACTIVE - 1) // length:
+            columns = slice(offset, offset + ACTIVE)
+            sent.append(
+                pltpu.make_async_copy(out_ref.at[:, columns], active_ref, sems.at[0])
+            )
+            sent[-1].start()
     for copy in sent:
         copy.wait()
 
@@ -202,8 +206,7 @@
         + [jax.ShapeDtypeStruct((height, ACTIVE), f32)],
         in_specs=[pl.BlockSpec(memory_space=pltpu.SMEM)]
         + [pl.BlockSpec(memory_space=pltpu.HBM)] * 2,
-        out_specs=[pl.BlockSpec(memory_space=pltpu.HBM)] * parts
-        + [pl.BlockSpec(memory_space=pltpu.VMEM)],
+        out_specs=[pl.BlockSpec(memory_space=pltpu.HBM)] * (parts + 1),
         scratch_shapes=[
             pltpu.VMEM((height, width), f32),
             pltpu.VMEM((height + ROWS, height), f32),
@@ -302,32 +305,48 @@
             acc_ref[angle, tile] = values
 
 
-def project_rows(held, operand, q, c, sizes, offset_ref, acc_ref):
+def row_operands(values):
+    rows = ray_operand(values, True)
+    count, width = rows.shape
+    spare = jnp.zeros((SPLIT - count, width), bf16)
+    empty = jnp.zeros((SPLIT, width), bf16)
+    return (
+        jnp.concatenate([rows, spare, empty], axis=0),
+        jnp.concatenate([empty, rows, spare], axis=0),
+    )
+
+
+def project_rows(held_ref, operands, q, c, sizes, offset_ref, acc_ref):
     angles, chunk = sizes[:2]
-    spare = jnp.zeros((LANES - operand.shape[0], operand.shape[1]), bf16)
-    operand = jnp.concatenate([operand, spare], axis=0)
-    sums = lax.dot_general(
-        held, operand, (((1,), (1,)), ((), ())), preferred_element_type=f32
-    )
+    half = chunk // 2
     for begin in range(0, chunk, GROUP):
+        sums = lax.dot_general(
+            held_ref[begin * WIN : (begin + GROUP) * WIN, :],
+            operands[begin // half],
+            (((1,), (1,)), ((), ())),
+            preferred_element_type=f32,
+        )
         places = []
-        for t in range(begin, min(begin + GROUP, chunk)):
-            angle = c * chunk + t
-            rows = pl.ds(offset_ref[q * angles + angle], WIN)
-            values = acc_ref[angle, rows, :] + sums[t * WIN : (t + 1) * WIN, :]
-            places.append((angle, rows, values))
-        for angle, rows, values in places:
-            acc_ref[angle, rows, :] = values
-
-
-def spread_rays(acc_ref, direct_ref, mirror_ref, total_ref, slices):
+        for t in range(begin, begin + GROUP):
+            rows = pl.ds(offset_ref[q * angles + c * chunk + t], WIN)
+            piece = sums[(t - begin) * WIN : (t - begin + 1) * WIN, :]
+            index = c * half + t % half
+            places.append((index, rows, acc_ref[index, rows, :] + piece))
+        for index, rows, values in places:
+            acc_ref[index, rows, :] = values
+
+
+def spread_rays(acc_ref, direct_ref, mirror_ref, total_ref, slices, chunk):
     both = 2 * slices
-
-    def spread(t):
-        rows = jnp.transpose(acc_ref[t]) * (1.0 / ROI)
-        direct_ref[t] = rows[0:slices] + rows[both : both + slices]
-        mirror_ref[t] = rows[slices:both] + rows[both + slices : 2 * both]
-        if total_ref is not None:
+    half = chunk // 2
+
+    def spread(index):
+        turned = jnp.transpose(acc_ref[index]) * (1.0 / ROI)
+        for part in range(2):
+            rows = turned[part * SPLIT : (part + 1) * SPLIT]
+            t = index // half * chunk + part * half + index % half
+            direct_ref[t] = rows[0:slices] + rows[both : both + slices]
+            mirror_ref[t] = rows[slices:both] + rows[both + slices : 2 * both]
             total_ref[t] = rows[2 * both : 2 * both + slices]
 
     repeat(acc_ref.shape[0], spread, 8)
@@ -433,18 +452,18 @@
     def cycle(index, carry):
         for step in range(CYCLE):
             q = index * CYCLE + step
-            operand = ray_operand(start_ref[q], True)
+            operands = row_operands(start_ref[q])
             for c in range(chunks):
                 more = jnp.minimum(q + (c + 1) // chunks, pairs - 1)
                 after = (step * chunks + c + 1) % CYCLE
                 weights.make(more, (c + 1) % chunks, held_refs[after])
-                here = held_refs[(step * chunks + c) % CYCLE][...]
-                project_rows(here, operand, q, c, sizes, offset_ref, acc_ref)
+                here = held_refs[(step * chunks + c) % CYCLE]
+                project_rows(here, operands, q, c, sizes, offset_ref, acc_ref)
         return carry
 
     weights.make(0, 0, held_refs[0])
     lax.fori_loop(0, pairs // CYCLE, cycle, 0)
-    spread_rays(acc_ref, predicted_ref, mirror_ref, gain_ref, slices)
+    spread_rays(acc_ref, predicted_ref, mirror_ref, gain_ref, slices, chunk)
     direct, mirror, weight_sums = predicted_ref[...], mirror_ref[0:angles], gain_ref[...]
     predicted_ref[...] = direct + turn_rays(mirror, flip)
     direct = weight_sums
@@ -594,13 +613,26 @@
 
     repeat(pairs, finish, 8)
     lead = slices * slots
+    lane = lax.broadcasted_iota(jnp.int32, (slices, LANES), 1)
     for d, out_ref in enumerate(out_refs):
         ray = rank_ref[0] ^ d
         for part in range(2):
             out_ref[0:lead, part * LANES : (part + 1) * LANES] = half_ref[part, ray]
-        for k in range(angles // rays):
-            begin = lead + k * slices
-            out_ref[begin : begin + slices, :] = direct_ref[k * rays + ray]
+        for k in range(0, angles // rays, 4):
+            begin = lead + k // 4 * 3 * slices
+            live = [
+                pltpu.roll(direct_ref[(k + i) * rays + ray], ACTIVE - EDGE, 1)
+                for i in range(4)
+            ]
+            rest = [part[:, LANES:] for part in live]
+            for i in range(2):
+                here = begin + i * slices
+                out_ref[here : here + slices, 0:LANES] = live[2 * i][:, 0:LANES]
+                out_ref[here : here + slices, LANES:] = live[2 * i + 1][:, 0:LANES]
+                here = begin + 2 * slices
+                out_ref[here : here + slices, i * LANES : (i + 1) * LANES] = jnp.where(
+                    lane < SPLIT, rest[2 * i], pltpu.roll(rest[2 * i + 1], SPLIT, 1)
+                )
 
 
 def call(kernel, name, inputs, held_in, held_out, outputs, scratch, micros):
@@ -667,14 +699,14 @@
         self.weight = ((chunk * WIN, 2 * VOX), bf16)
         self.held = (pairs // CYCLE + 1 if angles == chunk else 1,) + self.weight[0]
         self.acc = ((angles, 3, both, LANES), f32)
-        self.acc_rows = ((angles, ACTIVE, LANES), f32)
+        self.acc_rows = ((angles // 2, ACTIVE, LANES), f32)
         self.along = ((angles, ROWS, VOX), f32)
         self.by_ray = ((angles, slices, ACTIVE), f32)
         self.by_pair = ((pairs, both, VOX), f32)
         self.window = ((angles, 3, both, LANES), f32)
         self.half = ((2, rays, slices * slots, LANES), f32)
         self.mirror = ((max(pairs, angles), slices, ACTIVE), f32)
-        self.sent = [((slices * (slots + angles // rays), ACTIVE), f32)] * rays
+        self.sent = [((slices * (slots + angles // rays * 3 // 4), ACTIVE), f32)] * rays
 
     def first(self, volume):
         inputs = [self.place, self.offset, self.slot, self.cosine, self.sine, volume]
@@ -708,7 +740,7 @@
 
 
 def gather_kernel(rank_ref, *refs):
-    *part_refs, out_ref, sems = refs
+    *part_refs, out_ref, active_ref, sems = refs
     rank = rank_ref[0]
     copies = [
         pltpu.make_async_copy(part_ref, out_ref.at[rank ^ d], sems.at[d])
@@ -716,18 +748,25 @@
     ]
     for copy in copies:
         copy.start()
+    offset = (out_ref.shape[2] - ACTIVE) // 2
+    for d, part_ref in enumerate(part_refs):
+        active_ref[rank ^ d] = part_ref[:, offset : offset + ACTIVE]
     for copy in copies:
         copy.wait()
 
 
 def gather_parts(parts, rank):
     count = len(parts)
+    rows = parts[0].shape[0]
+    vmem = pl.BlockSpec(memory_space=pltpu.VMEM)
     return pl.pallas_call(
         gather_kernel,
-        out_shape=jax.ShapeDtypeStruct((count,) + parts[0].shape, f32),
-        in_specs=[pl.BlockSpec(memory_space=pltpu.SMEM)]
-        + [pl.BlockSpec(memory_space=pltpu.VMEM)] * count,
-        out_specs=pl.BlockSpec(memory_space=pl.ANY),
+        out_shape=(
+            jax.ShapeDtypeStruct((count,) + parts[0].shape, f32),
+            jax.ShapeDtypeStruct((count, rows, ACTIVE), f32),
+        ),
+        in_specs=[pl.BlockSpec(memory_space=pltpu.SMEM)] + [vmem] * count,
+        out_specs=(pl.BlockSpec(memory_space=pltpu.HBM), vmem),
         scratch_shapes=[pltpu.SemaphoreType.DMA((count,))],
         compiler_params=pltpu.CompilerParams(vmem_limit_bytes=8 * 2**20),
         cost_estimate=pl.CostEstimate(
@@ -738,18 +777,28 @@
 
 
 def finish_kernel(rank_ref, *refs):
-    *got_refs, _, rec_ref, out_ref, values_ref, active_ref, sems = refs
+    *got_refs, given_ref, _, rec_ref, out_ref, values_ref, active_ref, sems = refs
     rays = len(got_refs)
     slots = values_ref.shape[1]
     slabs = active_ref.shape[0]
     slices = values_ref.shape[0] // rays
     lead = slices * slots
+    lane = lax.broadcasted_iota(jnp.int32, (slices, ACTIVE), 1)
+    live = (lane >= EDGE) & (lane < ACTIVE - EDGE)
     for d, got_ref in enumerate(reversed(got_refs)):
         rows = pl.ds(pl.multiple_of((rank_ref[0] ^ d) * slices, slices), slices)
         values_ref[rows] = got_ref[0:lead, :].reshape(slices, slots, VOX)
         for k in range(slabs):
-            begin = lead + k * slices
-            active_ref[k, rows, :] = got_ref[begin : begin + slices, :]
+            begin = lead + k // 4 * 3 * slices
+            pair, side = k % 4 // 2, k % 2
+            here = begin + pair * slices
+            left = got_ref[here : here + slices, side * LANES : (side + 1) * LANES]
+            here = begin + 2 * slices
+            rest = got_ref[here : here + slices, pair * LANES : (pair + 1) * LANES]
+            if side:
+                rest = pltpu.roll(rest, SPLIT, 1)
+            whole = pltpu.roll(jnp.concatenate([left, rest], axis=1), EDGE, 1)
+            active_ref[k, rows, :] = jnp.where(live, whole, given_ref[k, rows, :])
     offset = (out_ref.shape[2] - ACTIVE) // 2
     copies = [
         pltpu.make_async_copy(values_ref, rec_ref, sems.at[0]),
@@ -763,9 +812,10 @@
         copy.wait()
 
 
-def finish(pieces, sinogram, rank, shape):
+def finish(pieces, given, sinogram, rank, shape):
     slabs, slab_rows, _ = sinogram.shape
     hbm = pl.BlockSpec(memory_space=pltpu.HBM)
+    vmem = pl.BlockSpec(memory_space=pltpu.VMEM)
     return pl.pallas_call(
         finish_kernel,
         out_shape=(
@@ -773,7 +823,7 @@
             jax.ShapeDtypeStruct(sinogram.shape, f32),
         ),
         in_specs=[pl.BlockSpec(memory_space=pltpu.SMEM)]
-        + [pl.BlockSpec(memory_space=pltpu.VMEM)] * len(pieces)
+        + [vmem] * (len(pieces) + 1)
         + [hbm],
         out_specs=[hbm, hbm],
         scratch_shapes=[
@@ -781,13 +831,13 @@
             pltpu.VMEM((slabs, slab_rows, ACTIVE), f32),
             pltpu.SemaphoreType.DMA((2,)),
         ],
-        input_output_aliases={len(pieces) + 1: 1},
+        input_output_aliases={len(pieces) + 2: 1},
         compiler_params=pltpu.CompilerParams(vmem_limit_bytes=8 * 2**20),
         cost_estimate=pl.CostEstimate(
             flops=0, bytes_accessed=8 * len(pieces) * pieces[0].size, transcendentals=0
         ),
         name="finish",
-    )(rank.reshape(1), *reversed(pieces), sinogram)
+    )(rank.reshape(1), *reversed(pieces), given, sinogram)
 
 
 def exchange(pieces, axis):
@@ -835,22 +885,26 @@
     if padded != slices:
         narrow = []
         for piece in pieces:
-            lower = piece[padded * slots :].reshape(n_slab, padded, ACTIVE)[:, :slices]
-            lower = lower.reshape(n_slab * slices, ACTIVE)
+            lower = piece[padded * slots :].reshape(-1, padded, ACTIVE)[:, :slices]
+            lower = lower.reshape(-1, ACTIVE)
             narrow.append(jnp.concatenate([piece[: slices * slots], lower], axis=0))
         pieces = narrow
     pieces = exchange(pieces, "ray")
-    sinogram = gather_parts(parts, rank)
+    sinogram, given = gather_parts(parts, rank)
     if padded == slices:
-        reconstruction, residual = finish(pieces, sinogram, ray_rank, volume.shape)
+        reconstruction, residual = finish(pieces, given, sinogram, ray_rank, volume.shape)
     else:
         order = ray_rank ^ jnp.arange(n_ray, dtype=jnp.int32)
         pieces = jnp.take(jnp.stack(pieces), order, axis=0)
         reconstruction = pieces[:, : slices * slots].reshape(volume.shape)
-        lower = pieces[:, slices * slots :].reshape(n_ray, n_slab, slices, ACTIVE)
-        lower = jnp.transpose(lower, (1, 0, 2, 3)).reshape(n_slab, n_ray * slices, ACTIVE)
-        begin = (band - ACTIVE) // 2
-        residual = lax.dynamic_update_slice(sinogram, lower, (0, 0, begin))
+        lower = pieces[:, slices * slots :].reshape(n_ray, -1, 3, slices, ACTIVE)
+        left = lower[:, :, :2].reshape(n_ray, -1, 2, slices, 2, LANES)
+        left = jnp.transpose(left, (1, 2, 4, 0, 3, 5)).reshape(n_slab, n_ray * slices, LANES)
+        rest = lower[:, :, 2].reshape(n_ray, -1, slices, 4, SPLIT)
+        rest = jnp.transpose(rest, (1, 3, 0, 2, 4)).reshape(n_slab, n_ray * slices, SPLIT)
+        begin = (band - ACTIVE) // 2 + EDGE
+        live = jnp.concatenate([left, rest], axis=2)
+        residual = lax.dynamic_update_slice(sinogram, live, (0, 0, begin))
     return (reconstruction, residual[:, None])
 
 

time: 90.9 us -> 88.6 us (0.975)
  Pallas kernels: 49.7 us -> 47.8 us
  starting transfers between devices: 30.9 us -> 29.7 us
    ppermute x10, starting transfers between devices: 20 us -> 18.7 us  [exchange(): lax.ppermute(pieces[d], axis, [(i, i ^ d) for i in range(count)])]
    pallas_call x1, Pallas kernels: 10.3 us -> 9.07 us  [paganin(): pl.pallas_call(filter_kernel, out_shape=[jax.ShapeDtypeStruct((height //...]
    all_to_all x2, waiting for transfers between devices: 4.04 us -> 5.27 us  [to_all(): return lax.all_to_all(values, axes, split_axis=0, concat_axis=0, tiled=True)]
  transfers between devices with their start and end apart: 12 -> 12, of which waited for: 4 -> 4; matrix products, arithmetic and copies ran while one was open for 0% -> 0% of each run, Pallas kernels for 54% -> 53%
where the time goes in v11:
time: 88.6 us; the launch traced here: 88.3 us
  Pallas kernels  47.8 us (54%)
  starting transfers between devices  29.7 us (34%)
  waiting for transfers between devices  8.53 us (10%)
  local copies, waits for them, and re-layouts  1.2 us (1%)
    pallas_call x2, Pallas kernels, call(): pl.pallas_call(kernel, out_shape=[jax.ShapeDtypeStruct(*value) for value...  36.4 us
    ppermute x10, starting transfers between devices, exchange(): lax.ppermute(pieces[d], axis, [(i, i ^ d) for i in range(count)])  18.7 us
    all_to_all x2, starting transfers between devices, to_all(): return lax.all_to_all(values, axes, split_axis=0, concat_axis=0, tiled=True)  11 us
    pallas_call x1, Pallas kernels, paganin(): pl.pallas_call(filter_kernel, out_shape=[jax.ShapeDtypeStruct((height //...  9.07 us
    all_to_all x2, waiting for transfers between devices, to_all(): return lax.all_to_all(values, axes, split_axis=0, concat_axis=0, tiled=True)  5.27 us
    ppermute x10, waiting for transfers between devices, exchange(): lax.ppermute(pieces[d], axis, [(i, i ^ d) for i in range(count)])  3.26 us
  transfers between devices with their start and end apart: 12, of which 4 were waited for; matrix products, arithmetic and copies ran while one was open for 0% of the time, Pallas kernels for 53%

profile of v11, /device:TPU:0, one launch (start us, length us, event | category | flops | bytes accessed | tf_op | source)
XLA Modules:
  0.0 88.3 jit_solution(7834091419197139675)
XLA Ops:
  0.6 7.3 %all-to-all-start = ((f32[8,64,256]{2,1,0:T(8,128)}), f32[8,64,256]{2,1,0:T(8,128)S(1)}, u32[]{:S(2)}, u32[]{:S(2)}) async-start(f32[8,64,256]{2,1,0:T(8,128)} %bitcast.9), calls=%async_computation | async-start | bytes 1048576 | tf_op jit(solution)/shard_map/all_to_all | solution.py:865
  7.9 0.1 sub.24
  8.0 0.0 copy-start.2
  8.0 0.0 copy-start.3
  8.0 0.0 copy-start.4
  8.0 9.1 %paganin.1 = (f32[64,2048]{1,0:T(8,128)}, f32[64,2048]{1,0:T(8,128)}, f32[64,2048]{1,0:T(8,128)}, f32[64,2048]{1,0:T(8,128)}, f32[256,256]{1,0:T(8,128)}) custom-call(s32[1]{0:T(128)} %bitcast.1.rank_ref, f32[256,2048]{1,0:T(8,128)} %bitcast.11, f32[264,256]{1,0:T(8,128)} %constant.78.clone.given_ref), custom_call_target="tpu_custom_call" | custom-call | flops 8589934592 | bytes 4194304 | tf_op jit(solution)/shard_map/paganin/pallas_call | solution.py:203
  17.1 5.3 %all-to-all-done.vol_ref = f32[8,64,256]{2,1,0:T(8,128)S(1)} async-done(((f32[8,64,256]{2,1,0:T(8,128)}), f32[8,64,256]{2,1,0:T(8,128)S(1)}, u32[]{:S(2)}, u32[]{:S(2)}) %all-to-all-start) | async-done | bytes 524320 | tf_op jit(solution)/shard_map/all_to_all | solution.py:865
  22.4 0.0 copy-done.12
  22.4 0.1 select_reduce_fusion.slot_ref
  22.5 0.0 copy-done.6
  22.5 0.1 cos.6.cos_ref
  22.6 0.1 sin.6.sin_ref
  22.7 3.7 %all-to-all-start.1 = ((f32[32,8,256]{2,1,0:T(8,128)}), f32[32,8,256]{2,1,0:T(8,128)S(1)}, u32[]{:S(2)}, u32[]{:S(2)}) async-start(f32[32,8,256]{2,1,0:T(8,128)} %bitcast.10), calls=%async_computation.1 | async-start | bytes 524288 | tf_op jit(solution)/shard_map/all_to_all | solution.py:865
  26.4 0.0 copy-done.7
  26.4 0.0 copy-done.8
  26.4 0.1 add_add_fusion
  26.5 0.1 add.64
  26.6 0.0 copy-done.2
  26.6 0.0 copy-done.3
  26.7 11.5 %first.1 = (f32[32,16,256]{2,1,0:T(8,128)S(1)}, f32[32,8,256]{2,1,0:T(8,128)S(1)}, f32[32,8,256]{2,1,0:T(8,128)S(1)}) custom-call(f32[1024]{0:T(1024)S(1)} %fusion.place_ref, s32[1024]{0:T(1024)S(1)} %get-tuple-element.100.offset_ref, s32[64]{0:T(128)S(1)} %select_reduce_fusion.slot_ref, f32[32]{0:T(128)S(1)} %cos.6.cos_ref, f32[32]{0:T(128)S(1)} %sin.6.sin_ref, ...), custom_call_target="tpu_custom_call" | custom-call | flops 14000000000 | bytes 4194304 | tf_op jit(solution)/shard_map/first/pallas_call | solution.py:642
  38.2 0.8 copy-done.5
  39.0 0.0 all-to-all-done.1.sino_ref
  39.0 0.0 copy-done.11
  39.0 0.2 collective-permute-start
  39.3 0.0 copy-done.10
  39.3 1.7 %collective-permute-start.1 = (f32[64,2048]{1,0:T(8,128)S(1)}, f32[64,2048]{1,0:T(8,128)S(1)}, u32[]{:S(2)}, u32[]{:S(2)}) collective-permute-start(f32[64,2048]{1,0:T(8,128)S(1)} %copy-done.10), channel_id=1, source_target_pairs={{0,16},{8,24},{16,0},{24,8},{1,17},{9,25},{17,1},{25,9},{2,18},{10... | collective-permute-start | bytes 1572872 | tf_op jit(solution)/shard_map/ppermute | solution.py:847
  41.0 0.0 collective-permute-start.2
  41.0 24.9 %second.1 = (f32[88,256]{1,0:T(8,128)S(1)}, f32[88,256]{1,0:T(8,128)S(1)}, f32[88,256]{1,0:T(8,128)S(1)}, f32[88,256]{1,0:T(8,128)S(1)}, f32[88,256]{1,0:T(8,128...) custom-call(s32[1]{0:T(128)} %bitcast.rank_ref, f32[1024]{0:T(1024)S(1)} %fusion.place_ref, ...), custom_call_target="tpu_custom_call" | custom-call | flops 25999998976 | bytes 4194304 | tf_op jit(solution)/shard_map/second/pallas_call | solution.py:642
  65.9 0.0 collective-permute-done.refs_1_
  66.0 0.0 collective-permute-done.1.refs_2_
  66.0 0.0 collective-permute-done.2.refs_3_
  66.0 4.5 %collective-permute-start.3 = (f32[88,256]{1,0:T(8,128)S(1)}, f32[88,256]{1,0:T(8,128)S(1)}, u32[]{:S(2)}, u32[]{:S(2)}) collective-permute-start(f32[88,256]{1,0:T(8,128)S(1)} %get-tuple-element.80), channel_id=1, source_target_pairs={{0,7},{1,6},{2,5},{3,4},{4,3},{5,2},{6,1},{7,0},{8,15},{9,14},{10,... | collective-permute-start | bytes 270344 | tf_op jit(solution)/shard_map/ppermute | solution.py:847
  70.5 0.5 collective-permute-start.4
  71.0 0.6 collective-permute-start.5
  71.5 2.1 %collective-permute-start.6 = (f32[88,256]{1,0:T(8,128)S(1)}, f32[88,256]{1,0:T(8,128)S(1)}, u32[]{:S(2)}, u32[]{:S(2)}) collective-permute-start(f32[88,256]{1,0:T(8,128)S(1)} %get-tuple-element.83), channel_id=1, source_target_pairs={{0,4},{1,5},{2,6},{3,7},{4,0},{5,1},{6,2},{7,3},{8,12},{9,13},{10,... | collective-permute-start | bytes 270344 | tf_op jit(solution)/shard_map/ppermute | solution.py:847
  73.7 2.1 %collective-permute-start.7 = (f32[88,256]{1,0:T(8,128)S(1)}, f32[88,256]{1,0:T(8,128)S(1)}, u32[]{:S(2)}, u32[]{:S(2)}) collective-permute-start(f32[88,256]{1,0:T(8,128)S(1)} %get-tuple-element.84), channel_id=1, source_target_pairs={{0,3},{1,2},{2,1},{3,0},{4,7},{5,6},{6,5},{7,4},{8,11},{9,10},{10,... | collective-permute-start | bytes 270344 | tf_op jit(solution)/shard_map/ppermute | solution.py:847
  75.8 0.0 collective-permute-done.3.refs_0_
  75.8 5.5 %collective-permute-start.8 = (f32[88,256]{1,0:T(8,128)S(1)}, f32[88,256]{1,0:T(8,128)S(1)}, u32[]{:S(2)}, u32[]{:S(2)}) collective-permute-start(f32[88,256]{1,0:T(8,128)S(1)} %get-tuple-element.85), channel_id=1, source_target_pairs={{0,2},{1,3},{2,0},{3,1},{4,6},{5,7},{6,4},{7,5},{8,10},{9,11},{10,... | collective-permute-start | bytes 270344 | tf_op jit(solution)/shard_map/ppermute | solution.py:847
  81.3 0.0 collective-permute-done.4.refs_1_
  81.3 1.5 %collective-permute-start.9 = (f32[88,256]{1,0:T(8,128)S(1)}, f32[88,256]{1,0:T(8,128)S(1)}, u32[]{:S(2)}, u32[]{:S(2)}) collective-permute-start(f32[88,256]{1,0:T(8,128)S(1)} %get-tuple-element.86), channel_id=1, source_target_pairs={{0,1},{1,0},{2,3},{3,2},{4,5},{5,4},{6,7},{7,6},{8,9},{9,8},{10,11... | collective-permute-start | bytes 270344 | tf_op jit(solution)/shard_map/ppermute | solution.py:847
  82.7 0.0 copy-done
  82.7 1.3 %gather_parts.1 = (f32[4,64,2048]{2,1,0:T(8,128)}, f32[4,64,256]{2,1,0:T(8,128)S(1)}) custom-call(s32[1]{0:T(128)} %bitcast.1.rank_ref, f32[64,2048]{1,0:T(8,128)S(1)} %copy-done, f32[64,2048]{1,0:T(8,128)S(1)} %collective-permute-done.refs_1_, f32[64,2048]{1,0:T(8,128)S(1)} %collective-permute-done.1.refs_2_, f32[64,2048]{1,0:T(8,128)S(1)} %collective-permute-done.2.refs_3_), custom_call_target="tpu_custom_call" | custom-call | bytes 4194304 | tf_op jit(solution)/shard_map/gather_parts/pallas_call | solution.py:762
  84.1 1.0 %collective-permute-done.5.refs_2_ = f32[88,256]{1,0:T(8,128)S(1)} collective-permute-done((f32[88,256]{1,0:T(8,128)S(1)}, f32[88,256]{1,0:T(8,128)S(1)}, u32[]{:S(2)}, u32[]{:S(2)}) %collective-permute-start.5) | collective-permute-done | bytes 90144 | tf_op jit(solution)/shard_map/ppermute | solution.py:847
  85.1 1.5 %collective-permute-done.6.refs_3_ = f32[88,256]{1,0:T(8,128)S(1)} collective-permute-done((f32[88,256]{1,0:T(8,128)S(1)}, f32[88,256]{1,0:T(8,128)S(1)}, u32[]{:S(2)}, u32[]{:S(2)}) %collective-permute-start.6) | collective-permute-done | bytes 90144 | tf_op jit(solution)/shard_map/ppermute | solution.py:847
  86.6 0.0 collective-permute-done.7.refs_4_
  86.6 0.7 collective-permute-done.8.refs_5_
  87.3 0.0 collective-permute-done.9.refs_6_
  87.3 1.0 %finish.1 = (f32[64,8,256]{2,1,0:T(8,128)}, f32[4,64,2048]{2,1,0:T(8,128)}) custom-call(s32[1]{0:T(128)} %bitcast.rank_ref, f32[88,256]{1,0:T(8,128)S(1)} %collective-permute-done.3.refs_0_, f32[88,256]{1,0:T(8,128)S(1)} %collective-permute-done.4.refs_1_, f32[88,256]{1,0:T(8,128)S(1)} %collective-permute-done.5.refs_2_, ...), custom_call_target="tpu_custom_call", output_to_operand_aliasing={{1}: (10, {})} | custom-call | bytes 1441792 | tf_op jit(solution)/shard_map/finish/pallas_call | solution.py:819
  (18 shorter events, 0.1 us)
Async XLA Ops:
  0.6 21.8 %all-to-all-start = ((f32[8,64,256]{2,1,0:T(8,128)}), f32[8,64,256]{2,1,0:T(8,128)S(1)}, u32[]{:S(2)}, u32[]{:S(2)}) async-start(f32[8,64,256]{2,1,0:T(8,128)} %bitcast.9), calls=%async_computation | async-start | bytes 1048576 | tf_op jit(solution)/shard_map/all_to_all | solution.py:865
  8.0 14.4 %copy-start.12 = (s32[64]{0:T(128)S(1)}, s32[64]{0:T(128)}, u32[]{:S(2)}) copy-start(s32[64]{0:T(128)} %param.13) | copy-start | bytes 772
  8.0 14.5 %copy-start.6 = (f32[4,8]{1,0:T(4,128)S(1)}, f32[4,8]{1,0:T(4,128)}, u32[]{:S(2)}) copy-start(f32[4,8]{1,0:T(4,128)} %param.11) | copy-start | bytes 388
  8.0 18.4 %copy-start.7 = (f32[32]{0:T(128)S(1)}, f32[32]{0:T(128)}, u32[]{:S(2)}) copy-start(f32[32]{0:T(128)} %constant.86) | copy-start | bytes 388
  8.0 18.4 %copy-start.8 = (f32[32]{0:T(128)S(1)}, f32[32]{0:T(128)}, u32[]{:S(2)}) copy-start(f32[32]{0:T(128)} %constant.85) | copy-start | bytes 388
  8.0 18.6 %copy-start.2 = (bf16[256,256]{1,0:T(8,128)(2,1)S(1)}, bf16[256,256]{1,0:T(8,128)(2,1)}, u32[]{:S(2)}) copy-start(bf16[256,256]{1,0:T(8,128)(2,1)} %constant.81.clone.flip_ref) | copy-start | bytes 393220
  8.0 18.6 %copy-start.3 = (f32[8,256]{1,0:T(8,128)S(1)}, f32[8,256]{1,0:T(8,128)}, u32[]{:S(2)}) copy-start(f32[8,256]{1,0:T(8,128)} %constant.83.clone.shift_y_ref) | copy-start | bytes 24580
  8.0 18.6 %copy-start.4 = (f32[8,256]{1,0:T(8,128)S(1)}, f32[8,256]{1,0:T(8,128)}, u32[]{:S(2)}) copy-start(f32[8,256]{1,0:T(8,128)} %constant.82.clone.shift_x_ref) | copy-start | bytes 24580
  22.4 15.8 %copy-start.1 = (f32[8,64,256]{2,1,0:T(8,128)}, f32[8,64,256]{2,1,0:T(8,128)S(1)}, u32[]{:S(2)}) copy-start(f32[8,64,256]{2,1,0:T(8,128)S(1)} %all-to-all-done.vol_ref) | copy-start | bytes 1572868
  22.7 16.3 %all-to-all-start.1 = ((f32[32,8,256]{2,1,0:T(8,128)}), f32[32,8,256]{2,1,0:T(8,128)S(1)}, u32[]{:S(2)}, u32[]{:S(2)}) async-start(f32[32,8,256]{2,1,0:T(8,128)} %bitcast.10), calls=%async_computation.1 | async-start | bytes 524288 | tf_op jit(solution)/shard_map/all_to_all | solution.py:865
  26.6 12.4 %copy-start.11 = (f32[64,2048]{1,0:T(8,128)S(1)}, f32[64,2048]{1,0:T(8,128)}, u32[]{:S(2)}) copy-start(f32[64,2048]{1,0:T(8,128)} %get-tuple-element.77) | copy-start | bytes 1572868
  26.7 12.6 %copy-start.10 = (f32[64,2048]{1,0:T(8,128)S(1)}, f32[64,2048]{1,0:T(8,128)}, u32[]{:S(2)}) copy-start(f32[64,2048]{1,0:T(8,128)} %get-tuple-element.78) | copy-start | bytes 1572868
  26.7 14.3 %copy-start.9 = (f32[64,2048]{1,0:T(8,128)S(1)}, f32[64,2048]{1,0:T(8,128)}, u32[]{:S(2)}) copy-start(f32[64,2048]{1,0:T(8,128)} %get-tuple-element.79) | copy-start | bytes 1572868
  38.2 0.8 copy-start.5
  39.0 26.9 %collective-permute-start = (f32[64,2048]{1,0:T(8,128)S(1)}, f32[64,2048]{1,0:T(8,128)S(1)}, u32[]{:S(2)}, u32[]{:S(2)}) collective-permute-start(f32[64,2048]{1,0:T(8,128)S(1)} %copy-done.11), channel_id=1, source_target_pairs={{0,8},{8,0},{16,24},{24,16},{1,9},{9,1},{17,25},{25,17},{2,10},{10... | collective-permute-start | bytes 1572872 | tf_op jit(solution)/shard_map/ppermute | solution.py:847
  39.3 26.7 %collective-permute-start.1 = (f32[64,2048]{1,0:T(8,128)S(1)}, f32[64,2048]{1,0:T(8,128)S(1)}, u32[]{:S(2)}, u32[]{:S(2)}) collective-permute-start(f32[64,2048]{1,0:T(8,128)S(1)} %copy-done.10), channel_id=1, source_target_pairs={{0,16},{8,24},{16,0},{24,8},{1,17},{9,25},{17,1},{25,9},{2,18},{10... | collective-permute-start | bytes 1572872 | tf_op jit(solution)/shard_map/ppermute | solution.py:847
  41.0 25.0 %collective-permute-start.2 = (f32[64,2048]{1,0:T(8,128)S(1)}, f32[64,2048]{1,0:T(8,128)S(1)}, u32[]{:S(2)}, u32[]{:S(2)}) collective-permute-start(f32[64,2048]{1,0:T(8,128)S(1)} %copy-done.9), channel_id=1, source_target_pairs={{0,24},{8,16},{16,8},{24,0},{1,25},{9,17},{17,9},{25,1},{2,26},{10... | collective-permute-start | bytes 1572872 | tf_op jit(solution)/shard_map/ppermute | solution.py:847
  41.0 41.7 %copy-start = (f32[64,2048]{1,0:T(8,128)S(1)}, f32[64,2048]{1,0:T(8,128)}, u32[]{:S(2)}) copy-start(f32[64,2048]{1,0:T(8,128)} %get-tuple-element.88.refs_0_) | copy-start | bytes 1572868
  66.0 9.8 %collective-permute-start.3 = (f32[88,256]{1,0:T(8,128)S(1)}, f32[88,256]{1,0:T(8,128)S(1)}, u32[]{:S(2)}, u32[]{:S(2)}) collective-permute-start(f32[88,256]{1,0:T(8,128)S(1)} %get-tuple-element.80), channel_id=1, source_target_pairs={{0,7},{1,6},{2,5},{3,4},{4,3},{5,2},{6,1},{7,0},{8,15},{9,14},{10,... | collective-permute-start | bytes 270344 | tf_op jit(solution)/shard_map/ppermute | solution.py:847
  70.5 10.8 %collective-permute-start.4 = (f32[88,256]{1,0:T(8,128)S(1)}, f32[88,256]{1,0:T(8,128)S(1)}, u32[]{:S(2)}, u32[]{:S(2)}) collective-permute-start(f32[88,256]{1,0:T(8,128)S(1)} %get-tuple-element.81), channel_id=1, source_target_pairs={{0,6},{1,7},{2,4},{3,5},{4,2},{5,3},{6,0},{7,1},{8,14},{9,15},{10,... | collective-permute-start | bytes 270344 | tf_op jit(solution)/shard_map/ppermute | solution.py:847
  71.0 14.2 %collective-permute-start.5 = (f32[88,256]{1,0:T(8,128)S(1)}, f32[88,256]{1,0:T(8,128)S(1)}, u32[]{:S(2)}, u32[]{:S(2)}) collective-permute-start(f32[88,256]{1,0:T(8,128)S(1)} %get-tuple-element.82), channel_id=1, source_target_pairs={{0,5},{1,4},{2,7},{3,6},{4,1},{5,0},{6,3},{7,2},{8,13},{9,12},{10,... | collective-permute-start | bytes 270344 | tf_op jit(solution)/shard_map/ppermute | solution.py:847
  71.5 15.1 %collective-permute-start.6 = (f32[88,256]{1,0:T(8,128)S(1)}, f32[88,256]{1,0:T(8,128)S(1)}, u32[]{:S(2)}, u32[]{:S(2)}) collective-permute-start(f32[88,256]{1,0:T(8,128)S(1)} %get-tuple-element.83), channel_id=1, source_target_pairs={{0,4},{1,5},{2,6},{3,7},{4,0},{5,1},{6,2},{7,3},{8,12},{9,13},{10,... | collective-permute-start | bytes 270344 | tf_op jit(solution)/shard_map/ppermute | solution.py:847
  73.7 12.9 %collective-permute-start.7 = (f32[88,256]{1,0:T(8,128)S(1)}, f32[88,256]{1,0:T(8,128)S(1)}, u32[]{:S(2)}, u32[]{:S(2)}) collective-permute-start(f32[88,256]{1,0:T(8,128)S(1)} %get-tuple-element.84), channel_id=1, source_target_pairs={{0,3},{1,2},{2,1},{3,0},{4,7},{5,6},{6,5},{7,4},{8,11},{9,10},{10,... | collective-permute-start | bytes 270344 | tf_op jit(solution)/shard_map/ppermute | solution.py:847
  75.8 11.6 %collective-permute-start.8 = (f32[88,256]{1,0:T(8,128)S(1)}, f32[88,256]{1,0:T(8,128)S(1)}, u32[]{:S(2)}, u32[]{:S(2)}) collective-permute-start(f32[88,256]{1,0:T(8,128)S(1)} %get-tuple-element.85), channel_id=1, source_target_pairs={{0,2},{1,3},{2,0},{3,1},{4,6},{5,7},{6,4},{7,5},{8,10},{9,11},{10,... | collective-permute-start | bytes 270344 | tf_op jit(solution)/shard_map/ppermute | solution.py:847
  81.3 6.1 %collective-permute-start.9 = (f32[88,256]{1,0:T(8,128)S(1)}, f32[88,256]{1,0:T(8,128)S(1)}, u32[]{:S(2)}, u32[]{:S(2)}) collective-permute-start(f32[88,256]{1,0:T(8,128)S(1)} %get-tuple-element.86), channel_id=1, source_target_pairs={{0,1},{1,0},{2,3},{3,2},{4,5},{5,4},{6,7},{7,6},{8,9},{9,8},{10,11... | collective-permute-start | bytes 270344 | tf_op jit(solution)/shard_map/ppermute | solution.py:847

commit v12 on v11

--- a/solution.py
+++ b/solution.py
@@ -271,42 +271,8 @@
     return jnp.concatenate(rows, axis=0)
 
 
-def project_pair(held, operand, q, c, both, sizes, tile_ref, turn_ref, acc_ref):
-    angles, chunk = sizes[:2]
-    rows = acc_ref.shape[2]
-    sums = lax.dot_general(
-        operand, held, (((1,), (1,)), ((), ())), preferred_element_type=f32
-    )
-    total = sums[0:both] + sums[both : 2 * both]
-    if rows != both:
-        total = jnp.concatenate([total, sums[2 * both : 2 * both + ROWS]], axis=0)
-    lane = lax.broadcasted_iota(jnp.int32, (rows, LANES), 1)
-    for begin in range(0, chunk, GROUP):
-        places = []
-        for t in range(begin, min(begin + GROUP, chunk)):
-            index = q * angles + c * chunk + t
-            first = t * WIN // LANES
-            last = (t * WIN + WIN - 1) // LANES
-            low = t * WIN - first * LANES
-            high = low + WIN
-            piece = total[:, first * LANES : (first + 1) * LANES]
-            if first == last:
-                piece = jnp.where((lane >= low) & (lane < high), piece, 0.0)
-            else:
-                other = total[:, last * LANES : (last + 1) * LANES]
-                piece = jnp.where(
-                    lane >= low, piece, jnp.where(lane < high - LANES, other, 0.0)
-                )
-            tile = tile_ref[index]
-            angle = c * chunk + t
-            piece = pltpu.roll(piece, (LANES - turn_ref[index]) % LANES, 1)
-            places.append((angle, tile, acc_ref[angle, tile] + piece))
-        for angle, tile, values in places:
-            acc_ref[angle, tile] = values
-
-
-def row_operands(values):
-    rows = ray_operand(values, True)
+def row_operands(values, sums_too):
+    rows = ray_operand(values, sums_too)
     count, width = rows.shape
     spare = jnp.zeros((SPLIT - count, width), bf16)
     empty = jnp.zeros((SPLIT, width), bf16)
@@ -347,17 +313,10 @@
             t = index // half * chunk + part * half + index % half
             direct_ref[t] = rows[0:slices] + rows[both : both + slices]
             mirror_ref[t] = rows[slices:both] + rows[both + slices : 2 * both]
-            total_ref[t] = rows[2 * both : 2 * both + slices]
+            if total_ref is not None:
+                total_ref[t] = rows[2 * both : 2 * both + slices]
 
     repeat(acc_ref.shape[0], spread, 8)
-
-
-def join_tiles(acc_ref, rows):
-    lane = lax.broadcasted_iota(jnp.int32, (acc_ref.shape[0], ROWS, LANES), 2)
-    middle = pltpu.roll(acc_ref[:, 1, rows, :], SPLIT, 2)
-    left = acc_ref[:, 0, rows, :] + jnp.where(lane >= SPLIT, middle, 0.0)
-    right = acc_ref[:, 2, rows, :] + jnp.where(lane < SPLIT, middle, 0.0)
-    return jnp.concatenate([left, right], axis=2) * (1.0 / ROI)
 
 
 def turn_rays(values, flip):
@@ -380,7 +339,7 @@
         window_ref[:, 1, rows, :] = pltpu.roll(mixed, SPLIT, 2)
 
 
-def update_pair(held, q, c, sizes, window_ref, tile_ref, turn_ref):
+def window_operand(q, c, sizes, window_ref, tile_ref, turn_ref):
     angles, chunk = sizes[:2]
     both = window_ref.shape[2]
     lane_rows = lax.broadcasted_iota(jnp.int32, (both, LANES), 1)
@@ -397,7 +356,12 @@
                     lane_rows >= begin - place * LANES, piece, tiles[place]
                 )
     high, low = halves(jnp.concatenate(tiles, axis=1))
-    sums = dot(jnp.concatenate([high, low], axis=0), held)
+    return jnp.concatenate([high, low], axis=0)
+
+
+def update_pair(operand, held):
+    both = operand.shape[0] // 2
+    sums = dot(operand, held)
     return sums[0:both, 0:VOX] + sums[both:, 0:VOX] + sums[0:both, VOX:]
 
 
@@ -452,7 +416,7 @@
     def cycle(index, carry):
         for step in range(CYCLE):
             q = index * CYCLE + step
-            operands = row_operands(start_ref[q])
+            operands = row_operands(start_ref[q], True)
             for c in range(chunks):
                 more = jnp.minimum(q + (c + 1) // chunks, pairs - 1)
                 after = (step * chunks + c + 1) % CYCLE
@@ -475,6 +439,7 @@
     sizes,
     step_size,
     rank_ref,
+    offset_ref,
     place_ref,
     tile_ref,
     turn_ref,
@@ -509,88 +474,92 @@
     weights.prepare(shift_x_ref, shift_y_ref, cos_ref, sin_ref)
     chunks = angles // chunk
     windows = (sizes, window_ref, tile_ref, turn_ref)
-    windows_out = (both, sizes, tile_ref, turn_ref, acc_ref)
+    rest = (sizes, offset_ref, acc_ref)
     fill_windows(
         (sino_ref[...] - predicted_ref[...]) * gain_ref[...] * (1.0 / ROI), flip, window_ref
     )
     acc_ref[...] = jnp.zeros(acc_ref.shape, f32)
     kept.wait()
 
-    def advance(q, held):
-        total = update_pair(held, q, 0, *windows)
+    def advance(q, operand, held):
+        total = update_pair(operand, held)
         update_ref[q] = total
         return start_ref[q] + step_size * total
 
     def forward(values, q, held):
-        project_pair(held, ray_operand(values, False), q, 0, *windows_out)
-
-    def cycle(index, values):
+        project_rows(held, row_operands(values, False), q, 0, *rest)
+
+    def cycle(index, carry):
+        values, operand = carry
         for step in range(CYCLE):
             q = index * CYCLE + step
             after = (step + 1) % CYCLE
             before = (step - 1) % CYCLE
             later = index + (step + 1) // CYCLE
             earlier = index if step else jnp.maximum(index - 1, 0)
-            weights.make(jnp.minimum(q + 1, pairs - 1), 0, held_refs[after].at[later])
-            new_values = advance(q, held_refs[step][index])
-            forward(values, jnp.maximum(q - 1, 0), held_refs[before][earlier])
-            values = new_values
-        return values
+            following = jnp.minimum(q + 1, pairs - 1)
+            next_operand = window_operand(following, 0, *windows)
+            weights.make(following, 0, held_refs[after].at[later])
+            new_values = advance(q, operand, held_refs[step][index])
+            forward(values, jnp.maximum(q - 1, 0), held_refs[before].at[earlier])
+            values, operand = new_values, next_operand
+        return values, operand
 
     def all_chunks(q, body):
         for c in range(chunks):
             weights.make(q, c, held_refs[0].at[0])
-            body(c, held_refs[0][0])
+            body(c, held_refs[0].at[0])
 
     def plain_update(q, carry):
         update_ref[q] = jnp.zeros(update_ref.shape[1:], f32)
 
         def add(c, held):
-            update_ref[q] = update_ref[q] + update_pair(held, q, c, *windows)
+            operand = window_operand(q, c, *windows)
+            update_ref[q] = update_ref[q] + update_pair(operand, held[...])
 
         all_chunks(q, add)
         return carry
 
     def plain_forward(q, carry):
-        operand = ray_operand(start_ref[q] + step_size * update_ref[q], False)
-        all_chunks(
-            q,
-            lambda c, held: project_pair(held, operand, q, c, *windows_out),
-        )
+        operands = row_operands(start_ref[q] + step_size * update_ref[q], False)
+        all_chunks(q, lambda c, held: project_rows(held, operands, q, c, *rest))
         return carry
 
     if chunks == 1:
         held_refs[CYCLE - 1][0] = jnp.zeros(held_refs[CYCLE - 1].shape[1:], bf16)
         weights.make(0, 0, held_refs[0].at[0])
-        values = lax.fori_loop(0, pairs // CYCLE, cycle, jnp.zeros((both, VOX), f32))
-        forward(values, pairs - 1, held_refs[CYCLE - 1][pairs // CYCLE - 1])
+        begin = (jnp.zeros((both, VOX), f32), window_operand(0, 0, *windows))
+        values, _ = lax.fori_loop(0, pairs // CYCLE, cycle, begin)
+        forward(values, pairs - 1, held_refs[CYCLE - 1].at[pairs // CYCLE - 1])
     else:
         lax.fori_loop(0, pairs, plain_update, 0)
         lax.fori_loop(0, pairs, plain_forward, 0)
 
-    direct, mirror = (
-        join_tiles(acc_ref, slice(part * ROWS, (part + 1) * ROWS)) for part in range(2)
-    )
-    direct_ref[...] = sino_ref[...] - direct - turn_rays(mirror, flip)
+    spread_rays(acc_ref, direct_ref, mirror_ref, None, slices, chunk)
+    turned = turn_rays(mirror_ref[0:angles], flip)
+    direct_ref[...] = sino_ref[...] - direct_ref[...] - turned
     fill_windows(direct_ref[...] * gain_ref[...] * (1.0 / ROI), flip, window_ref)
 
-    def last_cycle(index, carry):
+    def last_cycle(index, operand):
         for step in range(CYCLE):
             q = index * CYCLE + step
-            total = update_pair(held_refs[step][index], q, 0, *windows)
+            next_operand = window_operand(jnp.minimum(q + 1, pairs - 1), 0, *windows)
+            total = update_pair(operand, held_refs[step][index])
             update_ref[q] = (update_ref[q] + total) * step_size
-        return carry
+            operand = next_operand
+        return operand
 
     def plain_last(q, carry):
         def add(c, held):
-            update_ref[q] = update_ref[q] + update_pair(held, q, c, *windows)
+            operand = window_operand(q, c, *windows)
+            update_ref[q] = update_ref[q] + update_pair(operand, held[...])
 
         all_chunks(q, add)
         update_ref[q] = update_ref[q] * step_size
         return carry
 
     if chunks == 1:
-        lax.fori_loop(0, pairs // CYCLE, last_cycle, 0)
+        lax.fori_loop(0, pairs // CYCLE, last_cycle, window_operand(0, 0, *windows))
     else:
         lax.fori_loop(0, pairs, plain_last, 0)
 
@@ -698,7 +667,6 @@
         self.fixed = [jnp.asarray(flip), jnp.asarray(shift_x, f32), jnp.asarray(shift_y, f32)]
         self.weight = ((chunk * WIN, 2 * VOX), bf16)
         self.held = (pairs // CYCLE + 1 if angles == chunk else 1,) + self.weight[0]
-        self.acc = ((angles, 3, both, LANES), f32)
         self.acc_rows = ((angles // 2, ACTIVE, LANES), f32)
         self.along = ((angles, ROWS, VOX), f32)
         self.by_ray = ((angles, slices, ACTIVE), f32)
@@ -723,10 +691,10 @@
         )
 
     def second(self, rank, volume, start, predicted, gain, sino):
-        inputs = [rank.reshape(1), self.place, self.tile, self.turn, self.slot]
+        inputs = [rank.reshape(1), self.offset, self.place, self.tile, self.turn, self.slot]
         inputs += [self.cosine, self.sine, volume, predicted, gain, sino]
         scratch = [(self.held, bf16)] * CYCLE
-        scratch += [self.acc, self.along, self.by_ray, self.mirror, self.window]
+        scratch += [self.acc_rows, self.along, self.by_ray, self.mirror, self.window]
         return call(
             functools.partial(second_kernel, self.sizes, self.step_size),
             "second",

time: 88.6 us -> 87.3 us (0.985)
  Pallas kernels: 47.8 us -> 46.5 us
    pallas_call x2, Pallas kernels: 36.4 us -> 35.1 us  [call(): pl.pallas_call(kernel, out_shape=[jax.ShapeDtypeStruct(*value) for value...]
  transfers between devices with their start and end apart: 12 -> 12, of which waited for: 4 -> 4; matrix products, arithmetic and copies ran while one was open for 0% -> 0% of each run, Pallas kernels for 53% -> 52%
where the time goes in v12:
time: 87.3 us; the launch traced here: 87 us
  Pallas kernels  46.5 us (53%)
  starting transfers between devices  29.7 us (34%)
  waiting for transfers between devices  8.53 us (10%)
  local copies, waits for them, and re-layouts  1.2 us (1%)
    pallas_call x2, Pallas kernels, call(): pl.pallas_call(kernel, out_shape=[jax.ShapeDtypeStruct(*value) for value...  35.1 us
    ppermute x10, starting transfers between devices, exchange(): lax.ppermute(pieces[d], axis, [(i, i ^ d) for i in range(count)])  18.7 us
    all_to_all x2, starting transfers between devices, to_all(): return lax.all_to_all(values, axes, split_axis=0, concat_axis=0, tiled=True)  11 us
    pallas_call x1, Pallas kernels, paganin(): pl.pallas_call(filter_kernel, out_shape=[jax.ShapeDtypeStruct((height //...  9.07 us
    all_to_all x2, waiting for transfers between devices, to_all(): return lax.all_to_all(values, axes, split_axis=0, concat_axis=0, tiled=True)  5.27 us
    ppermute x10, waiting for transfers between devices, exchange(): lax.ppermute(pieces[d], axis, [(i, i ^ d) for i in range(count)])  3.27 us
  transfers between devices with their start and end apart: 12, of which 4 were waited for; matrix products, arithmetic and copies ran while one was open for 0% of the time, Pallas kernels for 52%

profile of v12, /device:TPU:0, one launch (start us, length us, event | category | flops | bytes accessed | tf_op | source)
XLA Modules:
  0.0 87.0 jit_solution(2429720934947102146)
XLA Ops:
  0.6 7.3 %all-to-all-start = ((f32[8,64,256]{2,1,0:T(8,128)}), f32[8,64,256]{2,1,0:T(8,128)S(1)}, u32[]{:S(2)}, u32[]{:S(2)}) async-start(f32[8,64,256]{2,1,0:T(8,128)} %bitcast.9), calls=%async_computation | async-start | bytes 1048576 | tf_op jit(solution)/shard_map/all_to_all | solution.py:833
  7.9 0.1 sub.24
  8.0 0.0 copy-start.2
  8.0 0.0 copy-start.3
  8.0 0.0 copy-start.4
  8.0 9.1 %paganin.1 = (f32[64,2048]{1,0:T(8,128)}, f32[64,2048]{1,0:T(8,128)}, f32[64,2048]{1,0:T(8,128)}, f32[64,2048]{1,0:T(8,128)}, f32[256,256]{1,0:T(8,128)}) custom-call(s32[1]{0:T(128)} %bitcast.1.rank_ref, f32[256,2048]{1,0:T(8,128)} %bitcast.11, f32[264,256]{1,0:T(8,128)} %constant.78.clone.given_ref), custom_call_target="tpu_custom_call" | custom-call | flops 8589934592 | bytes 4194304 | tf_op jit(solution)/shard_map/paganin/pallas_call | solution.py:203
  17.1 5.3 %all-to-all-done.vol_ref = f32[8,64,256]{2,1,0:T(8,128)S(1)} async-done(((f32[8,64,256]{2,1,0:T(8,128)}), f32[8,64,256]{2,1,0:T(8,128)S(1)}, u32[]{:S(2)}, u32[]{:S(2)}) %all-to-all-start) | async-done | bytes 524320 | tf_op jit(solution)/shard_map/all_to_all | solution.py:833
  22.4 0.0 copy-done.12
  22.4 0.1 select_reduce_fusion.slot_ref
  22.5 0.0 copy-done.6
  22.5 0.1 cos.6.cos_ref
  22.6 0.1 sin.6.sin_ref
  22.7 3.7 %all-to-all-start.1 = ((f32[32,8,256]{2,1,0:T(8,128)}), f32[32,8,256]{2,1,0:T(8,128)S(1)}, u32[]{:S(2)}, u32[]{:S(2)}) async-start(f32[32,8,256]{2,1,0:T(8,128)} %bitcast.10), calls=%async_computation.1 | async-start | bytes 524288 | tf_op jit(solution)/shard_map/all_to_all | solution.py:833
  26.4 0.0 copy-done.7
  26.4 0.0 copy-done.8
  26.4 0.1 add_add_fusion
  26.5 0.1 add.64
  26.6 0.0 copy-done.2
  26.6 0.0 copy-done.3
  26.7 11.5 %first.1 = (f32[32,16,256]{2,1,0:T(8,128)S(1)}, f32[32,8,256]{2,1,0:T(8,128)S(1)}, f32[32,8,256]{2,1,0:T(8,128)S(1)}) custom-call(f32[1024]{0:T(1024)S(1)} %fusion.1.place_ref, s32[1024]{0:T(1024)S(1)} %get-tuple-element.102.offset_ref, s32[64]{0:T(128)S(1)} %select_reduce_fusion.slot_ref, f32[32]{0:T(128)S(1)} %cos.6.cos_ref, f32[32]{0:T(128)S(1)} %sin.6.sin_ref, ...), custom_call_target="tpu_custom_call" | custom-call | flops 14000000000 | bytes 4194304 | tf_op jit(solution)/shard_map/first/pallas_call | solution.py:611
  38.2 0.0 copy-done.1
  38.2 0.0 copy-start.5
  38.2 0.8 copy-done.5
  39.0 0.0 all-to-all-done.1.sino_ref
  39.0 0.3 collective-permute-start
  39.3 1.7 %collective-permute-start.1 = (f32[64,2048]{1,0:T(8,128)S(1)}, f32[64,2048]{1,0:T(8,128)S(1)}, u32[]{:S(2)}, u32[]{:S(2)}) collective-permute-start(f32[64,2048]{1,0:T(8,128)S(1)} %copy-done.10), channel_id=1, source_target_pairs={{0,16},{8,24},{16,0},{24,8},{1,17},{9,25},{17,1},{25,9},{2,18},{10... | collective-permute-start | bytes 1572872 | tf_op jit(solution)/shard_map/ppermute | solution.py:815
  41.0 0.0 collective-permute-start.2
  41.0 23.6 %second.1 = (f32[88,256]{1,0:T(8,128)S(1)}, f32[88,256]{1,0:T(8,128)S(1)}, f32[88,256]{1,0:T(8,128)S(1)}, f32[88,256]{1,0:T(8,128)S(1)}, f32[88,256]{1,0:T(8,128...) custom-call(s32[1]{0:T(128)} %bitcast.rank_ref, ...), custom_call_target="tpu_custom_call" | custom-call | flops 25999998976 | bytes 4194304 | tf_op jit(solution)/shard_map/second/pallas_call | solution.py:611
  64.6 0.0 collective-permute-done.refs_1_
  64.6 0.0 collective-permute-done.1.refs_2_
  64.6 0.0 collective-permute-done.2.refs_3_
  64.7 4.5 %collective-permute-start.3 = (f32[88,256]{1,0:T(8,128)S(1)}, f32[88,256]{1,0:T(8,128)S(1)}, u32[]{:S(2)}, u32[]{:S(2)}) collective-permute-start(f32[88,256]{1,0:T(8,128)S(1)} %get-tuple-element.80), channel_id=1, source_target_pairs={{0,7},{1,6},{2,5},{3,4},{4,3},{5,2},{6,1},{7,0},{8,15},{9,14},{10,... | collective-permute-start | bytes 270344 | tf_op jit(solution)/shard_map/ppermute | solution.py:815
  69.2 0.5 collective-permute-start.4
  69.6 0.6 collective-permute-start.5
  70.2 2.1 %collective-permute-start.6 = (f32[88,256]{1,0:T(8,128)S(1)}, f32[88,256]{1,0:T(8,128)S(1)}, u32[]{:S(2)}, u32[]{:S(2)}) collective-permute-start(f32[88,256]{1,0:T(8,128)S(1)} %get-tuple-element.83), channel_id=1, source_target_pairs={{0,4},{1,5},{2,6},{3,7},{4,0},{5,1},{6,2},{7,3},{8,12},{9,13},{10,... | collective-permute-start | bytes 270344 | tf_op jit(solution)/shard_map/ppermute | solution.py:815
  72.4 2.1 %collective-permute-start.7 = (f32[88,256]{1,0:T(8,128)S(1)}, f32[88,256]{1,0:T(8,128)S(1)}, u32[]{:S(2)}, u32[]{:S(2)}) collective-permute-start(f32[88,256]{1,0:T(8,128)S(1)} %get-tuple-element.84), channel_id=1, source_target_pairs={{0,3},{1,2},{2,1},{3,0},{4,7},{5,6},{6,5},{7,4},{8,11},{9,10},{10,... | collective-permute-start | bytes 270344 | tf_op jit(solution)/shard_map/ppermute | solution.py:815
  74.5 0.0 collective-permute-done.3.refs_0_
  74.5 5.5 %collective-permute-start.8 = (f32[88,256]{1,0:T(8,128)S(1)}, f32[88,256]{1,0:T(8,128)S(1)}, u32[]{:S(2)}, u32[]{:S(2)}) collective-permute-start(f32[88,256]{1,0:T(8,128)S(1)} %get-tuple-element.85), channel_id=1, source_target_pairs={{0,2},{1,3},{2,0},{3,1},{4,6},{5,7},{6,4},{7,5},{8,10},{9,11},{10,... | collective-permute-start | bytes 270344 | tf_op jit(solution)/shard_map/ppermute | solution.py:815
  79.9 0.0 collective-permute-done.4.refs_1_
  80.0 1.5 %collective-permute-start.9 = (f32[88,256]{1,0:T(8,128)S(1)}, f32[88,256]{1,0:T(8,128)S(1)}, u32[]{:S(2)}, u32[]{:S(2)}) collective-permute-start(f32[88,256]{1,0:T(8,128)S(1)} %get-tuple-element.86), channel_id=1, source_target_pairs={{0,1},{1,0},{2,3},{3,2},{4,5},{5,4},{6,7},{7,6},{8,9},{9,8},{10,11... | collective-permute-start | bytes 270344 | tf_op jit(solution)/shard_map/ppermute | solution.py:815
  81.4 0.0 copy-done
  81.4 1.3 %gather_parts.1 = (f32[4,64,2048]{2,1,0:T(8,128)}, f32[4,64,256]{2,1,0:T(8,128)S(1)}) custom-call(s32[1]{0:T(128)} %bitcast.1.rank_ref, f32[64,2048]{1,0:T(8,128)S(1)} %copy-done, f32[64,2048]{1,0:T(8,128)S(1)} %collective-permute-done.refs_1_, f32[64,2048]{1,0:T(8,128)S(1)} %collective-permute-done.1.refs_2_, f32[64,2048]{1,0:T(8,128)S(1)} %collective-permute-done.2.refs_3_), custom_call_target="tpu_custom_call" | custom-call | bytes 4194304 | tf_op jit(solution)/shard_map/gather_parts/pallas_call | solution.py:730
  82.8 1.1 %collective-permute-done.5.refs_2_ = f32[88,256]{1,0:T(8,128)S(1)} collective-permute-done((f32[88,256]{1,0:T(8,128)S(1)}, f32[88,256]{1,0:T(8,128)S(1)}, u32[]{:S(2)}, u32[]{:S(2)}) %collective-permute-start.5) | collective-permute-done | bytes 90144 | tf_op jit(solution)/shard_map/ppermute | solution.py:815
  83.8 1.5 %collective-permute-done.6.refs_3_ = f32[88,256]{1,0:T(8,128)S(1)} collective-permute-done((f32[88,256]{1,0:T(8,128)S(1)}, f32[88,256]{1,0:T(8,128)S(1)}, u32[]{:S(2)}, u32[]{:S(2)}) %collective-permute-start.6) | collective-permute-done | bytes 90144 | tf_op jit(solution)/shard_map/ppermute | solution.py:815
  85.3 0.0 collective-permute-done.7.refs_4_
  85.3 0.7 collective-permute-done.8.refs_5_
  86.0 0.0 collective-permute-done.9.refs_6_
  86.0 1.0 %finish.1 = (f32[64,8,256]{2,1,0:T(8,128)}, f32[4,64,2048]{2,1,0:T(8,128)}) custom-call(s32[1]{0:T(128)} %bitcast.rank_ref, f32[88,256]{1,0:T(8,128)S(1)} %collective-permute-done.3.refs_0_, f32[88,256]{1,0:T(8,128)S(1)} %collective-permute-done.4.refs_1_, f32[88,256]{1,0:T(8,128)S(1)} %collective-permute-done.5.refs_2_, ...), custom_call_target="tpu_custom_call", output_to_operand_aliasing={{1}: (10, {})} | custom-call | bytes 1441792 | tf_op jit(solution)/shard_map/finish/pallas_call | solution.py:787
  (18 shorter events, 0.1 us)
Async XLA Ops:
  0.6 21.8 %all-to-all-start = ((f32[8,64,256]{2,1,0:T(8,128)}), f32[8,64,256]{2,1,0:T(8,128)S(1)}, u32[]{:S(2)}, u32[]{:S(2)}) async-start(f32[8,64,256]{2,1,0:T(8,128)} %bitcast.9), calls=%async_computation | async-start | bytes 1048576 | tf_op jit(solution)/shard_map/all_to_all | solution.py:833
  8.0 14.4 %copy-start.12 = (s32[64]{0:T(128)S(1)}, s32[64]{0:T(128)}, u32[]{:S(2)}) copy-start(s32[64]{0:T(128)} %param.13) | copy-start | bytes 772
  8.0 14.5 %copy-start.6 = (f32[4,8]{1,0:T(4,128)S(1)}, f32[4,8]{1,0:T(4,128)}, u32[]{:S(2)}) copy-start(f32[4,8]{1,0:T(4,128)} %param.11) | copy-start | bytes 388
  8.0 18.4 %copy-start.7 = (f32[32]{0:T(128)S(1)}, f32[32]{0:T(128)}, u32[]{:S(2)}) copy-start(f32[32]{0:T(128)} %constant.86) | copy-start | bytes 388
  8.0 18.4 %copy-start.8 = (f32[32]{0:T(128)S(1)}, f32[32]{0:T(128)}, u32[]{:S(2)}) copy-start(f32[32]{0:T(128)} %constant.85) | copy-start | bytes 388
  8.0 18.6 %copy-start.2 = (bf16[256,256]{1,0:T(8,128)(2,1)S(1)}, bf16[256,256]{1,0:T(8,128)(2,1)}, u32[]{:S(2)}) copy-start(bf16[256,256]{1,0:T(8,128)(2,1)} %constant.81.clone.flip_ref) | copy-start | bytes 393220
  8.0 18.6 %copy-start.3 = (f32[8,256]{1,0:T(8,128)S(1)}, f32[8,256]{1,0:T(8,128)}, u32[]{:S(2)}) copy-start(f32[8,256]{1,0:T(8,128)} %constant.83.clone.shift_y_ref) | copy-start | bytes 24580
  8.0 18.6 %copy-start.4 = (f32[8,256]{1,0:T(8,128)S(1)}, f32[8,256]{1,0:T(8,128)}, u32[]{:S(2)}) copy-start(f32[8,256]{1,0:T(8,128)} %constant.82.clone.shift_x_ref) | copy-start | bytes 24580
  22.4 15.8 %copy-start.1 = (f32[8,64,256]{2,1,0:T(8,128)}, f32[8,64,256]{2,1,0:T(8,128)S(1)}, u32[]{:S(2)}) copy-start(f32[8,64,256]{2,1,0:T(8,128)S(1)} %all-to-all-done.vol_ref) | copy-start | bytes 1572868
  22.7 16.3 %all-to-all-start.1 = ((f32[32,8,256]{2,1,0:T(8,128)}), f32[32,8,256]{2,1,0:T(8,128)S(1)}, u32[]{:S(2)}, u32[]{:S(2)}) async-start(f32[32,8,256]{2,1,0:T(8,128)} %bitcast.10), calls=%async_computation.1 | async-start | bytes 524288 | tf_op jit(solution)/shard_map/all_to_all | solution.py:833
  26.6 12.4 %copy-start.11 = (f32[64,2048]{1,0:T(8,128)S(1)}, f32[64,2048]{1,0:T(8,128)}, u32[]{:S(2)}) copy-start(f32[64,2048]{1,0:T(8,128)} %get-tuple-element.77) | copy-start | bytes 1572868
  26.7 12.6 %copy-start.10 = (f32[64,2048]{1,0:T(8,128)S(1)}, f32[64,2048]{1,0:T(8,128)}, u32[]{:S(2)}) copy-start(f32[64,2048]{1,0:T(8,128)} %get-tuple-element.78) | copy-start | bytes 1572868
  26.7 14.3 %copy-start.9 = (f32[64,2048]{1,0:T(8,128)S(1)}, f32[64,2048]{1,0:T(8,128)}, u32[]{:S(2)}) copy-start(f32[64,2048]{1,0:T(8,128)} %get-tuple-element.79) | copy-start | bytes 1572868
  38.2 0.8 copy-start.5
  39.0 25.6 %collective-permute-start = (f32[64,2048]{1,0:T(8,128)S(1)}, f32[64,2048]{1,0:T(8,128)S(1)}, u32[]{:S(2)}, u32[]{:S(2)}) collective-permute-start(f32[64,2048]{1,0:T(8,128)S(1)} %copy-done.11), channel_id=1, source_target_pairs={{0,8},{8,0},{16,24},{24,16},{1,9},{9,1},{17,25},{25,17},{2,10},{10... | collective-permute-start | bytes 1572872 | tf_op jit(solution)/shard_map/ppermute | solution.py:815
  39.3 25.3 %collective-permute-start.1 = (f32[64,2048]{1,0:T(8,128)S(1)}, f32[64,2048]{1,0:T(8,128)S(1)}, u32[]{:S(2)}, u32[]{:S(2)}) collective-permute-start(f32[64,2048]{1,0:T(8,128)S(1)} %copy-done.10), channel_id=1, source_target_pairs={{0,16},{8,24},{16,0},{24,8},{1,17},{9,25},{17,1},{25,9},{2,18},{10... | collective-permute-start | bytes 1572872 | tf_op jit(solution)/shard_map/ppermute | solution.py:815
  41.0 23.7 %collective-permute-start.2 = (f32[64,2048]{1,0:T(8,128)S(1)}, f32[64,2048]{1,0:T(8,128)S(1)}, u32[]{:S(2)}, u32[]{:S(2)}) collective-permute-start(f32[64,2048]{1,0:T(8,128)S(1)} %copy-done.9), channel_id=1, source_target_pairs={{0,24},{8,16},{16,8},{24,0},{1,25},{9,17},{17,9},{25,1},{2,26},{10... | collective-permute-start | bytes 1572872 | tf_op jit(solution)/shard_map/ppermute | solution.py:815
  41.0 40.4 %copy-start = (f32[64,2048]{1,0:T(8,128)S(1)}, f32[64,2048]{1,0:T(8,128)}, u32[]{:S(2)}) copy-start(f32[64,2048]{1,0:T(8,128)} %get-tuple-element.88.refs_0_) | copy-start | bytes 1572868
  64.7 9.8 %collective-permute-start.3 = (f32[88,256]{1,0:T(8,128)S(1)}, f32[88,256]{1,0:T(8,128)S(1)}, u32[]{:S(2)}, u32[]{:S(2)}) collective-permute-start(f32[88,256]{1,0:T(8,128)S(1)} %get-tuple-element.80), channel_id=1, source_target_pairs={{0,7},{1,6},{2,5},{3,4},{4,3},{5,2},{6,1},{7,0},{8,15},{9,14},{10,... | collective-permute-start | bytes 270344 | tf_op jit(solution)/shard_map/ppermute | solution.py:815
  69.2 10.8 %collective-permute-start.4 = (f32[88,256]{1,0:T(8,128)S(1)}, f32[88,256]{1,0:T(8,128)S(1)}, u32[]{:S(2)}, u32[]{:S(2)}) collective-permute-start(f32[88,256]{1,0:T(8,128)S(1)} %get-tuple-element.81), channel_id=1, source_target_pairs={{0,6},{1,7},{2,4},{3,5},{4,2},{5,3},{6,0},{7,1},{8,14},{9,15},{10,... | collective-permute-start | bytes 270344 | tf_op jit(solution)/shard_map/ppermute | solution.py:815
  69.6 14.2 %collective-permute-start.5 = (f32[88,256]{1,0:T(8,128)S(1)}, f32[88,256]{1,0:T(8,128)S(1)}, u32[]{:S(2)}, u32[]{:S(2)}) collective-permute-start(f32[88,256]{1,0:T(8,128)S(1)} %get-tuple-element.82), channel_id=1, source_target_pairs={{0,5},{1,4},{2,7},{3,6},{4,1},{5,0},{6,3},{7,2},{8,13},{9,12},{10,... | collective-permute-start | bytes 270344 | tf_op jit(solution)/shard_map/ppermute | solution.py:815
  70.2 15.1 %collective-permute-start.6 = (f32[88,256]{1,0:T(8,128)S(1)}, f32[88,256]{1,0:T(8,128)S(1)}, u32[]{:S(2)}, u32[]{:S(2)}) collective-permute-start(f32[88,256]{1,0:T(8,128)S(1)} %get-tuple-element.83), channel_id=1, source_target_pairs={{0,4},{1,5},{2,6},{3,7},{4,0},{5,1},{6,2},{7,3},{8,12},{9,13},{10,... | collective-permute-start | bytes 270344 | tf_op jit(solution)/shard_map/ppermute | solution.py:815
  72.4 12.9 %collective-permute-start.7 = (f32[88,256]{1,0:T(8,128)S(1)}, f32[88,256]{1,0:T(8,128)S(1)}, u32[]{:S(2)}, u32[]{:S(2)}) collective-permute-start(f32[88,256]{1,0:T(8,128)S(1)} %get-tuple-element.84), channel_id=1, source_target_pairs={{0,3},{1,2},{2,1},{3,0},{4,7},{5,6},{6,5},{7,4},{8,11},{9,10},{10,... | collective-permute-start | bytes 270344 | tf_op jit(solution)/shard_map/ppermute | solution.py:815
  74.5 11.6 %collective-permute-start.8 = (f32[88,256]{1,0:T(8,128)S(1)}, f32[88,256]{1,0:T(8,128)S(1)}, u32[]{:S(2)}, u32[]{:S(2)}) collective-permute-start(f32[88,256]{1,0:T(8,128)S(1)} %get-tuple-element.85), channel_id=1, source_target_pairs={{0,2},{1,3},{2,0},{3,1},{4,6},{5,7},{6,4},{7,5},{8,10},{9,11},{10,... | collective-permute-start | bytes 270344 | tf_op jit(solution)/shard_map/ppermute | solution.py:815
  80.0 6.1 %collective-permute-start.9 = (f32[88,256]{1,0:T(8,128)S(1)}, f32[88,256]{1,0:T(8,128)S(1)}, u32[]{:S(2)}, u32[]{:S(2)}) collective-permute-start(f32[88,256]{1,0:T(8,128)S(1)} %get-tuple-element.86), channel_id=1, source_target_pairs={{0,1},{1,0},{2,3},{3,2},{4,5},{5,4},{6,7},{7,6},{8,9},{9,8},{10,11... | collective-permute-start | bytes 270344 | tf_op jit(solution)/shard_map/ppermute | solution.py:815

commit v13 on v12

--- a/solution.py
+++ b/solution.py
@@ -241,7 +241,8 @@
 
     def prepare(self, shift_x_ref, shift_y_ref, cos_ref, sin_ref):
         def along_angle(t):
-            self.along_ref[t] = shift_x_ref[...] * cos_ref[t] + shift_y_ref[...] * sin_ref[t]
+            along = shift_x_ref[...] * cos_ref[t] + shift_y_ref[...] * sin_ref[t]
+            self.along_ref[t] = self.ray - along
 
         repeat(self.angles, along_angle, 8)
 
@@ -250,8 +251,7 @@
             pieces = []
             for t in (2 * two, 2 * two + 1):
                 angle = c * self.chunk + t
-                along = self.along_ref[angle] + self.place_ref[q * self.angles + angle]
-                base = self.ray - along
+                base = self.along_ref[angle] - self.place_ref[q * self.angles + angle]
                 for group in range(WIN // ROWS):
                     distance = base + float(group * ROWS)
                     pieces.append(jnp.maximum(0.0, 1.0 - jnp.abs(distance)))
@@ -430,8 +430,9 @@
     spread_rays(acc_ref, predicted_ref, mirror_ref, gain_ref, slices, chunk)
     direct, mirror, weight_sums = predicted_ref[...], mirror_ref[0:angles], gain_ref[...]
     predicted_ref[...] = direct + turn_rays(mirror, flip)
-    direct = weight_sums
-    gain_ref[...] = 1.0 / jnp.maximum(direct + turn_rays(direct, flip), row_floor)
+    turned = turn_rays(weight_sums[:, 0, :], flip)
+    total = weight_sums + turned[:, None, :]
+    gain_ref[...] = 1.0 / jnp.maximum(total, row_floor)
     kept.wait()
 
 
@@ -744,6 +745,12 @@
     )(rank.reshape(1), *parts)
 
 
+def message_order(count):
+    near = [d for d in (1, 2) if d < count // 2]
+    far = list(range(count - 1, count // 2 - 1, -1))
+    return near + far + [d for d in range(count // 2 - 1, -1, -1) if d not in near]
+
+
 def finish_kernel(rank_ref, *refs):
     *got_refs, given_ref, _, rec_ref, out_ref, values_ref, active_ref, sems = refs
     rays = len(got_refs)
@@ -753,7 +760,7 @@
     lead = slices * slots
     lane = lax.broadcasted_iota(jnp.int32, (slices, ACTIVE), 1)
     live = (lane >= EDGE) & (lane < ACTIVE - EDGE)
-    for d, got_ref in enumerate(reversed(got_refs)):
+    for d, got_ref in zip(message_order(rays), got_refs):
         rows = pl.ds(pl.multiple_of((rank_ref[0] ^ d) * slices, slices), slices)
         values_ref[rows] = got_ref[0:lead, :].reshape(slices, slots, VOX)
         for k in range(slabs):
@@ -805,7 +812,7 @@
             flops=0, bytes_accessed=8 * len(pieces) * pieces[0].size, transcendentals=0
         ),
         name="finish",
-    )(rank.reshape(1), *reversed(pieces), given, sinogram)
+    )(rank.reshape(1), *[pieces[d] for d in message_order(len(pieces))], given, sinogram)
 
 
 def exchange(pieces, axis):

time: 87.3 us -> 87.4 us (level)
  waiting for transfers between devices: 8.53 us -> 14.8 us
  starting transfers between devices: 29.7 us -> 23.8 us
    ppermute x10, waiting for transfers between devices: 3.27 us -> 9.54 us  [exchange(): lax.ppermute(pieces[d], axis, [(i, i ^ d) for i in range(count)])]
    ppermute x10, starting transfers between devices: 18.7 us -> 12.9 us  [exchange(): lax.ppermute(pieces[d], axis, [(i, i ^ d) for i in range(count)])]
where the time goes in v13:
time: 87.4 us; the launch traced here: 87.1 us
  Pallas kernels  46.2 us (53%)
  starting transfers between devices  23.8 us (27%)
  waiting for transfers between devices  14.8 us (17%)
  local copies, waits for them, and re-layouts  1.2 us (1%)
    pallas_call x2, Pallas kernels, call(): pl.pallas_call(kernel, out_shape=[jax.ShapeDtypeStruct(*value) for value...  34.8 us
    ppermute x10, starting transfers between devices, exchange(): lax.ppermute(pieces[d], axis, [(i, i ^ d) for i in range(count)])  12.9 us
    all_to_all x2, starting transfers between devices, to_all(): return lax.all_to_all(values, axes, split_axis=0, concat_axis=0, tiled=True)  11 us
    ppermute x10, waiting for transfers between devices, exchange(): lax.ppermute(pieces[d], axis, [(i, i ^ d) for i in range(count)])  9.54 us
    pallas_call x1, Pallas kernels, paganin(): pl.pallas_call(filter_kernel, out_shape=[jax.ShapeDtypeStruct((height //...  9.07 us
    all_to_all x2, waiting for transfers between devices, to_all(): return lax.all_to_all(values, axes, split_axis=0, concat_axis=0, tiled=True)  5.27 us
  transfers between devices with their start and end apart: 12, of which 4 were waited for; matrix products, arithmetic and copies ran while one was open for 0% of the time, Pallas kernels for 52%

profile of v13, /device:TPU:0, one launch (start us, length us, event | category | flops | bytes accessed | tf_op | source)
XLA Modules:
  0.0 87.1 jit_solution(3665839068939009824)
XLA Ops:
  0.6 7.3 %all-to-all-start = ((f32[8,64,256]{2,1,0:T(8,128)}), f32[8,64,256]{2,1,0:T(8,128)S(1)}, u32[]{:S(2)}, u32[]{:S(2)}) async-start(f32[8,64,256]{2,1,0:T(8,128)} %bitcast.9), calls=%async_computation | async-start | bytes 1048576 | tf_op jit(solution)/shard_map/all_to_all | solution.py:840
  7.9 0.1 sub.24
  8.0 0.0 copy-start.2
  8.0 0.0 copy-start.3
  8.0 0.0 copy-start.4
  8.0 9.1 %paganin.1 = (f32[64,2048]{1,0:T(8,128)}, f32[64,2048]{1,0:T(8,128)}, f32[64,2048]{1,0:T(8,128)}, f32[64,2048]{1,0:T(8,128)}, f32[256,256]{1,0:T(8,128)}) custom-call(s32[1]{0:T(128)} %bitcast.1.rank_ref, f32[256,2048]{1,0:T(8,128)} %bitcast.11, f32[264,256]{1,0:T(8,128)} %constant.78.clone.given_ref), custom_call_target="tpu_custom_call" | custom-call | flops 8589934592 | bytes 4194304 | tf_op jit(solution)/shard_map/paganin/pallas_call | solution.py:203
  17.1 5.3 %all-to-all-done.vol_ref = f32[8,64,256]{2,1,0:T(8,128)S(1)} async-done(((f32[8,64,256]{2,1,0:T(8,128)}), f32[8,64,256]{2,1,0:T(8,128)S(1)}, u32[]{:S(2)}, u32[]{:S(2)}) %all-to-all-start) | async-done | bytes 524320 | tf_op jit(solution)/shard_map/all_to_all | solution.py:840
  22.4 0.0 copy-done.12
  22.4 0.1 select_reduce_fusion.slot_ref
  22.5 0.0 copy-done.6
  22.5 0.1 cos.6.cos_ref
  22.6 0.1 sin.6.sin_ref
  22.7 3.7 %all-to-all-start.1 = ((f32[32,8,256]{2,1,0:T(8,128)}), f32[32,8,256]{2,1,0:T(8,128)S(1)}, u32[]{:S(2)}, u32[]{:S(2)}) async-start(f32[32,8,256]{2,1,0:T(8,128)} %bitcast.10), calls=%async_computation.1 | async-start | bytes 524288 | tf_op jit(solution)/shard_map/all_to_all | solution.py:840
  26.4 0.0 copy-done.7
  26.4 0.0 copy-done.8
  26.4 0.1 add_add_fusion
  26.5 0.1 add.64
  26.6 0.0 copy-done.2
  26.6 0.0 copy-done.3
  26.6 0.0 copy-done.4
  26.7 11.3 %first.1 = (f32[32,16,256]{2,1,0:T(8,128)S(1)}, f32[32,8,256]{2,1,0:T(8,128)S(1)}, f32[32,8,256]{2,1,0:T(8,128)S(1)}) custom-call(f32[1024]{0:T(1024)S(1)} %fusion.1.place_ref, s32[1024]{0:T(1024)S(1)} %get-tuple-element.102.offset_ref, s32[64]{0:T(128)S(1)} %select_reduce_fusion.slot_ref, f32[32]{0:T(128)S(1)} %cos.6.cos_ref, f32[32]{0:T(128)S(1)} %sin.6.sin_ref, ...), custom_call_target="tpu_custom_call" | custom-call | flops 14000000000 | bytes 4194304 | tf_op jit(solution)/shard_map/first/pallas_call | solution.py:612
  38.1 0.8 copy-done.5
  38.8 0.0 all-to-all-done.1.sino_ref
  38.8 0.3 collective-permute-start
  39.1 1.7 %collective-permute-start.1 = (f32[64,2048]{1,0:T(8,128)S(1)}, f32[64,2048]{1,0:T(8,128)S(1)}, u32[]{:S(2)}, u32[]{:S(2)}) collective-permute-start(f32[64,2048]{1,0:T(8,128)S(1)} %copy-done.10), channel_id=1, source_target_pairs={{0,16},{8,24},{16,0},{24,8},{1,17},{9,25},{17,1},{25,9},{2,18},{10... | collective-permute-start | bytes 1572872 | tf_op jit(solution)/shard_map/ppermute | solution.py:822
  40.8 0.0 copy-done.9
  40.8 0.0 collective-permute-start.2
  40.8 23.4 %second.1 = (f32[88,256]{1,0:T(8,128)S(1)}, f32[88,256]{1,0:T(8,128)S(1)}, f32[88,256]{1,0:T(8,128)S(1)}, f32[88,256]{1,0:T(8,128)S(1)}, f32[88,256]{1,0:T(8,128...) custom-call(s32[1]{0:T(128)} %bitcast.rank_ref, ...), custom_call_target="tpu_custom_call" | custom-call | flops 25999998976 | bytes 4194304 | tf_op jit(solution)/shard_map/second/pallas_call | solution.py:612
  64.3 0.0 collective-permute-done.refs_1_
  64.3 0.0 collective-permute-done.1.refs_2_
  64.3 0.0 collective-permute-done.2.refs_3_
  64.3 1.7 %collective-permute-start.3 = (f32[88,256]{1,0:T(8,128)S(1)}, f32[88,256]{1,0:T(8,128)S(1)}, u32[]{:S(2)}, u32[]{:S(2)}) collective-permute-start(f32[88,256]{1,0:T(8,128)S(1)} %get-tuple-element.80), channel_id=1, source_target_pairs={{0,1},{1,0},{2,3},{3,2},{4,5},{5,4},{6,7},{7,6},{8,9},{9,8},{10,11... | collective-permute-start | bytes 270344 | tf_op jit(solution)/shard_map/ppermute | solution.py:822
  66.0 1.5 %collective-permute-start.4 = (f32[88,256]{1,0:T(8,128)S(1)}, f32[88,256]{1,0:T(8,128)S(1)}, u32[]{:S(2)}, u32[]{:S(2)}) collective-permute-start(f32[88,256]{1,0:T(8,128)S(1)} %get-tuple-element.81), channel_id=1, source_target_pairs={{0,2},{1,3},{2,0},{3,1},{4,6},{5,7},{6,4},{7,5},{8,10},{9,11},{10,... | collective-permute-start | bytes 270344 | tf_op jit(solution)/shard_map/ppermute | solution.py:822
  67.5 2.4 %collective-permute-start.5 = (f32[88,256]{1,0:T(8,128)S(1)}, f32[88,256]{1,0:T(8,128)S(1)}, u32[]{:S(2)}, u32[]{:S(2)}) collective-permute-start(f32[88,256]{1,0:T(8,128)S(1)} %get-tuple-element.82), channel_id=1, source_target_pairs={{0,7},{1,6},{2,5},{3,4},{4,3},{5,2},{6,1},{7,0},{8,15},{9,14},{10,... | collective-permute-start | bytes 270344 | tf_op jit(solution)/shard_map/ppermute | solution.py:822
  69.8 1.5 %collective-permute-start.6 = (f32[88,256]{1,0:T(8,128)S(1)}, f32[88,256]{1,0:T(8,128)S(1)}, u32[]{:S(2)}, u32[]{:S(2)}) collective-permute-start(f32[88,256]{1,0:T(8,128)S(1)} %get-tuple-element.83), channel_id=1, source_target_pairs={{0,6},{1,7},{2,4},{3,5},{4,2},{5,3},{6,0},{7,1},{8,14},{9,15},{10,... | collective-permute-start | bytes 270344 | tf_op jit(solution)/shard_map/ppermute | solution.py:822
  71.3 1.5 %collective-permute-start.7 = (f32[88,256]{1,0:T(8,128)S(1)}, f32[88,256]{1,0:T(8,128)S(1)}, u32[]{:S(2)}, u32[]{:S(2)}) collective-permute-start(f32[88,256]{1,0:T(8,128)S(1)} %get-tuple-element.84), channel_id=1, source_target_pairs={{0,5},{1,4},{2,7},{3,6},{4,1},{5,0},{6,3},{7,2},{8,13},{9,12},{10,... | collective-permute-start | bytes 270344 | tf_op jit(solution)/shard_map/ppermute | solution.py:822
  72.8 0.0 collective-permute-done.3.refs_0_
  72.8 2.3 %collective-permute-start.8 = (f32[88,256]{1,0:T(8,128)S(1)}, f32[88,256]{1,0:T(8,128)S(1)}, u32[]{:S(2)}, u32[]{:S(2)}) collective-permute-start(f32[88,256]{1,0:T(8,128)S(1)} %get-tuple-element.85), channel_id=1, source_target_pairs={{0,4},{1,5},{2,6},{3,7},{4,0},{5,1},{6,2},{7,3},{8,12},{9,13},{10,... | collective-permute-start | bytes 270344 | tf_op jit(solution)/shard_map/ppermute | solution.py:822
  75.1 0.0 collective-permute-done.4.refs_1_
  75.1 0.1 collective-permute-start.9
  75.2 0.0 copy-done
  75.2 1.3 %gather_parts.1 = (f32[4,64,2048]{2,1,0:T(8,128)}, f32[4,64,256]{2,1,0:T(8,128)S(1)}) custom-call(s32[1]{0:T(128)} %bitcast.1.rank_ref, f32[64,2048]{1,0:T(8,128)S(1)} %copy-done, f32[64,2048]{1,0:T(8,128)S(1)} %collective-permute-done.refs_1_, f32[64,2048]{1,0:T(8,128)S(1)} %collective-permute-done.1.refs_2_, f32[64,2048]{1,0:T(8,128)S(1)} %collective-permute-done.2.refs_3_), custom_call_target="tpu_custom_call" | custom-call | bytes 4194304 | tf_op jit(solution)/shard_map/gather_parts/pallas_call | solution.py:731
  76.6 0.0 collective-permute-done.5.refs_2_
  76.6 0.7 collective-permute-done.6.refs_3_
  77.2 7.4 %collective-permute-done.7.refs_4_ = f32[88,256]{1,0:T(8,128)S(1)} collective-permute-done((f32[88,256]{1,0:T(8,128)S(1)}, f32[88,256]{1,0:T(8,128)S(1)}, u32[]{:S(2)}, u32[]{:S(2)}) %collective-permute-start.7) | collective-permute-done | bytes 90144 | tf_op jit(solution)/shard_map/ppermute | solution.py:822
  84.6 1.5 %collective-permute-done.8.refs_5_ = f32[88,256]{1,0:T(8,128)S(1)} collective-permute-done((f32[88,256]{1,0:T(8,128)S(1)}, f32[88,256]{1,0:T(8,128)S(1)}, u32[]{:S(2)}, u32[]{:S(2)}) %collective-permute-start.8) | collective-permute-done | bytes 90144 | tf_op jit(solution)/shard_map/ppermute | solution.py:822
  86.1 0.0 collective-permute-done.9.refs_6_
  86.1 1.0 %finish.1 = (f32[64,8,256]{2,1,0:T(8,128)}, f32[4,64,2048]{2,1,0:T(8,128)}) custom-call(s32[1]{0:T(128)} %bitcast.rank_ref, f32[88,256]{1,0:T(8,128)S(1)} %collective-permute-done.3.refs_0_, f32[88,256]{1,0:T(8,128)S(1)} %collective-permute-done.4.refs_1_, f32[88,256]{1,0:T(8,128)S(1)} %collective-permute-done.5.refs_2_, ...), custom_call_target="tpu_custom_call", output_to_operand_aliasing={{1}: (10, {})} | custom-call | bytes 1441792 | tf_op jit(solution)/shard_map/finish/pallas_call | solution.py:794
  (18 shorter events, 0.1 us)
Async XLA Ops:
  0.6 21.8 %all-to-all-start = ((f32[8,64,256]{2,1,0:T(8,128)}), f32[8,64,256]{2,1,0:T(8,128)S(1)}, u32[]{:S(2)}, u32[]{:S(2)}) async-start(f32[8,64,256]{2,1,0:T(8,128)} %bitcast.9), calls=%async_computation | async-start | bytes 1048576 | tf_op jit(solution)/shard_map/all_to_all | solution.py:840
  8.0 14.4 %copy-start.12 = (s32[64]{0:T(128)S(1)}, s32[64]{0:T(128)}, u32[]{:S(2)}) copy-start(s32[64]{0:T(128)} %param.13) | copy-start | bytes 772
  8.0 14.5 %copy-start.6 = (f32[4,8]{1,0:T(4,128)S(1)}, f32[4,8]{1,0:T(4,128)}, u32[]{:S(2)}) copy-start(f32[4,8]{1,0:T(4,128)} %param.11) | copy-start | bytes 388
  8.0 18.4 %copy-start.7 = (f32[32]{0:T(128)S(1)}, f32[32]{0:T(128)}, u32[]{:S(2)}) copy-start(f32[32]{0:T(128)} %constant.86) | copy-start | bytes 388
  8.0 18.4 %copy-start.8 = (f32[32]{0:T(128)S(1)}, f32[32]{0:T(128)}, u32[]{:S(2)}) copy-start(f32[32]{0:T(128)} %constant.85) | copy-start | bytes 388
  8.0 18.6 %copy-start.2 = (bf16[256,256]{1,0:T(8,128)(2,1)S(1)}, bf16[256,256]{1,0:T(8,128)(2,1)}, u32[]{:S(2)}) copy-start(bf16[256,256]{1,0:T(8,128)(2,1)} %constant.81.clone.flip_ref) | copy-start | bytes 393220
  8.0 18.6 %copy-start.3 = (f32[8,256]{1,0:T(8,128)S(1)}, f32[8,256]{1,0:T(8,128)}, u32[]{:S(2)}) copy-start(f32[8,256]{1,0:T(8,128)} %constant.83.clone.shift_y_ref) | copy-start | bytes 24580
  8.0 18.6 %copy-start.4 = (f32[8,256]{1,0:T(8,128)S(1)}, f32[8,256]{1,0:T(8,128)}, u32[]{:S(2)}) copy-start(f32[8,256]{1,0:T(8,128)} %constant.82.clone.shift_x_ref) | copy-start | bytes 24580
  22.4 15.7 %copy-start.1 = (f32[8,64,256]{2,1,0:T(8,128)}, f32[8,64,256]{2,1,0:T(8,128)S(1)}, u32[]{:S(2)}) copy-start(f32[8,64,256]{2,1,0:T(8,128)S(1)} %all-to-all-done.vol_ref) | copy-start | bytes 1572868
  22.7 16.1 %all-to-all-start.1 = ((f32[32,8,256]{2,1,0:T(8,128)}), f32[32,8,256]{2,1,0:T(8,128)S(1)}, u32[]{:S(2)}, u32[]{:S(2)}) async-start(f32[32,8,256]{2,1,0:T(8,128)} %bitcast.10), calls=%async_computation.1 | async-start | bytes 524288 | tf_op jit(solution)/shard_map/all_to_all | solution.py:840
  26.6 12.2 %copy-start.11 = (f32[64,2048]{1,0:T(8,128)S(1)}, f32[64,2048]{1,0:T(8,128)}, u32[]{:S(2)}) copy-start(f32[64,2048]{1,0:T(8,128)} %get-tuple-element.77) | copy-start | bytes 1572868
  26.7 12.4 %copy-start.10 = (f32[64,2048]{1,0:T(8,128)S(1)}, f32[64,2048]{1,0:T(8,128)}, u32[]{:S(2)}) copy-start(f32[64,2048]{1,0:T(8,128)} %get-tuple-element.78) | copy-start | bytes 1572868
  26.7 14.1 %copy-start.9 = (f32[64,2048]{1,0:T(8,128)S(1)}, f32[64,2048]{1,0:T(8,128)}, u32[]{:S(2)}) copy-start(f32[64,2048]{1,0:T(8,128)} %get-tuple-element.79) | copy-start | bytes 1572868
  38.0 0.8 copy-start.5
  38.8 25.4 %collective-permute-start = (f32[64,2048]{1,0:T(8,128)S(1)}, f32[64,2048]{1,0:T(8,128)S(1)}, u32[]{:S(2)}, u32[]{:S(2)}) collective-permute-start(f32[64,2048]{1,0:T(8,128)S(1)} %copy-done.11), channel_id=1, source_target_pairs={{0,8},{8,0},{16,24},{24,16},{1,9},{9,1},{17,25},{25,17},{2,10},{10... | collective-permute-start | bytes 1572872 | tf_op jit(solution)/shard_map/ppermute | solution.py:822
  39.1 25.2 %collective-permute-start.1 = (f32[64,2048]{1,0:T(8,128)S(1)}, f32[64,2048]{1,0:T(8,128)S(1)}, u32[]{:S(2)}, u32[]{:S(2)}) collective-permute-start(f32[64,2048]{1,0:T(8,128)S(1)} %copy-done.10), channel_id=1, source_target_pairs={{0,16},{8,24},{16,0},{24,8},{1,17},{9,25},{17,1},{25,9},{2,18},{10... | collective-permute-start | bytes 1572872 | tf_op jit(solution)/shard_map/ppermute | solution.py:822
  40.8 23.5 %collective-permute-start.2 = (f32[64,2048]{1,0:T(8,128)S(1)}, f32[64,2048]{1,0:T(8,128)S(1)}, u32[]{:S(2)}, u32[]{:S(2)}) collective-permute-start(f32[64,2048]{1,0:T(8,128)S(1)} %copy-done.9), channel_id=1, source_target_pairs={{0,24},{8,16},{16,8},{24,0},{1,25},{9,17},{17,9},{25,1},{2,26},{10... | collective-permute-start | bytes 1572872 | tf_op jit(solution)/shard_map/ppermute | solution.py:822
  40.8 34.4 %copy-start = (f32[64,2048]{1,0:T(8,128)S(1)}, f32[64,2048]{1,0:T(8,128)}, u32[]{:S(2)}) copy-start(f32[64,2048]{1,0:T(8,128)} %get-tuple-element.88.refs_0_) | copy-start | bytes 1572868
  64.3 8.6 %collective-permute-start.3 = (f32[88,256]{1,0:T(8,128)S(1)}, f32[88,256]{1,0:T(8,128)S(1)}, u32[]{:S(2)}, u32[]{:S(2)}) collective-permute-start(f32[88,256]{1,0:T(8,128)S(1)} %get-tuple-element.80), channel_id=1, source_target_pairs={{0,1},{1,0},{2,3},{3,2},{4,5},{5,4},{6,7},{7,6},{8,9},{9,8},{10,11... | collective-permute-start | bytes 270344 | tf_op jit(solution)/shard_map/ppermute | solution.py:822
  66.0 9.1 %collective-permute-start.4 = (f32[88,256]{1,0:T(8,128)S(1)}, f32[88,256]{1,0:T(8,128)S(1)}, u32[]{:S(2)}, u32[]{:S(2)}) collective-permute-start(f32[88,256]{1,0:T(8,128)S(1)} %get-tuple-element.81), channel_id=1, source_target_pairs={{0,2},{1,3},{2,0},{3,1},{4,6},{5,7},{6,4},{7,5},{8,10},{9,11},{10,... | collective-permute-start | bytes 270344 | tf_op jit(solution)/shard_map/ppermute | solution.py:822
  67.5 9.1 %collective-permute-start.5 = (f32[88,256]{1,0:T(8,128)S(1)}, f32[88,256]{1,0:T(8,128)S(1)}, u32[]{:S(2)}, u32[]{:S(2)}) collective-permute-start(f32[88,256]{1,0:T(8,128)S(1)} %get-tuple-element.82), channel_id=1, source_target_pairs={{0,7},{1,6},{2,5},{3,4},{4,3},{5,2},{6,1},{7,0},{8,15},{9,14},{10,... | collective-permute-start | bytes 270344 | tf_op jit(solution)/shard_map/ppermute | solution.py:822
  69.8 7.4 %collective-permute-start.6 = (f32[88,256]{1,0:T(8,128)S(1)}, f32[88,256]{1,0:T(8,128)S(1)}, u32[]{:S(2)}, u32[]{:S(2)}) collective-permute-start(f32[88,256]{1,0:T(8,128)S(1)} %get-tuple-element.83), channel_id=1, source_target_pairs={{0,6},{1,7},{2,4},{3,5},{4,2},{5,3},{6,0},{7,1},{8,14},{9,15},{10,... | collective-permute-start | bytes 270344 | tf_op jit(solution)/shard_map/ppermute | solution.py:822
  71.3 13.3 %collective-permute-start.7 = (f32[88,256]{1,0:T(8,128)S(1)}, f32[88,256]{1,0:T(8,128)S(1)}, u32[]{:S(2)}, u32[]{:S(2)}) collective-permute-start(f32[88,256]{1,0:T(8,128)S(1)} %get-tuple-element.84), channel_id=1, source_target_pairs={{0,5},{1,4},{2,7},{3,6},{4,1},{5,0},{6,3},{7,2},{8,13},{9,12},{10,... | collective-permute-start | bytes 270344 | tf_op jit(solution)/shard_map/ppermute | solution.py:822
  72.8 13.3 %collective-permute-start.8 = (f32[88,256]{1,0:T(8,128)S(1)}, f32[88,256]{1,0:T(8,128)S(1)}, u32[]{:S(2)}, u32[]{:S(2)}) collective-permute-start(f32[88,256]{1,0:T(8,128)S(1)} %get-tuple-element.85), channel_id=1, source_target_pairs={{0,4},{1,5},{2,6},{3,7},{4,0},{5,1},{6,2},{7,3},{8,12},{9,13},{10,... | collective-permute-start | bytes 270344 | tf_op jit(solution)/shard_map/ppermute | solution.py:822
  75.1 11.0 %collective-permute-start.9 = (f32[88,256]{1,0:T(8,128)S(1)}, f32[88,256]{1,0:T(8,128)S(1)}, u32[]{:S(2)}, u32[]{:S(2)}) collective-permute-start(f32[88,256]{1,0:T(8,128)S(1)} %get-tuple-element.86), channel_id=1, source_target_pairs={{0,3},{1,2},{2,1},{3,0},{4,7},{5,6},{6,5},{7,4},{8,11},{9,10},{10,... | collective-permute-start | bytes 270344 | tf_op jit(solution)/shard_map/ppermute | solution.py:822

commit v14 on v13

--- a/solution.py
+++ b/solution.py
@@ -22,7 +22,7 @@
 SPLIT = 64
 EDGE = 32
 GROUP = 8
-CYCLE = 4
+CYCLE = 8
 
 paganin_strength = 10.0
 relax = 1.8

time: 87.4 us -> 86.5 us (0.990)
  Pallas kernels: 46.2 us -> 44.4 us
  waiting for transfers between devices: 14.8 us -> 15.7 us
    pallas_call x2, Pallas kernels: 34.8 us -> 33 us  [call(): pl.pallas_call(kernel, out_shape=[jax.ShapeDtypeStruct(*value) for value...]
  transfers between devices with their start and end apart: 12 -> 12, of which waited for: 4 -> 5; matrix products, arithmetic and copies ran while one was open for 0% -> 0% of each run, Pallas kernels for 52% -> 50%
where the time goes in v14:
time: 86.5 us; the launch traced here: 86.2 us
  Pallas kernels  44.4 us (51%)
  starting transfers between devices  23.7 us (27%)
  waiting for transfers between devices  15.7 us (18%)
  local copies, waits for them, and re-layouts  1.2 us (1%)
  between operations  1 us (1%)
    pallas_call x2, Pallas kernels, call(): pl.pallas_call(kernel, out_shape=[jax.ShapeDtypeStruct(*value) for value...  33 us
    ppermute x10, starting transfers between devices, exchange(): lax.ppermute(pieces[d], axis, [(i, i ^ d) for i in range(count)])  12.6 us
    all_to_all x2, starting transfers between devices, to_all(): return lax.all_to_all(values, axes, split_axis=0, concat_axis=0, tiled=True)  11.1 us
    ppermute x10, waiting for transfers between devices, exchange(): lax.ppermute(pieces[d], axis, [(i, i ^ d) for i in range(count)])  10.4 us
    pallas_call x1, Pallas kernels, paganin(): pl.pallas_call(filter_kernel, out_shape=[jax.ShapeDtypeStruct((height //...  9.07 us
    all_to_all x2, waiting for transfers between devices, to_all(): return lax.all_to_all(values, axes, split_axis=0, concat_axis=0, tiled=True)  5.27 us
  transfers between devices with their start and end apart: 12, of which 5 were waited for; matrix products, arithmetic and copies ran while one was open for 0% of the time, Pallas kernels for 50%

profile of v14, /device:TPU:0, one launch (start us, length us, event | category | flops | bytes accessed | tf_op | source)
XLA Modules:
  0.0 86.2 jit_solution(10478821199572426430)
XLA Ops:
  0.6 7.3 %all-to-all-start = ((f32[8,64,256]{2,1,0:T(8,128)}), f32[8,64,256]{2,1,0:T(8,128)S(1)}, u32[]{:S(2)}, u32[]{:S(2)}) async-start(f32[8,64,256]{2,1,0:T(8,128)} %bitcast.9), calls=%async_computation | async-start | bytes 1048576 | tf_op jit(solution)/shard_map/all_to_all | solution.py:840
  7.9 0.1 sub.24
  8.0 0.0 copy-start.2
  8.0 0.0 copy-start.3
  8.0 0.0 copy-start.4
  8.0 9.1 %paganin.1 = (f32[64,2048]{1,0:T(8,128)}, f32[64,2048]{1,0:T(8,128)}, f32[64,2048]{1,0:T(8,128)}, f32[64,2048]{1,0:T(8,128)}, f32[256,256]{1,0:T(8,128)}) custom-call(s32[1]{0:T(128)} %bitcast.1.rank_ref, f32[256,2048]{1,0:T(8,128)} %bitcast.11, f32[264,256]{1,0:T(8,128)} %constant.78.clone.given_ref), custom_call_target="tpu_custom_call" | custom-call | flops 8589934592 | bytes 4194304 | tf_op jit(solution)/shard_map/paganin/pallas_call | solution.py:203
  17.1 5.3 %all-to-all-done.vol_ref = f32[8,64,256]{2,1,0:T(8,128)S(1)} async-done(((f32[8,64,256]{2,1,0:T(8,128)}), f32[8,64,256]{2,1,0:T(8,128)S(1)}, u32[]{:S(2)}, u32[]{:S(2)}) %all-to-all-start) | async-done | bytes 524320 | tf_op jit(solution)/shard_map/all_to_all | solution.py:840
  22.4 0.1 select_reduce_fusion.slot_ref
  22.5 0.0 copy-done.6
  22.5 0.1 cos.6.cos_ref
  22.6 0.1 sin.6.sin_ref
  22.7 3.9 %all-to-all-start.1 = ((f32[32,8,256]{2,1,0:T(8,128)}), f32[32,8,256]{2,1,0:T(8,128)S(1)}, u32[]{:S(2)}, u32[]{:S(2)}) async-start(f32[32,8,256]{2,1,0:T(8,128)} %bitcast.10), calls=%async_computation.1 | async-start | bytes 524288 | tf_op jit(solution)/shard_map/all_to_all | solution.py:840
  26.6 0.1 add_add_fusion
  26.7 0.1 add.64
  26.8 0.0 copy-done.2
  26.8 0.0 copy-done.3
  26.8 0.0 copy-done.4
  26.8 0.0 copy-start.11
  26.8 0.0 copy-start.10
  26.8 0.0 copy-start.9
  26.9 10.7 %first.1 = (f32[32,16,256]{2,1,0:T(8,128)S(1)}, f32[32,8,256]{2,1,0:T(8,128)S(1)}, f32[32,8,256]{2,1,0:T(8,128)S(1)}) custom-call(f32[1024]{0:T(1024)S(1)} %fusion.1.place_ref, s32[1024]{0:T(1024)S(1)} %get-tuple-element.102.offset_ref, s32[64]{0:T(128)S(1)} %select_reduce_fusion.slot_ref, f32[32]{0:T(128)S(1)} %cos.6.cos_ref, f32[32]{0:T(128)S(1)} %sin.6.sin_ref, ...), custom_call_target="tpu_custom_call" | custom-call | flops 14000000000 | bytes 4194304 | tf_op jit(solution)/shard_map/first/pallas_call | solution.py:612
  37.6 0.0 copy-done.1
  37.6 0.0 copy-start.5
  37.6 0.8 copy-done.5
  38.4 0.0 all-to-all-done.1.sino_ref
  38.4 0.1 collective-permute-start
  38.5 1.7 %collective-permute-start.1 = (f32[64,2048]{1,0:T(8,128)S(1)}, f32[64,2048]{1,0:T(8,128)S(1)}, u32[]{:S(2)}, u32[]{:S(2)}) collective-permute-start(f32[64,2048]{1,0:T(8,128)S(1)} %copy-done.10), channel_id=1, source_target_pairs={{0,16},{8,24},{16,0},{24,8},{1,17},{9,25},{17,1},{25,9},{2,18},{10... | collective-permute-start | bytes 1572872 | tf_op jit(solution)/shard_map/ppermute | solution.py:822
  40.2 0.1 collective-permute-start.2
  40.3 22.3 %second.1 = (f32[88,256]{1,0:T(8,128)S(1)}, f32[88,256]{1,0:T(8,128)S(1)}, f32[88,256]{1,0:T(8,128)S(1)}, f32[88,256]{1,0:T(8,128)S(1)}, f32[88,256]{1,0:T(8,128...) custom-call(s32[1]{0:T(128)} %bitcast.rank_ref, ...), custom_call_target="tpu_custom_call" | custom-call | flops 25999998976 | bytes 4194304 | tf_op jit(solution)/shard_map/second/pallas_call | solution.py:612
  62.6 0.0 collective-permute-done.refs_1_
  62.6 0.0 collective-permute-done.1.refs_2_
  62.6 0.9 %collective-permute-done.2.refs_3_ = f32[64,2048]{1,0:T(8,128)S(1)} collective-permute-done((f32[64,2048]{1,0:T(8,128)S(1)}, f32[64,2048]{1,0:T(8,128)S(1)}, u32[]{:S(2)}, u32[]{:S(2)}) %collective-permute-start.2) | collective-permute-done | bytes 524320 | tf_op jit(solution)/shard_map/ppermute | solution.py:822
  63.5 1.5 %collective-permute-start.3 = (f32[88,256]{1,0:T(8,128)S(1)}, f32[88,256]{1,0:T(8,128)S(1)}, u32[]{:S(2)}, u32[]{:S(2)}) collective-permute-start(f32[88,256]{1,0:T(8,128)S(1)} %get-tuple-element.80), channel_id=1, source_target_pairs={{0,1},{1,0},{2,3},{3,2},{4,5},{5,4},{6,7},{7,6},{8,9},{9,8},{10,11... | collective-permute-start | bytes 270344 | tf_op jit(solution)/shard_map/ppermute | solution.py:822
  65.0 1.5 %collective-permute-start.4 = (f32[88,256]{1,0:T(8,128)S(1)}, f32[88,256]{1,0:T(8,128)S(1)}, u32[]{:S(2)}, u32[]{:S(2)}) collective-permute-start(f32[88,256]{1,0:T(8,128)S(1)} %get-tuple-element.81), channel_id=1, source_target_pairs={{0,2},{1,3},{2,0},{3,1},{4,6},{5,7},{6,4},{7,5},{8,10},{9,11},{10,... | collective-permute-start | bytes 270344 | tf_op jit(solution)/shard_map/ppermute | solution.py:822
  66.5 2.4 %collective-permute-start.5 = (f32[88,256]{1,0:T(8,128)S(1)}, f32[88,256]{1,0:T(8,128)S(1)}, u32[]{:S(2)}, u32[]{:S(2)}) collective-permute-start(f32[88,256]{1,0:T(8,128)S(1)} %get-tuple-element.82), channel_id=1, source_target_pairs={{0,7},{1,6},{2,5},{3,4},{4,3},{5,2},{6,1},{7,0},{8,15},{9,14},{10,... | collective-permute-start | bytes 270344 | tf_op jit(solution)/shard_map/ppermute | solution.py:822
  68.9 1.5 %collective-permute-start.6 = (f32[88,256]{1,0:T(8,128)S(1)}, f32[88,256]{1,0:T(8,128)S(1)}, u32[]{:S(2)}, u32[]{:S(2)}) collective-permute-start(f32[88,256]{1,0:T(8,128)S(1)} %get-tuple-element.83), channel_id=1, source_target_pairs={{0,6},{1,7},{2,4},{3,5},{4,2},{5,3},{6,0},{7,1},{8,14},{9,15},{10,... | collective-permute-start | bytes 270344 | tf_op jit(solution)/shard_map/ppermute | solution.py:822
  70.3 1.5 %collective-permute-start.7 = (f32[88,256]{1,0:T(8,128)S(1)}, f32[88,256]{1,0:T(8,128)S(1)}, u32[]{:S(2)}, u32[]{:S(2)}) collective-permute-start(f32[88,256]{1,0:T(8,128)S(1)} %get-tuple-element.84), channel_id=1, source_target_pairs={{0,5},{1,4},{2,7},{3,6},{4,1},{5,0},{6,3},{7,2},{8,13},{9,12},{10,... | collective-permute-start | bytes 270344 | tf_op jit(solution)/shard_map/ppermute | solution.py:822
  71.9 0.0 collective-permute-done.3.refs_0_
  71.9 2.3 %collective-permute-start.8 = (f32[88,256]{1,0:T(8,128)S(1)}, f32[88,256]{1,0:T(8,128)S(1)}, u32[]{:S(2)}, u32[]{:S(2)}) collective-permute-start(f32[88,256]{1,0:T(8,128)S(1)} %get-tuple-element.85), channel_id=1, source_target_pairs={{0,4},{1,5},{2,6},{3,7},{4,0},{5,1},{6,2},{7,3},{8,12},{9,13},{10,... | collective-permute-start | bytes 270344 | tf_op jit(solution)/shard_map/ppermute | solution.py:822
  74.2 0.0 collective-permute-done.4.refs_1_
  74.2 0.1 collective-permute-start.9
  74.2 1.3 %gather_parts.1 = (f32[4,64,2048]{2,1,0:T(8,128)}, f32[4,64,256]{2,1,0:T(8,128)S(1)}) custom-call(s32[1]{0:T(128)} %bitcast.1.rank_ref, f32[64,2048]{1,0:T(8,128)S(1)} %copy-done, f32[64,2048]{1,0:T(8,128)S(1)} %collective-permute-done.refs_1_, f32[64,2048]{1,0:T(8,128)S(1)} %collective-permute-done.1.refs_2_, f32[64,2048]{1,0:T(8,128)S(1)} %collective-permute-done.2.refs_3_), custom_call_target="tpu_custom_call" | custom-call | bytes 4194304 | tf_op jit(solution)/shard_map/gather_parts/pallas_call | solution.py:731
  75.6 0.0 collective-permute-done.5.refs_2_
  75.6 0.7 collective-permute-done.6.refs_3_
  76.3 7.5 %collective-permute-done.7.refs_4_ = f32[88,256]{1,0:T(8,128)S(1)} collective-permute-done((f32[88,256]{1,0:T(8,128)S(1)}, f32[88,256]{1,0:T(8,128)S(1)}, u32[]{:S(2)}, u32[]{:S(2)}) %collective-permute-start.7) | collective-permute-done | bytes 90144 | tf_op jit(solution)/shard_map/ppermute | solution.py:822
  83.8 1.3 %collective-permute-done.8.refs_5_ = f32[88,256]{1,0:T(8,128)S(1)} collective-permute-done((f32[88,256]{1,0:T(8,128)S(1)}, f32[88,256]{1,0:T(8,128)S(1)}, u32[]{:S(2)}, u32[]{:S(2)}) %collective-permute-start.8) | collective-permute-done | bytes 90144 | tf_op jit(solution)/shard_map/ppermute | solution.py:822
  85.0 0.0 collective-permute-done.9.refs_6_
  85.0 1.0 %finish.1 = (f32[64,8,256]{2,1,0:T(8,128)}, f32[4,64,2048]{2,1,0:T(8,128)}) custom-call(s32[1]{0:T(128)} %bitcast.rank_ref, f32[88,256]{1,0:T(8,128)S(1)} %collective-permute-done.3.refs_0_, f32[88,256]{1,0:T(8,128)S(1)} %collective-permute-done.4.refs_1_, f32[88,256]{1,0:T(8,128)S(1)} %collective-permute-done.5.refs_2_, ...), custom_call_target="tpu_custom_call", output_to_operand_aliasing={{1}: (10, {})} | custom-call | bytes 1441792 | tf_op jit(solution)/shard_map/finish/pallas_call | solution.py:794
  (18 shorter events, 0.1 us)
Async XLA Ops:
  0.6 21.8 %all-to-all-start = ((f32[8,64,256]{2,1,0:T(8,128)}), f32[8,64,256]{2,1,0:T(8,128)S(1)}, u32[]{:S(2)}, u32[]{:S(2)}) async-start(f32[8,64,256]{2,1,0:T(8,128)} %bitcast.9), calls=%async_computation | async-start | bytes 1048576 | tf_op jit(solution)/shard_map/all_to_all | solution.py:840
  8.0 14.4 %copy-start.12 = (s32[64]{0:T(128)S(1)}, s32[64]{0:T(128)}, u32[]{:S(2)}) copy-start(s32[64]{0:T(128)} %param.13) | copy-start | bytes 772
  8.0 14.5 %copy-start.6 = (f32[4,8]{1,0:T(4,128)S(1)}, f32[4,8]{1,0:T(4,128)}, u32[]{:S(2)}) copy-start(f32[4,8]{1,0:T(4,128)} %param.11) | copy-start | bytes 388
  8.0 18.6 %copy-start.7 = (f32[32]{0:T(128)S(1)}, f32[32]{0:T(128)}, u32[]{:S(2)}) copy-start(f32[32]{0:T(128)} %constant.86) | copy-start | bytes 388
  8.0 18.6 %copy-start.8 = (f32[32]{0:T(128)S(1)}, f32[32]{0:T(128)}, u32[]{:S(2)}) copy-start(f32[32]{0:T(128)} %constant.85) | copy-start | bytes 388
  8.0 18.8 %copy-start.2 = (bf16[256,256]{1,0:T(8,128)(2,1)S(1)}, bf16[256,256]{1,0:T(8,128)(2,1)}, u32[]{:S(2)}) copy-start(bf16[256,256]{1,0:T(8,128)(2,1)} %constant.81.clone.flip_ref) | copy-start | bytes 393220
  8.0 18.8 %copy-start.3 = (f32[8,256]{1,0:T(8,128)S(1)}, f32[8,256]{1,0:T(8,128)}, u32[]{:S(2)}) copy-start(f32[8,256]{1,0:T(8,128)} %constant.83.clone.shift_y_ref) | copy-start | bytes 24580
  8.0 18.8 %copy-start.4 = (f32[8,256]{1,0:T(8,128)S(1)}, f32[8,256]{1,0:T(8,128)}, u32[]{:S(2)}) copy-start(f32[8,256]{1,0:T(8,128)} %constant.82.clone.shift_x_ref) | copy-start | bytes 24580
  22.4 15.2 %copy-start.1 = (f32[8,64,256]{2,1,0:T(8,128)}, f32[8,64,256]{2,1,0:T(8,128)S(1)}, u32[]{:S(2)}) copy-start(f32[8,64,256]{2,1,0:T(8,128)S(1)} %all-to-all-done.vol_ref) | copy-start | bytes 1572868
  22.7 15.7 %all-to-all-start.1 = ((f32[32,8,256]{2,1,0:T(8,128)}), f32[32,8,256]{2,1,0:T(8,128)S(1)}, u32[]{:S(2)}, u32[]{:S(2)}) async-start(f32[32,8,256]{2,1,0:T(8,128)} %bitcast.10), calls=%async_computation.1 | async-start | bytes 524288 | tf_op jit(solution)/shard_map/all_to_all | solution.py:840
  26.8 11.6 %copy-start.11 = (f32[64,2048]{1,0:T(8,128)S(1)}, f32[64,2048]{1,0:T(8,128)}, u32[]{:S(2)}) copy-start(f32[64,2048]{1,0:T(8,128)} %get-tuple-element.77) | copy-start | bytes 1572868
  26.8 11.7 %copy-start.10 = (f32[64,2048]{1,0:T(8,128)S(1)}, f32[64,2048]{1,0:T(8,128)}, u32[]{:S(2)}) copy-start(f32[64,2048]{1,0:T(8,128)} %get-tuple-element.78) | copy-start | bytes 1572868
  26.8 13.3 %copy-start.9 = (f32[64,2048]{1,0:T(8,128)S(1)}, f32[64,2048]{1,0:T(8,128)}, u32[]{:S(2)}) copy-start(f32[64,2048]{1,0:T(8,128)} %get-tuple-element.79) | copy-start | bytes 1572868
  37.6 0.8 copy-start.5
  38.4 24.2 %collective-permute-start = (f32[64,2048]{1,0:T(8,128)S(1)}, f32[64,2048]{1,0:T(8,128)S(1)}, u32[]{:S(2)}, u32[]{:S(2)}) collective-permute-start(f32[64,2048]{1,0:T(8,128)S(1)} %copy-done.11), channel_id=1, source_target_pairs={{0,8},{8,0},{16,24},{24,16},{1,9},{9,1},{17,25},{25,17},{2,10},{10... | collective-permute-start | bytes 1572872 | tf_op jit(solution)/shard_map/ppermute | solution.py:822
  38.5 24.1 %collective-permute-start.1 = (f32[64,2048]{1,0:T(8,128)S(1)}, f32[64,2048]{1,0:T(8,128)S(1)}, u32[]{:S(2)}, u32[]{:S(2)}) collective-permute-start(f32[64,2048]{1,0:T(8,128)S(1)} %copy-done.10), channel_id=1, source_target_pairs={{0,16},{8,24},{16,0},{24,8},{1,17},{9,25},{17,1},{25,9},{2,18},{10... | collective-permute-start | bytes 1572872 | tf_op jit(solution)/shard_map/ppermute | solution.py:822
  40.2 23.4 %collective-permute-start.2 = (f32[64,2048]{1,0:T(8,128)S(1)}, f32[64,2048]{1,0:T(8,128)S(1)}, u32[]{:S(2)}, u32[]{:S(2)}) collective-permute-start(f32[64,2048]{1,0:T(8,128)S(1)} %copy-done.9), channel_id=1, source_target_pairs={{0,24},{8,16},{16,8},{24,0},{1,25},{9,17},{17,9},{25,1},{2,26},{10... | collective-permute-start | bytes 1572872 | tf_op jit(solution)/shard_map/ppermute | solution.py:822
  40.3 33.9 %copy-start = (f32[64,2048]{1,0:T(8,128)S(1)}, f32[64,2048]{1,0:T(8,128)}, u32[]{:S(2)}) copy-start(f32[64,2048]{1,0:T(8,128)} %get-tuple-element.88.refs_0_) | copy-start | bytes 1572868
  63.5 8.3 %collective-permute-start.3 = (f32[88,256]{1,0:T(8,128)S(1)}, f32[88,256]{1,0:T(8,128)S(1)}, u32[]{:S(2)}, u32[]{:S(2)}) collective-permute-start(f32[88,256]{1,0:T(8,128)S(1)} %get-tuple-element.80), channel_id=1, source_target_pairs={{0,1},{1,0},{2,3},{3,2},{4,5},{5,4},{6,7},{7,6},{8,9},{9,8},{10,11... | collective-permute-start | bytes 270344 | tf_op jit(solution)/shard_map/ppermute | solution.py:822
  65.0 9.1 %collective-permute-start.4 = (f32[88,256]{1,0:T(8,128)S(1)}, f32[88,256]{1,0:T(8,128)S(1)}, u32[]{:S(2)}, u32[]{:S(2)}) collective-permute-start(f32[88,256]{1,0:T(8,128)S(1)} %get-tuple-element.81), channel_id=1, source_target_pairs={{0,2},{1,3},{2,0},{3,1},{4,6},{5,7},{6,4},{7,5},{8,10},{9,11},{10,... | collective-permute-start | bytes 270344 | tf_op jit(solution)/shard_map/ppermute | solution.py:822
  66.5 9.1 %collective-permute-start.5 = (f32[88,256]{1,0:T(8,128)S(1)}, f32[88,256]{1,0:T(8,128)S(1)}, u32[]{:S(2)}, u32[]{:S(2)}) collective-permute-start(f32[88,256]{1,0:T(8,128)S(1)} %get-tuple-element.82), channel_id=1, source_target_pairs={{0,7},{1,6},{2,5},{3,4},{4,3},{5,2},{6,1},{7,0},{8,15},{9,14},{10,... | collective-permute-start | bytes 270344 | tf_op jit(solution)/shard_map/ppermute | solution.py:822
  68.9 7.4 %collective-permute-start.6 = (f32[88,256]{1,0:T(8,128)S(1)}, f32[88,256]{1,0:T(8,128)S(1)}, u32[]{:S(2)}, u32[]{:S(2)}) collective-permute-start(f32[88,256]{1,0:T(8,128)S(1)} %get-tuple-element.83), channel_id=1, source_target_pairs={{0,6},{1,7},{2,4},{3,5},{4,2},{5,3},{6,0},{7,1},{8,14},{9,15},{10,... | collective-permute-start | bytes 270344 | tf_op jit(solution)/shard_map/ppermute | solution.py:822
  70.3 13.4 %collective-permute-start.7 = (f32[88,256]{1,0:T(8,128)S(1)}, f32[88,256]{1,0:T(8,128)S(1)}, u32[]{:S(2)}, u32[]{:S(2)}) collective-permute-start(f32[88,256]{1,0:T(8,128)S(1)} %get-tuple-element.84), channel_id=1, source_target_pairs={{0,5},{1,4},{2,7},{3,6},{4,1},{5,0},{6,3},{7,2},{8,13},{9,12},{10,... | collective-permute-start | bytes 270344 | tf_op jit(solution)/shard_map/ppermute | solution.py:822
  71.9 13.2 %collective-permute-start.8 = (f32[88,256]{1,0:T(8,128)S(1)}, f32[88,256]{1,0:T(8,128)S(1)}, u32[]{:S(2)}, u32[]{:S(2)}) collective-permute-start(f32[88,256]{1,0:T(8,128)S(1)} %get-tuple-element.85), channel_id=1, source_target_pairs={{0,4},{1,5},{2,6},{3,7},{4,0},{5,1},{6,2},{7,3},{8,12},{9,13},{10,... | collective-permute-start | bytes 270344 | tf_op jit(solution)/shard_map/ppermute | solution.py:822
  74.2 10.9 %collective-permute-start.9 = (f32[88,256]{1,0:T(8,128)S(1)}, f32[88,256]{1,0:T(8,128)S(1)}, u32[]{:S(2)}, u32[]{:S(2)}) collective-permute-start(f32[88,256]{1,0:T(8,128)S(1)} %get-tuple-element.86), channel_id=1, source_target_pairs={{0,3},{1,2},{2,1},{3,0},{4,7},{5,6},{6,5},{7,4},{8,11},{9,10},{10,... | collective-permute-start | bytes 270344 | tf_op jit(solution)/shard_map/ppermute | solution.py:822

commit v15 on v14

--- a/solution.py
+++ b/solution.py
@@ -22,7 +22,7 @@
 SPLIT = 64
 EDGE = 32
 GROUP = 8
-CYCLE = 8
+CYCLE = 16
 
 paganin_strength = 10.0
 relax = 1.8
@@ -285,21 +285,23 @@
 def project_rows(held_ref, operands, q, c, sizes, offset_ref, acc_ref):
     angles, chunk = sizes[:2]
     half = chunk // 2
-    for begin in range(0, chunk, GROUP):
+    for side in range(2):
         sums = lax.dot_general(
-            held_ref[begin * WIN : (begin + GROUP) * WIN, :],
-            operands[begin // half],
+            held_ref[side * half * WIN : (side + 1) * half * WIN, :],
+            operands[side],
             (((1,), (1,)), ((), ())),
             preferred_element_type=f32,
         )
-        places = []
-        for t in range(begin, begin + GROUP):
-            rows = pl.ds(offset_ref[q * angles + c * chunk + t], WIN)
-            piece = sums[(t - begin) * WIN : (t - begin + 1) * WIN, :]
-            index = c * half + t % half
-            places.append((index, rows, acc_ref[index, rows, :] + piece))
-        for index, rows, values in places:
-            acc_ref[index, rows, :] = values
+        for begin in range(0, half, GROUP):
+            places = []
+            for i in range(begin, begin + GROUP):
+                t = side * half + i
+                rows = pl.ds(offset_ref[q * angles + c * chunk + t], WIN)
+                index = c * half + i
+                piece = sums[i * WIN : (i + 1) * WIN, :]
+                places.append((index, rows, acc_ref[index, rows, :] + piece))
+            for index, rows, values in places:
+                acc_ref[index, rows, :] = values
 
 
 def spread_rays(acc_ref, direct_ref, mirror_ref, total_ref, slices, chunk):

time: 86.5 us -> 86.1 us (level)
  no operation moved by 1% of the time
where the time goes in v15:
time: 86.1 us; the launch traced here: 85.8 us
  Pallas kernels  43.6 us (51%)
  starting transfers between devices  24 us (28%)
  waiting for transfers between devices  15.8 us (18%)
  local copies, waits for them, and re-layouts  1.2 us (1%)
  between operations  1 us (1%)
    pallas_call x2, Pallas kernels, call(): pl.pallas_call(kernel, out_shape=[jax.ShapeDtypeStruct(*value) for value...  32.2 us
    ppermute x10, starting transfers between devices, exchange(): lax.ppermute(pieces[d], axis, [(i, i ^ d) for i in range(count)])  13 us
    all_to_all x2, starting transfers between devices, to_all(): return lax.all_to_all(values, axes, split_axis=0, concat_axis=0, tiled=True)  11 us
    ppermute x10, waiting for transfers between devices, exchange(): lax.ppermute(pieces[d], axis, [(i, i ^ d) for i in range(count)])  10.5 us
    pallas_call x1, Pallas kernels, paganin(): pl.pallas_call(filter_kernel, out_shape=[jax.ShapeDtypeStruct((height //...  9.07 us
    all_to_all x2, waiting for transfers between devices, to_all(): return lax.all_to_all(values, axes, split_axis=0, concat_axis=0, tiled=True)  5.27 us
  transfers between devices with their start and end apart: 12, of which 5 were waited for; matrix products, arithmetic and copies ran while one was open for 0% of the time, Pallas kernels for 50%

profile of v15, /device:TPU:0, one launch (start us, length us, event | category | flops | bytes accessed | tf_op | source)
XLA Modules:
  0.0 85.8 jit_solution(11760822126162417797)
XLA Ops:
  0.6 7.3 %all-to-all-start = ((f32[8,64,256]{2,1,0:T(8,128)}), f32[8,64,256]{2,1,0:T(8,128)S(1)}, u32[]{:S(2)}, u32[]{:S(2)}) async-start(f32[8,64,256]{2,1,0:T(8,128)} %bitcast.9), calls=%async_computation | async-start | bytes 1048576 | tf_op jit(solution)/shard_map/all_to_all | solution.py:842
  7.9 0.1 sub.24
  8.0 0.0 copy-start.2
  8.0 0.0 copy-start.3
  8.0 0.0 copy-start.4
  8.0 9.1 %paganin.1 = (f32[64,2048]{1,0:T(8,128)}, f32[64,2048]{1,0:T(8,128)}, f32[64,2048]{1,0:T(8,128)}, f32[64,2048]{1,0:T(8,128)}, f32[256,256]{1,0:T(8,128)}) custom-call(s32[1]{0:T(128)} %bitcast.1.rank_ref, f32[256,2048]{1,0:T(8,128)} %bitcast.11, f32[264,256]{1,0:T(8,128)} %constant.78.clone.given_ref), custom_call_target="tpu_custom_call" | custom-call | flops 8589934592 | bytes 4194304 | tf_op jit(solution)/shard_map/paganin/pallas_call | solution.py:203
  17.1 5.3 %all-to-all-done.vol_ref = f32[8,64,256]{2,1,0:T(8,128)S(1)} async-done(((f32[8,64,256]{2,1,0:T(8,128)}), f32[8,64,256]{2,1,0:T(8,128)S(1)}, u32[]{:S(2)}, u32[]{:S(2)}) %all-to-all-start) | async-done | bytes 524320 | tf_op jit(solution)/shard_map/all_to_all | solution.py:842
  22.4 0.0 copy-done.12
  22.4 0.1 select_reduce_fusion.slot_ref
  22.5 0.0 copy-done.6
  22.5 0.1 cos.6.cos_ref
  22.6 0.1 sin.6.sin_ref
  22.7 3.7 %all-to-all-start.1 = ((f32[32,8,256]{2,1,0:T(8,128)}), f32[32,8,256]{2,1,0:T(8,128)S(1)}, u32[]{:S(2)}, u32[]{:S(2)}) async-start(f32[32,8,256]{2,1,0:T(8,128)} %bitcast.10), calls=%async_computation.1 | async-start | bytes 524288 | tf_op jit(solution)/shard_map/all_to_all | solution.py:842
  26.4 0.0 copy-done.7
  26.4 0.0 copy-done.8
  26.4 0.1 add_add_fusion
  26.5 0.1 add.64
  26.6 0.0 copy-done.2
  26.6 0.0 copy-done.3
  26.6 0.0 copy-done.4
  26.7 10.3 %first.1 = (f32[32,16,256]{2,1,0:T(8,128)S(1)}, f32[32,8,256]{2,1,0:T(8,128)S(1)}, f32[32,8,256]{2,1,0:T(8,128)S(1)}) custom-call(f32[1024]{0:T(1024)S(1)} %fusion.1.place_ref, s32[1024]{0:T(1024)S(1)} %get-tuple-element.102.offset_ref, s32[64]{0:T(128)S(1)} %select_reduce_fusion.slot_ref, f32[32]{0:T(128)S(1)} %cos.6.cos_ref, f32[32]{0:T(128)S(1)} %sin.6.sin_ref, ...), custom_call_target="tpu_custom_call" | custom-call | flops 14000000000 | bytes 4194304 | tf_op jit(solution)/shard_map/first/pallas_call | solution.py:614
  37.0 0.8 copy-done.5
  37.8 0.0 all-to-all-done.1.sino_ref
  37.8 0.0 copy-done.11
  37.8 0.3 collective-permute-start
  38.1 0.0 copy-done.10
  38.1 1.7 %collective-permute-start.1 = (f32[64,2048]{1,0:T(8,128)S(1)}, f32[64,2048]{1,0:T(8,128)S(1)}, u32[]{:S(2)}, u32[]{:S(2)}) collective-permute-start(f32[64,2048]{1,0:T(8,128)S(1)} %copy-done.10), channel_id=1, source_target_pairs={{0,16},{8,24},{16,0},{24,8},{1,17},{9,25},{17,1},{25,9},{2,18},{10... | collective-permute-start | bytes 1572872 | tf_op jit(solution)/shard_map/ppermute | solution.py:824
  39.7 0.0 collective-permute-start.2
  39.8 21.9 %second.1 = (f32[88,256]{1,0:T(8,128)S(1)}, f32[88,256]{1,0:T(8,128)S(1)}, f32[88,256]{1,0:T(8,128)S(1)}, f32[88,256]{1,0:T(8,128)S(1)}, f32[88,256]{1,0:T(8,128...) custom-call(s32[1]{0:T(128)} %bitcast.rank_ref, ...), custom_call_target="tpu_custom_call" | custom-call | flops 25999998976 | bytes 4194304 | tf_op jit(solution)/shard_map/second/pallas_call | solution.py:614
  61.6 0.0 collective-permute-done.refs_1_
  61.7 0.0 collective-permute-done.1.refs_2_
  61.7 1.1 %collective-permute-done.2.refs_3_ = f32[64,2048]{1,0:T(8,128)S(1)} collective-permute-done((f32[64,2048]{1,0:T(8,128)S(1)}, f32[64,2048]{1,0:T(8,128)S(1)}, u32[]{:S(2)}, u32[]{:S(2)}) %collective-permute-start.2) | collective-permute-done | bytes 524320 | tf_op jit(solution)/shard_map/ppermute | solution.py:824
  62.7 1.9 %collective-permute-start.3 = (f32[88,256]{1,0:T(8,128)S(1)}, f32[88,256]{1,0:T(8,128)S(1)}, u32[]{:S(2)}, u32[]{:S(2)}) collective-permute-start(f32[88,256]{1,0:T(8,128)S(1)} %get-tuple-element.80), channel_id=1, source_target_pairs={{0,1},{1,0},{2,3},{3,2},{4,5},{5,4},{6,7},{7,6},{8,9},{9,8},{10,11... | collective-permute-start | bytes 270344 | tf_op jit(solution)/shard_map/ppermute | solution.py:824
  64.6 1.5 %collective-permute-start.4 = (f32[88,256]{1,0:T(8,128)S(1)}, f32[88,256]{1,0:T(8,128)S(1)}, u32[]{:S(2)}, u32[]{:S(2)}) collective-permute-start(f32[88,256]{1,0:T(8,128)S(1)} %get-tuple-element.81), channel_id=1, source_target_pairs={{0,2},{1,3},{2,0},{3,1},{4,6},{5,7},{6,4},{7,5},{8,10},{9,11},{10,... | collective-permute-start | bytes 270344 | tf_op jit(solution)/shard_map/ppermute | solution.py:824
  66.1 2.4 %collective-permute-start.5 = (f32[88,256]{1,0:T(8,128)S(1)}, f32[88,256]{1,0:T(8,128)S(1)}, u32[]{:S(2)}, u32[]{:S(2)}) collective-permute-start(f32[88,256]{1,0:T(8,128)S(1)} %get-tuple-element.82), channel_id=1, source_target_pairs={{0,7},{1,6},{2,5},{3,4},{4,3},{5,2},{6,1},{7,0},{8,15},{9,14},{10,... | collective-permute-start | bytes 270344 | tf_op jit(solution)/shard_map/ppermute | solution.py:824
  68.4 1.5 %collective-permute-start.6 = (f32[88,256]{1,0:T(8,128)S(1)}, f32[88,256]{1,0:T(8,128)S(1)}, u32[]{:S(2)}, u32[]{:S(2)}) collective-permute-start(f32[88,256]{1,0:T(8,128)S(1)} %get-tuple-element.83), channel_id=1, source_target_pairs={{0,6},{1,7},{2,4},{3,5},{4,2},{5,3},{6,0},{7,1},{8,14},{9,15},{10,... | collective-permute-start | bytes 270344 | tf_op jit(solution)/shard_map/ppermute | solution.py:824
  69.9 1.5 %collective-permute-start.7 = (f32[88,256]{1,0:T(8,128)S(1)}, f32[88,256]{1,0:T(8,128)S(1)}, u32[]{:S(2)}, u32[]{:S(2)}) collective-permute-start(f32[88,256]{1,0:T(8,128)S(1)} %get-tuple-element.84), channel_id=1, source_target_pairs={{0,5},{1,4},{2,7},{3,6},{4,1},{5,0},{6,3},{7,2},{8,13},{9,12},{10,... | collective-permute-start | bytes 270344 | tf_op jit(solution)/shard_map/ppermute | solution.py:824
  71.4 0.0 collective-permute-done.3.refs_0_
  71.4 2.3 %collective-permute-start.8 = (f32[88,256]{1,0:T(8,128)S(1)}, f32[88,256]{1,0:T(8,128)S(1)}, u32[]{:S(2)}, u32[]{:S(2)}) collective-permute-start(f32[88,256]{1,0:T(8,128)S(1)} %get-tuple-element.85), channel_id=1, source_target_pairs={{0,4},{1,5},{2,6},{3,7},{4,0},{5,1},{6,2},{7,3},{8,12},{9,13},{10,... | collective-permute-start | bytes 270344 | tf_op jit(solution)/shard_map/ppermute | solution.py:824
  73.7 0.0 collective-permute-done.4.refs_1_
  73.7 0.1 collective-permute-start.9
  73.8 1.3 %gather_parts.1 = (f32[4,64,2048]{2,1,0:T(8,128)}, f32[4,64,256]{2,1,0:T(8,128)S(1)}) custom-call(s32[1]{0:T(128)} %bitcast.1.rank_ref, f32[64,2048]{1,0:T(8,128)S(1)} %copy-done, f32[64,2048]{1,0:T(8,128)S(1)} %collective-permute-done.refs_1_, f32[64,2048]{1,0:T(8,128)S(1)} %collective-permute-done.1.refs_2_, f32[64,2048]{1,0:T(8,128)S(1)} %collective-permute-done.2.refs_3_), custom_call_target="tpu_custom_call" | custom-call | bytes 4194304 | tf_op jit(solution)/shard_map/gather_parts/pallas_call | solution.py:733
  75.2 0.0 collective-permute-done.5.refs_2_
  75.2 0.7 collective-permute-done.6.refs_3_
  75.8 7.5 %collective-permute-done.7.refs_4_ = f32[88,256]{1,0:T(8,128)S(1)} collective-permute-done((f32[88,256]{1,0:T(8,128)S(1)}, f32[88,256]{1,0:T(8,128)S(1)}, u32[]{:S(2)}, u32[]{:S(2)}) %collective-permute-start.7) | collective-permute-done | bytes 90144 | tf_op jit(solution)/shard_map/ppermute | solution.py:824
  83.3 1.3 %collective-permute-done.8.refs_5_ = f32[88,256]{1,0:T(8,128)S(1)} collective-permute-done((f32[88,256]{1,0:T(8,128)S(1)}, f32[88,256]{1,0:T(8,128)S(1)}, u32[]{:S(2)}, u32[]{:S(2)}) %collective-permute-start.8) | collective-permute-done | bytes 90144 | tf_op jit(solution)/shard_map/ppermute | solution.py:824
  84.6 0.0 collective-permute-done.9.refs_6_
  84.6 1.0 %finish.1 = (f32[64,8,256]{2,1,0:T(8,128)}, f32[4,64,2048]{2,1,0:T(8,128)}) custom-call(s32[1]{0:T(128)} %bitcast.rank_ref, f32[88,256]{1,0:T(8,128)S(1)} %collective-permute-done.3.refs_0_, f32[88,256]{1,0:T(8,128)S(1)} %collective-permute-done.4.refs_1_, f32[88,256]{1,0:T(8,128)S(1)} %collective-permute-done.5.refs_2_, ...), custom_call_target="tpu_custom_call", output_to_operand_aliasing={{1}: (10, {})} | custom-call | bytes 1441792 | tf_op jit(solution)/shard_map/finish/pallas_call | solution.py:796
  (18 shorter events, 0.1 us)
Async XLA Ops:
  0.6 21.8 %all-to-all-start = ((f32[8,64,256]{2,1,0:T(8,128)}), f32[8,64,256]{2,1,0:T(8,128)S(1)}, u32[]{:S(2)}, u32[]{:S(2)}) async-start(f32[8,64,256]{2,1,0:T(8,128)} %bitcast.9), calls=%async_computation | async-start | bytes 1048576 | tf_op jit(solution)/shard_map/all_to_all | solution.py:842
  8.0 14.4 %copy-start.12 = (s32[64]{0:T(128)S(1)}, s32[64]{0:T(128)}, u32[]{:S(2)}) copy-start(s32[64]{0:T(128)} %param.13) | copy-start | bytes 772
  8.0 14.5 %copy-start.6 = (f32[4,8]{1,0:T(4,128)S(1)}, f32[4,8]{1,0:T(4,128)}, u32[]{:S(2)}) copy-start(f32[4,8]{1,0:T(4,128)} %param.11) | copy-start | bytes 388
  8.0 18.4 %copy-start.7 = (f32[32]{0:T(128)S(1)}, f32[32]{0:T(128)}, u32[]{:S(2)}) copy-start(f32[32]{0:T(128)} %constant.86) | copy-start | bytes 388
  8.0 18.4 %copy-start.8 = (f32[32]{0:T(128)S(1)}, f32[32]{0:T(128)}, u32[]{:S(2)}) copy-start(f32[32]{0:T(128)} %constant.85) | copy-start | bytes 388
  8.0 18.6 %copy-start.2 = (bf16[256,256]{1,0:T(8,128)(2,1)S(1)}, bf16[256,256]{1,0:T(8,128)(2,1)}, u32[]{:S(2)}) copy-start(bf16[256,256]{1,0:T(8,128)(2,1)} %constant.81.clone.flip_ref) | copy-start | bytes 393220
  8.0 18.6 %copy-start.3 = (f32[8,256]{1,0:T(8,128)S(1)}, f32[8,256]{1,0:T(8,128)}, u32[]{:S(2)}) copy-start(f32[8,256]{1,0:T(8,128)} %constant.83.clone.shift_y_ref) | copy-start | bytes 24580
  8.0 18.6 %copy-start.4 = (f32[8,256]{1,0:T(8,128)S(1)}, f32[8,256]{1,0:T(8,128)}, u32[]{:S(2)}) copy-start(f32[8,256]{1,0:T(8,128)} %constant.82.clone.shift_x_ref) | copy-start | bytes 24580
  22.4 14.6 %copy-start.1 = (f32[8,64,256]{2,1,0:T(8,128)}, f32[8,64,256]{2,1,0:T(8,128)S(1)}, u32[]{:S(2)}) copy-start(f32[8,64,256]{2,1,0:T(8,128)S(1)} %all-to-all-done.vol_ref) | copy-start | bytes 1572868
  22.7 15.1 %all-to-all-start.1 = ((f32[32,8,256]{2,1,0:T(8,128)}), f32[32,8,256]{2,1,0:T(8,128)S(1)}, u32[]{:S(2)}, u32[]{:S(2)}) async-start(f32[32,8,256]{2,1,0:T(8,128)} %bitcast.10), calls=%async_computation.1 | async-start | bytes 524288 | tf_op jit(solution)/shard_map/all_to_all | solution.py:842
  26.6 11.2 %copy-start.11 = (f32[64,2048]{1,0:T(8,128)S(1)}, f32[64,2048]{1,0:T(8,128)}, u32[]{:S(2)}) copy-start(f32[64,2048]{1,0:T(8,128)} %get-tuple-element.77) | copy-start | bytes 1572868
  26.7 11.4 %copy-start.10 = (f32[64,2048]{1,0:T(8,128)S(1)}, f32[64,2048]{1,0:T(8,128)}, u32[]{:S(2)}) copy-start(f32[64,2048]{1,0:T(8,128)} %get-tuple-element.78) | copy-start | bytes 1572868
  26.7 13.1 %copy-start.9 = (f32[64,2048]{1,0:T(8,128)S(1)}, f32[64,2048]{1,0:T(8,128)}, u32[]{:S(2)}) copy-start(f32[64,2048]{1,0:T(8,128)} %get-tuple-element.79) | copy-start | bytes 1572868
  37.0 0.8 copy-start.5
  37.8 23.8 %collective-permute-start = (f32[64,2048]{1,0:T(8,128)S(1)}, f32[64,2048]{1,0:T(8,128)S(1)}, u32[]{:S(2)}, u32[]{:S(2)}) collective-permute-start(f32[64,2048]{1,0:T(8,128)S(1)} %copy-done.11), channel_id=1, source_target_pairs={{0,8},{8,0},{16,24},{24,16},{1,9},{9,1},{17,25},{25,17},{2,10},{10... | collective-permute-start | bytes 1572872 | tf_op jit(solution)/shard_map/ppermute | solution.py:824
  38.1 23.6 %collective-permute-start.1 = (f32[64,2048]{1,0:T(8,128)S(1)}, f32[64,2048]{1,0:T(8,128)S(1)}, u32[]{:S(2)}, u32[]{:S(2)}) collective-permute-start(f32[64,2048]{1,0:T(8,128)S(1)} %copy-done.10), channel_id=1, source_target_pairs={{0,16},{8,24},{16,0},{24,8},{1,17},{9,25},{17,1},{25,9},{2,18},{10... | collective-permute-start | bytes 1572872 | tf_op jit(solution)/shard_map/ppermute | solution.py:824
  39.7 23.0 %collective-permute-start.2 = (f32[64,2048]{1,0:T(8,128)S(1)}, f32[64,2048]{1,0:T(8,128)S(1)}, u32[]{:S(2)}, u32[]{:S(2)}) collective-permute-start(f32[64,2048]{1,0:T(8,128)S(1)} %copy-done.9), channel_id=1, source_target_pairs={{0,24},{8,16},{16,8},{24,0},{1,25},{9,17},{17,9},{25,1},{2,26},{10... | collective-permute-start | bytes 1572872 | tf_op jit(solution)/shard_map/ppermute | solution.py:824
  39.8 34.0 %copy-start = (f32[64,2048]{1,0:T(8,128)S(1)}, f32[64,2048]{1,0:T(8,128)}, u32[]{:S(2)}) copy-start(f32[64,2048]{1,0:T(8,128)} %get-tuple-element.88.refs_0_) | copy-start | bytes 1572868
  62.7 8.7 %collective-permute-start.3 = (f32[88,256]{1,0:T(8,128)S(1)}, f32[88,256]{1,0:T(8,128)S(1)}, u32[]{:S(2)}, u32[]{:S(2)}) collective-permute-start(f32[88,256]{1,0:T(8,128)S(1)} %get-tuple-element.80), channel_id=1, source_target_pairs={{0,1},{1,0},{2,3},{3,2},{4,5},{5,4},{6,7},{7,6},{8,9},{9,8},{10,11... | collective-permute-start | bytes 270344 | tf_op jit(solution)/shard_map/ppermute | solution.py:824
  64.6 9.1 %collective-permute-start.4 = (f32[88,256]{1,0:T(8,128)S(1)}, f32[88,256]{1,0:T(8,128)S(1)}, u32[]{:S(2)}, u32[]{:S(2)}) collective-permute-start(f32[88,256]{1,0:T(8,128)S(1)} %get-tuple-element.81), channel_id=1, source_target_pairs={{0,2},{1,3},{2,0},{3,1},{4,6},{5,7},{6,4},{7,5},{8,10},{9,11},{10,... | collective-permute-start | bytes 270344 | tf_op jit(solution)/shard_map/ppermute | solution.py:824
  66.1 9.1 %collective-permute-start.5 = (f32[88,256]{1,0:T(8,128)S(1)}, f32[88,256]{1,0:T(8,128)S(1)}, u32[]{:S(2)}, u32[]{:S(2)}) collective-permute-start(f32[88,256]{1,0:T(8,128)S(1)} %get-tuple-element.82), channel_id=1, source_target_pairs={{0,7},{1,6},{2,5},{3,4},{4,3},{5,2},{6,1},{7,0},{8,15},{9,14},{10,... | collective-permute-start | bytes 270344 | tf_op jit(solution)/shard_map/ppermute | solution.py:824
  68.4 7.4 %collective-permute-start.6 = (f32[88,256]{1,0:T(8,128)S(1)}, f32[88,256]{1,0:T(8,128)S(1)}, u32[]{:S(2)}, u32[]{:S(2)}) collective-permute-start(f32[88,256]{1,0:T(8,128)S(1)} %get-tuple-element.83), channel_id=1, source_target_pairs={{0,6},{1,7},{2,4},{3,5},{4,2},{5,3},{6,0},{7,1},{8,14},{9,15},{10,... | collective-permute-start | bytes 270344 | tf_op jit(solution)/shard_map/ppermute | solution.py:824
  69.9 13.4 %collective-permute-start.7 = (f32[88,256]{1,0:T(8,128)S(1)}, f32[88,256]{1,0:T(8,128)S(1)}, u32[]{:S(2)}, u32[]{:S(2)}) collective-permute-start(f32[88,256]{1,0:T(8,128)S(1)} %get-tuple-element.84), channel_id=1, source_target_pairs={{0,5},{1,4},{2,7},{3,6},{4,1},{5,0},{6,3},{7,2},{8,13},{9,12},{10,... | collective-permute-start | bytes 270344 | tf_op jit(solution)/shard_map/ppermute | solution.py:824
  71.4 13.2 %collective-permute-start.8 = (f32[88,256]{1,0:T(8,128)S(1)}, f32[88,256]{1,0:T(8,128)S(1)}, u32[]{:S(2)}, u32[]{:S(2)}) collective-permute-start(f32[88,256]{1,0:T(8,128)S(1)} %get-tuple-element.85), channel_id=1, source_target_pairs={{0,4},{1,5},{2,6},{3,7},{4,0},{5,1},{6,2},{7,3},{8,12},{9,13},{10,... | collective-permute-start | bytes 270344 | tf_op jit(solution)/shard_map/ppermute | solution.py:824
  73.7 10.9 %collective-permute-start.9 = (f32[88,256]{1,0:T(8,128)S(1)}, f32[88,256]{1,0:T(8,128)S(1)}, u32[]{:S(2)}, u32[]{:S(2)}) collective-permute-start(f32[88,256]{1,0:T(8,128)S(1)} %get-tuple-element.86), channel_id=1, source_target_pairs={{0,3},{1,2},{2,1},{3,0},{4,7},{5,6},{6,5},{7,4},{8,11},{9,10},{10,... | collective-permute-start | bytes 270344 | tf_op jit(solution)/shard_map/ppermute | solution.py:824

commit v16 on v15

--- a/solution.py
+++ b/solution.py
@@ -38,14 +38,6 @@
     return high, low
 
 
-def thirds(values):
-    high = values.astype(bf16)
-    rest = values - high.astype(f32)
-    middle = rest.astype(bf16)
-    low = (rest - middle.astype(f32)).astype(bf16)
-    return high, middle, low
-
-
 def dot(left, right):
     return jnp.dot(left, right, preferred_element_type=f32)
 
@@ -85,7 +77,7 @@
     sems, out_sems = refs[-2:]
     height, width = image_ref.shape
     rank = rank_ref[0]
-    share = height // len(part_refs)
+    share = height // (2 * len(part_refs))
     length = width // ROWS
     blocks = height // LANES
     unroll = 8
@@ -179,12 +171,11 @@
         filtered = 1.0 - jnp.transpose(transform(spectrum))
         columns = slice(c * length, (c + 1) * length)
         out_ref[:, columns] = -jnp.log(filtered)
-        for d, part_ref in enumerate(part_refs):
+        for d in range(2 * len(part_refs)):
             rows = pl.ds(pl.multiple_of((rank ^ d) * share, share), share)
+            there = part_refs[d // 2].at[d % 2 * share : (d % 2 + 1) * share, columns]
             sent.append(
-                pltpu.make_async_copy(
-                    out_ref.at[rows, columns], part_ref.at[:, columns], out_sems.at[c, d]
-                )
+                pltpu.make_async_copy(out_ref.at[rows, columns], there, out_sems.at[c, d])
             )
             sent[-1].start()
         if c == (offset + ACTIVE - 1) // length:
@@ -202,11 +193,11 @@
     blocks = height // LANES
     return pl.pallas_call(
         filter_kernel,
-        out_shape=[jax.ShapeDtypeStruct((height // parts, width), f32)] * parts
+        out_shape=[jax.ShapeDtypeStruct((2 * height // parts, width), f32)] * (parts // 2)
         + [jax.ShapeDtypeStruct((height, ACTIVE), f32)],
         in_specs=[pl.BlockSpec(memory_space=pltpu.SMEM)]
         + [pl.BlockSpec(memory_space=pltpu.HBM)] * 2,
-        out_specs=[pl.BlockSpec(memory_space=pltpu.HBM)] * (parts + 1),
+        out_specs=[pl.BlockSpec(memory_space=pltpu.HBM)] * (parts // 2 + 1),
         scratch_shapes=[
             pltpu.VMEM((height, width), f32),
             pltpu.VMEM((height + ROWS, height), f32),
@@ -228,7 +219,7 @@
 
 
 def reversed_exact(values, flip):
-    return sum(dot(part, flip) for part in thirds(values))
+    return sum(dot(part, flip) for part in halves(values))
 
 
 class Weights:
@@ -713,35 +704,36 @@
 def gather_kernel(rank_ref, *refs):
     *part_refs, out_ref, active_ref, sems = refs
     rank = rank_ref[0]
+    rows = out_ref.shape[1]
     copies = [
-        pltpu.make_async_copy(part_ref, out_ref.at[rank ^ d], sems.at[d])
+        pltpu.make_async_copy(part_ref.at[0:rows], out_ref.at[rank ^ d], sems.at[d])
         for d, part_ref in enumerate(part_refs)
     ]
     for copy in copies:
         copy.start()
     offset = (out_ref.shape[2] - ACTIVE) // 2
     for d, part_ref in enumerate(part_refs):
-        active_ref[rank ^ d] = part_ref[:, offset : offset + ACTIVE]
+        active_ref[rank ^ d] = part_ref[0:rows, offset : offset + ACTIVE]
     for copy in copies:
         copy.wait()
 
 
 def gather_parts(parts, rank):
     count = len(parts)
-    rows = parts[0].shape[0]
+    rows, width = parts[1].shape
     vmem = pl.BlockSpec(memory_space=pltpu.VMEM)
     return pl.pallas_call(
         gather_kernel,
         out_shape=(
-            jax.ShapeDtypeStruct((count,) + parts[0].shape, f32),
+            jax.ShapeDtypeStruct((count, rows, width), f32),
             jax.ShapeDtypeStruct((count, rows, ACTIVE), f32),
         ),
         in_specs=[pl.BlockSpec(memory_space=pltpu.SMEM)] + [vmem] * count,
         out_specs=(pl.BlockSpec(memory_space=pltpu.HBM), vmem),
         scratch_shapes=[pltpu.SemaphoreType.DMA((count,))],
-        compiler_params=pltpu.CompilerParams(vmem_limit_bytes=8 * 2**20),
+        compiler_params=pltpu.CompilerParams(vmem_limit_bytes=12 * 2**20),
         cost_estimate=pl.CostEstimate(
-            flops=0, bytes_accessed=8 * count * parts[0].size, transcendentals=0
+            flops=0, bytes_accessed=8 * count * rows * width, transcendentals=0
         ),
         name="gather_parts",
     )(rank.reshape(1), *parts)
@@ -817,11 +809,16 @@
     )(rank.reshape(1), *[pieces[d] for d in message_order(len(pieces))], given, sinogram)
 
 
+def partner(values, axis, d):
+    count = lax.axis_size(axis)
+    return lax.ppermute(values, axis, [(i, i ^ d) for i in range(count)])
+
+
 def exchange(pieces, axis):
     count = len(pieces)
     results = list(pieces)
     for d in range(count - 1, 0, -1):
-        results[d] = lax.ppermute(pieces[d], axis, [(i, i ^ d) for i in range(count)])
+        results[d] = partner(pieces[d], axis, d)
     return results
 
 
@@ -856,9 +853,11 @@
     sirt = Sirt(angles.reshape(-1), vol_list, padded, slots, n_ray, step_size)
     start, predicted, gain = sirt.first(own_volume)
     own_rays, parts, start = lax.optimization_barrier((own_rays, parts, start))
-    parts = exchange(parts, "slab")
+    share = parts[0].shape[0] // 2
+    parts = [partner(part, "slab", 2 * j) if j else part for j, part in enumerate(parts)]
+    swapped = [partner(parts[0][share:], "slab", 1)]
     pieces = sirt.second(ray_rank, own_volume, start, predicted, gain, own_rays)
-    pieces, parts = lax.optimization_barrier((pieces, parts))
+    pieces, parts, swapped = lax.optimization_barrier((pieces, parts, swapped))
     if padded != slices:
         narrow = []
         for piece in pieces:
@@ -867,6 +866,8 @@
             narrow.append(jnp.concatenate([piece[: slices * slots], lower], axis=0))
         pieces = narrow
     pieces = exchange(pieces, "ray")
+    swapped += [partner(part[share:], "slab", 1) for part in parts[1:]]
+    parts = [part for two in zip(parts, swapped) for part in two]
     sinogram, given = gather_parts(parts, rank)
     if padded == slices:
         reconstruction, residual = finish(pieces, given, sinogram, ray_rank, volume.shape)

time: 86.1 us -> 87.2 us (1.013)
  waiting for transfers between devices: 15.8 us -> 17.1 us
    ppermute x10, waiting for transfers between devices: 10.5 us -> 11.9 us  [partner(): return lax.ppermute(values, axis, [(i, i ^ d) for i in range(count)])]
  transfers between devices with their start and end apart: 12 -> 12, of which waited for: 5 -> 5; matrix products, arithmetic and copies ran while one was open for 0% -> 0% of each run, Pallas kernels for 50% -> 49%
where the time goes in v16:
time: 87.2 us; the launch traced here: 86.8 us
  Pallas kernels  43.3 us (50%)
  starting transfers between devices  23.9 us (27%)
  waiting for transfers between devices  17.1 us (20%)
  local copies, waits for them, and re-layouts  1.26 us (1%)
  between operations  1.02 us (1%)
    pallas_call x2, Pallas kernels, call(): pl.pallas_call(kernel, out_shape=[jax.ShapeDtypeStruct(*value) for value...  31.9 us
    ppermute x10, starting transfers between devices, partner(): return lax.ppermute(values, axis, [(i, i ^ d) for i in range(count)])  12.7 us
    ppermute x10, waiting for transfers between devices, partner(): return lax.ppermute(values, axis, [(i, i ^ d) for i in range(count)])  11.9 us
    all_to_all x2, starting transfers between devices, to_all(): return lax.all_to_all(values, axes, split_axis=0, concat_axis=0, tiled=True)  11.1 us
    pallas_call x1, Pallas kernels, paganin(): pl.pallas_call(filter_kernel, out_shape=[jax.ShapeDtypeStruct((2 * height...  9.09 us
    all_to_all x2, waiting for transfers between devices, to_all(): return lax.all_to_all(values, axes, split_axis=0, concat_axis=0, tiled=True)  5.25 us
  transfers between devices with their start and end apart: 12, of which 5 were waited for; matrix products, arithmetic and copies ran while one was open for 0% of the time, Pallas kernels for 49%

profile of v16, /device:TPU:0, one launch (start us, length us, event | category | flops | bytes accessed | tf_op | source)
XLA Modules:
  0.0 86.8 jit_solution(5958638891017624184)
XLA Ops:
  0.6 7.3 %all-to-all-start = ((f32[8,64,256]{2,1,0:T(8,128)}), f32[8,64,256]{2,1,0:T(8,128)S(1)}, u32[]{:S(2)}, u32[]{:S(2)}) async-start(f32[8,64,256]{2,1,0:T(8,128)} %bitcast.9), calls=%async_computation | async-start | bytes 1048576 | tf_op jit(solution)/shard_map/all_to_all | solution.py:839
  7.9 0.1 sub.24
  8.0 0.0 copy-start.2
  8.0 0.0 copy-start.3
  8.0 0.0 copy-start.4
  8.0 9.1 %paganin.1 = (f32[128,2048]{1,0:T(8,128)}, f32[128,2048]{1,0:T(8,128)}, f32[256,256]{1,0:T(8,128)}) custom-call(s32[1]{0:T(128)} %bitcast.1.rank_ref, f32[256,2048]{1,0:T(8,128)} %bitcast.11, f32[264,256]{1,0:T(8,128)} %constant.78.clone.given_ref), custom_call_target="tpu_custom_call" | custom-call | flops 8589934592 | bytes 4194304 | tf_op jit(solution)/shard_map/paganin/pallas_call | solution.py:194
  17.1 5.2 %all-to-all-done.vol_ref = f32[8,64,256]{2,1,0:T(8,128)S(1)} async-done(((f32[8,64,256]{2,1,0:T(8,128)}), f32[8,64,256]{2,1,0:T(8,128)S(1)}, u32[]{:S(2)}, u32[]{:S(2)}) %all-to-all-start) | async-done | bytes 524320 | tf_op jit(solution)/shard_map/all_to_all | solution.py:839
  22.4 0.0 copy-done.9
  22.4 0.1 select_reduce_fusion.slot_ref
  22.5 0.0 copy-done.6
  22.5 0.1 cos.6.cos_ref
  22.6 0.1 sin.6.sin_ref
  22.7 3.9 %all-to-all-start.1 = ((f32[32,8,256]{2,1,0:T(8,128)}), f32[32,8,256]{2,1,0:T(8,128)S(1)}, u32[]{:S(2)}, u32[]{:S(2)}) async-start(f32[32,8,256]{2,1,0:T(8,128)} %bitcast.10), calls=%async_computation.1 | async-start | bytes 524288 | tf_op jit(solution)/shard_map/all_to_all | solution.py:839
  26.6 0.0 copy-done.7
  26.6 0.0 copy-done.8
  26.6 0.1 add_add_fusion
  26.7 0.1 add.64
  26.8 0.0 copy-done.2
  26.8 0.0 copy-done.3
  26.8 0.0 copy-start
  26.8 10.2 %first.1 = (f32[32,16,256]{2,1,0:T(8,128)S(1)}, f32[32,8,256]{2,1,0:T(8,128)S(1)}, f32[32,8,256]{2,1,0:T(8,128)S(1)}) custom-call(f32[1024]{0:T(1024)S(1)} %fusion.1.place_ref, s32[1024]{0:T(1024)S(1)} %get-tuple-element.88.offset_ref, s32[64]{0:T(128)S(1)} %select_reduce_fusion.slot_ref, f32[32]{0:T(128)S(1)} %cos.6.cos_ref, f32[32]{0:T(128)S(1)} %sin.6.sin_ref, ...), custom_call_target="tpu_custom_call" | custom-call | flops 14000000000 | bytes 4194304 | tf_op jit(solution)/shard_map/first/pallas_call | solution.py:605
  37.1 0.0 copy-done.1
  37.1 0.0 copy-start.5
  37.1 0.8 copy-done.5
  37.9 0.0 all-to-all-done.1.sino_ref
  37.9 0.1 collective-permute-start.1
  38.1 1.7 %collective-permute-start = (f32[128,2048]{1,0:T(8,128)}, f32[128,2048]{1,0:T(8,128)S(1)}, u32[]{:S(2)}, u32[]{:S(2)}) collective-permute-start(f32[128,2048]{1,0:T(8,128)} %get-tuple-element.66), channel_id=1, source_target_pairs={{0,16},{8,24},{16,0},{24,8},{1,17},{9,25},{17,1},{25,9},{2,18},{10... | collective-permute-start | bytes 3145736 | tf_op jit(solution)/shard_map/ppermute | solution.py:814
  39.7 21.7 %second.1 = (f32[88,256]{1,0:T(8,128)S(1)}, f32[88,256]{1,0:T(8,128)S(1)}, f32[88,256]{1,0:T(8,128)S(1)}, f32[88,256]{1,0:T(8,128)S(1)}, f32[88,256]{1,0:T(8,128...) custom-call(s32[1]{0:T(128)} %bitcast.rank_ref, ...), custom_call_target="tpu_custom_call" | custom-call | flops 25999998976 | bytes 4194304 | tf_op jit(solution)/shard_map/second/pallas_call | solution.py:605
  61.4 0.0 collective-permute-done.1.refs_1_
  61.4 2.4 %collective-permute-done.refs_2_ = f32[128,2048]{1,0:T(8,128)S(1)} collective-permute-done((f32[128,2048]{1,0:T(8,128)}, f32[128,2048]{1,0:T(8,128)S(1)}, u32[]{:S(2)}, u32[]{:S(2)}) %collective-permute-start) | collective-permute-done | bytes 1048608 | tf_op jit(solution)/shard_map/ppermute | solution.py:814
  63.8 0.1 collective-permute-start.9
  63.9 1.6 %collective-permute-start.2 = (f32[88,256]{1,0:T(8,128)S(1)}, f32[88,256]{1,0:T(8,128)S(1)}, u32[]{:S(2)}, u32[]{:S(2)}) collective-permute-start(f32[88,256]{1,0:T(8,128)S(1)} %get-tuple-element.67), channel_id=1, source_target_pairs={{0,1},{1,0},{2,3},{3,2},{4,5},{5,4},{6,7},{7,6},{8,9},{9,8},{10,11... | collective-permute-start | bytes 270344 | tf_op jit(solution)/shard_map/ppermute | solution.py:814
  65.5 1.5 %collective-permute-start.3 = (f32[88,256]{1,0:T(8,128)S(1)}, f32[88,256]{1,0:T(8,128)S(1)}, u32[]{:S(2)}, u32[]{:S(2)}) collective-permute-start(f32[88,256]{1,0:T(8,128)S(1)} %get-tuple-element.68), channel_id=1, source_target_pairs={{0,2},{1,3},{2,0},{3,1},{4,6},{5,7},{6,4},{7,5},{8,10},{9,11},{10,... | collective-permute-start | bytes 270344 | tf_op jit(solution)/shard_map/ppermute | solution.py:814
  67.0 2.4 %collective-permute-start.4 = (f32[88,256]{1,0:T(8,128)S(1)}, f32[88,256]{1,0:T(8,128)S(1)}, u32[]{:S(2)}, u32[]{:S(2)}) collective-permute-start(f32[88,256]{1,0:T(8,128)S(1)} %get-tuple-element.69), channel_id=1, source_target_pairs={{0,7},{1,6},{2,5},{3,4},{4,3},{5,2},{6,1},{7,0},{8,15},{9,14},{10,... | collective-permute-start | bytes 270344 | tf_op jit(solution)/shard_map/ppermute | solution.py:814
  69.4 1.5 %collective-permute-start.5 = (f32[88,256]{1,0:T(8,128)S(1)}, f32[88,256]{1,0:T(8,128)S(1)}, u32[]{:S(2)}, u32[]{:S(2)}) collective-permute-start(f32[88,256]{1,0:T(8,128)S(1)} %get-tuple-element.70), channel_id=1, source_target_pairs={{0,6},{1,7},{2,4},{3,5},{4,2},{5,3},{6,0},{7,1},{8,14},{9,15},{10,... | collective-permute-start | bytes 270344 | tf_op jit(solution)/shard_map/ppermute | solution.py:814
  70.8 0.0 collective-permute-done.2.refs_0_
  70.8 1.5 %collective-permute-start.6 = (f32[88,256]{1,0:T(8,128)S(1)}, f32[88,256]{1,0:T(8,128)S(1)}, u32[]{:S(2)}, u32[]{:S(2)}) collective-permute-start(f32[88,256]{1,0:T(8,128)S(1)} %get-tuple-element.71), channel_id=1, source_target_pairs={{0,5},{1,4},{2,7},{3,6},{4,1},{5,0},{6,3},{7,2},{8,13},{9,12},{10,... | collective-permute-start | bytes 270344 | tf_op jit(solution)/shard_map/ppermute | solution.py:814
  72.4 0.0 collective-permute-done.3.refs_1_
  72.4 2.3 %collective-permute-start.7 = (f32[88,256]{1,0:T(8,128)S(1)}, f32[88,256]{1,0:T(8,128)S(1)}, u32[]{:S(2)}, u32[]{:S(2)}) collective-permute-start(f32[88,256]{1,0:T(8,128)S(1)} %get-tuple-element.72), channel_id=1, source_target_pairs={{0,4},{1,5},{2,6},{3,7},{4,0},{5,1},{6,2},{7,3},{8,12},{9,13},{10,... | collective-permute-start | bytes 270344 | tf_op jit(solution)/shard_map/ppermute | solution.py:814
  74.7 0.0 collective-permute-done.9.refs_3_
  74.7 0.1 collective-permute-start.8
  74.7 1.3 %gather_parts.1 = (f32[4,64,2048]{2,1,0:T(8,128)}, f32[4,64,256]{2,1,0:T(8,128)S(1)}) custom-call(s32[1]{0:T(128)} %bitcast.1.rank_ref, f32[128,2048]{1,0:T(8,128)S(1)} %copy-done, f32[64,2048]{1,0:T(8,128)S(1)} %collective-permute-done.1.refs_1_, f32[128,2048]{1,0:T(8,128)S(1)} %collective-permute-done.refs_2_, f32[64,2048]{1,0:T(8,128)S(1)} %collective-permute-done.9.refs_3_), custom_call_target="tpu_custom_call" | custom-call | bytes 4194304 | tf_op jit(solution)/shard_map/gather_parts/pallas_call | solution.py:725
  76.1 0.0 collective-permute-done.4.refs_2_
  76.1 0.7 collective-permute-done.5.refs_3_
  76.8 7.4 %collective-permute-done.6.refs_4_ = f32[88,256]{1,0:T(8,128)S(1)} collective-permute-done((f32[88,256]{1,0:T(8,128)S(1)}, f32[88,256]{1,0:T(8,128)S(1)}, u32[]{:S(2)}, u32[]{:S(2)}) %collective-permute-start.6) | collective-permute-done | bytes 90144 | tf_op jit(solution)/shard_map/ppermute | solution.py:814
  84.2 1.5 %collective-permute-done.7.refs_5_ = f32[88,256]{1,0:T(8,128)S(1)} collective-permute-done((f32[88,256]{1,0:T(8,128)S(1)}, f32[88,256]{1,0:T(8,128)S(1)}, u32[]{:S(2)}, u32[]{:S(2)}) %collective-permute-start.7) | collective-permute-done | bytes 90144 | tf_op jit(solution)/shard_map/ppermute | solution.py:814
  85.6 0.0 collective-permute-done.8.refs_6_
  85.6 1.0 %finish.1 = (f32[64,8,256]{2,1,0:T(8,128)}, f32[4,64,2048]{2,1,0:T(8,128)}) custom-call(s32[1]{0:T(128)} %bitcast.rank_ref, f32[88,256]{1,0:T(8,128)S(1)} %collective-permute-done.2.refs_0_, f32[88,256]{1,0:T(8,128)S(1)} %collective-permute-done.3.refs_1_, f32[88,256]{1,0:T(8,128)S(1)} %collective-permute-done.4.refs_2_, ...), custom_call_target="tpu_custom_call", output_to_operand_aliasing={{1}: (10, {})} | custom-call | bytes 1441792 | tf_op jit(solution)/shard_map/finish/pallas_call | solution.py:788
  (14 shorter events, 0.2 us)
Async XLA Ops:
  0.6 21.8 %all-to-all-start = ((f32[8,64,256]{2,1,0:T(8,128)}), f32[8,64,256]{2,1,0:T(8,128)S(1)}, u32[]{:S(2)}, u32[]{:S(2)}) async-start(f32[8,64,256]{2,1,0:T(8,128)} %bitcast.9), calls=%async_computation | async-start | bytes 1048576 | tf_op jit(solution)/shard_map/all_to_all | solution.py:839
  8.0 14.4 %copy-start.9 = (s32[64]{0:T(128)S(1)}, s32[64]{0:T(128)}, u32[]{:S(2)}) copy-start(s32[64]{0:T(128)} %param.13) | copy-start | bytes 772
  8.0 14.5 %copy-start.6 = (f32[4,8]{1,0:T(4,128)S(1)}, f32[4,8]{1,0:T(4,128)}, u32[]{:S(2)}) copy-start(f32[4,8]{1,0:T(4,128)} %param.11) | copy-start | bytes 388
  8.0 18.6 %copy-start.7 = (f32[32]{0:T(128)S(1)}, f32[32]{0:T(128)}, u32[]{:S(2)}) copy-start(f32[32]{0:T(128)} %constant.86) | copy-start | bytes 388
  8.0 18.6 %copy-start.8 = (f32[32]{0:T(128)S(1)}, f32[32]{0:T(128)}, u32[]{:S(2)}) copy-start(f32[32]{0:T(128)} %constant.85) | copy-start | bytes 388
  8.0 18.8 %copy-start.2 = (bf16[256,256]{1,0:T(8,128)(2,1)S(1)}, bf16[256,256]{1,0:T(8,128)(2,1)}, u32[]{:S(2)}) copy-start(bf16[256,256]{1,0:T(8,128)(2,1)} %constant.81.clone.flip_ref) | copy-start | bytes 393220
  8.0 18.8 %copy-start.3 = (f32[8,256]{1,0:T(8,128)S(1)}, f32[8,256]{1,0:T(8,128)}, u32[]{:S(2)}) copy-start(f32[8,256]{1,0:T(8,128)} %constant.83.clone.shift_y_ref) | copy-start | bytes 24580
  8.0 18.8 %copy-start.4 = (f32[8,256]{1,0:T(8,128)S(1)}, f32[8,256]{1,0:T(8,128)}, u32[]{:S(2)}) copy-start(f32[8,256]{1,0:T(8,128)} %constant.82.clone.shift_x_ref) | copy-start | bytes 24580
  22.4 14.7 %copy-start.1 = (f32[8,64,256]{2,1,0:T(8,128)}, f32[8,64,256]{2,1,0:T(8,128)S(1)}, u32[]{:S(2)}) copy-start(f32[8,64,256]{2,1,0:T(8,128)S(1)} %all-to-all-done.vol_ref) | copy-start | bytes 1572868
  22.7 15.2 %all-to-all-start.1 = ((f32[32,8,256]{2,1,0:T(8,128)}), f32[32,8,256]{2,1,0:T(8,128)S(1)}, u32[]{:S(2)}, u32[]{:S(2)}) async-start(f32[32,8,256]{2,1,0:T(8,128)} %bitcast.10), calls=%async_computation.1 | async-start | bytes 524288 | tf_op jit(solution)/shard_map/all_to_all | solution.py:839
  26.8 11.0 %copy-start = (f32[128,2048]{1,0:T(8,128)S(1)}, f32[128,2048]{1,0:T(8,128)}, u32[]{:S(2)}) copy-start(f32[128,2048]{1,0:T(8,128)} %get-tuple-element.75.refs_0_) | copy-start | bytes 3145732
  37.1 0.8 copy-start.5
  37.9 23.5 %collective-permute-start.1 = (f32[64,2048]{1,0:T(8,128)S(1)}, f32[64,2048]{1,0:T(8,128)S(1)}, u32[]{:S(2)}, u32[]{:S(2)}) collective-permute-start(f32[64,2048]{1,0:T(8,128)S(1)} %slice.6), channel_id=1, source_target_pairs={{0,8},{8,0},{16,24},{24,16},{1,9},{9,1},{17,25},{25,17},{2,10},{10... | collective-permute-start | bytes 1572872 | tf_op jit(solution)/shard_map/ppermute | solution.py:814
  38.1 25.7 %collective-permute-start = (f32[128,2048]{1,0:T(8,128)}, f32[128,2048]{1,0:T(8,128)S(1)}, u32[]{:S(2)}, u32[]{:S(2)}) collective-permute-start(f32[128,2048]{1,0:T(8,128)} %get-tuple-element.66), channel_id=1, source_target_pairs={{0,16},{8,24},{16,0},{24,8},{1,17},{9,25},{17,1},{25,9},{2,18},{10... | collective-permute-start | bytes 3145736 | tf_op jit(solution)/shard_map/ppermute | solution.py:814
  63.8 10.8 %collective-permute-start.9 = (f32[64,2048]{1,0:T(8,128)S(1)}, f32[64,2048]{1,0:T(8,128)S(1)}, u32[]{:S(2)}, u32[]{:S(2)}) collective-permute-start(f32[64,2048]{1,0:T(8,128)S(1)} %slice.7), channel_id=1, source_target_pairs={{0,8},{8,0},{16,24},{24,16},{1,9},{9,1},{17,25},{25,17},{2,10},{10... | collective-permute-start | bytes 1572872 | tf_op jit(solution)/shard_map/ppermute | solution.py:814
  63.9 6.9 %collective-permute-start.2 = (f32[88,256]{1,0:T(8,128)S(1)}, f32[88,256]{1,0:T(8,128)S(1)}, u32[]{:S(2)}, u32[]{:S(2)}) collective-permute-start(f32[88,256]{1,0:T(8,128)S(1)} %get-tuple-element.67), channel_id=1, source_target_pairs={{0,1},{1,0},{2,3},{3,2},{4,5},{5,4},{6,7},{7,6},{8,9},{9,8},{10,11... | collective-permute-start | bytes 270344 | tf_op jit(solution)/shard_map/ppermute | solution.py:814
  65.5 6.8 %collective-permute-start.3 = (f32[88,256]{1,0:T(8,128)S(1)}, f32[88,256]{1,0:T(8,128)S(1)}, u32[]{:S(2)}, u32[]{:S(2)}) collective-permute-start(f32[88,256]{1,0:T(8,128)S(1)} %get-tuple-element.68), channel_id=1, source_target_pairs={{0,2},{1,3},{2,0},{3,1},{4,6},{5,7},{6,4},{7,5},{8,10},{9,11},{10,... | collective-permute-start | bytes 270344 | tf_op jit(solution)/shard_map/ppermute | solution.py:814
  67.0 9.1 %collective-permute-start.4 = (f32[88,256]{1,0:T(8,128)S(1)}, f32[88,256]{1,0:T(8,128)S(1)}, u32[]{:S(2)}, u32[]{:S(2)}) collective-permute-start(f32[88,256]{1,0:T(8,128)S(1)} %get-tuple-element.69), channel_id=1, source_target_pairs={{0,7},{1,6},{2,5},{3,4},{4,3},{5,2},{6,1},{7,0},{8,15},{9,14},{10,... | collective-permute-start | bytes 270344 | tf_op jit(solution)/shard_map/ppermute | solution.py:814
  69.4 7.4 %collective-permute-start.5 = (f32[88,256]{1,0:T(8,128)S(1)}, f32[88,256]{1,0:T(8,128)S(1)}, u32[]{:S(2)}, u32[]{:S(2)}) collective-permute-start(f32[88,256]{1,0:T(8,128)S(1)} %get-tuple-element.70), channel_id=1, source_target_pairs={{0,6},{1,7},{2,4},{3,5},{4,2},{5,3},{6,0},{7,1},{8,14},{9,15},{10,... | collective-permute-start | bytes 270344 | tf_op jit(solution)/shard_map/ppermute | solution.py:814
  70.8 13.3 %collective-permute-start.6 = (f32[88,256]{1,0:T(8,128)S(1)}, f32[88,256]{1,0:T(8,128)S(1)}, u32[]{:S(2)}, u32[]{:S(2)}) collective-permute-start(f32[88,256]{1,0:T(8,128)S(1)} %get-tuple-element.71), channel_id=1, source_target_pairs={{0,5},{1,4},{2,7},{3,6},{4,1},{5,0},{6,3},{7,2},{8,13},{9,12},{10,... | collective-permute-start | bytes 270344 | tf_op jit(solution)/shard_map/ppermute | solution.py:814
  72.4 13.3 %collective-permute-start.7 = (f32[88,256]{1,0:T(8,128)S(1)}, f32[88,256]{1,0:T(8,128)S(1)}, u32[]{:S(2)}, u32[]{:S(2)}) collective-permute-start(f32[88,256]{1,0:T(8,128)S(1)} %get-tuple-element.72), channel_id=1, source_target_pairs={{0,4},{1,5},{2,6},{3,7},{4,0},{5,1},{6,2},{7,3},{8,12},{9,13},{10,... | collective-permute-start | bytes 270344 | tf_op jit(solution)/shard_map/ppermute | solution.py:814
  74.7 11.0 %collective-permute-start.8 = (f32[88,256]{1,0:T(8,128)S(1)}, f32[88,256]{1,0:T(8,128)S(1)}, u32[]{:S(2)}, u32[]{:S(2)}) collective-permute-start(f32[88,256]{1,0:T(8,128)S(1)} %get-tuple-element.73), channel_id=1, source_target_pairs={{0,3},{1,2},{2,1},{3,0},{4,7},{5,6},{6,5},{7,4},{8,11},{9,10},{10,... | collective-permute-start | bytes 270344 | tf_op jit(solution)/shard_map/ppermute | solution.py:814
